TPU v7x, 32 devices: a whole 2x2x4 slice. The times are simulated.
32 devices in a mesh: dp: 16 (over z, x, core), tensor: 2 (over y).
Axes of the slice: x: 2, y: 2, z: 4, core: 2. Of those that a mesh axis runs over, the one named last changes fastest.
Arguments:
- block_in: bfloat16 [32, 256, 768], P('dp'), may hold values from -7.2 to 7.2
- out_grad: bfloat16 [32, 256, 768], P('dp'), may hold values from -6 to 6
- segments: int32 [32, 256], P('dp'), may hold values from 0 to 3, never falling along the last dimension, each value on 1 to 128 neighbouring positions
- weights: float32 [2, 2, 3538944], P(None, 'tensor', 'dp'), may hold values from -0.57735027 to 0.57735027
- weights_first: float32 [2, 2, 3538944], P(None, 'tensor', 'dp'), may hold values from -0.00390625 to 0.00390625
- weights_second: float32 [2, 2, 3538944], P(None, 'tensor', 'dp'), may hold values from 7.064254e-08 to 2.8257017e-07
- split_vectors: float32 [2, 2, 2304], P(None, 'tensor', 'dp'), may hold values from -1.2 to 1.2
- split_first: float32 [2, 2, 2304], P(None, 'tensor', 'dp'), may hold values from -0.01171875 to 0.01171875
- split_second: float32 [2, 2, 2304], P(None, 'tensor', 'dp'), may hold values from 6.357829e-07 to 2.5431316e-06
- rep_vectors: float32 [2, 6, 768], P(None, None, 'dp'), may hold values from -0.9 to 2.2
- rep_first: float32 [2, 6, 768], P(None, None, 'dp'), may hold values from -0.01171875 to 0.01171875
- rep_second: float32 [2, 6, 768], P(None, None, 'dp'), may hold values from 6.357829e-07 to 2.5431316e-06
Outputs:
- block_out: bfloat16 [32, 256, 768], P('dp')
- input_grad: float32 [32, 256, 768], P('dp')
- grad_norm: float32 [], replicated
- new_weights: float32 [2, 2, 3538944], P(None, 'tensor', 'dp')
- weights_first_new: float32 [2, 2, 3538944], P(None, 'tensor', 'dp')
- weights_second_new: float32 [2, 2, 3538944], P(None, 'tensor', 'dp')
- weights_low: bfloat16 [2, 2, 3538944], P(None, 'tensor', 'dp')
- new_split: float32 [2, 2, 2304], P(None, 'tensor', 'dp')
- split_first_new: float32 [2, 2, 2304], P(None, 'tensor', 'dp')
- split_second_new: float32 [2, 2, 2304], P(None, 'tensor', 'dp')
- split_low: bfloat16 [2, 2, 2304], P(None, 'tensor', 'dp')
- new_rep: float32 [2, 6, 768], P(None, None, 'dp')
- rep_first_new: float32 [2, 6, 768], P(None, None, 'dp')
- rep_second_new: float32 [2, 6, 768], P(None, None, 'dp')
- rep_low: bfloat16 [2, 6, 768], P(None, None, 'dp')
- output_bias_grad: float32 [2, 768], P(None, 'dp')
Inputs may be any that keep to these rules, and one draw needn't show every extreme that they name: `segments`: segment numbers never fall along a row.
All inputs are finite; a program needn't handle non-finite values.
Results may differ from a plain program's by a relative error of at most 0.038.
Values may be sent and summed in bfloat16 or wider, within the bound.
No kernel may reach another device: no remote copies, remote signals or barrier semaphores. Data moves between devices by JAX's collectives and lax.ppermute only.
A program may use at most 192 MiB of HBM per device.

v0:
```python
from functools import partial

import jax
import jax.numpy as jnp
from jax import lax
from jax.sharding import PartitionSpec as P

D = 768
HEAD_DIM = 64
FF = 3072
LAYERS = 2
SEQ = 256
MICRO = 2
STEP = 3


clip_limit = 1.0
weight_rate = 0.03
weight_decay = 0.01
vector_rate = 0.3
lane_width = 128
contract_last = (((1,), (1,)), ((), ()))
contract_first = (((0,), (0,)), ((), ()))


def norm_rows(value, gain, shift):
    center = value - jnp.mean(value, axis=-1, keepdims=True)
    scale = lax.rsqrt(jnp.mean(center * center, axis=-1, keepdims=True) + 1e-12)
    normed = center * scale
    return (normed * gain + shift, normed, scale)


def norm_back(grad_out, normed, scale, gain):
    inner = grad_out * gain
    back = scale * (
        inner
        - jnp.mean(inner, axis=-1, keepdims=True)
        - normed * jnp.mean(inner * normed, axis=-1, keepdims=True)
    )
    return (back, jnp.sum(grad_out * normed, axis=0), jnp.sum(grad_out, axis=0))


def four_dims(flat_rows, row_count):
    return flat_rows.reshape(row_count, SEQ, flat_rows.shape[1] // HEAD_DIM, HEAD_DIM)


def attend_scores(query_four, keys_four, same):
    scores = jnp.einsum(
        "bqhe,bkhe->bhqk", query_four, keys_four, preferred_element_type=jnp.float32
    ) * HEAD_DIM ** (-0.5)
    return jnp.where(same, scores, -1000000000.0)


def attend_forward(query, keys_in, values_in, same):
    row_count = same.shape[0]
    scores = attend_scores(four_dims(query, row_count), four_dims(keys_in, row_count), same)
    highest = jnp.max(scores, axis=-1, keepdims=True)
    raised = jnp.exp(scores - highest)
    totals = jnp.sum(raised, axis=-1, keepdims=True)
    probs_low = (raised / totals).astype(jnp.bfloat16)
    context = jnp.einsum(
        "bhqk,bkhe->bqhe",
        probs_low,
        four_dims(values_in, row_count),
        preferred_element_type=jnp.float32,
    )
    return (context.reshape(query.shape).astype(jnp.bfloat16), highest + jnp.log(totals))


def attend_backward(grad_context, query, keys_in, values_in, log_total, same):
    row_count = same.shape[0]
    query_four = four_dims(query, row_count)
    keys_four = four_dims(keys_in, row_count)
    values_four = four_dims(values_in, row_count)
    grad_four = four_dims(grad_context, row_count)
    probs = jnp.exp(attend_scores(query_four, keys_four, same) - log_total)
    grad_probs = jnp.einsum(
        "bqhe,bkhe->bhqk", grad_four, values_four, preferred_element_type=jnp.float32
    )
    centered = grad_probs - jnp.sum(probs * grad_probs, axis=-1, keepdims=True)
    grad_scores = (probs * centered).astype(jnp.bfloat16)
    factor = HEAD_DIM ** (-0.5)
    grad_query = (
        jnp.einsum("bhqk,bkhe->bqhe", grad_scores, keys_four, preferred_element_type=jnp.float32)
        * factor
    ).astype(jnp.bfloat16)
    grad_keys = (
        jnp.einsum("bhqk,bqhe->bkhe", grad_scores, query_four, preferred_element_type=jnp.float32)
        * factor
    ).astype(jnp.bfloat16)
    grad_values = jnp.einsum(
        "bhqk,bqhe->bkhe", probs.astype(jnp.bfloat16), grad_four, preferred_element_type=jnp.float32
    ).astype(jnp.bfloat16)
    return (
        grad_query.reshape(query.shape),
        grad_keys.reshape(query.shape),
        grad_values.reshape(query.shape),
    )


def layer_forward(hidden, same, blocks, vector, repeated):
    w_qkv, w_out, w_up, w_down = blocks
    head_cols = w_out.shape[1]
    entry = hidden.astype(jnp.bfloat16)
    mixed = jnp.dot(entry, w_qkv, preferred_element_type=jnp.float32)
    query = (mixed[:, :head_cols] + vector[:head_cols]).astype(jnp.bfloat16)
    keys_in = mixed[:, head_cols : 2 * head_cols].astype(jnp.bfloat16)
    values_in = (
        mixed[:, 2 * head_cols : 3 * head_cols] + vector[head_cols : 2 * head_cols]
    ).astype(jnp.bfloat16)
    context, log_total = attend_forward(query, keys_in, values_in, same)
    attn_part = lax.dot_general(
        context, w_out, contract_last, preferred_element_type=jnp.float32
    ).astype(jnp.bfloat16)
    attn_out = lax.psum(attn_part, "tensor").astype(jnp.float32)
    first, normed_one, scale_one = norm_rows(
        hidden + attn_out + repeated[0], repeated[1], repeated[2]
    )
    first_low = first.astype(jnp.bfloat16)
    inner = jnp.dot(first_low, w_up, preferred_element_type=jnp.float32) + vector[2 * head_cols :]
    active = jax.nn.gelu(inner, approximate=False).astype(jnp.bfloat16)
    ffn_part = lax.dot_general(
        active, w_down, contract_last, preferred_element_type=jnp.float32
    ).astype(jnp.bfloat16)
    ffn_out = lax.psum(ffn_part, "tensor").astype(jnp.float32)
    result, normed_two, scale_two = norm_rows(
        first + ffn_out + repeated[3], repeated[4], repeated[5]
    )
    kept = (
        entry,
        query,
        keys_in,
        values_in,
        log_total,
        context,
        normed_one,
        scale_one,
        first_low,
        inner,
        active,
        normed_two,
        scale_two,
    )
    return (result, kept)


def layer_backward(grad_out, kept, same, blocks, repeated):
    w_qkv, w_out, w_up, w_down = blocks
    (
        entry,
        query,
        keys_in,
        values_in,
        log_total,
        context,
        normed_one,
        scale_one,
        first_low,
        inner,
        active,
        normed_two,
        scale_two,
    ) = kept
    back_two, gain_two, shift_two = norm_back(grad_out, normed_two, scale_two, repeated[4])
    grad_ffn = back_two.astype(jnp.bfloat16)
    grad_active = jnp.dot(grad_ffn, w_down, preferred_element_type=jnp.float32)
    unused, gelu_pull = jax.vjp(partial(jax.nn.gelu, approximate=False), inner)
    grad_inner = gelu_pull(grad_active)[0].astype(jnp.bfloat16)
    ffn_back = lax.dot_general(
        grad_inner, w_up, contract_last, preferred_element_type=jnp.float32
    ).astype(jnp.bfloat16)
    grad_first = back_two + lax.psum(ffn_back, "tensor").astype(jnp.float32)
    back_one, gain_one, shift_one = norm_back(grad_first, normed_one, scale_one, repeated[1])
    grad_attn = back_one.astype(jnp.bfloat16)
    grad_context = jnp.dot(grad_attn, w_out, preferred_element_type=jnp.float32).astype(
        jnp.bfloat16
    )
    grad_query, grad_keys, grad_values = attend_backward(
        grad_context, query, keys_in, values_in, log_total, same
    )
    grad_mixed = jnp.concatenate([grad_query, grad_keys, grad_values], axis=1)
    attn_back = lax.dot_general(
        grad_mixed, w_qkv, contract_last, preferred_element_type=jnp.float32
    ).astype(jnp.bfloat16)
    grad_hidden = back_one + lax.psum(attn_back, "tensor").astype(jnp.float32)
    operands = (entry, grad_mixed, grad_attn, context, first_low, grad_inner, grad_ffn, active)
    vector_grad = jnp.concatenate(
        [
            jnp.sum(grad_query.astype(jnp.float32), axis=0),
            jnp.sum(grad_values.astype(jnp.float32), axis=0),
            jnp.sum(grad_inner.astype(jnp.float32), axis=0),
        ]
    )
    repeat_grad = jnp.stack(
        [
            jnp.sum(back_one, axis=0),
            gain_one,
            shift_one,
            jnp.sum(back_two, axis=0),
            gain_two,
            shift_two,
        ]
    )
    return (grad_hidden, operands, vector_grad, repeat_grad)


def matrix_gradient(stored):
    joined = [
        jnp.concatenate([entry_set[position] for entry_set in stored], axis=0)
        for position in range(8)
    ]
    pieces = []
    for pair_index in range(4):
        pieces.append(
            lax.dot_general(
                joined[2 * pair_index],
                joined[2 * pair_index + 1],
                contract_first,
                preferred_element_type=jnp.float32,
            )
        )
    return jnp.concatenate(pieces, axis=1)


def adamw(value, first, second, grad, rate, decay):
    first = 0.5 * first + 0.5 * grad
    second = 0.5 * second + 0.5 * grad * grad
    correct = 1.0 - 0.5**STEP
    direction = first / correct / (jnp.sqrt(second / correct) + 1e-08)
    return (value - rate * (direction + decay * value), first, second)


def per_device(
    block_in,
    out_grad,
    segments,
    weights,
    weights_first,
    weights_second,
    split_vectors,
    split_first,
    split_second,
    rep_vectors,
    rep_first,
    rep_second,
):
    head_cols = D // lax.axis_size("tensor")
    hidden_cols = FF // lax.axis_size("tensor")
    shard_shape = weights.shape
    tiled_shape = (LAYERS, -1, lane_width)
    weights_tiled = weights.reshape(tiled_shape)
    matrix_all, vector_all, repeat_all = (
        lax.all_gather(weights_tiled.astype(jnp.bfloat16), "dp", axis=1, tiled=True),
        lax.all_gather(split_vectors.astype(jnp.bfloat16), "dp", axis=2, tiled=True),
        lax.all_gather(rep_vectors.astype(jnp.bfloat16), "dp", axis=2, tiled=True),
    )
    blocks_all = []
    for layer_index in range(LAYERS):
        matrix = matrix_all[layer_index].reshape(D, -1)
        blocks_all.append(
            (
                matrix[:, : 3 * head_cols],
                matrix[:, 3 * head_cols : 4 * head_cols],
                matrix[:, 4 * head_cols : 4 * head_cols + hidden_cols],
                matrix[:, 4 * head_cols + hidden_cols :],
            )
        )
    vectors = [vector_all[layer_index, 0].astype(jnp.float32) for layer_index in range(LAYERS)]
    repeats = [repeat_all[layer_index].astype(jnp.float32) for layer_index in range(LAYERS)]
    per_batch = block_in.shape[0] // MICRO
    matrix_grads = [None] * LAYERS
    stored = [[] for layer_index in range(LAYERS)]
    vector_grads = [jnp.zeros(vectors[0].shape, jnp.float32) for layer_index in range(LAYERS)]
    repeat_grads = [jnp.zeros((6, D), jnp.float32) for layer_index in range(LAYERS)]
    outputs = []
    in_grads = []
    for micro_index in range(MICRO):
        lower = micro_index * per_batch
        hidden = block_in[lower : lower + per_batch].reshape(per_batch * SEQ, D).astype(jnp.float32)
        seg_rows = segments[lower : lower + per_batch]
        same = (seg_rows[:, :, None] == seg_rows[:, None, :])[:, None]
        kept_all = []
        for layer_index in range(LAYERS):
            hidden, kept = layer_forward(
                hidden, same, blocks_all[layer_index], vectors[layer_index], repeats[layer_index]
            )
            kept_all.append(kept)
        outputs.append(hidden.astype(jnp.bfloat16).reshape(per_batch, SEQ, D))
        grad_hidden = (
            out_grad[lower : lower + per_batch].reshape(per_batch * SEQ, D).astype(jnp.float32)
        )
        for layer_index in reversed(range(LAYERS)):
            grad_hidden, operands, vector_grad, repeat_grad = layer_backward(
                grad_hidden,
                kept_all[layer_index],
                same,
                blocks_all[layer_index],
                repeats[layer_index],
            )
            stored[layer_index].append(operands)
            vector_grads[layer_index] = vector_grads[layer_index] + vector_grad
            repeat_grads[layer_index] = repeat_grads[layer_index] + repeat_grad
            if micro_index == MICRO - 1:
                matrix_grads[layer_index] = matrix_gradient(stored[layer_index])
        in_grads.append(grad_hidden.reshape(per_batch, SEQ, D))
    grad_tiled, grad_split, grad_rep = (
        lax.psum_scatter(
            jnp.stack(matrix_grads).reshape(tiled_shape), "dp", scatter_dimension=1, tiled=True
        ),
        lax.psum_scatter(
            jnp.stack(vector_grads).reshape(LAYERS, 1, -1), "dp", scatter_dimension=2, tiled=True
        ),
        lax.psum_scatter(jnp.stack(repeat_grads), "dp", scatter_dimension=2, tiled=True),
    )
    tensor_first = (lax.axis_index("tensor") == 0).astype(jnp.float32)
    local_squares = (
        jnp.sum(grad_tiled * grad_tiled)
        + jnp.sum(grad_split * grad_split)
        + tensor_first * jnp.sum(grad_rep * grad_rep)
    )
    grad_norm = jnp.sqrt(lax.psum(local_squares, ("dp", "tensor")))
    factor = jnp.minimum(1.0, clip_limit / (grad_norm + 1e-06))
    clipped_rep = grad_rep * factor
    new_tiled, first_tiled, second_tiled = adamw(
        weights_tiled,
        weights_first.reshape(tiled_shape),
        weights_second.reshape(tiled_shape),
        grad_tiled * factor,
        weight_rate,
        weight_decay,
    )
    new_weights = new_tiled.reshape(shard_shape)
    weights_first_new = first_tiled.reshape(shard_shape)
    weights_second_new = second_tiled.reshape(shard_shape)
    weights_low = new_tiled.astype(jnp.bfloat16).reshape(shard_shape)
    new_split, split_first_new, split_second_new = adamw(
        split_vectors, split_first, split_second, grad_split * factor, vector_rate, 0.0
    )
    new_rep, rep_first_new, rep_second_new = adamw(
        rep_vectors, rep_first, rep_second, clipped_rep, vector_rate, 0.0
    )
    output_bias_grad = clipped_rep[:, 0, :]
    block_out = jnp.concatenate(outputs, axis=0)
    input_grad = jnp.concatenate(in_grads, axis=0)
    return (
        block_out,
        input_grad,
        grad_norm,
        new_weights,
        weights_first_new,
        weights_second_new,
        weights_low,
        new_split,
        split_first_new,
        split_second_new,
        new_split.astype(jnp.bfloat16),
        new_rep,
        rep_first_new,
        rep_second_new,
        new_rep.astype(jnp.bfloat16),
        output_bias_grad,
    )


def solution(mesh):
    placed = (
        P("dp", None, None),
        P("dp", None, None),
        P("dp", None),
        P(None, "tensor", "dp"),
        P(None, "tensor", "dp"),
        P(None, "tensor", "dp"),
        P(None, "tensor", "dp"),
        P(None, "tensor", "dp"),
        P(None, "tensor", "dp"),
        P(None, None, "dp"),
        P(None, None, "dp"),
        P(None, None, "dp"),
    )
    return jax.shard_map(
        per_device,
        mesh=mesh,
        in_specs=placed,
        out_specs=(
            P("dp", None, None),
            P("dp", None, None),
            P(),
            P(None, "tensor", "dp"),
            P(None, "tensor", "dp"),
            P(None, "tensor", "dp"),
            P(None, "tensor", "dp"),
            P(None, "tensor", "dp"),
            P(None, "tensor", "dp"),
            P(None, "tensor", "dp"),
            P(None, "tensor", "dp"),
            P(None, None, "dp"),
            P(None, None, "dp"),
            P(None, None, "dp"),
            P(None, None, "dp"),
            P(None, "dp"),
        ),
        check_vma=False,
    )
```

profile of v0, /device:TPU:0, one launch (start us, length us, event | category | flops | bytes accessed | tf_op | source)
XLA Modules:
  0.0 1083.3 jit_solution(8171840648683022600)
XLA Ops:
  10.2 29.5 %all_gather.10 = bf16[2,1,2304]{1,0,2:T(2,128)(2,1)S(1)} all-gather(bf16[2,1,144]{1,0,2:T(2,128)(2,1)S(1)} %copy.189), channel_id=1, replica_groups=mesh['dp'=16,'tensor'=2] {'dp'}, dimensions={2}, use_global_device_ids=true | all-gather | bytes 9792 | tf_op jit(solution)/shard_map/all_gather | solution.py:254
  39.7 23.5 %all_gather.11 = bf16[2,6,768]{1,0,2:T(2,128)(2,1)} all-gather(bf16[2,6,48]{1,0,2:T(2,128)(2,1)S(1)} %copy.194), channel_id=1, replica_groups=mesh['dp'=16,'tensor'=2] {'dp'}, dimensions={2}, use_global_device_ids=true | all-gather | bytes 19584 | tf_op jit(solution)/shard_map/all_gather | solution.py:255
  70.4 59.0 %all-gather.2.cloned.1.call-done = bf16[2,27648,128]{2,1,0:T(8,128)(2,1)} async-done(((bf16[2,1728,128]{2,1,0:T(8,128)(2,1)}), bf16[2,27648,128]{2,1,0:T(8,128)(2,1)}) %all-gather.2.cloned.1.call-update) | async-done | bytes 14155792 | tf_op jit(solution)/shard_map/all_gather | solution.py:253
  129.4 10.1 fusion.303
  139.5 13.2 %reshape_squeeze.6 = bf16[768,4608]{1,0:T(8,128)(2,1)} reshape(bf16[1,27648,128]{2,1,0:T(8,128)(2,1)} %get-tuple-element.191) | data formatting | bytes 14155776 | tf_op jit(solution)/shard_map/reshape;squeeze | solution.py:259
  169.8 13.1 %slice_reduce_fusion = (f32[1536]{0:T(1024)}, f32[1536]{0:T(1024)}) fusion(f32[1,1,2304]{1,0,2:T(1,128)S(1)} %copy-done.32, f32[1,1,2304]{1,0,2:T(1,128)} %copy-done.33), kind=kLoop, calls=%fused_computation.268 | loop fusion | bytes 24576 | tf_op jit(solution)/shard_map/slice | solution.py:120
  182.9 13.7 %slice_reduce_fusion.9 = (f32[768]{0:T(1024)S(1)}, f32[768]{0:T(1024)S(1)}, f32[768]{0:T(1024)}, f32[768]{0:T(1024)}, f32[768]{0:T(1024)S(1)}, /*index=5*/f32[768]{0:T(1024)S(1)}) fusion(f32[1,6,768]{1,0,2:T(1,128)S(1)} %get-tuple-element.215), kind=kLoop, calls=%fused_computation.418 | loop fusion | bytes 36864 | tf_op jit(solution)/shard_map/slice | solution.py:127
  204.6 7.7 multiply_convert_fusion.5
  213.9 5.1 multiply_convert_fusion.7
  221.6 13.2 %reshape_squeeze.7 = bf16[768,4608]{1,0:T(8,128)(2,1)} reshape(bf16[1,27648,128]{2,1,0:T(8,128)(2,1)} %get-tuple-element.190) | data formatting | bytes 14155776 | tf_op jit(solution)/shard_map/reshape;squeeze | solution.py:259
  234.8 21.4 %all-reduce.29.cloned.1.call-done = (bf16[256,768]{1,0:T(8,128)(2,1)}, bf16[256,768]{1,0:T(8,128)(2,1)}) async-done(((bf16[256,768]{1,0:T(8,128)(2,1)}, bf16[256,768]{1,0:T(8,128)(2,1)}), (bf16[256,768]{1,0:T(8,128)(2,1)}, bf16[256,768]{1,0:T(8,128)(2,1)})) %all-reduce.29.cloned.1.call-update) | async-done | bytes 786448 | tf_op jit(solution)/shard_map/psum | solution.py:125
  290.5 13.2 %slice_reduce_fusion.3 = (f32[768]{0:T(1024)}, f32[768]{0:T(1024)}, f32[768]{0:T(1024)}, f32[768]{0:T(1024)}, f32[768]{0:T(1024)S(1)}, /*index=5*/f32[768]{0:T(1024)}) fusion(f32[1,6,768]{1,0,2:T(1,128)S(1)} %get-tuple-element.216), kind=kLoop, calls=%fused_computation.406 | loop fusion | bytes 36864 | tf_op jit(solution)/shard_map/slice | solution.py:127
  303.7 16.9 %all-reduce.27.cloned.1.call-done = (bf16[256,768]{1,0:T(8,128)(2,1)}, bf16[256,768]{1,0:T(8,128)(2,1)}) async-done(((bf16[256,768]{1,0:T(8,128)(2,1)}, bf16[256,768]{1,0:T(8,128)(2,1)}), (bf16[256,768]{1,0:T(8,128)(2,1)}, bf16[256,768]{1,0:T(8,128)(2,1)})) %all-reduce.27.cloned.1.call-update) | async-done | bytes 786448 | tf_op jit(solution)/shard_map/psum | solution.py:115
  324.0 7.6 multiply_convert_fusion.4
  333.2 5.4 multiply_convert_fusion.6
  346.2 29.4 %all-reduce.25.cloned.1.call-done = (bf16[256,768]{1,0:T(8,128)(2,1)}, bf16[256,768]{1,0:T(8,128)(2,1)}) async-done(((bf16[256,768]{1,0:T(8,128)(2,1)}, bf16[256,768]{1,0:T(8,128)(2,1)}), (bf16[256,768]{1,0:T(8,128)(2,1)}, bf16[256,768]{1,0:T(8,128)(2,1)})) %all-reduce.25.cloned.1.call-update) | async-done | bytes 786448 | tf_op jit(solution)/shard_map/psum | solution.py:125
  397.1 5.3 fusion.17
  406.1 19.9 %all-reduce.23.cloned.1.call-done = (bf16[256,768]{1,0:T(8,128)(2,1)}, bf16[256,768]{1,0:T(8,128)(2,1)}) async-done(((bf16[256,768]{1,0:T(8,128)(2,1)}, bf16[256,768]{1,0:T(8,128)(2,1)}), (bf16[256,768]{1,0:T(8,128)(2,1)}, bf16[256,768]{1,0:T(8,128)(2,1)})) %all-reduce.23.cloned.1.call-update) | async-done | bytes 786448 | tf_op jit(solution)/shard_map/psum | solution.py:172
  467.5 10.3 pad_maximum_fusion.2
  477.8 14.2 %stack.104 = f32[1,27648,128]{2,1,0:T(8,128)} reshape(f32[768,4608]{1,0:T(8,128)} %pad_maximum_fusion.2) | data formatting | bytes 28311552 | tf_op jit(solution)/shard_map/stack | solution.py:308
  493.0 9.0 all-reduce.21.cloned.1.call-done
  538.1 5.2 fusion.9
  547.0 13.1 %all-reduce.19.cloned.1.call-done = (bf16[256,768]{1,0:T(8,128)(2,1)}, bf16[256,768]{1,0:T(8,128)(2,1)}) async-done(((bf16[256,768]{1,0:T(8,128)(2,1)}, bf16[256,768]{1,0:T(8,128)(2,1)}), (bf16[256,768]{1,0:T(8,128)(2,1)}, bf16[256,768]{1,0:T(8,128)(2,1)})) %all-reduce.19.cloned.1.call-update) | async-done | bytes 786448 | tf_op jit(solution)/shard_map/psum | solution.py:172
  586.1 4.9 bitcast_reduce_fusion
  600.2 5.5 pad_maximum_fusion.1
  608.7 14.1 %stack.103 = f32[1,27648,128]{2,1,0:T(8,128)} reshape(f32[768,4608]{1,0:T(8,128)} %pad_maximum_fusion.1) | data formatting | bytes 28311552 | tf_op jit(solution)/shard_map/stack | solution.py:308
  622.8 21.0 %pad_maximum_fusion = f32[2,27648,128]{2,1,0:T(8,128)} fusion(f32[1,27648,128]{2,1,0:T(8,128)} %stack.104, f32[1,27648,128]{2,1,0:T(8,128)} %stack.103), kind=kLoop, calls=%fused_computation | loop fusion | flops 7077888 | bytes 56623104 | tf_op jit(solution)/shard_map/stack | solution.py:308
  651.2 56.5 %reduce-scatter.12.cloned.1.call-done = f32[48,12]{1,0:T(8,128)} async-done(((f32[768,12]{1,0:T(8,128)}), f32[48,12]{1,0:T(8,128)}) %reduce-scatter.12.cloned.1.call-update) | async-done | bytes 2320
  709.9 34.2 %all-reduce.17.cloned.1.call-done = (bf16[256,768]{1,0:T(8,128)(2,1)}, bf16[256,768]{1,0:T(8,128)(2,1)}) async-done(((bf16[256,768]{1,0:T(8,128)(2,1)}, bf16[256,768]{1,0:T(8,128)(2,1)}), (bf16[256,768]{1,0:T(8,128)(2,1)}, bf16[256,768]{1,0:T(8,128)(2,1)})) %all-reduce.17.cloned.1.call-update) | async-done | bytes 786448 | tf_op jit(solution)/shard_map/psum | solution.py:185
  747.1 271.0 %reduce-scatter.8.cloned.1.call-done = f32[2,1728,128]{2,1,0:T(8,128)} async-done(((f32[2,27648,128]{2,1,0:T(8,128)}), f32[2,1728,128]{2,1,0:T(8,128)}) %reduce-scatter.8.cloned.1.call-update) | async-done | bytes 1769488 | tf_op jit(solution)/shard_map/reduce_scatter | solution.py:307
  1024.6 39.3 %psum.135 = f32[]{:T(128)} all-reduce(f32[]{:T(128)S(6)} %add.573), channel_id=1, replica_groups=mesh['dp'=16,'tensor'=2] {'dp','tensor'}, use_global_device_ids=true, to_apply=%region_102.103 | all-reduce | flops 1 | bytes 8 | tf_op jit(solution)/shard_map/psum | solution.py:321
  1064.7 5.6 fusion.281
  (697 shorter events, 251.2 us)
Async XLA Ops:
  7.2 122.2 %all-gather.2.cloned.1.call-start = ((), (), s32[]{:S(2)}) async-start(), calls=%async_computation.3 | async-start | bytes 15040512 | tf_op jit(solution)/shard_map/all_gather | solution.py:253
  9.8 190.7 %all-reduce.31.cloned.1.call-start = ((), (), s32[]{:S(2)}) async-start(), calls=%async_computation.14 | async-start | bytes 1572864 | tf_op jit(solution)/shard_map/psum | solution.py:115
  69.7 88.1 %copy-start.62 = (pred[256,256]{0,1:T(8,128)(4,1)}, pred[256,256]{0,1:T(8,128)(4,1)S(1)}, u32[]{:S(2)}) copy-start(pred[256,256]{0,1:T(8,128)(4,1)S(1)} %broadcast_compare_fusion) | copy-start | bytes 196612
  167.6 88.5 %all-reduce.29.cloned.1.call-start = ((), (), s32[]{:S(2)}) async-start(), calls=%async_computation.13 | async-start | bytes 1572864 | tf_op jit(solution)/shard_map/psum | solution.py:125
  196.6 62.7 %copy-start.115 = (f32[768]{0:T(1024)}, f32[768]{0:T(1024)S(1)}, u32[]{:S(2)}) copy-start(f32[768]{0:T(1024)S(1)} %get-tuple-element.120) | copy-start | bytes 9220
  221.5 99.1 %all-reduce.27.cloned.1.call-start = ((), (), s32[]{:S(2)}) async-start(), calls=%async_computation.12 | async-start | bytes 1572864 | tf_op jit(solution)/shard_map/psum | solution.py:115
  285.9 89.8 %all-reduce.25.cloned.1.call-start = ((), (), s32[]{:S(2)}) async-start(), calls=%async_computation.11 | async-start | bytes 1572864 | tf_op jit(solution)/shard_map/psum | solution.py:125
  341.0 85.1 %all-reduce.23.cloned.1.call-start = ((), (), s32[]{:S(2)}) async-start(), calls=%async_computation.10 | async-start | bytes 1572864 | tf_op jit(solution)/shard_map/psum | solution.py:172
  391.4 110.5 %all-reduce.21.cloned.1.call-start = ((), (), s32[]{:S(2)}) async-start(), calls=%async_computation.9 | async-start | bytes 1572864 | tf_op jit(solution)/shard_map/psum | solution.py:185
  406.1 22.6 %copy-start.118 = (f32[256]{0:T(256)S(1)}, f32[256]{0:T(256)}, u32[]{:S(2)}) copy-start(f32[256]{0:T(256)} %copy-done.117) | copy-start | bytes 3076
  406.1 22.6 %copy-start.120 = (f32[256]{0:T(256)S(1)}, f32[256]{0:T(256)}, u32[]{:S(2)}) copy-start(f32[256]{0:T(256)} %copy-done.119) | copy-start | bytes 3076
  406.1 22.6 %copy-start.139 = (f32[256]{0:T(256)S(1)}, f32[256]{0:T(256)}, u32[]{:S(2)}) copy-start(f32[256]{0:T(256)} %copy-done.138) | copy-start | bytes 3076
  406.1 22.6 %copy-start.141 = (f32[256]{0:T(256)S(1)}, f32[256]{0:T(256)}, u32[]{:S(2)}) copy-start(f32[256]{0:T(256)} %copy-done.140) | copy-start | bytes 3076
  467.3 92.8 %all-reduce.19.cloned.1.call-start = ((), (), s32[]{:S(2)}) async-start(), calls=%async_computation.8 | async-start | bytes 1572864 | tf_op jit(solution)/shard_map/psum | solution.py:172
  477.8 14.4 %copy-start.167 = (f32[6,64]{1,0:T(8,128)S(1)}, f32[6,64]{1,0:T(8,128)}, u32[]{:S(2)}) copy-start(f32[6,64]{1,0:T(8,128)} %get-tuple-element.265) | copy-start | bytes 4612
  477.8 14.4 %copy-start.168 = (f32[6,64]{1,0:T(8,128)S(1)}, f32[6,64]{1,0:T(8,128)}, u32[]{:S(2)}) copy-start(f32[6,64]{1,0:T(8,128)} %get-tuple-element.269) | copy-start | bytes 4612
  477.8 14.5 %copy-start.169 = (f32[6,64]{1,0:T(8,128)S(1)}, f32[6,64]{1,0:T(8,128)}, u32[]{:S(2)}) copy-start(f32[6,64]{1,0:T(8,128)} %get-tuple-element.271) | copy-start | bytes 4612
  477.8 14.6 %copy-start.153 = (f32[1,1536]{1,0:T(1,128)S(1)}, f32[1,1536]{1,0:T(1,128)}, u32[]{:S(2)}) copy-start(f32[1,1536]{1,0:T(1,128)} %concatenate.199) | copy-start | bytes 18436
  477.8 14.6 %copy-start.154 = (f32[1,1536]{1,0:T(1,128)S(1)}, f32[1,1536]{1,0:T(1,128)}, u32[]{:S(2)}) copy-start(f32[1,1536]{1,0:T(1,128)} %concatenate.203) | copy-start | bytes 18436
  477.8 24.2 %copy-start.127 = (f32[256]{0:T(256)S(1)}, f32[256]{0:T(256)}, u32[]{:S(2)}) copy-start(f32[256]{0:T(256)} %copy-done.126) | copy-start | bytes 3076
  477.8 24.2 %copy-start.146 = (f32[256]{0:T(256)S(1)}, f32[256]{0:T(256)}, u32[]{:S(2)}) copy-start(f32[256]{0:T(256)} %copy-done.145) | copy-start | bytes 3076
  518.7 17.5 %copy-start.157 = (f32[768]{0:T(1024)S(1)}, f32[768]{0:T(1024)}, u32[]{:S(2)}) copy-start(f32[768]{0:T(1024)} %get-tuple-element.109) | copy-start | bytes 9220
  525.4 123.9 %reduce-scatter.10.cloned.1.call-start = ((), (), s32[]{:S(2)}) async-start(), calls=%async_computation.5 | async-start | bytes 1253376
  543.4 16.7 %copy-start.16 = (bf16[256,768]{1,0:T(8,128)(2,1)S(1)}, bf16[256,768]{1,0:T(8,128)(2,1)}, u32[]{:S(2)}) copy-start(bf16[256,768]{1,0:T(8,128)(2,1)} %get-tuple-element.139) | copy-start | bytes 1179652
  543.4 16.7 %copy-start.129 = (f32[256]{0:T(256)S(1)}, f32[256]{0:T(256)}, u32[]{:S(2)}) copy-start(f32[256]{0:T(256)} %copy-done.128) | copy-start | bytes 3076
  543.4 16.7 %copy-start.131 = (f32[256]{0:T(256)S(1)}, f32[256]{0:T(256)}, u32[]{:S(2)}) copy-start(f32[256]{0:T(256)} %copy-done.130) | copy-start | bytes 3076
  591.1 116.6 %reduce-scatter.12.cloned.1.call-start = ((), (), s32[]{:S(2)}) async-start(), calls=%async_computation.6 | async-start | bytes 417792
  594.4 149.7 %all-reduce.17.cloned.1.call-start = ((), (), s32[]{:S(2)}) async-start(), calls=%async_computation.7 | async-start | bytes 1572864 | tf_op jit(solution)/shard_map/psum | solution.py:185
  622.8 395.2 %reduce-scatter.8.cloned.1.call-start = ((), (), s32[]{:S(2)}) async-start(), calls=%async_computation.4 | async-start | bytes 30081024 | tf_op jit(solution)/shard_map/reduce_scatter | solution.py:307
  647.2 96.9 %copy-start.28 = (f32[256,768]{1,0:T(8,128)S(1)}, f32[256,768]{1,0:T(8,128)}, u32[]{:S(2)}) copy-start(f32[256,768]{1,0:T(8,128)} %copy-done.27) | copy-start | bytes 2359300
  648.2 97.9 %copy-start.26 = (f32[256,768]{1,0:T(8,128)S(1)}, f32[256,768]{1,0:T(8,128)}, u32[]{:S(2)}) copy-start(f32[256,768]{1,0:T(8,128)} %get-tuple-element.159) | copy-start | bytes 2359300
  1021.9 42.8 %copy-start.22 = (f32[2,1,221184]{2,1,0:T(1,128)S(1)}, f32[2,1,221184]{2,1,0:T(1,128)}, u32[]{:S(2)}) copy-start(f32[2,1,221184]{2,1,0:T(1,128)} %broadcast_multiply_fusion.1) | copy-start | bytes 5308420
  (198 other events, 633.1 us)
Sparse Core Ops, SparseCore 0:
  10.9 118.4 all-gather.1
  167.8 32.6 all-reduce.30
  221.6 34.5 all-reduce.28
  286.0 34.4 all-reduce.26
  341.1 34.4 all-reduce.24
  391.5 34.4 all-reduce.22
  467.4 34.5 all-reduce.20
  525.5 34.4 all-reduce.18
  591.2 58.0 reduce-scatter.9
  653.1 54.5 reduce-scatter.11
  710.6 33.4 all-reduce.16
  748.7 269.2 reduce-scatter.7
where the time goes:
time: 1090 us; the launch traced here: 1080 us
  waiting for transfers between devices  536 us (49%)
  local copies, waits for them, and re-layouts  183 us (17%)
  matrix products  135 us (12%)
  other arithmetic  116 us (11%)
  blocking collectives  92.4 us (8%)
  between operations  20.7 us (2%)
    reduce_scatter x1, waiting for transfers between devices, per_device(): lax.psum_scatter(jnp.stack(matrix_grads).reshape(tiled_shape), 'dp', scat...  271 us
    all_gather x1, waiting for transfers between devices, per_device(): lax.all_gather(weights_tiled.astype(jnp.bfloat16), 'dp', axis=1, tiled=True)  59 us
    unnamed x14, waiting for transfers between devices  57.8 us
    psum x2, waiting for transfers between devices, layer_forward(): ffn_out = lax.psum(ffn_part, 'tensor').astype(jnp.float32)  50.8 us
    unnamed x466, local copies, waits for them, and re-layouts  45.2 us
    psum x2, waiting for transfers between devices, layer_backward(): grad_hidden = back_one + lax.psum(attn_back, 'tensor').astype(jnp.float32)  43.2 us
    psum x1, blocking collectives, per_device(): grad_norm = jnp.sqrt(lax.psum(local_squares, ('dp', 'tensor')))  39.3 us
    psum x2, waiting for transfers between devices, layer_backward(): grad_first = back_two + lax.psum(ffn_back, 'tensor').astype(jnp.float32)  33 us
  transfers between devices with their start and end apart: 12, of which 12 were waited for; matrix products, arithmetic and copies ran while one was open for 18% of the time, Pallas kernels for 0%

commit v1 on v0

v1 whole, which is shorter than its diff:
```python
from functools import partial

import jax
import jax.numpy as jnp
from jax import lax
from jax.experimental import pallas as pl
from jax.experimental.pallas import tpu as pltpu
from jax.sharding import PartitionSpec as P

D = 768
HEAD_DIM = 64
LAYERS = 2
SEQ = 256
MICRO = 2
STEP = 3
HD = 384
FFT = 1536
QKV = 3 * HD
ATT = 4 * HD
COLS = ATT + 2 * FFT
VCOL = 2 * HD + FFT
LANES = 128
TILES = COLS // LANES

clip_limit = 1.0
weight_rate = 0.03
weight_decay = 0.01
vector_rate = 0.3
contract_last = (((1,), (1,)), ((), ()))
contract_first = (((0,), (0,)), ((), ()))
f32 = jnp.float32
b16 = jnp.bfloat16
VMEM_LIMIT = 56 * 1024 * 1024
ANY = pl.BlockSpec(memory_space=pl.ANY)
VM = pl.BlockSpec(memory_space=pltpu.VMEM)


def call(body, outs, in_specs, scratch=(), flops=0, moved=0, out_specs=None, trans=0):
    if out_specs is None:
        out_specs = [VM] * len(outs)
    return pl.pallas_call(
        body,
        out_shape=[jax.ShapeDtypeStruct(s, d) for s, d in outs],
        in_specs=in_specs,
        out_specs=out_specs,
        scratch_shapes=list(scratch),
        compiler_params=pltpu.CompilerParams(vmem_limit_bytes=VMEM_LIMIT),
        cost_estimate=pl.CostEstimate(flops=flops, bytes_accessed=moved, transcendentals=trans),
    )


def dot(a, b, dims=(((1,), (0,)), ((), ()))):
    return lax.dot_general(a, b, dims, preferred_element_type=f32)


def norm_rows(value):
    center = value - jnp.mean(value, axis=-1, keepdims=True)
    scale = lax.rsqrt(jnp.mean(center * center, axis=-1, keepdims=True) + 1e-12)
    return center * scale, scale


def norm_back(grad_out, normed, scale, gain):
    inner = grad_out * gain
    back = scale * (
        inner
        - jnp.mean(inner, axis=-1, keepdims=True)
        - normed * jnp.mean(inner * normed, axis=-1, keepdims=True)
    )
    return (
        back,
        jnp.sum(grad_out * normed, axis=0, keepdims=True),
        jnp.sum(grad_out, axis=0, keepdims=True),
    )


def places(ring):
    me = lax.axis_index("dp")
    return lax.div(me, 4), lax.rem(lax.div(me, 2), 2), lax.rem(me, 2)


def pairs_of(ndp, kind):
    if kind == "ring":
        return [(i, (i + 4) % ndp) for i in range(ndp)]
    if kind == "x":
        return [(i, i ^ 2) for i in range(ndp)]
    return [(i, i ^ 1) for i in range(ndp)]


def move(a, kind):
    return lax.ppermute(a, "dp", pairs_of(lax.axis_size("dp"), kind))


def exchange(a):
    return lax.ppermute(a, "tensor", [(0, 1), (1, 0)])


def assemble(parts):
    half = len(parts) // 2

    def body(*refs):
        ins, out, sem = refs[: 2 * half], refs[2 * half], refs[2 * half + 1]
        copies = []
        for i in range(2 * half):
            copies.append(pltpu.make_async_copy(ins[i], out.at[i // half, i % half], sem.at[i]))
            copies[-1].start()
        for cp in copies:
            cp.wait()

    rows, cols = parts[0].shape
    size = len(parts) * rows * cols * 2
    return call(
        body,
        [((2, half, rows, cols), b16)],
        [ANY] * len(parts),
        [pltpu.SemaphoreType.DMA((2 * half,))],
        moved=2 * size,
        out_specs=[ANY],
    )(*parts)[0]


def gather_chunk(own):
    ring = lax.axis_size("dp") // 4
    rounds = [own]
    for _ in range(ring - 1):
        rounds.append(move(rounds[-1], "ring"))
    across = [move(r, "x") for r in rounds]
    mine = assemble(rounds + across)
    return mine, move(mine, "core")


def start_load(pieces, target, sem, first=0, cols=None):
    if len(pieces) == 1:
        width = target.shape[1]
        src = pieces[0].at[:, pl.ds(first, width)]
        copies = [pltpu.make_async_copy(src, target, sem.at[0])]
    else:
        ring, rows = pieces[0].shape[1], pieces[0].shape[2]
        width = target.shape[1]
        z, x, c = places(ring)
        copies = []
        for other in range(2):
            for xo in range(2):
                for k in range(ring):
                    zz = lax.rem(z - k + ring, ring)
                    xx = lax.rem(x + xo, 2)
                    cc = lax.rem(c + other, 2)
                    row = pl.multiple_of(((zz * 2 + xx) * 2 + cc) * rows, 16)
                    copies.append(
                        pltpu.make_async_copy(
                            pieces[other].at[xo, k, :, pl.ds(first, width)],
                            target.at[pl.ds(row, rows), :],
                            sem.at[len(copies)],
                        )
                    )
    for cp in copies:
        cp.start()
    return copies


def load_count(pieces):
    return 1 if len(pieces) == 1 else 4 * pieces[0].shape[1]


def prep(weights_tiled, rep, split):
    tiled_rows = weights_tiled.shape[1]
    rows = tiled_rows // TILES
    per = split.shape[1]

    def body(w_ref, rep_ref, split_ref, a0, f0, a1, f1):
        for layer, (a_ref, f_ref) in enumerate(((a0, f0), (a1, f1))):
            for c in range(TILES):
                piece = w_ref[layer, pl.ds(c, rows, stride=TILES), :].astype(b16)
                if c < ATT // LANES:
                    a_ref[:, c * LANES : (c + 1) * LANES] = piece
                else:
                    at = c * LANES - ATT
                    f_ref[:, at : at + LANES] = piece
        row = lax.broadcasted_iota(jnp.int32, (rows, rows), 0)
        col = lax.broadcasted_iota(jnp.int32, (rows, rows), 1)
        eye = (row == col).astype(b16)
        row3 = lax.broadcasted_iota(jnp.int32, (rows, per), 0)
        col3 = lax.broadcasted_iota(jnp.int32, (rows, per), 1)
        gap = col3 - 3 * row3
        block = jnp.zeros((rows, LANES), f32)
        lane = lax.broadcasted_iota(jnp.int32, (rows, LANES), 1)
        rep_cols = dot(eye, rep_ref[...].astype(b16), contract_last)
        rep_wide = jnp.concatenate(
            [rep_cols, jnp.zeros((rows, LANES - 6 * LAYERS), f32)], axis=1
        )
        block = rep_wide
        low = split_ref[...].astype(b16).astype(f32)
        for layer in range(LAYERS):
            for j in range(3):
                pick = jnp.where(gap == j, jnp.broadcast_to(low[layer : layer + 1], (rows, per)), 0.0)
                value = jnp.sum(pick, axis=1, keepdims=True)
                block = jnp.where(lane == 6 * LAYERS + 3 * layer + j, value, block)
        a0[:, ATT:] = block.astype(b16)

    return call(
        body,
        [
            ((rows, ATT + LANES), b16),
            ((rows, 2 * FFT), b16),
            ((rows, ATT), b16),
            ((rows, 2 * FFT), b16),
        ],
        [VM] * 3,
        moved=weights_tiled.size * 6,
    )(weights_tiled, rep, split)


def spread_mask(first_row, rows, first, cols):
    row = first_row + lax.broadcasted_iota(jnp.int32, (rows, cols), 0)
    col = first + lax.broadcasted_iota(jnp.int32, (rows, cols), 1)
    gap = col - 3 * row
    return jnp.where((gap >= 0) & (gap < 3), 1.0, 0.0).astype(b16)


def unpack(pieces):
    count = load_count(pieces)

    def body(*refs):
        ins, (rep_ref, split_ref, cols_ref, sem) = refs[: len(pieces)], refs[len(pieces) :]
        for cp in start_load(ins, cols_ref, sem, first=ATT):
            cp.wait()
        flat = cols_ref[...]
        turned = flat.astype(f32).T
        rep_ref[...] = turned[:16]
        low = turned[:24].astype(b16)
        step = VCOL // 3
        for i in range(3):
            rows = D // 3
            mask = spread_mask(i * rows, rows, i * step, step)
            spread = dot(low[:, i * rows : (i + 1) * rows], mask)
            phase = lax.rem(lax.broadcasted_iota(jnp.int32, (1, step), 1), 3)
            for layer in range(LAYERS):
                at = 6 * LAYERS + 3 * layer
                value = jnp.where(
                    phase == 0,
                    spread[at : at + 1],
                    jnp.where(phase == 1, spread[at + 1 : at + 2], spread[at + 2 : at + 3]),
                )
                split_ref[layer : layer + 1, i * step : (i + 1) * step] = value

    return call(
        body,
        [((16, D), f32), ((8, VCOL), f32)],
        [ANY] * len(pieces),
        [pltpu.VMEM((D, LANES), b16), pltpu.SemaphoreType.DMA((count,))],
        moved=D * LANES * 2,
        flops=24 * D * VCOL,
    )(*pieces)


def gelu_parts(inner):
    cdf = 0.5 * (1.0 + lax.erf(inner * (0.5**0.5)))
    dens = jnp.exp(-0.5 * inner * inner) * 0.3989422804014327
    return inner * cdf, cdf + inner * dens


def attend(h_low, layer, w_ref, split_ref, seg_ref, part_ref, qkv_ref, probs_ref, ctx_ref):
    mixed = dot(h_low, w_ref[:, :QKV])
    qkv_ref[:, :HD] = (mixed[:, :HD] + split_ref[layer : layer + 1, :HD]).astype(b16)
    qkv_ref[:, HD : 2 * HD] = mixed[:, HD : 2 * HD].astype(b16)
    qkv_ref[:, 2 * HD :] = (
        mixed[:, 2 * HD :] + split_ref[layer : layer + 1, HD : 2 * HD]
    ).astype(b16)
    seg = jnp.broadcast_to(seg_ref[...].astype(f32), (SEQ, SEQ))
    same = seg == seg.T
    low_half = lax.broadcasted_iota(jnp.int32, (1, LANES), 1) < HEAD_DIM
    for pair in range(HD // LANES):
        at = pair * LANES
        query = qkv_ref[:, at : at + LANES].astype(f32) * HEAD_DIM ** (-0.5)
        keys = qkv_ref[:, HD + at : HD + at + LANES]
        values = qkv_ref[:, 2 * HD + at : 2 * HD + at + LANES].astype(f32)
        total = jnp.zeros((SEQ, LANES), f32)
        for half in range(2):
            mine = low_half if half == 0 else ~low_half
            scores = dot(jnp.where(mine, query, 0.0).astype(b16), keys, contract_last)
            scores = jnp.where(same, scores, -1000000000.0)
            raised = jnp.exp(scores - jnp.max(scores, axis=-1, keepdims=True))
            probs = (raised * (1.0 / jnp.sum(raised, axis=-1, keepdims=True))).astype(b16)
            probs_ref[2 * pair + half] = probs
            total = total + dot(probs, jnp.where(mine, values, 0.0).astype(b16))
        ctx_ref[:, at : at + LANES] = total.astype(b16)
    part_ref[...] = dot(ctx_ref[...], w_ref[:, QKV:ATT], contract_last).astype(b16)


ATT_FLOPS = 2 * SEQ * D * ATT + 4 * SEQ * SEQ * HD * 2
FFN_FLOPS = 2 * SEQ * D * 2 * FFT


def weight_scratch(pieces, cols):
    return [pltpu.VMEM((D, cols), b16), pltpu.SemaphoreType.DMA((load_count(pieces),))]


def attention_first(micro, block_in, segments, split, pieces):
    def body(h_ref, seg_ref, split_ref, *refs):
        ins, refs = refs[: len(pieces)], refs[len(pieces) :]
        part_ref, qkv_ref, probs_ref, ctx_ref, w_ref, sem = refs
        for cp in start_load(ins, w_ref, sem):
            cp.wait()
        attend(
            h_ref[micro], 0, w_ref, split_ref, seg_ref[micro], part_ref, qkv_ref, probs_ref, ctx_ref
        )

    return call(
        body,
        [
            ((SEQ, D), b16),
            ((SEQ, QKV), b16),
            ((HD // HEAD_DIM, SEQ, SEQ), b16),
            ((SEQ, HD), b16),
        ],
        [VM] * 3 + [ANY] * len(pieces),
        weight_scratch(pieces, ATT),
        flops=ATT_FLOPS,
        moved=6 << 20,
    )(block_in, segments, split, *pieces)


def attention_next(micro, layer, normed, part_own, part_other, rep, segments, split, pieces):
    base = 6 * (layer - 1)

    def body(n_ref, own_ref, other_ref, rep_ref, seg_ref, split_ref, *refs):
        ins, refs = refs[: len(pieces)], refs[len(pieces) :]
        part_ref, qkv_ref, probs_ref, ctx_ref, n2_ref, s2_ref, low_ref, w_ref, sem = refs
        copies = start_load(ins, w_ref, sem)
        first = n_ref[...] * rep_ref[base + 1 : base + 2] + rep_ref[base + 2 : base + 3]
        added = own_ref[...].astype(f32) + other_ref[...].astype(f32)
        n2, s2 = norm_rows(first + added + rep_ref[base + 3 : base + 4])
        n2_ref[...] = n2
        s2_ref[...] = s2
        low_ref[...] = (n2 * rep_ref[base + 4 : base + 5] + rep_ref[base + 5 : base + 6]).astype(b16)
        for cp in copies:
            cp.wait()
        attend(
            low_ref[...],
            layer,
            w_ref,
            split_ref,
            seg_ref[micro],
            part_ref,
            qkv_ref,
            probs_ref,
            ctx_ref,
        )

    return call(
        body,
        [
            ((SEQ, D), b16),
            ((SEQ, QKV), b16),
            ((HD // HEAD_DIM, SEQ, SEQ), b16),
            ((SEQ, HD), b16),
            ((SEQ, D), f32),
            ((SEQ, 1), f32),
            ((SEQ, D), b16),
        ],
        [VM] * 6 + [ANY] * len(pieces),
        weight_scratch(pieces, ATT),
        flops=ATT_FLOPS,
        moved=8 << 20,
    )(normed, part_own, part_other, rep, segments, split, *pieces)


def feed_forward(micro, layer, hidden, part_own, part_other, rep, split, pieces):
    base = 6 * layer

    def body(h_ref, own_ref, other_ref, rep_ref, split_ref, *refs):
        ins, refs = refs[: len(pieces)], refs[len(pieces) :]
        part_ref, n1_ref, s1_ref, low_ref, act_ref, slope_ref, w_ref, sem = refs
        copies = start_load(ins, w_ref, sem)
        if layer == 0:
            hidden_in = h_ref[micro].astype(f32)
        else:
            hidden_in = h_ref[...] * rep_ref[base - 2 : base - 1] + rep_ref[base - 1 : base]
        added = own_ref[...].astype(f32) + other_ref[...].astype(f32)
        n1, s1 = norm_rows(hidden_in + added + rep_ref[base : base + 1])
        n1_ref[...] = n1
        s1_ref[...] = s1
        low_ref[...] = (n1 * rep_ref[base + 1 : base + 2] + rep_ref[base + 2 : base + 3]).astype(b16)
        for cp in copies:
            cp.wait()
        step = 512
        for at in range(0, FFT, step):
            inner = (
                dot(low_ref[...], w_ref[:, at : at + step])
                + split_ref[layer : layer + 1, 2 * HD + at : 2 * HD + at + step]
            )
            active, slope = gelu_parts(inner)
            act_ref[:, at : at + step] = active.astype(b16)
            slope_ref[:, at : at + step] = slope.astype(b16)
        part_ref[...] = dot(act_ref[...], w_ref[:, FFT:], contract_last).astype(b16)

    return call(
        body,
        [
            ((SEQ, D), b16),
            ((SEQ, D), f32),
            ((SEQ, 1), f32),
            ((SEQ, D), b16),
            ((SEQ, FFT), b16),
            ((SEQ, FFT), b16),
        ],
        [VM] * 5 + [ANY] * len(pieces),
        weight_scratch(pieces, 2 * FFT),
        flops=FFN_FLOPS,
        moved=10 << 20,
    )(hidden, part_own, part_other, rep, split, *pieces)


def feed_back_tail(grad, n2, s2, layer, rep_ref, act_slope, copies, w_ref, outs):
    base = 6 * layer
    part_ref, res_ref, dffn_ref, din_ref, vec_ref = outs
    slope_ref = act_slope
    back, gain, shift = norm_back(grad, n2, s2, rep_ref[base + 4 : base + 5])
    res_ref[...] = back
    dffn_ref[...] = back.astype(b16)
    vec_ref[...] = jnp.zeros_like(vec_ref)
    vec_ref[0:1] = jnp.sum(back, axis=0, keepdims=True)
    vec_ref[1:2] = gain
    vec_ref[2:3] = shift
    for cp in copies:
        cp.wait()
    step = 384
    for at in range(0, FFT, step):
        grad_act = dot(dffn_ref[...], w_ref[:, FFT + at : FFT + at + step])
        grad_in = (slope_ref[:, at : at + step].astype(f32) * grad_act).astype(b16)
        din_ref[:, at : at + step] = grad_in
        row, lane = 3 + at // D, at % D
        vec_ref[row : row + 1, lane : lane + step] = jnp.sum(
            grad_in.astype(f32), axis=0, keepdims=True
        )
    part_ref[...] = dot(din_ref[...], w_ref[:, :FFT], contract_last).astype(b16)


BACK_OUTS = [
    ((SEQ, D), b16),
    ((SEQ, D), f32),
    ((SEQ, D), b16),
    ((SEQ, FFT), b16),
    ((8, D), f32),
]


def feed_back_top(micro, layer, out_grad, n1, part_own, part_other, rep, slope, pieces):
    base = 6 * layer

    def body(g_ref, n_ref, own_ref, other_ref, rep_ref, slope_ref, *refs):
        ins, refs = refs[: len(pieces)], refs[len(pieces) :]
        out_ref, w_ref, sem = refs[5:]
        copies = start_load(ins, w_ref, sem)
        first = n_ref[...] * rep_ref[base + 1 : base + 2] + rep_ref[base + 2 : base + 3]
        added = own_ref[...].astype(f32) + other_ref[...].astype(f32)
        n2, s2 = norm_rows(first + added + rep_ref[base + 3 : base + 4])
        out_ref[...] = (n2 * rep_ref[base + 4 : base + 5] + rep_ref[base + 5 : base + 6]).astype(b16)
        feed_back_tail(
            g_ref[micro].astype(f32), n2, s2, layer, rep_ref, slope_ref, copies, w_ref, refs[:5]
        )

    return call(
        body,
        BACK_OUTS + [((SEQ, D), b16)],
        [VM] * 6 + [ANY] * len(pieces),
        weight_scratch(pieces, 2 * FFT),
        flops=FFN_FLOPS,
        moved=11 << 20,
    )(out_grad, n1, part_own, part_other, rep, slope, *pieces)


def feed_back(layer, mid, part_own, part_other, n2, s2, rep, slope, pieces):
    def body(mid_ref, own_ref, other_ref, n2_ref, s2_ref, rep_ref, slope_ref, *refs):
        ins, refs = refs[: len(pieces)], refs[len(pieces) :]
        w_ref, sem = refs[5:]
        copies = start_load(ins, w_ref, sem)
        added = own_ref[...].astype(f32) + other_ref[...].astype(f32)
        feed_back_tail(
            mid_ref[...] + added,
            n2_ref[...],
            s2_ref[...],
            layer,
            rep_ref,
            slope_ref,
            copies,
            w_ref,
            refs[:5],
        )

    return call(
        body,
        BACK_OUTS,
        [VM] * 7 + [ANY] * len(pieces),
        weight_scratch(pieces, 2 * FFT),
        flops=FFN_FLOPS,
        moved=11 << 20,
    )(mid, part_own, part_other, n2, s2, rep, slope, *pieces)


def attention_back(layer, res, part_own, part_other, n1, s1, rep, qkv, probs, ctx, pieces):
    base = 6 * layer

    def body(
        res_ref, own_ref, other_ref, n1_ref, s1_ref, rep_ref, qkv_ref, probs_ref, ctx_ref, *refs
    ):
        ins, refs = refs[: len(pieces)], refs[len(pieces) :]
        part_ref, mid_ref, datt_ref, dqkv_ref, vec_ref, w_ref, sem = refs
        copies = start_load(ins, w_ref, sem)
        grad = res_ref[...] + (own_ref[...].astype(f32) + other_ref[...].astype(f32))
        back, gain, shift = norm_back(grad, n1_ref[...], s1_ref[...], rep_ref[base + 1 : base + 2])
        mid_ref[...] = back
        datt_ref[...] = back.astype(b16)
        vec_ref[...] = jnp.zeros_like(vec_ref)
        vec_ref[0:1] = jnp.sum(back, axis=0, keepdims=True)
        vec_ref[1:2] = gain
        vec_ref[2:3] = shift
        for cp in copies:
            cp.wait()
        dctx = dot(datt_ref[...], w_ref[:, QKV:ATT]).astype(b16).astype(f32)
        low_half = lax.broadcasted_iota(jnp.int32, (1, LANES), 1) < HEAD_DIM
        factor = HEAD_DIM ** (-0.5)
        for pair in range(HD // LANES):
            at = pair * LANES
            query = qkv_ref[:, at : at + LANES].astype(f32) * factor
            keys = qkv_ref[:, HD + at : HD + at + LANES].astype(f32) * factor
            values = qkv_ref[:, 2 * HD + at : 2 * HD + at + LANES]
            dc = dctx[:, at : at + LANES]
            weighed = dc * ctx_ref[:, at : at + LANES].astype(f32)
            dq = jnp.zeros((SEQ, LANES), f32)
            dk = jnp.zeros((SEQ, LANES), f32)
            dv = jnp.zeros((SEQ, LANES), f32)
            for half in range(2):
                mine = low_half if half == 0 else ~low_half
                dcm = jnp.where(mine, dc, 0.0).astype(b16)
                delta = jnp.sum(jnp.where(mine, weighed, 0.0), axis=-1, keepdims=True)
                probs = probs_ref[2 * pair + half]
                dprobs = dot(dcm, values, contract_last)
                dscores = (probs.astype(f32) * (dprobs - delta)).astype(b16)
                dq = dq + dot(dscores, jnp.where(mine, keys, 0.0).astype(b16))
                dk = dk + dot(dscores, jnp.where(mine, query, 0.0).astype(b16), contract_first)
                dv = dv + dot(probs, dcm, contract_first)
            dqkv_ref[:, at : at + LANES] = dq.astype(b16)
            dqkv_ref[:, HD + at : HD + at + LANES] = dk.astype(b16)
            dqkv_ref[:, 2 * HD + at : 2 * HD + at + LANES] = dv.astype(b16)
        vec_ref[3:4, :HD] = jnp.sum(dqkv_ref[:, :HD].astype(f32), axis=0, keepdims=True)
        vec_ref[3:4, HD:] = jnp.sum(dqkv_ref[:, 2 * HD :].astype(f32), axis=0, keepdims=True)
        part_ref[...] = dot(dqkv_ref[...], w_ref[:, :QKV], contract_last).astype(b16)

    return call(
        body,
        [
            ((SEQ, D), b16),
            ((SEQ, D), f32),
            ((SEQ, D), b16),
            ((SEQ, QKV), b16),
            ((8, D), f32),
        ],
        [VM] * 9 + [ANY] * len(pieces),
        weight_scratch(pieces, ATT),
        flops=2 * ATT_FLOPS,
        moved=9 << 20,
    )(res, part_own, part_other, n1, s1, rep, qkv, probs, ctx, *pieces)


def finish_input(mids, owns, others):
    def body(*refs):
        for micro in range(MICRO):
            m, a, b = refs[3 * micro : 3 * micro + 3]
            refs[-1][micro] = m[...] + (a[...].astype(f32) + b[...].astype(f32))

    args = []
    for micro in range(MICRO):
        args += [mids[micro], owns[micro], others[micro]]
    return call(body, [((MICRO, SEQ, D), f32)], [VM] * len(args), moved=7 << 20)(*args)[0]


def store_slots(product_ref, outs, at, width):
    if len(outs) == 1:
        outs[0][:, at : at + width] = product_ref[:, :width].astype(b16)
        return
    ring, rows = outs[0].shape[1], outs[0].shape[2]
    z, x, c = places(ring)
    for other in range(2):
        for xo in range(2):
            for k in range(ring):
                zz = lax.rem(z + k, ring)
                xx = lax.rem(x + xo, 2)
                cc = lax.rem(c + other, 2)
                row = pl.multiple_of(((zz * 2 + xx) * 2 + cc) * rows, 16)
                outs[other][xo, k, :, at : at + width] = product_ref[
                    pl.ds(row, rows), :width
                ].astype(b16)


def grad_outs(ndp, pieced, cols):
    rows = D // ndp
    if pieced:
        return [((2, ndp // 4, rows, cols), b16)] * 2
    return [((D, cols), b16)]


def matrix_gradient(sets, pieced, ndp, vectors=None):
    widths = [s[2] for s in sets]
    total = sum(widths) + (LANES if vectors is not None else 0)
    outs = grad_outs(ndp, pieced, total)
    args, specs = [], []
    for left, right, _ in sets:
        for micro in range(MICRO):
            specs.append(VM)
            args.append(left[micro])
        for micro in range(MICRO):
            args.append(right[micro])
            specs.append(VM)
    plain = len(args)
    if vectors is not None:
        args += vectors
        specs += [VM] * len(vectors)
    n_in = len(args)
    step = 384

    def body(*refs):
        out_refs = refs[n_in : n_in + len(outs)]
        prod_ref = refs[n_in + len(outs)]
        at = 0
        for index, width in enumerate(widths):
            l0, l1, r0, r1 = refs[4 * index : 4 * index + 4]
            left = [r[m] if len(r.shape) == 3 else r[...] for m, r in enumerate((l0, l1))]
            for col in range(0, width, step):
                prod_ref[...] = dot(left[0], r0[:, col : col + step], contract_first) + dot(
                    left[1], r1[:, col : col + step], contract_first
                )
                store_slots(prod_ref, out_refs, at, step)
                at += step
        if vectors is not None:
            pack_vectors(refs[plain:n_in], prod_ref)
            store_slots(prod_ref, out_refs, at, LANES)

    moved = sum(a.size * 2 for a in args[:plain]) + D * total * 2
    return call(
        body,
        outs,
        specs,
        [pltpu.VMEM((D, step), f32)],
        flops=2 * MICRO * SEQ * D * total,
        moved=moved,
    )(*args)


def pack_vectors(vec_refs, prod_ref):
    sums = []
    for layer in range(LAYERS):
        a0, a1, b0, b1 = vec_refs[4 * layer : 4 * layer + 4]
        sums.append((a0[...] + a1[...], b0[...] + b1[...]))
    rows = []
    for att, ffn in sums:
        rows += [att[0:1], att[1:2], att[2:3], ffn[0:1], ffn[1:2], ffn[2:3]]
    rows.append(jnp.zeros((4, D), f32))
    turned = jnp.concatenate(rows, axis=0)
    turned = jnp.concatenate([turned, jnp.zeros((LANES - 16, D), f32)], axis=0).T
    step = VCOL // 3
    phase = lax.rem(lax.broadcasted_iota(jnp.int32, (1, step), 1), 3)
    lane = lax.broadcasted_iota(jnp.int32, (1, LANES), 1)
    for i in range(3):
        picked = []
        for att, ffn in sums:
            line = (att[3:4], ffn[3:4], ffn[4:5])[i]
            for j in range(3):
                picked.append(jnp.where(phase == j, line, 0.0))
        picked = jnp.concatenate(
            [jnp.zeros((12, step), f32)] + picked + [jnp.zeros((LANES - 18, step), f32)], axis=0
        ).astype(b16)
        n_rows = D // 3
        mask = spread_mask(i * n_rows, n_rows, i * step, step)
        part = dot(mask, picked, contract_last)
        keep = turned[i * n_rows : (i + 1) * n_rows]
        prod_ref[i * n_rows : (i + 1) * n_rows, :LANES] = jnp.where(lane < 12, keep, part)


def reduce_chunk(pieces):
    ndp = lax.axis_size("dp")
    if len(pieces) == 1:
        return lax.psum_scatter(pieces[0], "dp", scatter_dimension=0, tiled=True).astype(f32)
    own, other = pieces
    ring = own.shape[1]
    met = move(other, "core")
    sent = (own[1].astype(f32) + met[1].astype(f32)).astype(b16)
    got = move(sent, "x")
    sums = [
        own[0, k].astype(f32) + met[0, k].astype(f32) + got[k].astype(f32) for k in range(ring)
    ]
    total = sums[ring - 1]
    for k in range(ring - 2, -1, -1):
        total = sums[k] + move(total.astype(b16), "ring").astype(f32)
    return total


def adamw(value, first, second, grad, rate, decay):
    first = 0.5 * first + 0.5 * grad
    second = 0.5 * second + 0.5 * grad * grad
    correct = 1.0 - 0.5**STEP
    direction = first / correct / (jnp.sqrt(second / correct) + 1e-08)
    return (value - rate * (direction + decay * value), first, second)


def update_matrices(tiled, first, second, grads, factor):
    rows = grads[0].shape[0]
    step = 8 if rows % 8 == 0 else rows
    n_steps = rows // step
    block = (1, step * TILES, LANES)

    def body(f_ref, w_ref, m_ref, v_ref, a0, f0, a1, f1, nw, nm, nv, nl):
        scale = f_ref[0, 0]
        layer = pl.program_id(0)
        for c in range(TILES):
            if c < ATT // LANES:
                lo = c * LANES
                grad = jnp.where(layer == 0, a0[:, lo : lo + LANES], a1[:, lo : lo + LANES])
            else:
                lo = c * LANES - ATT
                grad = jnp.where(layer == 0, f0[:, lo : lo + LANES], f1[:, lo : lo + LANES])
            where = (0, pl.ds(c, step, stride=TILES), slice(None))
            new = adamw(
                w_ref[where], m_ref[where], v_ref[where], grad * scale, weight_rate, weight_decay
            )
            nw[where], nm[where], nv[where] = new
        nl[...] = nw[...].astype(b16)

    big = pl.BlockSpec(block, lambda l, i: (l, i, 0))
    shape = tiled.shape
    return pl.pallas_call(
        body,
        grid=(LAYERS, n_steps),
        out_shape=[jax.ShapeDtypeStruct(shape, f32)] * 3 + [jax.ShapeDtypeStruct(shape, b16)],
        in_specs=[pl.BlockSpec(memory_space=pltpu.SMEM), big, big, big]
        + [pl.BlockSpec((step, g.shape[1]), lambda l, i: (i, 0)) for g in grads],
        out_specs=[big] * 4,
        compiler_params=pltpu.CompilerParams(vmem_limit_bytes=VMEM_LIMIT),
        cost_estimate=pl.CostEstimate(
            flops=20 * tiled.size, bytes_accessed=30 * tiled.size, transcendentals=tiled.size
        ),
    )(factor.reshape(1, 1), tiled, first, second, *grads)


def sum_everywhere(value):
    ndp = lax.axis_size("dp")
    if ndp & (ndp - 1):
        return lax.psum(value, ("dp", "tensor"))
    bit = 1
    while bit < ndp:
        value = value + lax.ppermute(value, "dp", [(i, i ^ bit) for i in range(ndp)])
        bit *= 2
    return value + exchange(value)


def per_device(
    block_in,
    out_grad,
    segments,
    weights,
    weights_first,
    weights_second,
    split_vectors,
    split_first,
    split_second,
    rep_vectors,
    rep_first,
    rep_second,
):
    ndp = lax.axis_size("dp")
    rows = D // ndp
    per = split_vectors.shape[2]
    pieced = ndp % 4 == 0 and rows % 16 == 0
    shard_shape = weights.shape
    tiled_shape = (LAYERS, -1, LANES)
    weights_tiled = weights.reshape(tiled_shape)
    rep_flat = rep_vectors.reshape(LAYERS * 6, -1)
    split_flat = split_vectors.reshape(LAYERS, per)
    if pieced:
        a0, f0, a1, f1 = prep(weights_tiled, rep_flat, split_flat)
        att = [gather_chunk(a0), None]
        ffn = [gather_chunk(f0), None]
        att[1] = gather_chunk(a1)
        ffn[1] = gather_chunk(f1)
    else:
        low = weights.astype(b16).reshape(LAYERS, rows, COLS)
        block = jnp.concatenate(
            [
                rep_flat.T,
                split_flat.reshape(LAYERS, rows, 3).transpose(1, 0, 2).reshape(rows, 6),
                jnp.zeros((rows, LANES - 18), f32),
            ],
            axis=1,
        ).astype(b16)
        gather = partial(lax.all_gather, axis_name="dp", axis=0, tiled=True)
        att = [
            (gather(jnp.concatenate([low[0, :, :ATT], block], axis=1)),),
            (gather(low[1, :, :ATT]),),
        ]
        ffn = [(gather(low[layer, :, ATT:]),) for layer in range(LAYERS)]
    rep, split = unpack(att[0])
    both = range(MICRO)
    seg = segments.reshape(MICRO, 1, SEQ)

    out = [attention_first(m, block_in, seg, split, att[0]) for m in both]
    qkv0, probs0, ctx0 = ([o[i] for o in out] for i in (1, 2, 3))
    met = [exchange(o[0]) for o in out]
    out = [
        feed_forward(m, 0, block_in, out[m][0], met[m], rep, split, ffn[0]) for m in both
    ]
    n1_0, s1_0, low1_0, act0, slope0 = ([o[i] for o in out] for i in range(1, 6))
    met = [exchange(o[0]) for o in out]
    out = [
        attention_next(m, 1, n1_0[m], out[m][0], met[m], rep, seg, split, att[1]) for m in both
    ]
    qkv1, probs1, ctx1, n2_0, s2_0, low_h1 = ([o[i] for o in out] for i in range(1, 7))
    met = [exchange(o[0]) for o in out]
    out = [
        feed_forward(m, 1, n2_0[m], out[m][0], met[m], rep, split, ffn[1]) for m in both
    ]
    n1_1, s1_1, low1_1, act1, slope1 = ([o[i] for o in out] for i in range(1, 6))
    met = [exchange(o[0]) for o in out]

    out = [
        feed_back_top(m, 1, out_grad, n1_1[m], out[m][0], met[m], rep, slope1[m], ffn[1])
        for m in both
    ]
    res, dffn, din, vec_f1 = ([o[i] for o in out] for i in range(1, 5))
    block_out = jnp.stack([o[5] for o in out])
    met = [exchange(o[0]) for o in out]
    out = [
        attention_back(
            1, res[m], out[m][0], met[m], n1_1[m], s1_1[m], rep, qkv1[m], probs1[m], ctx1[m], att[1]
        )
        for m in both
    ]
    grad_f1 = reduce_chunk(
        matrix_gradient([(low1_1, din, FFT), (dffn, act1, FFT)], pieced, ndp)
    )
    mid, datt, dqkv, vec_a1 = ([o[i] for o in out] for i in range(1, 5))
    met = [exchange(o[0]) for o in out]
    out = [
        feed_back(0, mid[m], out[m][0], met[m], n2_0[m], s2_0[m], rep, slope0[m], ffn[0])
        for m in both
    ]
    grad_a1 = reduce_chunk(
        matrix_gradient([(low_h1, dqkv, QKV), (datt, ctx1, HD)], pieced, ndp)
    )
    res, dffn, din, vec_f0 = ([o[i] for o in out] for i in range(1, 5))
    met = [exchange(o[0]) for o in out]
    out = [
        attention_back(
            0, res[m], out[m][0], met[m], n1_0[m], s1_0[m], rep, qkv0[m], probs0[m], ctx0[m], att[0]
        )
        for m in both
    ]
    grad_f0 = reduce_chunk(
        matrix_gradient([(low1_0, din, FFT), (dffn, act0, FFT)], pieced, ndp)
    )
    mid, datt, dqkv, vec_a0 = ([o[i] for o in out] for i in range(1, 5))
    met = [exchange(o[0]) for o in out]
    grad_a0 = reduce_chunk(
        matrix_gradient(
            [([block_in] * MICRO, dqkv, QKV), (datt, ctx0, HD)],
            pieced,
            ndp,
            vectors=vec_a0 + vec_f0 + vec_a1 + vec_f1,
        )
    )
    input_grad = finish_input(mid, [o[0] for o in out], met)

    block = grad_a0[:, ATT:]
    grad_rep = block[:, :12].T.reshape(rep_vectors.shape)
    grad_split = (
        block[:, 12:18].reshape(rows, LAYERS, 3).transpose(1, 0, 2).reshape(split_vectors.shape)
    )
    tensor_first = (lax.axis_index("tensor") == 0).astype(f32)
    square = lambda a: jnp.sum(a * a)
    local_squares = (
        square(grad_a0[:, :ATT])
        + square(grad_f0)
        + square(grad_a1)
        + square(grad_f1)
        + square(block[:, 12:18])
        + tensor_first * square(block[:, :12])
    )
    total = sum_everywhere(jnp.full((8, LANES), local_squares, f32))[0, 0]
    grad_norm = jnp.sqrt(total)
    factor = jnp.minimum(1.0, clip_limit / (grad_norm + 1e-06))
    clipped_rep = grad_rep * factor
    masters = [a.reshape(tiled_shape) for a in (weights, weights_first, weights_second)]
    if pieced:
        new = update_matrices(*masters, [grad_a0, grad_f0, grad_a1, grad_f1], factor)
    else:
        grad = jnp.stack(
            [
                jnp.concatenate([grad_a0[:, :ATT], grad_f0], axis=1),
                jnp.concatenate([grad_a1, grad_f1], axis=1),
            ]
        ).reshape(tiled_shape)
        new = adamw(*masters, grad * factor, weight_rate, weight_decay)
        new = (*new, new[0].astype(b16))
    new_weights, weights_first_new, weights_second_new, weights_low = (
        a.reshape(shard_shape) for a in new
    )
    new_split, split_first_new, split_second_new = adamw(
        split_vectors, split_first, split_second, grad_split * factor, vector_rate, 0.0
    )
    new_rep, rep_first_new, rep_second_new = adamw(
        rep_vectors, rep_first, rep_second, clipped_rep, vector_rate, 0.0
    )
    return (
        block_out,
        input_grad,
        grad_norm,
        new_weights,
        weights_first_new,
        weights_second_new,
        weights_low,
        new_split,
        split_first_new,
        split_second_new,
        new_split.astype(b16),
        new_rep,
        rep_first_new,
        rep_second_new,
        new_rep.astype(b16),
        clipped_rep[:, 0, :],
    )


def solution(mesh):
    rows, packed, vector = P("dp", None, None), P(None, "tensor", "dp"), P(None, None, "dp")
    return jax.shard_map(
        per_device,
        mesh=mesh,
        in_specs=(rows, rows, P("dp", None)) + (packed,) * 6 + (vector,) * 3,
        out_specs=(rows, rows, P()) + (packed,) * 8 + (vector,) * 4 + (P(None, "dp"),),
        check_vma=False,
    )
```

time: 1090 us -> 698 us (0.64)
  Pallas kernels: 0 us -> 376 us
  waiting for transfers between devices: 536 us -> 198 us
  local copies, waits for them, and re-layouts: 183 us -> 27.6 us
  matrix products: 135 us -> 0 us
  blocking collectives: 92.4 us -> 0 us
  other arithmetic: 116 us -> 26.7 us
  starting transfers between devices: 1.47 us -> 56.4 us
  between operations: 20.7 us -> 7.75 us
    pallas_call x0 -> x28, Pallas kernels: none -> 376 us  [the longest x4 222 us: assemble(): call(body, [((2, half, rows, cols), b16)], [ANY] * len(parts), [pltpu.Sem...]
    reduce_scatter x1 -> x0, waiting for transfers between devices: 271 us -> none  [per_device(): lax.psum_scatter(jnp.stack(matrix_grads).reshape(tiled_shape), 'dp', scat...]
    ppermute x0 -> x73, waiting for transfers between devices: none -> 198 us  [the longest x52 179 us: move(): return lax.ppermute(a, 'dp', pairs_of(lax.axis_size('dp'), kind))]
    psum x8 -> x0, waiting for transfers between devices: 148 us -> none  [the longest x2 50.8 us: layer_forward(): ffn_out = lax.psum(ffn_part, 'tensor').astype(jnp.float32)]
    dot_general x64 -> x0, matrix products: 135 us -> none  [the longest x8 26.7 us: matrix_gradient(): lax.dot_general(joined[2 * pair_index], joined[2 * pair_index + 1], contr...]
    all_gather x1 -> x0, waiting for transfers between devices: 59 us -> none  [per_device(): lax.all_gather(weights_tiled.astype(jnp.bfloat16), 'dp', axis=1, tiled=True)]
    slice x14 -> x2, local copies, waits for them, and re-layouts: 59 us -> 1.09 us  [the longest x1 0.58 us: per_device(): clipped_rep[:, 0, :]]
    unnamed x14 -> x0, waiting for transfers between devices: 57.8 us -> none
  transfers between devices with their start and end apart: 12 -> 73, of which waited for: 12 -> 37; matrix products, arithmetic and copies ran while one was open for 18% -> 3% of each run, Pallas kernels for 0% -> 51%
where the time goes in v1:
time: 698 us; the launch traced here: 693 us
  Pallas kernels  376 us (54%)
  waiting for transfers between devices  198 us (28%)
  starting transfers between devices  56.4 us (8%)
  local copies, waits for them, and re-layouts  27.6 us (4%)
  other arithmetic  26.7 us (4%)
  between operations  7.75 us (1%)
    pallas_call x4, Pallas kernels, assemble(): call(body, [((2, half, rows, cols), b16)], [ANY] * len(parts), [pltpu.Sem...  222 us
    ppermute x52, waiting for transfers between devices, move(): return lax.ppermute(a, 'dp', pairs_of(lax.axis_size('dp'), kind))  179 us
    ppermute x52, starting transfers between devices, move(): return lax.ppermute(a, 'dp', pairs_of(lax.axis_size('dp'), kind))  34.3 us
    pallas_call x4, Pallas kernels, attention_back(): call(body, [((SEQ, D), b16), ((SEQ, D), f32), ((SEQ, D), b16), ((SEQ, QKV...  28.8 us
    pallas_call x4, Pallas kernels, matrix_gradient(): call(body, outs, specs, [pltpu.VMEM((D, step), f32)], flops=2 * MICRO * S...  27.6 us
    pallas_call x4, Pallas kernels, feed_forward(): call(body, [((SEQ, D), b16), ((SEQ, D), f32), ((SEQ, 1), f32), ((SEQ, D),...  26.6 us
    unnamed x155, local copies, waits for them, and re-layouts  22.7 us
    ppermute x17, starting transfers between devices, exchange(): return lax.ppermute(a, 'tensor', [(0, 1), (1, 0)])  18.4 us
  transfers between devices with their start and end apart: 73, of which 37 were waited for; matrix products, arithmetic and copies ran while one was open for 3% of the time, Pallas kernels for 51%

profile of v1, /device:TPU:0, one launch (start us, length us, event | category | flops | bytes accessed | tf_op | source)
XLA Modules:
  0.0 693.0 jit_solution(12047157348693293977)
XLA Ops:
  8.7 9.2 %collective-permute-done.9.refs_1_ = bf16[48,3072]{1,0:T(8,128)(2,1)S(1)} collective-permute-done((bf16[48,3072]{1,0:T(8,128)(2,1)}, bf16[48,3072]{1,0:T(8,128)(2,1)S(1)}, u32[]{:S(2)}, u32[]{:S(2)}) %collective-permute-start.9) | collective-permute-done | bytes 294944 | tf_op jit(solution)/shard_map/ppermute | solution.py:90
  18.0 10.0 %collective-permute-done.10.refs_2_ = bf16[48,3072]{1,0:T(8,128)(2,1)S(1)} collective-permute-done((bf16[48,3072]{1,0:T(8,128)(2,1)S(1)}, bf16[48,3072]{1,0:T(8,128)(2,1)S(1)}, u32[]{:S(2)}, u32[]{:S(2)}) %collective-permute-start.10) | collective-permute-done | bytes 294944 | tf_op jit(solution)/shard_map/ppermute | solution.py:90
  44.4 6.3 collective-permute-done.14.refs_6_
  55.2 72.6 %shard_map.247.refs_0_ = bf16[2,4,48,3072]{3,2,1,0:T(8,128)(2,1)} custom-call(bf16[48,3072]{1,0:T(8,128)(2,1)} %get-tuple-element.126.refs_0_, bf16[48,3072]{1,0:T(8,128)(2,1)} %copy-done.40, bf16[48,3072]{1,0:T(8,128)(2,1)} %copy-done.41, bf16[48,3072]{1,0:T(8,128)(2,1)} %copy-done.42, bf16[48,3072]{1,0:T(8,128)(2,1)} %copy-done.43, ...), custom_call_target="tpu_custom_call" | custom-call | bytes 4718592 | tf_op jit(solution)/shard_map/pallas_call | solution.py:111
  130.4 12.2 %collective-permute-done.1.refs_2_ = bf16[48,1664]{1,0:T(8,128)(2,1)S(1)} collective-permute-done((bf16[48,1664]{1,0:T(8,128)(2,1)S(1)}, bf16[48,1664]{1,0:T(8,128)(2,1)S(1)}, u32[]{:S(2)}, u32[]{:S(2)}) %collective-permute-start.1) | collective-permute-done | bytes 159776 | tf_op jit(solution)/shard_map/ppermute | solution.py:90
  145.1 6.3 collective-permute-done.2.refs_3_
  158.8 39.9 %shard_map.244.refs_0_ = bf16[2,4,48,1664]{3,2,1,0:T(8,128)(2,1)} custom-call(bf16[48,1664]{1,0:T(8,128)(2,1)} %get-tuple-element.122.refs_0_, bf16[48,1664]{1,0:T(8,128)(2,1)} %copy-done.51, bf16[48,1664]{1,0:T(8,128)(2,1)} %copy-done.52, bf16[48,1664]{1,0:T(8,128)(2,1)} %copy-done.55, bf16[48,1664]{1,0:T(8,128)(2,1)} %copy-done.53, ...), custom_call_target="tpu_custom_call" | custom-call | bytes 2555904 | tf_op jit(solution)/shard_map/pallas_call | solution.py:111
  201.9 6.8 collective-permute-done.31.refs_5_
  208.6 6.3 collective-permute-done.32.refs_6_
  221.6 72.6 %shard_map.251.refs_0_ = bf16[2,4,48,3072]{3,2,1,0:T(8,128)(2,1)} custom-call(bf16[48,3072]{1,0:T(8,128)(2,1)} %get-tuple-element.132.refs_0_, bf16[48,3072]{1,0:T(8,128)(2,1)} %copy-done.36, bf16[48,3072]{1,0:T(8,128)(2,1)} %copy-done.37, bf16[48,3072]{1,0:T(8,128)(2,1)} %copy-done.39, bf16[48,3072]{1,0:T(8,128)(2,1)} %copy-done.38, ...), custom_call_target="tpu_custom_call" | custom-call | bytes 4718592 | tf_op jit(solution)/shard_map/pallas_call | solution.py:111
  295.5 6.9 collective-permute-done.18.refs_1_
  322.6 36.9 %shard_map.249.refs_0_ = bf16[2,4,48,1536]{3,2,1,0:T(8,128)(2,1)} custom-call(bf16[48,1536]{1,0:T(8,128)(2,1)} %get-tuple-element.129.refs_0_, bf16[48,1536]{1,0:T(8,128)(2,1)} %copy-done.59, bf16[48,1536]{1,0:T(8,128)(2,1)} %copy-done.61, bf16[48,1536]{1,0:T(8,128)(2,1)} %copy-done.63, bf16[48,1536]{1,0:T(8,128)(2,1)} %copy-done.60, ...), custom_call_target="tpu_custom_call" | custom-call | bytes 2359296 | tf_op jit(solution)/shard_map/pallas_call | solution.py:111
  383.3 6.7 shard_map.255
  391.8 6.6 shard_map.248
  401.4 6.9 %shard_map.256 = (bf16[256,768]{1,0:T(8,128)(2,1)}, bf16[256,1152]{1,0:T(8,128)(2,1)}, bf16[6,256,256]{2,1,0:T(8,128)(2,1)}, bf16[256,384]{1,0:T(8,128)(2,1)}, f...) custom-call(f32[256,768]{1,0:T(8,128)} %get-tuple-element.138.n_ref.n1_ref, ...), custom_call_target="tpu_custom_call" | custom-call | flops 805306368 | bytes 8388608 | tf_op jit(solution)/shard_map/pallas_call | solution.py:349
  410.3 6.5 shard_map.250
  419.3 6.7 shard_map.257
  427.9 6.7 shard_map.252
  436.3 6.7 shard_map.258
  445.0 6.9 shard_map.253
  453.7 7.2 %shard_map.262 = (bf16[256,768]{1,0:T(8,128)(2,1)}, f32[256,768]{1,0:T(8,128)}, bf16[256,768]{1,0:T(8,128)(2,1)}, bf16[256,1152]{1,0:T(8,128)(2,1)}, f32[8,768]{1,0:T(8,128)}) custom-call(f32[256,768]{1,0:T(8,128)} %get-tuple-element.164.res_ref, bf16[256,768]{1,0:T(8,128)(2,1)} %get-tuple-element.165.own_ref, bf16[256,768]{1,0:T(8,128)(2,1)} %copy-done.23, ...), custom_call_target="tpu_custom_call" | custom-call | flops 1610612736 | bytes 9437184 | tf_op jit(solution)/shard_map/pallas_call | solution.py:549
  461.7 7.2 %shard_map.259 = (bf16[256,768]{1,0:T(8,128)(2,1)}, f32[256,768]{1,0:T(8,128)}, bf16[256,768]{1,0:T(8,128)(2,1)}, bf16[256,1152]{1,0:T(8,128)(2,1)}, f32[8,768]{1,0:T(8,128)}) custom-call(f32[256,768]{1,0:T(8,128)} %get-tuple-element.146.res_ref, bf16[256,768]{1,0:T(8,128)(2,1)} %get-tuple-element.147.own_ref, bf16[256,768]{1,0:T(8,128)(2,1)} %copy-done.25, ...), custom_call_target="tpu_custom_call" | custom-call | flops 1610612736 | bytes 9437184 | tf_op jit(solution)/shard_map/pallas_call | solution.py:549
  476.2 8.1 %shard_map.269 = (bf16[2,4,48,3072]{3,2,1,0:T(8,128)(2,1)}, bf16[2,4,48,3072]{3,2,1,0:T(8,128)(2,1)}) custom-call(bf16[256,768]{1,0:T(8,128)(2,1)} %get-tuple-element.214.refs_0_, bf16[256,768]{1,0:T(8,128)(2,1)} %get-tuple-element.215.refs_1_, bf16[256,1536]{1,0:T(8,128)(2,1)} %get-tuple-element.216.refs_2_, bf16[256,1536]{1,0:T(8,128)(2,1)} %get-tuple-element.217.refs_3_, ...), custom_call_target="tpu_custom_call" | custom-call | flops 2415919104 | bytes 9437184 | tf_op jit(solution)/shard_map/pallas_call | solution.py:639
  486.9 7.0 %shard_map.263 = (bf16[256,768]{1,0:T(8,128)(2,1)}, f32[256,768]{1,0:T(8,128)}, bf16[256,768]{1,0:T(8,128)(2,1)}, bf16[256,1536]{1,0:T(8,128)(2,1)}, f32[8,768]{1,0:T(8,128)}) custom-call(f32[256,768]{1,0:T(8,128)} %get-tuple-element.170.mid_ref, bf16[256,768]{1,0:T(8,128)(2,1)} %get-tuple-element.171.own_ref, bf16[256,768]{1,0:T(8,128)(2,1)} %copy-done.16, ...), custom_call_target="tpu_custom_call" | custom-call | flops 1207959552 | bytes 11534336 | tf_op jit(solution)/shard_map/pallas_call | solution.py:490
  495.8 6.8 shard_map.260
  506.3 7.2 %shard_map.264 = (bf16[256,768]{1,0:T(8,128)(2,1)}, f32[256,768]{1,0:T(8,128)}, bf16[256,768]{1,0:T(8,128)(2,1)}, bf16[256,1152]{1,0:T(8,128)(2,1)}, f32[8,768]{1,0:T(8,128)}) custom-call(f32[256,768]{1,0:T(8,128)} %get-tuple-element.174.res_ref, bf16[256,768]{1,0:T(8,128)(2,1)} %get-tuple-element.175.own_ref, bf16[256,768]{1,0:T(8,128)(2,1)} %copy-done.21, ...), custom_call_target="tpu_custom_call" | custom-call | flops 1610612736 | bytes 9437184 | tf_op jit(solution)/shard_map/pallas_call | solution.py:549
  514.3 7.2 %shard_map.261 = (bf16[256,768]{1,0:T(8,128)(2,1)}, f32[256,768]{1,0:T(8,128)}, bf16[256,768]{1,0:T(8,128)(2,1)}, bf16[256,1152]{1,0:T(8,128)(2,1)}, f32[8,768]{1,0:T(8,128)}) custom-call(f32[256,768]{1,0:T(8,128)} %get-tuple-element.156.res_ref, bf16[256,768]{1,0:T(8,128)(2,1)} %get-tuple-element.157.own_ref, bf16[256,768]{1,0:T(8,128)(2,1)} %copy-done.22, ...), custom_call_target="tpu_custom_call" | custom-call | flops 1610612736 | bytes 9437184 | tf_op jit(solution)/shard_map/pallas_call | solution.py:549
  528.1 8.2 %shard_map.267 = (bf16[2,4,48,3072]{3,2,1,0:T(8,128)(2,1)}, bf16[2,4,48,3072]{3,2,1,0:T(8,128)(2,1)}) custom-call(bf16[256,768]{1,0:T(8,128)(2,1)} %get-tuple-element.196.refs_0_, bf16[256,768]{1,0:T(8,128)(2,1)} %get-tuple-element.197.refs_1_, bf16[256,1536]{1,0:T(8,128)(2,1)} %get-tuple-element.198.refs_2_, bf16[256,1536]{1,0:T(8,128)(2,1)} %get-tuple-element.199.refs_3_, ...), custom_call_target="tpu_custom_call" | custom-call | flops 2415919104 | bytes 9437184 | tf_op jit(solution)/shard_map/pallas_call | solution.py:639
  547.2 9.5 %collective-permute-done.49 = bf16[4,48,1664]{2,1,0:T(8,128)(2,1)S(1)} collective-permute-done((bf16[4,48,1664]{2,1,0:T(8,128)(2,1)S(1)}, bf16[4,48,1664]{2,1,0:T(8,128)(2,1)S(1)}, u32[]{:S(2)}, u32[]{:S(2)}) %collective-permute-start.49) | collective-permute-done | bytes 639008 | tf_op jit(solution)/shard_map/ppermute | solution.py:90
  574.0 8.0 %collective-permute-done.64 = bf16[4,48,3072]{2,1,0:T(8,128)(2,1)S(1)} collective-permute-done((bf16[4,48,3072]{2,1,0:T(8,128)(2,1)S(1)}, bf16[4,48,3072]{2,1,0:T(8,128)(2,1)S(1)}, u32[]{:S(2)}, u32[]{:S(2)}) %collective-permute-start.64) | collective-permute-done | bytes 1179680 | tf_op jit(solution)/shard_map/ppermute | solution.py:90
  585.9 20.4 %collective-permute-done.54 = bf16[4,48,3072]{2,1,0:T(8,128)(2,1)S(1)} collective-permute-done((bf16[4,48,3072]{2,1,0:T(8,128)(2,1)S(1)}, bf16[4,48,3072]{2,1,0:T(8,128)(2,1)S(1)}, u32[]{:S(2)}, u32[]{:S(2)}) %collective-permute-start.54) | collective-permute-done | bytes 1179680 | tf_op jit(solution)/shard_map/ppermute | solution.py:90
  679.0 10.1 %shard_map.270 = (f32[2,1728,128]{2,1,0:T(8,128)}, f32[2,1728,128]{2,1,0:T(8,128)}, f32[2,1728,128]{2,1,0:T(8,128)}, bf16[2,1728,128]{2,1,0:T(8,128)(2,1)}) custom-call(f32[1,1]{1,0:T(1,128)} %bitcast.40.f_ref, f32[2,1728,128]{2,1,0:T(8,128)} %bitcast.146, f32[2,1728,128]{2,1,0:T(8,128)} %bitcast.147, f32[2,1728,128]{2,1,0:T(8,128)} %bitcast.148, ...), custom_call_target="tpu_custom_call" | custom-call | flops 8847360 | bytes 13271040 | tf_op jit(solution)/shard_map/pallas_call | solution.py:730
  (342 shorter events, 238.4 us)
Async XLA Ops:
  5.7 12.3 %collective-permute-start.9 = (bf16[48,3072]{1,0:T(8,128)(2,1)}, bf16[48,3072]{1,0:T(8,128)(2,1)S(1)}, u32[]{:S(2)}, u32[]{:S(2)}) collective-permute-start(bf16[48,3072]{1,0:T(8,128)(2,1)} %get-tuple-element.126.refs_0_), channel_id=1, source_target_pairs={{0,8},{2,10},{4,12},{6,14},{8,16},{10,18},{12,20},{14,22},{16,24},... | collective-permute-start | bytes 884744 | tf_op jit(solution)/shard_map/ppermute | solution.py:90
  29.2 15.2 %collective-permute-start.13 = (bf16[48,3072]{1,0:T(8,128)(2,1)S(1)}, bf16[48,3072]{1,0:T(8,128)(2,1)S(1)}, u32[]{:S(2)}, u32[]{:S(2)}) collective-permute-start(bf16[48,3072]{1,0:T(8,128)(2,1)S(1)} %collective-permute-done.9.refs_1_), channel_id=1, source_target_pairs={{0,4},{2,6},{4,0},{6,2},{8,12},{10,14},{12,8},{14,10},{16,20},{18,... | collective-permute-start | bytes 884744 | tf_op jit(solution)/shard_map/ppermute | solution.py:90
  30.0 20.8 %collective-permute-start.14 = (bf16[48,3072]{1,0:T(8,128)(2,1)S(1)}, bf16[48,3072]{1,0:T(8,128)(2,1)S(1)}, u32[]{:S(2)}, u32[]{:S(2)}) collective-permute-start(bf16[48,3072]{1,0:T(8,128)(2,1)S(1)} %collective-permute-done.10.refs_2_), channel_id=1, source_target_pairs={{0,4},{2,6},{4,0},{6,2},{8,12},{10,14},{12,8},{14,10},{16,20},{18,... | collective-permute-start | bytes 884744 | tf_op jit(solution)/shard_map/ppermute | solution.py:90
  37.0 17.4 %collective-permute-start.15 = (bf16[48,3072]{1,0:T(8,128)(2,1)S(1)}, bf16[48,3072]{1,0:T(8,128)(2,1)S(1)}, u32[]{:S(2)}, u32[]{:S(2)}) collective-permute-start(bf16[48,3072]{1,0:T(8,128)(2,1)S(1)} %collective-permute-done.11.refs_3_), channel_id=1, source_target_pairs={{0,4},{2,6},{4,0},{6,2},{8,12},{10,14},{12,8},{14,10},{16,20},{18,... | collective-permute-start | bytes 884744 | tf_op jit(solution)/shard_map/ppermute | solution.py:90
  38.0 89.9 %collective-permute-start.27 = (bf16[48,3072]{1,0:T(8,128)(2,1)}, bf16[48,3072]{1,0:T(8,128)(2,1)S(1)}, u32[]{:S(2)}, u32[]{:S(2)}) collective-permute-start(bf16[48,3072]{1,0:T(8,128)(2,1)} %get-tuple-element.132.refs_0_), channel_id=1, source_target_pairs={{0,8},{2,10},{4,12},{6,14},{8,16},{10,18},{12,20},{14,22},{16,24},... | collective-permute-start | bytes 884744 | tf_op jit(solution)/shard_map/ppermute | solution.py:90
  38.1 89.9 %collective-permute-start = (bf16[48,1664]{1,0:T(8,128)(2,1)}, bf16[48,1664]{1,0:T(8,128)(2,1)S(1)}, u32[]{:S(2)}, u32[]{:S(2)}) collective-permute-start(bf16[48,1664]{1,0:T(8,128)(2,1)} %get-tuple-element.122.refs_0_), channel_id=1, source_target_pairs={{0,8},{2,10},{4,12},{6,14},{8,16},{10,18},{12,20},{14,22},{16,24},... | collective-permute-start | bytes 479240 | tf_op jit(solution)/shard_map/ppermute | solution.py:90
  127.8 253.9 %collective-permute-start.16 = (bf16[2,4,48,3072]{3,2,1,0:T(8,128)(2,1)}, bf16[2,4,48,3072]{3,2,1,0:T(8,128)(2,1)S(1)}, u32[]{:S(2)}, u32[]{:S(2)}) collective-permute-start(bf16[2,4,48,3072]{3,2,1,0:T(8,128)(2,1)} %shard_map.247.refs_0_), channel_id=1, source_target_pairs={{0,2},{2,0},{4,6},{6,4},{8,10},{10,8},{12,14},{14,12},{16,18},{18,... | collective-permute-start | bytes 7077896 | tf_op jit(solution)/shard_map/ppermute | solution.py:90
  127.9 15.7 %collective-permute-start.28 = (bf16[48,3072]{1,0:T(8,128)(2,1)S(1)}, bf16[48,3072]{1,0:T(8,128)(2,1)S(1)}, u32[]{:S(2)}, u32[]{:S(2)}) collective-permute-start(bf16[48,3072]{1,0:T(8,128)(2,1)S(1)} %collective-permute-done.27.refs_1_), channel_id=1, source_target_pairs={{0,8},{2,10},{4,12},{6,14},{8,16},{10,18},{12,20},{14,22},{16,24},... | collective-permute-start | bytes 884744 | tf_op jit(solution)/shard_map/ppermute | solution.py:90
  128.0 14.5 %collective-permute-start.1 = (bf16[48,1664]{1,0:T(8,128)(2,1)S(1)}, bf16[48,1664]{1,0:T(8,128)(2,1)S(1)}, u32[]{:S(2)}, u32[]{:S(2)}) collective-permute-start(bf16[48,1664]{1,0:T(8,128)(2,1)S(1)} %collective-permute-done.refs_1_), channel_id=1, source_target_pairs={{0,8},{2,10},{4,12},{6,14},{8,16},{10,18},{12,20},{14,22},{16,24},... | collective-permute-start | bytes 479240 | tf_op jit(solution)/shard_map/ppermute | solution.py:90
  128.4 14.2 %collective-permute-start.3 = (bf16[48,1664]{1,0:T(8,128)(2,1)S(1)}, bf16[48,1664]{1,0:T(8,128)(2,1)S(1)}, u32[]{:S(2)}, u32[]{:S(2)}) collective-permute-start(bf16[48,1664]{1,0:T(8,128)(2,1)S(1)} %copy-done.50), channel_id=1, source_target_pairs={{0,4},{2,6},{4,0},{6,2},{8,12},{10,14},{12,8},{14,10},{16,20},{18,... | collective-permute-start | bytes 479240 | tf_op jit(solution)/shard_map/ppermute | solution.py:90
  129.6 14.4 %collective-permute-start.4 = (bf16[48,1664]{1,0:T(8,128)(2,1)S(1)}, bf16[48,1664]{1,0:T(8,128)(2,1)S(1)}, u32[]{:S(2)}, u32[]{:S(2)}) collective-permute-start(bf16[48,1664]{1,0:T(8,128)(2,1)S(1)} %collective-permute-done.refs_1_), channel_id=1, source_target_pairs={{0,4},{2,6},{4,0},{6,2},{8,12},{10,14},{12,8},{14,10},{16,20},{18,... | collective-permute-start | bytes 479240 | tf_op jit(solution)/shard_map/ppermute | solution.py:90
  142.6 57.2 %collective-permute-start.30 = (bf16[48,3072]{1,0:T(8,128)(2,1)S(1)}, bf16[48,3072]{1,0:T(8,128)(2,1)S(1)}, u32[]{:S(2)}, u32[]{:S(2)}) collective-permute-start(bf16[48,3072]{1,0:T(8,128)(2,1)S(1)} %copy-done.35), channel_id=1, source_target_pairs={{0,4},{2,6},{4,0},{6,2},{8,12},{10,14},{12,8},{14,10},{16,20},{18,... | collective-permute-start | bytes 884744 | tf_op jit(solution)/shard_map/ppermute | solution.py:90
  143.7 57.2 %collective-permute-start.29 = (bf16[48,3072]{1,0:T(8,128)(2,1)S(1)}, bf16[48,3072]{1,0:T(8,128)(2,1)S(1)}, u32[]{:S(2)}, u32[]{:S(2)}) collective-permute-start(bf16[48,3072]{1,0:T(8,128)(2,1)S(1)} %collective-permute-done.28.refs_2_), channel_id=1, source_target_pairs={{0,8},{2,10},{4,12},{6,14},{8,16},{10,18},{12,20},{14,22},{16,24},... | collective-permute-start | bytes 884744 | tf_op jit(solution)/shard_map/ppermute | solution.py:90
  198.7 161.5 %collective-permute-start.7 = (bf16[2,4,48,1664]{3,2,1,0:T(8,128)(2,1)}, bf16[2,4,48,1664]{3,2,1,0:T(8,128)(2,1)S(1)}, u32[]{:S(2)}, u32[]{:S(2)}) collective-permute-start(bf16[2,4,48,1664]{3,2,1,0:T(8,128)(2,1)} %shard_map.244.refs_0_), channel_id=1, source_target_pairs={{0,2},{2,0},{4,6},{6,4},{8,10},{10,8},{12,14},{14,12},{16,18},{18,... | collective-permute-start | bytes 3833864 | tf_op jit(solution)/shard_map/ppermute | solution.py:90
  199.8 15.1 %collective-permute-start.32 = (bf16[48,3072]{1,0:T(8,128)(2,1)S(1)}, bf16[48,3072]{1,0:T(8,128)(2,1)S(1)}, u32[]{:S(2)}, u32[]{:S(2)}) collective-permute-start(bf16[48,3072]{1,0:T(8,128)(2,1)S(1)} %collective-permute-done.28.refs_2_), channel_id=1, source_target_pairs={{0,4},{2,6},{4,0},{6,2},{8,12},{10,14},{12,8},{14,10},{16,20},{18,... | collective-permute-start | bytes 884744 | tf_op jit(solution)/shard_map/ppermute | solution.py:90
  200.9 20.0 %collective-permute-start.33 = (bf16[48,3072]{1,0:T(8,128)(2,1)S(1)}, bf16[48,3072]{1,0:T(8,128)(2,1)S(1)}, u32[]{:S(2)}, u32[]{:S(2)}) collective-permute-start(bf16[48,3072]{1,0:T(8,128)(2,1)S(1)} %collective-permute-done.29.refs_3_), channel_id=1, source_target_pairs={{0,4},{2,6},{4,0},{6,2},{8,12},{10,14},{12,8},{14,10},{16,20},{18,... | collective-permute-start | bytes 884744 | tf_op jit(solution)/shard_map/ppermute | solution.py:90
  294.3 123.6 %collective-permute-start.34 = (bf16[2,4,48,3072]{3,2,1,0:T(8,128)(2,1)}, bf16[2,4,48,3072]{3,2,1,0:T(8,128)(2,1)S(1)}, u32[]{:S(2)}, u32[]{:S(2)}) collective-permute-start(bf16[2,4,48,3072]{3,2,1,0:T(8,128)(2,1)} %shard_map.251.refs_0_), channel_id=1, source_target_pairs={{0,2},{2,0},{4,6},{6,4},{8,10},{10,8},{12,14},{14,12},{16,18},{18,... | collective-permute-start | bytes 7077896 | tf_op jit(solution)/shard_map/ppermute | solution.py:90
  359.5 40.0 %collective-permute-start.25 = (bf16[2,4,48,1536]{3,2,1,0:T(8,128)(2,1)}, bf16[2,4,48,1536]{3,2,1,0:T(8,128)(2,1)S(1)}, u32[]{:S(2)}, u32[]{:S(2)}) collective-permute-start(bf16[2,4,48,1536]{3,2,1,0:T(8,128)(2,1)} %shard_map.249.refs_0_), channel_id=1, source_target_pairs={{0,2},{2,0},{4,6},{6,4},{8,10},{10,8},{12,14},{14,12},{16,18},{18,... | collective-permute-start | bytes 3538952 | tf_op jit(solution)/shard_map/ppermute | solution.py:90
  369.6 12.2 %collective-permute-start.36 = (bf16[256,768]{1,0:T(8,128)(2,1)}, bf16[256,768]{1,0:T(8,128)(2,1)S(1)}, u32[]{:S(2)}, u32[]{:S(2)}) collective-permute-start(bf16[256,768]{1,0:T(8,128)(2,1)} %get-tuple-element.137.own_ref), channel_id=1, source_target_pairs={{0,1},{1,0},{2,3},{3,2},{4,5},{5,4},{6,7},{7,6},{8,9},{9,8},{10,11... | collective-permute-start | bytes 1179656 | tf_op jit(solution)/shard_map/ppermute | solution.py:94
  376.7 14.3 %collective-permute-start.8 = (bf16[256,768]{1,0:T(8,128)(2,1)}, bf16[256,768]{1,0:T(8,128)(2,1)S(1)}, u32[]{:S(2)}, u32[]{:S(2)}) collective-permute-start(bf16[256,768]{1,0:T(8,128)(2,1)} %get-tuple-element.124.own_ref), channel_id=1, source_target_pairs={{0,1},{1,0},{2,3},{3,2},{4,5},{5,4},{6,7},{7,6},{8,9},{9,8},{10,11... | collective-permute-start | bytes 1179656 | tf_op jit(solution)/shard_map/ppermute | solution.py:94
  474.1 29.5 %collective-permute-start.58 = (bf16[2,4,48,1536]{3,2,1,0:T(8,128)(2,1)}, bf16[2,4,48,1536]{3,2,1,0:T(8,128)(2,1)S(1)}, u32[]{:S(2)}, u32[]{:S(2)}) collective-permute-start(bf16[2,4,48,1536]{3,2,1,0:T(8,128)(2,1)} %get-tuple-element.213), channel_id=1, source_target_pairs={{0,2},{2,0},{4,6},{6,4},{8,10},{10,8},{12,14},{14,12},{16,18},{18,... | collective-permute-start | bytes 3538952 | tf_op jit(solution)/shard_map/ppermute | solution.py:90
  475.3 19.7 %collective-permute-start.41 = (bf16[256,768]{1,0:T(8,128)(2,1)S(1)}, bf16[256,768]{1,0:T(8,128)(2,1)S(1)}, u32[]{:S(2)}, u32[]{:S(2)}) collective-permute-start(bf16[256,768]{1,0:T(8,128)(2,1)S(1)} %copy-done.13), channel_id=1, source_target_pairs={{0,1},{1,0},{2,3},{3,2},{4,5},{5,4},{6,7},{7,6},{8,9},{9,8},{10,11... | collective-permute-start | bytes 1179656 | tf_op jit(solution)/shard_map/ppermute | solution.py:94
  484.4 56.3 %collective-permute-start.63 = (bf16[2,4,48,3072]{3,2,1,0:T(8,128)(2,1)}, bf16[2,4,48,3072]{3,2,1,0:T(8,128)(2,1)}, u32[]{:S(2)}, u32[]{:S(2)}) collective-permute-start(bf16[2,4,48,3072]{3,2,1,0:T(8,128)(2,1)} %get-tuple-element.223), channel_id=1, source_target_pairs={{0,2},{2,0},{4,6},{6,4},{8,10},{10,8},{12,14},{14,12},{16,18},{18,... | collective-permute-start | bytes 7077896 | tf_op jit(solution)/shard_map/ppermute | solution.py:90
  503.8 23.9 %collective-permute-start.59 = (bf16[4,48,1536]{2,1,0:T(8,128)(2,1)S(1)}, bf16[4,48,1536]{2,1,0:T(8,128)(2,1)S(1)}, u32[]{:S(2)}, u32[]{:S(2)}) collective-permute-start(bf16[4,48,1536]{2,1,0:T(8,128)(2,1)S(1)} %fusion.3), channel_id=1, source_target_pairs={{0,4},{2,6},{4,0},{6,2},{8,12},{10,14},{12,8},{14,10},{16,20},{18,... | collective-permute-start | bytes 1769480 | tf_op jit(solution)/shard_map/ppermute | solution.py:90
  536.3 29.8 %collective-permute-start.53 = (bf16[2,4,48,3072]{3,2,1,0:T(8,128)(2,1)}, bf16[2,4,48,3072]{3,2,1,0:T(8,128)(2,1)S(1)}, u32[]{:S(2)}, u32[]{:S(2)}) collective-permute-start(bf16[2,4,48,3072]{3,2,1,0:T(8,128)(2,1)} %get-tuple-element.205), channel_id=1, source_target_pairs={{0,2},{2,0},{4,6},{6,4},{8,10},{10,8},{12,14},{14,12},{16,18},{18,... | collective-permute-start | bytes 7077896 | tf_op jit(solution)/shard_map/ppermute | solution.py:90
  539.4 17.3 %collective-permute-start.49 = (bf16[4,48,1664]{2,1,0:T(8,128)(2,1)S(1)}, bf16[4,48,1664]{2,1,0:T(8,128)(2,1)S(1)}, u32[]{:S(2)}, u32[]{:S(2)}) collective-permute-start(bf16[4,48,1664]{2,1,0:T(8,128)(2,1)S(1)} %fusion.2), channel_id=1, source_target_pairs={{0,4},{2,6},{4,0},{6,2},{8,12},{10,14},{12,8},{14,10},{16,20},{18,... | collective-permute-start | bytes 1916936 | tf_op jit(solution)/shard_map/ppermute | solution.py:90
  542.3 39.7 %collective-permute-start.64 = (bf16[4,48,3072]{2,1,0:T(8,128)(2,1)S(1)}, bf16[4,48,3072]{2,1,0:T(8,128)(2,1)S(1)}, u32[]{:S(2)}, u32[]{:S(2)}) collective-permute-start(bf16[4,48,3072]{2,1,0:T(8,128)(2,1)S(1)} %fusion.1), channel_id=1, source_target_pairs={{0,4},{2,6},{4,0},{6,2},{8,12},{10,14},{12,8},{14,10},{16,20},{18,... | collective-permute-start | bytes 3538952 | tf_op jit(solution)/shard_map/ppermute | solution.py:90
  566.5 39.7 %collective-permute-start.54 = (bf16[4,48,3072]{2,1,0:T(8,128)(2,1)S(1)}, bf16[4,48,3072]{2,1,0:T(8,128)(2,1)S(1)}, u32[]{:S(2)}, u32[]{:S(2)}) collective-permute-start(bf16[4,48,3072]{2,1,0:T(8,128)(2,1)S(1)} %fusion), channel_id=1, source_target_pairs={{0,4},{2,6},{4,0},{6,2},{8,12},{10,14},{12,8},{14,10},{16,20},{18,... | collective-permute-start | bytes 3538952 | tf_op jit(solution)/shard_map/ppermute | solution.py:90
  583.3 23.6 %collective-permute-start.65 = (bf16[48,3072]{1,0:T(8,128)(2,1)S(1)}, bf16[48,3072]{1,0:T(8,128)(2,1)S(1)}, u32[]{:S(2)}, u32[]{:S(2)}) collective-permute-start(bf16[48,3072]{1,0:T(8,128)(2,1)S(1)} %fusion.4), channel_id=1, source_target_pairs={{0,8},{2,10},{4,12},{6,14},{8,16},{10,18},{12,20},{14,22},{16,24},... | collective-permute-start | bytes 884744 | tf_op jit(solution)/shard_map/ppermute | solution.py:90
  608.0 16.5 %collective-permute-start.66 = (bf16[48,3072]{1,0:T(8,128)(2,1)S(1)}, bf16[48,3072]{1,0:T(8,128)(2,1)S(1)}, u32[]{:S(2)}, u32[]{:S(2)}) collective-permute-start(bf16[48,3072]{1,0:T(8,128)(2,1)S(1)} %fusion.6), channel_id=1, source_target_pairs={{0,8},{2,10},{4,12},{6,14},{8,16},{10,18},{12,20},{14,22},{16,24},... | collective-permute-start | bytes 884744 | tf_op jit(solution)/shard_map/ppermute | solution.py:90
  647.9 16.1 %collective-permute-start.47 = (bf16[256,768]{1,0:T(8,128)(2,1)S(1)}, bf16[256,768]{1,0:T(8,128)(2,1)S(1)}, u32[]{:S(2)}, u32[]{:S(2)}) collective-permute-start(bf16[256,768]{1,0:T(8,128)(2,1)S(1)} %copy-done.17), channel_id=1, source_target_pairs={{0,1},{1,0},{2,3},{3,2},{4,5},{5,4},{6,7},{7,6},{8,9},{9,8},{10,11... | collective-permute-start | bytes 1179656 | tf_op jit(solution)/shard_map/ppermute | solution.py:94
  649.2 18.7 %collective-permute-start.43 = (bf16[256,768]{1,0:T(8,128)(2,1)S(1)}, bf16[256,768]{1,0:T(8,128)(2,1)S(1)}, u32[]{:S(2)}, u32[]{:S(2)}) collective-permute-start(bf16[256,768]{1,0:T(8,128)(2,1)S(1)} %copy-done.18), channel_id=1, source_target_pairs={{0,1},{1,0},{2,3},{3,2},{4,5},{5,4},{6,7},{7,6},{8,9},{9,8},{10,11... | collective-permute-start | bytes 1179656 | tf_op jit(solution)/shard_map/ppermute | solution.py:94
  (114 other events, 1638.4 us)

commit v2 on v1

v2 whole, which is shorter than its diff:
```python
from functools import partial

import jax
import jax.numpy as jnp
from jax import lax
from jax.experimental import pallas as pl
from jax.experimental.pallas import tpu as pltpu
from jax.sharding import PartitionSpec as P

D = 768
HEAD_DIM = 64
LAYERS = 2
SEQ = 256
MICRO = 2
STEP = 3
HD = 384
FFT = 1536
QKV = 3 * HD
ATT = 4 * HD
COLS = ATT + 2 * FFT
VCOL = 2 * HD + FFT
LANES = 128
TILES = COLS // LANES

clip_limit = 1.0
weight_rate = 0.03
weight_decay = 0.01
vector_rate = 0.3
contract_last = (((1,), (1,)), ((), ()))
contract_first = (((0,), (0,)), ((), ()))
f32 = jnp.float32
b16 = jnp.bfloat16
VMEM_LIMIT = 13 * 1024 * 1024
VM = pl.BlockSpec(memory_space=pltpu.VMEM)


def call(body, outs, in_specs, scratch=(), flops=0, moved=0, out_specs=None, trans=0, limit=13):
    if out_specs is None:
        out_specs = [VM] * len(outs)
    return pl.pallas_call(
        body,
        out_shape=[jax.ShapeDtypeStruct(s, d) for s, d in outs],
        in_specs=in_specs,
        out_specs=out_specs,
        scratch_shapes=list(scratch),
        compiler_params=pltpu.CompilerParams(vmem_limit_bytes=limit * 1024 * 1024),
        cost_estimate=pl.CostEstimate(flops=flops, bytes_accessed=moved, transcendentals=trans),
    )


def dot(a, b, dims=(((1,), (0,)), ((), ()))):
    return lax.dot_general(a, b, dims, preferred_element_type=f32)


def norm_rows(value):
    center = value - jnp.mean(value, axis=-1, keepdims=True)
    scale = lax.rsqrt(jnp.mean(center * center, axis=-1, keepdims=True) + 1e-12)
    return center * scale, scale


def norm_back(grad_out, normed, scale, gain):
    inner = grad_out * gain
    back = scale * (
        inner
        - jnp.mean(inner, axis=-1, keepdims=True)
        - normed * jnp.mean(inner * normed, axis=-1, keepdims=True)
    )
    return (
        back,
        jnp.sum(grad_out * normed, axis=0, keepdims=True),
        jnp.sum(grad_out, axis=0, keepdims=True),
    )


def places(ring):
    me = lax.axis_index("dp")
    return lax.div(me, 4), lax.rem(lax.div(me, 2), 2), lax.rem(me, 2)


def pairs_of(ndp, kind):
    if kind in (1, 2, 3):
        return [(i, (i + 4 * kind) % ndp) for i in range(ndp)]
    if kind == "x":
        return [(i, i ^ 2) for i in range(ndp)]
    return [(i, i ^ 1) for i in range(ndp)]


def move(a, kind):
    return lax.ppermute(a, "dp", pairs_of(lax.axis_size("dp"), kind))


def exchange(a):
    return lax.ppermute(a, "tensor", [(0, 1), (1, 0)])


def after(value, *others):
    return lax.optimization_barrier((value,) + others)[0]


def tie(*arrays):
    return lax.optimization_barrier(arrays)


def unique(entries):
    entries = [e if isinstance(e, tuple) else (e, Ellipsis) for e in entries]
    arrays, at = [], []
    for array, _ in entries:
        found = [i for i, a in enumerate(arrays) if a is array]
        if not found:
            found = [len(arrays)]
            arrays.append(array)
        at.append(found[0])
    return arrays, at, [where for _, where in entries]


def stack(entries, rows, cols, lead=None):
    arrays, at, where = unique(entries)
    lead = (len(entries),) if lead is None else lead

    def body(*refs):
        for i in range(len(entries)):
            place = (i,) if len(lead) == 1 else (i // lead[1], i % lead[1])
            refs[-1][place] = refs[at[i]][where[i]]

    size = len(entries) * rows * cols
    return call(body, [(lead + (rows, cols), b16)], [VM] * len(arrays), moved=4 * size)(*arrays)[0]


def settle(mine, met):
    _, ring, rows, cols = mine.shape

    def body(mine_ref, met_ref, out_ref):
        z, x, c = places(ring)
        for other in range(2):
            source = (mine_ref, met_ref)[other]
            for xo in range(2):
                for k in range(ring):
                    zz = lax.rem(z - k + ring, ring)
                    xx = lax.rem(x + xo, 2)
                    cc = lax.rem(c + other, 2)
                    row = pl.multiple_of(((zz * 2 + xx) * 2 + cc) * rows, 16)
                    out_ref[pl.ds(row, rows), :] = source[xo, k]

    return call(
        body, [((4 * ring * rows, cols), b16)], [VM] * 2, moved=16 * ring * rows * cols
    )(mine, met)[0]


def prep(weights_tiled, rep, split):
    tiled_rows = weights_tiled.shape[1]
    rows = tiled_rows // TILES
    per = split.shape[1]

    def body(w_ref, rep_ref, split_ref, a0, f0, l1, every):
        a1, f1 = l1.at[:, :ATT], l1.at[:, ATT:]
        for layer, (a_ref, f_ref) in enumerate(((a0, f0), (a1, f1))):
            for c in range(TILES):
                piece = w_ref[layer, pl.ds(c, rows, stride=TILES), :].astype(b16)
                if c < ATT // LANES:
                    a_ref[:, c * LANES : (c + 1) * LANES] = piece
                else:
                    at = c * LANES - ATT
                    f_ref[:, at : at + LANES] = piece
        row = lax.broadcasted_iota(jnp.int32, (rows, rows), 0)
        col = lax.broadcasted_iota(jnp.int32, (rows, rows), 1)
        eye = (row == col).astype(b16)
        row3 = lax.broadcasted_iota(jnp.int32, (rows, per), 0)
        col3 = lax.broadcasted_iota(jnp.int32, (rows, per), 1)
        gap = col3 - 3 * row3
        block = jnp.zeros((rows, LANES), f32)
        lane = lax.broadcasted_iota(jnp.int32, (rows, LANES), 1)
        rep_cols = dot(eye, rep_ref[...].astype(b16), contract_last)
        rep_wide = jnp.concatenate(
            [rep_cols, jnp.zeros((rows, LANES - 6 * LAYERS), f32)], axis=1
        )
        block = rep_wide
        low = split_ref[...].astype(b16).astype(f32)
        for layer in range(LAYERS):
            for j in range(3):
                pick = jnp.where(gap == j, jnp.broadcast_to(low[layer : layer + 1], (rows, per)), 0.0)
                value = jnp.sum(pick, axis=1, keepdims=True)
                block = jnp.where(lane == 6 * LAYERS + 3 * layer + j, value, block)
        a0[:, ATT:] = block.astype(b16)
        every[:, : ATT + LANES] = a0[...]
        every[:, ATT + LANES : COLS + LANES] = f0[...]
        every[:, COLS + LANES :] = l1[...]

    return call(
        body,
        [
            ((rows, ATT + LANES), b16),
            ((rows, 2 * FFT), b16),
            ((rows, COLS), b16),
            ((rows, 2 * COLS + LANES), b16),
        ],
        [VM] * 3,
        moved=weights_tiled.size * 6,
    )(weights_tiled, rep, split)


def spread_mask(first_row, rows, first, cols):
    row = first_row + lax.broadcasted_iota(jnp.int32, (rows, cols), 0)
    col = first + lax.broadcasted_iota(jnp.int32, (rows, cols), 1)
    gap = col - 3 * row
    return jnp.where((gap >= 0) & (gap < 3), 1.0, 0.0).astype(b16)


def unpack(gathered):
    def body(w_ref, rep_ref, split_ref):
        flat = w_ref[:, ATT:]
        turned = flat.astype(f32).T
        rep_ref[...] = turned[:16]
        low = turned[:24].astype(b16)
        step = VCOL // 3
        for i in range(3):
            rows = D // 3
            mask = spread_mask(i * rows, rows, i * step, step)
            spread = dot(low[:, i * rows : (i + 1) * rows], mask)
            phase = lax.rem(lax.broadcasted_iota(jnp.int32, (1, step), 1), 3)
            for layer in range(LAYERS):
                at = 6 * LAYERS + 3 * layer
                value = jnp.where(
                    phase == 0,
                    spread[at : at + 1],
                    jnp.where(phase == 1, spread[at + 1 : at + 2], spread[at + 2 : at + 3]),
                )
                split_ref[layer : layer + 1, i * step : (i + 1) * step] = value

    return call(
        body,
        [((16, D), f32), ((8, VCOL), f32)],
        [VM],
        moved=D * LANES * 2,
        flops=24 * D * VCOL,
    )(gathered)


def gelu_parts(inner):
    cdf = 0.5 * (1.0 + lax.erf(inner * (0.5**0.5)))
    dens = jnp.exp(-0.5 * inner * inner) * 0.3989422804014327
    return inner * cdf, cdf + inner * dens


def attend(h_low, layer, w_ref, split_ref, seg_ref, part_ref, qkv_ref, probs_ref, ctx_ref):
    mixed = dot(h_low, w_ref[:, :QKV])
    qkv_ref[:, :HD] = (mixed[:, :HD] + split_ref[layer : layer + 1, :HD]).astype(b16)
    qkv_ref[:, HD : 2 * HD] = mixed[:, HD : 2 * HD].astype(b16)
    qkv_ref[:, 2 * HD :] = (
        mixed[:, 2 * HD :] + split_ref[layer : layer + 1, HD : 2 * HD]
    ).astype(b16)
    seg = jnp.broadcast_to(seg_ref[...].astype(f32), (SEQ, SEQ))
    same = seg == seg.T
    low_half = lax.broadcasted_iota(jnp.int32, (1, LANES), 1) < HEAD_DIM
    for pair in range(HD // LANES):
        at = pair * LANES
        query = qkv_ref[:, at : at + LANES].astype(f32) * HEAD_DIM ** (-0.5)
        keys = qkv_ref[:, HD + at : HD + at + LANES]
        values = qkv_ref[:, 2 * HD + at : 2 * HD + at + LANES].astype(f32)
        total = jnp.zeros((SEQ, LANES), f32)
        for half in range(2):
            mine = low_half if half == 0 else ~low_half
            scores = dot(jnp.where(mine, query, 0.0).astype(b16), keys, contract_last)
            scores = jnp.where(same, scores, -1000000000.0)
            raised = jnp.exp(scores - jnp.max(scores, axis=-1, keepdims=True))
            probs = (raised * (1.0 / jnp.sum(raised, axis=-1, keepdims=True))).astype(b16)
            probs_ref[2 * pair + half] = probs
            total = total + dot(probs, jnp.where(mine, values, 0.0).astype(b16))
        ctx_ref[:, at : at + LANES] = total.astype(b16)
    part_ref[...] = dot(ctx_ref[...], w_ref[:, QKV:ATT], contract_last).astype(b16)


ATT_FLOPS = 2 * SEQ * D * ATT + 4 * SEQ * SEQ * HD * 2
FFN_FLOPS = 2 * SEQ * D * 2 * FFT


ATT_OUTS = [((MICRO, SEQ, QKV), b16), ((MICRO, HD // HEAD_DIM, SEQ, SEQ), b16), ((MICRO, SEQ, HD), b16)]


def attention_first(block_in, segments, split, matrix):
    def body(h_ref, seg_ref, split_ref, w_ref, part_ref, qkv_ref, probs_ref, ctx_ref):
        for m in range(MICRO):
            views = [r.at[m] for r in (part_ref, qkv_ref, probs_ref, ctx_ref)]
            attend(h_ref[m], 0, w_ref, split_ref, seg_ref[m], *views)

    return call(
        body,
        [((MICRO, SEQ, D), b16)] + ATT_OUTS,
        [VM] * 4,
        flops=2 * ATT_FLOPS,
        moved=12 << 20,
        limit=16,
    )(block_in, segments, split, matrix)


def attention_next(layer, normed, part_own, part_other, rep, segments, split, matrix):
    base = 6 * (layer - 1)

    def body(n_ref, own_ref, other_ref, rep_ref, seg_ref, split_ref, w_ref, *refs):
        parts, (qkv_ref, probs_ref, ctx_ref, n2_ref, s2_ref, low_ref) = refs[:MICRO], refs[MICRO:]
        for m in range(MICRO):
            first = n_ref[m] * rep_ref[base + 1 : base + 2] + rep_ref[base + 2 : base + 3]
            added = own_ref[m].astype(f32) + other_ref[m].astype(f32)
            n2, s2 = norm_rows(first + added + rep_ref[base + 3 : base + 4])
            n2_ref[m] = n2
            s2_ref[m] = s2
            low = (n2 * rep_ref[base + 4 : base + 5] + rep_ref[base + 5 : base + 6]).astype(b16)
            low_ref[m] = low
            views = [r.at[m] for r in (qkv_ref, probs_ref, ctx_ref)]
            attend(low, layer, w_ref, split_ref, seg_ref[m], parts[m], *views)

    return call(
        body,
        [((SEQ, D), b16)] * MICRO
        + ATT_OUTS
        + [((MICRO, SEQ, D), f32), ((MICRO, SEQ, 1), f32), ((MICRO, SEQ, D), b16)],
        [VM] * 7,
        flops=2 * ATT_FLOPS,
        moved=16 << 20,
        limit=22,
    )(normed, part_own, part_other, rep, segments, split, matrix)


def feed_step(hidden_in, added, layer, rep_ref, split_ref, w_ref, outs):
    base = 6 * layer
    part_ref, n1_ref, s1_ref, low_ref, act_ref, slope_ref = outs
    n1, s1 = norm_rows(hidden_in + added + rep_ref[base : base + 1])
    n1_ref[...] = n1
    s1_ref[...] = s1
    low_ref[...] = (n1 * rep_ref[base + 1 : base + 2] + rep_ref[base + 2 : base + 3]).astype(b16)
    step = 512
    for at in range(0, FFT, step):
        inner = (
            dot(low_ref[...], w_ref[:, at : at + step])
            + split_ref[layer : layer + 1, 2 * HD + at : 2 * HD + at + step]
        )
        active, slope = gelu_parts(inner)
        act_ref[:, at : at + step] = active.astype(b16)
        slope_ref[:, at : at + step] = slope.astype(b16)
    part_ref[...] = dot(act_ref[...], w_ref[:, FFT:], contract_last).astype(b16)


FEED_OUTS = [
    ((SEQ, D), b16),
    ((SEQ, D), f32),
    ((SEQ, 1), f32),
    ((SEQ, D), b16),
    ((SEQ, FFT), b16),
    ((SEQ, FFT), b16),
]


def feed_first(hidden, part_own, part_other, rep, split, matrix):
    def body(h_ref, own_ref, other_ref, rep_ref, split_ref, w_ref, *outs):
        for m in range(MICRO):
            added = own_ref[m].astype(f32) + other_ref[m].astype(f32)
            views = [r.at[m] for r in outs]
            feed_step(h_ref[m].astype(f32), added, 0, rep_ref, split_ref, w_ref, views)

    return call(
        body,
        [((MICRO,) + shape, kind) for shape, kind in FEED_OUTS],
        [VM] * 6,
        flops=2 * FFN_FLOPS,
        moved=20 << 20,
        limit=22,
    )(hidden, part_own, part_other, rep, split, matrix)


def feed_forward(micro, layer, hidden, part_own, part_other, rep, split, matrix):
    base = 6 * layer

    def body(h_ref, own_ref, other_ref, rep_ref, split_ref, w_ref, *outs):
        hidden_in = h_ref[micro] * rep_ref[base - 2 : base - 1] + rep_ref[base - 1 : base]
        added = own_ref[...].astype(f32) + other_ref[...].astype(f32)
        feed_step(hidden_in, added, layer, rep_ref, split_ref, w_ref, outs)

    return call(
        body,
        FEED_OUTS,
        [VM] * 6,
        flops=FFN_FLOPS,
        moved=10 << 20,
    )(hidden, part_own, part_other, rep, split, matrix)


def view(ref, micro):
    return ref.at[micro] if ref.shape[0] == MICRO else ref


def feed_back_tail(grad, n2, s2, layer, rep_ref, slope_ref, w_ref, outs):
    base = 6 * layer
    part_ref, res_ref, dffn_ref, din_ref, vec_ref = outs
    back, gain, shift = norm_back(grad, n2, s2, rep_ref[base + 4 : base + 5])
    res_ref[...] = back
    dffn_ref[...] = back.astype(b16)
    vec_ref[...] = jnp.zeros_like(vec_ref)
    vec_ref[0:1] = jnp.sum(back, axis=0, keepdims=True)
    vec_ref[1:2] = gain
    vec_ref[2:3] = shift
    step = 384
    for at in range(0, FFT, step):
        grad_act = dot(dffn_ref[...], w_ref[:, FFT + at : FFT + at + step])
        grad_in = (slope_ref[:, at : at + step].astype(f32) * grad_act).astype(b16)
        din_ref[:, at : at + step] = grad_in
        row, lane = 3 + at // D, at % D
        vec_ref[row : row + 1, lane : lane + step] = jnp.sum(
            grad_in.astype(f32), axis=0, keepdims=True
        )
    part_ref[...] = dot(din_ref[...], w_ref[:, :FFT], contract_last).astype(b16)


BACK_OUTS = [
    ((SEQ, D), b16),
    ((SEQ, D), f32),
    ((SEQ, D), b16),
    ((SEQ, FFT), b16),
    ((8, D), f32),
]


def feed_back_top(micro, layer, out_grad, n1, part_own, part_other, rep, slope, matrix):
    base = 6 * layer

    def body(g_ref, n_ref, own_ref, other_ref, rep_ref, slope_ref, w_ref, *refs):
        out_ref = refs[5]
        first = n_ref[...] * rep_ref[base + 1 : base + 2] + rep_ref[base + 2 : base + 3]
        added = own_ref[...].astype(f32) + other_ref[...].astype(f32)
        n2, s2 = norm_rows(first + added + rep_ref[base + 3 : base + 4])
        out_ref[...] = (n2 * rep_ref[base + 4 : base + 5] + rep_ref[base + 5 : base + 6]).astype(b16)
        feed_back_tail(
            g_ref[micro].astype(f32), n2, s2, layer, rep_ref, slope_ref, w_ref, refs[:5]
        )

    return call(
        body,
        BACK_OUTS + [((SEQ, D), b16)],
        [VM] * 6 + [VM],
        flops=FFN_FLOPS,
        moved=11 << 20,
    )(out_grad, n1, part_own, part_other, rep, slope, matrix)


def feed_back(micro, layer, mid, part_own, part_other, n2, s2, rep, slope, matrix):
    def body(mid_ref, own_ref, other_ref, n2_ref, s2_ref, rep_ref, slope_ref, w_ref, *refs):
        added = own_ref[...].astype(f32) + other_ref[...].astype(f32)
        feed_back_tail(
            mid_ref[...] + added,
            view(n2_ref, micro)[...],
            view(s2_ref, micro)[...],
            layer,
            rep_ref,
            view(slope_ref, micro),
            w_ref,
            refs[:5],
        )

    return call(
        body,
        BACK_OUTS,
        [VM] * 7 + [VM],
        flops=FFN_FLOPS,
        moved=11 << 20,
    )(mid, part_own, part_other, n2, s2, rep, slope, matrix)


def attention_back(micro, layer, res, part_own, part_other, n1, s1, rep, qkv, probs, ctx, matrix):
    base = 6 * layer

    def body(
        res_ref, own_ref, other_ref, n1_ref, s1_ref, rep_ref, qkv_ref, probs_ref, ctx_ref, w_ref, *refs
    ):
        part_ref, mid_ref, datt_ref, dqkv_ref, vec_ref = refs
        n1_ref, s1_ref, qkv_ref, probs_ref, ctx_ref = (
            view(r, micro) for r in (n1_ref, s1_ref, qkv_ref, probs_ref, ctx_ref)
        )
        grad = res_ref[...] + (own_ref[...].astype(f32) + other_ref[...].astype(f32))
        back, gain, shift = norm_back(grad, n1_ref[...], s1_ref[...], rep_ref[base + 1 : base + 2])
        mid_ref[...] = back
        datt_ref[...] = back.astype(b16)
        vec_ref[...] = jnp.zeros_like(vec_ref)
        vec_ref[0:1] = jnp.sum(back, axis=0, keepdims=True)
        vec_ref[1:2] = gain
        vec_ref[2:3] = shift
        dctx = dot(datt_ref[...], w_ref[:, QKV:ATT]).astype(b16).astype(f32)
        low_half = lax.broadcasted_iota(jnp.int32, (1, LANES), 1) < HEAD_DIM
        factor = HEAD_DIM ** (-0.5)
        for pair in range(HD // LANES):
            at = pair * LANES
            query = qkv_ref[:, at : at + LANES].astype(f32) * factor
            keys = qkv_ref[:, HD + at : HD + at + LANES].astype(f32) * factor
            values = qkv_ref[:, 2 * HD + at : 2 * HD + at + LANES]
            dc = dctx[:, at : at + LANES]
            weighed = dc * ctx_ref[:, at : at + LANES].astype(f32)
            dq = jnp.zeros((SEQ, LANES), f32)
            dk = jnp.zeros((SEQ, LANES), f32)
            dv = jnp.zeros((SEQ, LANES), f32)
            for half in range(2):
                mine = low_half if half == 0 else ~low_half
                dcm = jnp.where(mine, dc, 0.0).astype(b16)
                delta = jnp.sum(jnp.where(mine, weighed, 0.0), axis=-1, keepdims=True)
                probs = probs_ref[2 * pair + half]
                dprobs = dot(dcm, values, contract_last)
                dscores = (probs.astype(f32) * (dprobs - delta)).astype(b16)
                dq = dq + dot(dscores, jnp.where(mine, keys, 0.0).astype(b16))
                dk = dk + dot(dscores, jnp.where(mine, query, 0.0).astype(b16), contract_first)
                dv = dv + dot(probs, dcm, contract_first)
            dqkv_ref[:, at : at + LANES] = dq.astype(b16)
            dqkv_ref[:, HD + at : HD + at + LANES] = dk.astype(b16)
            dqkv_ref[:, 2 * HD + at : 2 * HD + at + LANES] = dv.astype(b16)
        vec_ref[3:4, :HD] = jnp.sum(dqkv_ref[:, :HD].astype(f32), axis=0, keepdims=True)
        vec_ref[3:4, HD:] = jnp.sum(dqkv_ref[:, 2 * HD :].astype(f32), axis=0, keepdims=True)
        part_ref[...] = dot(dqkv_ref[...], w_ref[:, :QKV], contract_last).astype(b16)

    return call(
        body,
        [
            ((SEQ, D), b16),
            ((SEQ, D), f32),
            ((SEQ, D), b16),
            ((SEQ, QKV), b16),
            ((8, D), f32),
        ],
        [VM] * 9 + [VM],
        flops=2 * ATT_FLOPS,
        moved=9 << 20,
    )(res, part_own, part_other, n1, s1, rep, qkv, probs, ctx, matrix)


def finish_input(mids, owns, others):
    def body(*refs):
        for micro in range(MICRO):
            m, a, b = refs[3 * micro : 3 * micro + 3]
            refs[-1][micro] = m[...] + (a[...].astype(f32) + b[...].astype(f32))

    args = []
    for micro in range(MICRO):
        args += [mids[micro], owns[micro], others[micro]]
    return call(body, [((MICRO, SEQ, D), f32)], [VM] * len(args), moved=7 << 20)(*args)[0]


def store_slots(product_ref, outs, at, width):
    if len(outs) == 1:
        outs[0][:, at : at + width] = product_ref[:, :width].astype(b16)
        return
    ring, rows = outs[0].shape[1], outs[0].shape[2]
    z, x, c = places(ring)
    for other in range(2):
        for xo in range(2):
            for k in range(ring):
                zz = lax.rem(z + k, ring)
                xx = lax.rem(x + xo, 2)
                cc = lax.rem(c + other, 2)
                row = pl.multiple_of(((zz * 2 + xx) * 2 + cc) * rows, 16)
                outs[other][xo, k, :, at : at + width] = product_ref[
                    pl.ds(row, rows), :width
                ].astype(b16)


def grad_outs(ndp, pieced, cols):
    rows = D // ndp
    if pieced:
        return [((2, ndp // 4, rows, cols), b16)] * 2
    return [((D, cols), b16)]


def matrix_gradient(sets, pieced, ndp, vectors=None):
    widths = [s[2] for s in sets]
    total = sum(widths) + (LANES if vectors is not None else 0)
    outs = grad_outs(ndp, pieced, total)
    args, specs = [], []
    for left, right, _ in sets:
        for micro in range(MICRO):
            specs.append(VM)
            args.append(left[micro])
        for micro in range(MICRO):
            args.append(right[micro])
            specs.append(VM)
    plain = len(args)
    if vectors is not None:
        args += vectors
        specs += [VM] * len(vectors)
    n_in = len(args)
    step = 384

    def body(*refs):
        out_refs = refs[n_in : n_in + len(outs)]
        prod_ref = refs[n_in + len(outs)]
        at = 0
        for index, width in enumerate(widths):
            l0, l1, r0, r1 = refs[4 * index : 4 * index + 4]
            left = [r[m] if len(r.shape) == 3 else r[...] for m, r in enumerate((l0, l1))]
            r0, r1 = (r.at[m] if len(r.shape) == 3 else r for m, r in enumerate((r0, r1)))
            for col in range(0, width, step):
                prod_ref[...] = dot(left[0], r0[:, col : col + step], contract_first) + dot(
                    left[1], r1[:, col : col + step], contract_first
                )
                store_slots(prod_ref, out_refs, at, step)
                at += step
        if vectors is not None:
            pack_vectors(refs[plain:n_in], prod_ref)
            store_slots(prod_ref, out_refs, at, LANES)

    moved = sum(a.size * 2 for a in args[:plain]) + D * total * 2
    return call(
        body,
        outs,
        specs,
        [pltpu.VMEM((D, step), f32)],
        flops=2 * MICRO * SEQ * D * total,
        moved=moved,
    )(*args)


def pack_vectors(vec_refs, prod_ref):
    sums = []
    for layer in range(LAYERS):
        a0, a1, b0, b1 = vec_refs[4 * layer : 4 * layer + 4]
        sums.append((a0[...] + a1[...], b0[...] + b1[...]))
    rows = []
    for att, ffn in sums:
        rows += [att[0:1], att[1:2], att[2:3], ffn[0:1], ffn[1:2], ffn[2:3]]
    rows.append(jnp.zeros((4, D), f32))
    turned = jnp.concatenate(rows, axis=0)
    turned = jnp.concatenate([turned, jnp.zeros((LANES - 16, D), f32)], axis=0).T
    step = VCOL // 3
    phase = lax.rem(lax.broadcasted_iota(jnp.int32, (1, step), 1), 3)
    lane = lax.broadcasted_iota(jnp.int32, (1, LANES), 1)
    for i in range(3):
        picked = []
        for att, ffn in sums:
            line = (att[3:4], ffn[3:4], ffn[4:5])[i]
            for j in range(3):
                picked.append(jnp.where(phase == j, line, 0.0))
        picked = jnp.concatenate(
            [jnp.zeros((12, step), f32)] + picked + [jnp.zeros((LANES - 18, step), f32)], axis=0
        ).astype(b16)
        n_rows = D // 3
        mask = spread_mask(i * n_rows, n_rows, i * step, step)
        part = dot(mask, picked, contract_last)
        keep = turned[i * n_rows : (i + 1) * n_rows]
        prod_ref[i * n_rows : (i + 1) * n_rows, :LANES] = jnp.where(lane < 12, keep, part)


def meet(own, met, places):
    lo, hi = places[0], places[-1] + 1
    return (own[1, lo:hi].astype(f32) + met[1, lo:hi].astype(f32)).astype(b16)


def pass_on(own, met, got, places):
    lo, hi = places[0], places[-1] + 1
    total = own[0, lo:hi].astype(f32) + met[0, lo:hi].astype(f32) + got.astype(f32)
    return [total[i].astype(b16) for i in range(hi - lo)]


def pass_both(own, met, k, received=None):
    total = own[:, k].astype(f32) + met[:, k].astype(f32)
    if received is not None:
        total = total + received.astype(f32)
    return total.astype(b16)


def close(own, met, parts, vectors=False):
    _, _, rows, cols = own.shape
    mats = cols - LANES if vectors else cols
    parts = [p if isinstance(p, tuple) else (p, None) for p in parts]
    n = len(parts)

    def body(own_ref, met_ref, *refs):
        out_ref, sq_ref = refs[n:]
        total = jnp.zeros((rows, LANES), f32)
        for at in range(0, cols, LANES):
            s = slice(at, at + LANES)
            value = own_ref[0, 0, :, s].astype(f32) + met_ref[0, 0, :, s].astype(f32)
            for (_, index), ref in zip(parts, refs[:n]):
                value = value + (ref[:, s] if index is None else ref[index, :, s]).astype(f32)
            out_ref[:, s] = value
            square = value * value
            if at >= mats:
                lane = lax.broadcasted_iota(jnp.int32, (rows, LANES), 1)
                twice = (lane < 6 * LAYERS) & (lax.axis_index("tensor") != 0)
                square = jnp.where(twice, 0.0, square)
            total = total + square
        part = total[:8]
        for i in range(8, rows, 8):
            part = part + total[i : i + 8]
        sq_ref[...] = part

    return call(
        body,
        [((rows, cols), f32), ((8, LANES), f32)],
        [VM] * (2 + n),
        moved=rows * cols * 14,
    )(own, met, *[p[0] for p in parts])


def adamw(value, first, second, grad, rate, decay):
    first = 0.5 * first + 0.5 * grad
    second = 0.5 * second + 0.5 * grad * grad
    correct = 1.0 - 0.5**STEP
    direction = first / correct / (jnp.sqrt(second / correct) + 1e-08)
    return (value - rate * (direction + decay * value), first, second)


def clip_factor(squares):
    norm = jnp.sqrt(jnp.sum(squares, keepdims=True))
    return norm, jnp.minimum(1.0, clip_limit / (norm + 1e-06))


def ready(tiled, first, second):
    def body(w_ref, m_ref, v_ref, w_out, m_out, v_out):
        w_out[...] = w_ref[...] * (1.0 - weight_rate * weight_decay)
        m_out[...] = 0.5 * m_ref[...]
        v_out[...] = 0.5 * v_ref[...]

    return call(body, [(tiled.shape, f32)] * 3, [VM] * 3, moved=24 * tiled.size)(tiled, first, second)


def stepped(decayed, half_first, half_second, grad, rate):
    first = half_first + 0.5 * grad
    second = half_second + 0.5 * grad * grad
    correct = 1.0 - 0.5**STEP
    direction = first / correct / (jnp.sqrt(second / correct) + 1e-08)
    return decayed - rate * direction, first, second


def update_vectors(block, squares, reps, splits):
    rows = block.shape[0]
    per = splits[0].shape[2]

    def body(b_ref, q_ref, rw, rm, rv, sw, sm, sv, norm_ref, rwo, rmo, rvo, rlo, go, swo, smo, svo, slo):
        norm, scale = clip_factor(q_ref[...])
        norm_ref[...] = norm
        turned = jnp.concatenate([b_ref[...], jnp.zeros((LANES - rows, LANES), f32)], axis=0).T
        for layer in range(LAYERS):
            at = slice(layer, layer + 1)
            for kind in range(6):
                grad = turned[6 * layer + kind : 6 * layer + kind + 1, :rows] * scale
                new = adamw(rw[kind, at], rm[kind, at], rv[kind, at], grad, vector_rate, 0.0)
                rwo[kind, at], rmo[kind, at], rvo[kind, at] = new
                rlo[kind, at] = new[0].astype(b16)
                if kind == 0:
                    go[at] = grad
        row = lax.broadcasted_iota(jnp.int32, (rows, per), 0)
        col = lax.broadcasted_iota(jnp.int32, (rows, per), 1)
        gap = col - 3 * row
        mask = jnp.where((gap >= 0) & (gap < 3), 1.0, 0.0)
        wide = lax.dot_general(
            turned[6 * LAYERS : 6 * LAYERS + 8, :rows],
            mask,
            (((1,), (0,)), ((), ())),
            preferred_element_type=f32,
            precision=lax.Precision.HIGHEST,
        )
        phase = lax.rem(lax.broadcasted_iota(jnp.int32, (1, per), 1), 3)
        for layer in range(LAYERS):
            one, two, three = (wide[3 * layer + j : 3 * layer + j + 1] for j in range(3))
            grad = jnp.where(phase == 0, one, jnp.where(phase == 1, two, three)) * scale
            new = adamw(sw[layer], sm[layer], sv[layer], grad, vector_rate, 0.0)
            swo[layer], smo[layer], svo[layer] = new
            slo[layer] = new[0].astype(b16)

    rep, split = reps[0].shape, splits[0].shape
    return call(
        body,
        [((1, 1), f32)]
        + [(rep, f32)] * 3
        + [(rep, b16), ((LAYERS, rows), f32)]
        + [(split, f32)] * 3
        + [(split, b16)],
        [VM] * 8,
        moved=1 << 18,
    )(block, squares, *reps, *splits)


def update_matrices(decayed, first, second, grads, squares):
    rows = grads[0].shape[0]
    tiled = decayed
    step = 8 if rows % 8 == 0 else rows
    n_steps = rows // step
    block = (1, step * TILES, LANES)

    def body(f_ref, w_ref, m_ref, v_ref, a0, f0, a1, f1, nw, nm, nv, nl):
        scale = clip_factor(f_ref[...])[1]
        layer = pl.program_id(0)
        for c in range(TILES):
            if c < ATT // LANES:
                lo = c * LANES
                grad = jnp.where(layer == 0, a0[:, lo : lo + LANES], a1[:, lo : lo + LANES])
            else:
                lo = c * LANES - ATT
                grad = jnp.where(layer == 0, f0[:, lo : lo + LANES], f1[:, lo : lo + LANES])
            where = (0, pl.ds(c, step, stride=TILES), slice(None))
            new = stepped(w_ref[where], m_ref[where], v_ref[where], grad * scale, weight_rate)
            nw[where], nm[where], nv[where] = new
        nl[...] = nw[...].astype(b16)

    big = pl.BlockSpec(block, lambda l, i: (l, i, 0))
    shape = tiled.shape
    return pl.pallas_call(
        body,
        grid=(LAYERS, n_steps),
        out_shape=[jax.ShapeDtypeStruct(shape, f32)] * 3 + [jax.ShapeDtypeStruct(shape, b16)],
        in_specs=[pl.BlockSpec((8, LANES), lambda l, i: (0, 0)), big, big, big]
        + [pl.BlockSpec((step, g.shape[1]), lambda l, i: (i, 0)) for g in grads],
        out_specs=[big] * 4,
        compiler_params=pltpu.CompilerParams(vmem_limit_bytes=VMEM_LIMIT),
        cost_estimate=pl.CostEstimate(
            flops=20 * tiled.size, bytes_accessed=30 * tiled.size, transcendentals=tiled.size
        ),
    )(squares, tiled, first, second, *grads)


def sum_everywhere(value):
    ndp = lax.axis_size("dp")
    if ndp & (ndp - 1) or ndp < 4:
        return lax.psum(value, ("dp", "tensor"))

    def level(a, first, second):
        one, two, both = ppermute_bits(a, first), ppermute_bits(a, second), ppermute_bits(a, first | second)
        return (a + one) + (two + both)

    value = value + ppermute_bits(value, 2)
    value = level(value, 4, 1)
    bit = 8
    while bit < 2 * ndp:
        if 2 * bit < 2 * ndp:
            value = level(value, bit, 2 * bit)
        else:
            value = value + ppermute_bits(value, bit)
        bit *= 4
    return value


def ppermute_bits(value, bits):
    n = 2 * lax.axis_size("dp")
    return lax.ppermute(value, ("dp", "tensor"), [(i, i ^ bits) for i in range(n)])


def per_device(
    block_in,
    out_grad,
    segments,
    weights,
    weights_first,
    weights_second,
    split_vectors,
    split_first,
    split_second,
    rep_vectors,
    rep_first,
    rep_second,
):
    ndp = lax.axis_size("dp")
    rows = D // ndp
    per = split_vectors.shape[2]
    pieced = ndp == 16 and rows % 16 == 0
    shard_shape = weights.shape
    tiled_shape = (LAYERS, -1, LANES)
    masters = [a.reshape(tiled_shape) for a in (weights, weights_first, weights_second)]
    weights_tiled = masters[0]
    rep_flat = rep_vectors.reshape(LAYERS * 6, -1)
    split_flat = split_vectors.reshape(LAYERS, per)
    both = range(MICRO)
    seg = segments.reshape(MICRO, 1, SEQ)
    if pieced:
        a0, f0, l1, every = prep(weights_tiled, rep_flat, split_flat)
        across = partial(move, kind="x")
        third = slice(COLS + LANES, COLS + LANES + ATT)
        fourth = slice(COLS + LANES + ATT, None)

        def finish(slots, cols):
            mine = stack(slots, rows, cols, (2, 4))
            return settle(mine, move(mine, "core"))

        def cut(array, cols):
            return (array, (slice(None), cols))

        x0 = across(every)
        a0_r1, a0_r2, a0_r3, f0 = tie(move(a0, 1), move(a0, 2), move(a0, 3), f0)
        a0_x = across(stack([a0_r1, a0_r2, a0_r3], rows, ATT + LANES))
        f0_r1, f0_r3 = move(f0, 1), move(f0, 3)
        mine0 = stack(
            [a0, a0_r1, a0_r2, a0_r3, cut(x0, slice(0, ATT + LANES)), (a0_x, 0), (a0_x, 1), (a0_x, 2)],
            rows,
            ATT + LANES,
            (2, 4),
        )
        mine0, f0_r1, f0_r3, l1 = tie(mine0, f0_r1, f0_r3, l1)
        watt0 = settle(mine0, move(mine0, "core"))
        f0_x13 = across(stack([f0_r1, f0_r3], rows, 2 * FFT))
        f0_r2 = move(f0_r1, 1)
        l1_r1, l1_r3 = move(l1, 1), move(l1, 3)
        f0_x2 = across(f0_r2)
    else:
        low = weights.astype(b16).reshape(LAYERS, rows, COLS)
        block = jnp.concatenate(
            [
                rep_flat.T,
                split_flat.reshape(LAYERS, rows, 3).transpose(1, 0, 2).reshape(rows, 6),
                jnp.zeros((rows, LANES - 18), f32),
            ],
            axis=1,
        ).astype(b16)
        gather = partial(lax.all_gather, axis_name="dp", axis=0, tiled=True)
        watt0 = gather(jnp.concatenate([low[0, :, :ATT], block], axis=1))
        watt1 = gather(low[1, :, :ATT])
        wffn0, wffn1 = (gather(low[layer, :, ATT:]) for layer in range(LAYERS))
    rep, split = unpack(watt0)

    done, qkv0, probs0, ctx0 = attention_first(block_in, seg, split, watt0)
    met = exchange(done)
    if pieced:
        f0_x13, f0_x2, l1_r1, l1_r3, met = tie(f0_x13, f0_x2, l1_r1, l1_r3, met)
        a1_x13 = across(stack([cut(l1_r1, slice(0, ATT)), cut(l1_r3, slice(0, ATT))], rows, ATT))
        l1_r2 = move(l1_r1, 1)
        wffn0 = finish(
            [f0, f0_r1, f0_r2, f0_r3]
            + [cut(x0, slice(ATT + LANES, COLS + LANES)), (f0_x13, 0), f0_x2, (f0_x13, 1)],
            2 * FFT,
        )
    done, n1_0, s1_0, low1_0, act0, slope0 = feed_first(block_in, done, met, rep, split, wffn0)
    if pieced:
        a1_x13, l1_r2, done = tie(a1_x13, l1_r2, done)
        head, tail = slice(0, ATT), slice(ATT, None)
        a1_x2 = across(stack([cut(l1_r2, head)], rows, ATT))
        f1_x13 = across(stack([cut(l1_r1, tail), cut(l1_r3, tail)], rows, 2 * FFT))
        watt1 = finish(
            [cut(r, head) for r in (l1, l1_r1, l1_r2, l1_r3)]
            + [cut(x0, third), (a1_x13, 0), (a1_x2, 0), (a1_x13, 1)],
            ATT,
        )
    met = exchange(done)
    if pieced:
        f1_x13, met = tie(f1_x13, met)
    out = attention_next(1, n1_0, done, met, rep, seg, split, watt1)
    done, (qkv1, probs1, ctx1, n2_0, s2_0, low_h1) = list(out[:MICRO]), out[MICRO:]
    if pieced:
        f1_x2 = across(stack([cut(l1_r2, tail)], rows, 2 * FFT))
        wffn1 = finish(
            [cut(r, tail) for r in (l1, l1_r1, l1_r2, l1_r3)]
            + [cut(x0, fourth), (f1_x13, 0), (f1_x2, 0), (f1_x13, 1)],
            2 * FFT,
        )
    met = [exchange(a) for a in done]
    out = [feed_forward(m, 1, n2_0, done[m], met[m], rep, split, wffn1) for m in both]
    n1_1, s1_1, low1_1, act1, slope1 = ([o[i] for o in out] for i in range(1, 6))
    met = [exchange(o[0]) for o in out]

    out = [
        feed_back_top(m, 1, out_grad, n1_1[m], out[m][0], met[m], rep, slope1[m], wffn1)
        for m in both
    ]
    res, dffn, din, vec_f1 = ([o[i] for o in out] for i in range(1, 5))
    block_out = jnp.stack([o[5] for o in out])
    done = [o[0] for o in out]
    met = [exchange(o[0]) for o in out]
    g_f1 = matrix_gradient([(low1_1, din, FFT), (dffn, act1, FFT)], pieced, ndp)
    res[0] = after(res[0], g_f1[0])

    def back_1(m):
        return attention_back(
            m, 1, res[m], done[m], met[m], n1_1[m], s1_1[m], rep, qkv1, probs1, ctx1, watt1
        )

    out = [back_1(0)]
    if pieced:
        f1_own, f1_met = g_f1[0], move(g_f1[1], "core")
        f1_t = pass_both(f1_own, after(f1_met, out[0][0]), 3)
        f1_rec = move(f1_t, 1)
        res[1] = after(res[1], f1_t)
    out += [back_1(1)]
    mid, datt, dqkv, vec_a1 = ([o[i] for o in out] for i in range(1, 5))
    done = [o[0] for o in out]
    met = [exchange(o[0]) for o in out]
    g_a1 = matrix_gradient([([low_h1] * 2, dqkv, QKV), (datt, [ctx1] * 2, HD)], pieced, ndp)
    mid[0] = after(mid[0], g_a1[0])
    def back_2(m):
        return feed_back(m, 0, mid[m], done[m], met[m], n2_0, s2_0, rep, slope0, wffn0)

    out = [back_2(0)]
    if pieced:
        a1_own, a1_met = g_a1[0], move(g_a1[1], "core")
        a1_s = meet(a1_own, after(a1_met, out[0][0]), (0, 1, 2, 3))
        a1_got = across(a1_s)
        f1_t = pass_both(f1_own, f1_met, 2, after(f1_rec, out[0][0]))
        f1_rec = move(f1_t, 1)
        mid[1] = after(mid[1], a1_s, f1_t)
    out += [back_2(1)]
    res, dffn, din, vec_f0 = ([o[i] for o in out] for i in range(1, 5))
    done = [o[0] for o in out]
    met = [exchange(o[0]) for o in out]
    g_f0 = matrix_gradient([([low1_0] * 2, din, FFT), (dffn, [act0] * 2, FFT)], pieced, ndp)
    res[0] = after(res[0], g_f0[0])
    if pieced:
        f1_t = pass_both(f1_own, f1_met, 1, after(f1_rec, g_f0[0]))
        f1_rec = move(f1_t, 1)
        res[0] = after(res[0], f1_t)

    def back_3(m):
        return attention_back(
            m, 0, res[m], done[m], met[m], n1_0, s1_0, rep, qkv0, probs0, ctx0, watt0
        )

    out = [back_3(0)]
    if pieced:
        f0_own, f0_met = g_f0[0], move(g_f0[1], "core")
        f0_s = meet(f0_own, after(f0_met, out[0][0]), (2, 3))
        f0_got_hi = across(f0_s)
        a1_t1, a1_t2, a1_t3 = pass_on(a1_own, a1_met, after(a1_got, out[0][0])[1:], (1, 2, 3))
        a1_r = [move(t, k) for k, t in ((1, a1_t1), (2, a1_t2), (3, a1_t3))]
        res[1] = after(res[1], f0_s, a1_t3)
    out += [back_3(1)]
    mid, datt, dqkv, vec_a0 = ([o[i] for o in out] for i in range(1, 5))
    done = [o[0] for o in out]
    met = [exchange(o[0]) for o in out]
    g_a0 = matrix_gradient(
        [([block_in] * MICRO, dqkv, QKV), (datt, [ctx0] * 2, HD)],
        pieced,
        ndp,
        vectors=vec_a0 + vec_f0 + vec_a1 + vec_f1,
    )
    if pieced:
        masters = ready(*(after(a, g_a0[0]) for a in masters))
        input_grad = finish_input(mid, done, met)
        a0_own, a0_met = g_a0[0], move(g_a0[1], "core")
        a0_s, f0_got_hi, f1_rec = tie(meet(a0_own, a0_met, (0, 1, 2, 3)), f0_got_hi, f1_rec)
        a0_got = across(a0_s)
        f1_last = pass_both(f1_own, f1_met, 0, f1_rec)
        f1_got = across(f1_last[1])
        f0_t2, f0_t3 = pass_on(f0_own, f0_met, f0_got_hi, (2, 3))
        f0_r3, f0_r2 = move(f0_t3, 3), move(f0_t2, 2)
        a0_got, f0_r3, f0_r2, *a1_r = tie(a0_got, f0_r3, f0_r2, *a1_r)
        f0_got_lo = across(meet(f0_own, f0_met, (0, 1)))
        a0_t = pass_on(a0_own, a0_met, a0_got[1:], (1, 2, 3))
        a0_r = [move(t, k + 1) for k, t in enumerate(a0_t)]
        grad_a1, sq_a1 = close(a1_own, a1_met, [(a1_got, 0)] + a1_r)
        grad_f1, sq_f1 = close(f1_own, f1_met, [f1_got, (f1_rec, 0)])
        f0_got_lo, grad_f1, grad_a1, block_out, input_grad, *rest = tie(
            f0_got_lo, grad_f1, grad_a1, block_out, input_grad, *a0_r, *masters
        )
        a0_r, masters = rest[:3], rest[3:]
        f0_r1 = move(pass_on(f0_own, f0_met, f0_got_lo[1:], (1,))[0], 1)
        grad_a0, sq_a0 = close(a0_own, a0_met, [(a0_got, 0)] + a0_r, vectors=True)
        grad_f0, sq_f0 = close(f0_own, f0_met, [(f0_got_lo, 0), f0_r1, f0_r2, f0_r3])
        squares = (sq_f1 + sq_a1) + (sq_f0 + sq_a0)
    else:
        input_grad = finish_input(mid, done, met)
        scatter = lambda g: lax.psum_scatter(g[0], "dp", scatter_dimension=0, tiled=True).astype(f32)
        grad_f1, grad_a1, grad_f0, grad_a0 = (scatter(g) for g in (g_f1, g_a1, g_f0, g_a0))
        once = jnp.where(lax.axis_index("tensor") == 0, 1.0, 0.0).astype(f32)
        square = lambda a: jnp.sum(a * a)
        squares = (
            square(grad_a0[:, :ATT])
            + square(grad_f0)
            + square(grad_a1)
            + square(grad_f1)
            + square(grad_a0[:, ATT + 12 :])
            + once * square(grad_a0[:, ATT : ATT + 12])
        )
        squares = jnp.full((8, LANES), squares / (8 * LANES), f32)

    squares = sum_everywhere(squares)
    if pieced:
        new = update_matrices(*masters, [grad_a0, grad_f0, grad_a1, grad_f1], squares)
        turn = lambda a: jnp.transpose(a, (1, 0, 2))
        vectors = update_vectors(
            grad_a0[:, ATT:],
            squares,
            [turn(a) for a in (rep_vectors, rep_first, rep_second)],
            (split_vectors, split_first, split_second),
        )
        grad_norm = vectors[0][0, 0]
        new_rep, rep_first_new, rep_second_new, rep_low = (turn(a) for a in vectors[1:5])
        bias_grad = vectors[5]
        new_split, split_first_new, split_second_new, split_low = vectors[6:]
    else:
        block = grad_a0[:, ATT:]
        grad_rep = block[:, :12].T.reshape(rep_vectors.shape)
        grad_split = (
            block[:, 12:18].reshape(rows, LAYERS, 3).transpose(1, 0, 2).reshape(split_vectors.shape)
        )
        grad_norm, factor = (a[0, 0] for a in clip_factor(squares))
        clipped_rep = grad_rep * factor
        grad = jnp.stack(
            [
                jnp.concatenate([grad_a0[:, :ATT], grad_f0], axis=1),
                jnp.concatenate([grad_a1, grad_f1], axis=1),
            ]
        ).reshape(tiled_shape)
        new = adamw(*masters, grad * factor, weight_rate, weight_decay)
        new = (*new, new[0].astype(b16))
        new_split, split_first_new, split_second_new = adamw(
            split_vectors, split_first, split_second, grad_split * factor, vector_rate, 0.0
        )
        new_rep, rep_first_new, rep_second_new = adamw(
            rep_vectors, rep_first, rep_second, clipped_rep, vector_rate, 0.0
        )
        split_low, rep_low = new_split.astype(b16), new_rep.astype(b16)
        bias_grad = clipped_rep[:, 0, :]
    new_weights, weights_first_new, weights_second_new, weights_low = (
        a.reshape(shard_shape) for a in new
    )
    return (
        block_out,
        input_grad,
        grad_norm,
        new_weights,
        weights_first_new,
        weights_second_new,
        weights_low,
        new_split,
        split_first_new,
        split_second_new,
        split_low,
        new_rep,
        rep_first_new,
        rep_second_new,
        rep_low,
        bias_grad,
    )


def solution(mesh):
    rows, packed, vector = P("dp", None, None), P(None, "tensor", "dp"), P(None, None, "dp")
    return jax.shard_map(
        per_device,
        mesh=mesh,
        in_specs=(rows, rows, P("dp", None)) + (packed,) * 6 + (vector,) * 3,
        out_specs=(rows, rows, P()) + (packed,) * 8 + (vector,) * 4 + (P(None, "dp"),),
        check_vma=False,
    )
```

time: 698 us -> 344 us (0.49)
  Pallas kernels: 376 us -> 64.2 us
  other arithmetic: 26.7 us -> 3.18 us
  local copies, waits for them, and re-layouts: 27.6 us -> 7.4 us
  starting transfers between devices: 56.4 us -> 76.1 us
  waiting for transfers between devices: 198 us -> 187 us
    pallas_call x18 -> x31, Pallas kernels: 307 us -> 32.5 us  [the longest x2 5.09 us: feed_forward(): call(body, FEED_OUTS, [VM] * 6, flops=FFN_FLOPS, moved=10 << 20)]
    ppermute x52 -> x42, waiting for transfers between devices: 179 us -> 129 us  [move(): return lax.ppermute(a, 'dp', pairs_of(lax.axis_size('dp'), kind))]
    ppermute x17 -> x14, waiting for transfers between devices: 11.1 us -> 51 us  [exchange(): return lax.ppermute(a, 'tensor', [(0, 1), (1, 0)])]
    ppermute x52 -> x42, starting transfers between devices: 34.3 us -> 51.4 us  [move(): return lax.ppermute(a, 'dp', pairs_of(lax.axis_size('dp'), kind))]
    unnamed x155 -> x29, local copies, waits for them, and re-layouts: 22.7 us -> 5.84 us
    pallas_call x4, Pallas kernels: 28.8 us -> 12.4 us  [attention_back(): call(body, [((SEQ, D), b16), ((SEQ, D), f32), ((SEQ, D), b16), ((SEQ, QKV...]
    pallas_call x4, Pallas kernels: 27.6 us -> 12 us  [matrix_gradient(): call(body, outs, specs, [pltpu.VMEM((D, step), f32)], flops=2 * MICRO * S...]
    convert_element_type x18 -> x6, other arithmetic: 15 us -> 1.22 us  [the longest x3 0.67 us: meet(): return (own[1, lo:hi].astype(f32) + met[1, lo:hi].astype(f32)).astype(b16)]
  transfers between devices with their start and end apart: 73 -> 63, of which waited for: 37 -> 41; matrix products, arithmetic and copies ran while one was open for 3% -> 1% of each run, Pallas kernels for 51% -> 12%
where the time goes in v2:
time: 344 us; the launch traced here: 339 us
  waiting for transfers between devices  187 us (54%)
  starting transfers between devices  76.1 us (22%)
  Pallas kernels  64.2 us (19%)
  local copies, waits for them, and re-layouts  7.4 us (2%)
    ppermute x42, waiting for transfers between devices, move(): return lax.ppermute(a, 'dp', pairs_of(lax.axis_size('dp'), kind))  129 us
    ppermute x42, starting transfers between devices, move(): return lax.ppermute(a, 'dp', pairs_of(lax.axis_size('dp'), kind))  51.4 us
    ppermute x14, waiting for transfers between devices, exchange(): return lax.ppermute(a, 'tensor', [(0, 1), (1, 0)])  51 us
    ppermute x14, starting transfers between devices, exchange(): return lax.ppermute(a, 'tensor', [(0, 1), (1, 0)])  16.8 us
    pallas_call x4, Pallas kernels, attention_back(): call(body, [((SEQ, D), b16), ((SEQ, D), f32), ((SEQ, D), b16), ((SEQ, QKV...  12.4 us
    pallas_call x4, Pallas kernels, matrix_gradient(): call(body, outs, specs, [pltpu.VMEM((D, step), f32)], flops=2 * MICRO * S...  12 us
    ppermute x7, starting transfers between devices, ppermute_bits(): lax.ppermute(value, ('dp', 'tensor'), [(i, i ^ bits) for i in range(n)])  7.94 us
  transfers between devices with their start and end apart: 63, of which 41 were waited for; matrix products, arithmetic and copies ran while one was open for 1% of the time, Pallas kernels for 12%

profile of v2, /device:TPU:0, one launch (start us, length us, event | category | flops | bytes accessed | tf_op | source)
XLA Modules:
  0.0 339.0 jit_solution(1929674588405419750)
XLA Ops:
  12.3 3.4 %collective-permute-done.refs_0_.refs_1_ = bf16[48,1664]{1,0:T(8,128)(2,1)S(1)} collective-permute-done((bf16[48,1664]{1,0:T(8,128)(2,1)S(1)}, bf16[48,1664]{1,0:T(8,128)(2,1)S(1)}, u32[]{:S(2)}, u32[]{:S(2)}) %collective-permute-start) | collective-permute-done | bytes 159776 | tf_op jit(solution)/shard_map/ppermute | solution.py:89
  15.7 5.4 %collective-permute-done.1.refs_1_.refs_2_ = bf16[48,1664]{1,0:T(8,128)(2,1)S(1)} collective-permute-done((bf16[48,1664]{1,0:T(8,128)(2,1)S(1)}, bf16[48,1664]{1,0:T(8,128)(2,1)S(1)}, u32[]{:S(2)}, u32[]{:S(2)}) %collective-permute-start.1) | collective-permute-done | bytes 159776 | tf_op jit(solution)/shard_map/ppermute | solution.py:89
  21.8 3.9 %collective-permute-start.5 = (bf16[48,3072]{1,0:T(8,128)(2,1)S(1)}, bf16[48,3072]{1,0:T(8,128)(2,1)S(1)}, u32[]{:S(2)}, u32[]{:S(2)}) collective-permute-start(bf16[48,3072]{1,0:T(8,128)(2,1)S(1)} %get-tuple-element.187.refs_0_), channel_id=1, source_target_pairs={{0,8},{2,10},{4,12},{6,14},{8,16},{10,18},{12,20},{14,22},{16,24},... | collective-permute-start | bytes 884744 | tf_op jit(solution)/shard_map/ppermute | solution.py:89
  26.7 10.2 %collective-permute-done.4.refs_5_ = bf16[3,48,1664]{2,1,0:T(8,128)(2,1)S(1)} collective-permute-done((bf16[3,48,1664]{2,1,0:T(8,128)(2,1)S(1)}, bf16[3,48,1664]{2,1,0:T(8,128)(2,1)S(1)}, u32[]{:S(2)}, u32[]{:S(2)}) %collective-permute-start.4) | collective-permute-done | bytes 479264 | tf_op jit(solution)/shard_map/ppermute | solution.py:89
  43.0 4.4 %shard_map.248 = (bf16[2,256,768]{2,1,0:T(8,128)(2,1)S(1)}, bf16[2,256,1152]{2,1,0:T(8,128)(2,1)S(1)}, bf16[2,6,256,256]{3,2,1,0:T(8,128)(2,1)S(1)}, bf16[2,256,384]{2,1,0:T(8,128)(2,1)S(1)}) custom-call(bf16[2,256,768]{2,1,0:T(8,128)(2,1)S(1)} %copy-done.11, s32[2,1,256]{2,1,0:T(1,128)S(1)} %reshape.140.seg_ref, ...), custom_call_target="tpu_custom_call" | custom-call | flops 1610612736 | bytes 12582912 | tf_op jit(solution)/shard_map/pallas_call | solution.py:285
  54.9 5.9 %collective-permute-done.9.refs_2_ = bf16[48,3072]{1,0:T(8,128)(2,1)S(1)} collective-permute-done((bf16[48,3072]{1,0:T(8,128)(2,1)S(1)}, bf16[48,3072]{1,0:T(8,128)(2,1)S(1)}, u32[]{:S(2)}, u32[]{:S(2)}) %collective-permute-start.9) | collective-permute-done | bytes 294944 | tf_op jit(solution)/shard_map/ppermute | solution.py:89
  62.2 7.9 %collective-permute-done.11.refs_0_.refs_1_ = bf16[48,4608]{1,0:T(8,128)(2,1)S(1)} collective-permute-done((bf16[48,4608]{1,0:T(8,128)(2,1)S(1)}, bf16[48,4608]{1,0:T(8,128)(2,1)S(1)}, u32[]{:S(2)}, u32[]{:S(2)}) %collective-permute-start.11) | collective-permute-done | bytes 442400 | tf_op jit(solution)/shard_map/ppermute | solution.py:89
  70.1 8.6 %collective-permute-done.12.refs_1_.refs_3_ = bf16[48,4608]{1,0:T(8,128)(2,1)S(1)} collective-permute-done((bf16[48,4608]{1,0:T(8,128)(2,1)S(1)}, bf16[48,4608]{1,0:T(8,128)(2,1)S(1)}, u32[]{:S(2)}, u32[]{:S(2)}) %collective-permute-start.12) | collective-permute-done | bytes 442400 | tf_op jit(solution)/shard_map/ppermute | solution.py:89
  83.9 4.3 %shard_map.252 = (bf16[2,256,768]{2,1,0:T(8,128)(2,1)S(1)}, f32[2,256,768]{2,1,0:T(8,128)S(1)}, f32[2,256,1]{2,1,0:T(8,128)S(1)}, bf16[2,256,768]{2,1,0:T(8,128)...) custom-call(bf16[2,256,768]{2,1,0:T(8,128)(2,1)S(1)} %copy-done.11, ...), custom_call_target="tpu_custom_call" | custom-call | flops 2415919104 | bytes 20971520 | tf_op jit(solution)/shard_map/pallas_call | solution.py:359
  88.9 4.6 %collective-permute-done.16.refs_0_.refs_2_ = bf16[48,4608]{1,0:T(8,128)(2,1)S(1)} collective-permute-done((bf16[48,4608]{1,0:T(8,128)(2,1)S(1)}, bf16[48,4608]{1,0:T(8,128)(2,1)S(1)}, u32[]{:S(2)}, u32[]{:S(2)}) %collective-permute-start.16) | collective-permute-done | bytes 442400 | tf_op jit(solution)/shard_map/ppermute | solution.py:89
  96.3 14.1 %collective-permute-done.17.refs_5_ = bf16[2,48,3072]{2,1,0:T(8,128)(2,1)S(1)} collective-permute-done((bf16[2,48,3072]{2,1,0:T(8,128)(2,1)S(1)}, bf16[2,48,3072]{2,1,0:T(8,128)(2,1)S(1)}, u32[]{:S(2)}, u32[]{:S(2)}) %collective-permute-start.17) | collective-permute-done | bytes 589856 | tf_op jit(solution)/shard_map/ppermute | solution.py:89
  116.9 4.8 %collective-permute-done.19.refs_6_ = bf16[1,48,1536]{2,1,0:T(8,128)(2,1)S(1)} collective-permute-done((bf16[1,48,1536]{2,1,0:T(8,128)(2,1)S(1)}, bf16[1,48,1536]{2,1,0:T(8,128)(2,1)S(1)}, u32[]{:S(2)}, u32[]{:S(2)}) %collective-permute-start.19) | collective-permute-done | bytes 147488 | tf_op jit(solution)/shard_map/ppermute | solution.py:89
  124.8 4.9 %shard_map.258 = (bf16[256,768]{1,0:T(8,128)(2,1)S(1)}, bf16[256,768]{1,0:T(8,128)(2,1)S(1)}, bf16[2,256,1152]{2,1,0:T(8,128)(2,1)S(1)}, bf16[2,6,256,256]{3,2,1...) custom-call(f32[2,256,768]{2,1,0:T(8,128)S(1)} %get-tuple-element.20, ...), custom_call_target="tpu_custom_call" | custom-call | flops 1610612736 | bytes 16777216 | tf_op jit(solution)/shard_map/pallas_call | solution.py:311
  132.2 9.6 %collective-permute-done.25.other_ref = bf16[256,768]{1,0:T(8,128)(2,1)S(1)} collective-permute-done((bf16[256,768]{1,0:T(8,128)(2,1)S(1)}, bf16[256,768]{1,0:T(8,128)(2,1)S(1)}, u32[]{:S(2)}, u32[]{:S(2)}) %collective-permute-start.25) | collective-permute-done | bytes 393248 | tf_op jit(solution)/shard_map/ppermute | solution.py:93
  146.0 4.1 %collective-permute-done.21.other_ref = bf16[256,768]{1,0:T(8,128)(2,1)S(1)} collective-permute-done((bf16[256,768]{1,0:T(8,128)(2,1)S(1)}, bf16[256,768]{1,0:T(8,128)(2,1)S(1)}, u32[]{:S(2)}, u32[]{:S(2)}) %collective-permute-start.21) | collective-permute-done | bytes 393248 | tf_op jit(solution)/shard_map/ppermute | solution.py:93
  154.2 4.4 %collective-permute-done.26.other_ref = bf16[256,768]{1,0:T(8,128)(2,1)S(1)} collective-permute-done((bf16[256,768]{1,0:T(8,128)(2,1)S(1)}, bf16[256,768]{1,0:T(8,128)(2,1)S(1)}, u32[]{:S(2)}, u32[]{:S(2)}) %collective-permute-start.26) | collective-permute-done | bytes 393248 | tf_op jit(solution)/shard_map/ppermute | solution.py:93
  161.1 5.1 %collective-permute-done.24.other_ref = bf16[256,768]{1,0:T(8,128)(2,1)S(1)} collective-permute-done((bf16[256,768]{1,0:T(8,128)(2,1)S(1)}, bf16[256,768]{1,0:T(8,128)(2,1)S(1)}, u32[]{:S(2)}, u32[]{:S(2)}) %collective-permute-start.24) | collective-permute-done | bytes 393248 | tf_op jit(solution)/shard_map/ppermute | solution.py:93
  168.7 3.7 %shard_map.266 = (bf16[2,4,48,3072]{3,2,1,0:T(8,128)(2,1)S(1)}, bf16[2,4,48,3072]{3,2,1,0:T(8,128)(2,1)S(1)}) custom-call(bf16[256,768]{1,0:T(8,128)(2,1)S(1)} %get-tuple-element.215.refs_0_, bf16[256,768]{1,0:T(8,128)(2,1)S(1)} %get-tuple-element.217.refs_1_, bf16[256,1536]{1,0:T(8,128)(2,1)S(1)} %get-tuple-element.218.refs_2_, ...), custom_call_target="tpu_custom_call" | custom-call | flops 2415919104 | bytes 9437184 | tf_op jit(solution)/shard_map/pallas_call | solution.py:604
  174.7 9.9 %collective-permute-done.27.other_ref = bf16[256,768]{1,0:T(8,128)(2,1)S(1)} collective-permute-done((bf16[256,768]{1,0:T(8,128)(2,1)S(1)}, bf16[256,768]{1,0:T(8,128)(2,1)S(1)}, u32[]{:S(2)}, u32[]{:S(2)}) %collective-permute-start.27) | collective-permute-done | bytes 393248 | tf_op jit(solution)/shard_map/ppermute | solution.py:93
  184.6 3.4 %shard_map.267 = (bf16[256,768]{1,0:T(8,128)(2,1)S(1)}, f32[256,768]{1,0:T(8,128)S(1)}, bf16[256,768]{1,0:T(8,128)(2,1)S(1)}, bf16[256,1152]{1,0:T(8,128)(2,1)S(1)}, f32[8,768]{1,0:T(8,128)S(1)}) custom-call(f32[256,768]{1,0:T(8,128)S(1)} %get-tuple-element.228.res_ref, bf16[256,768]{1,0:T(8,128)(2,1)S(1)} %get-tuple-element.229.own_ref, ...), custom_call_target="tpu_custom_call" | custom-call | flops 1610612736 | bytes 9437184 | tf_op jit(solution)/shard_map/pallas_call | solution.py:514
  190.0 3.0 collective-permute-done.29.other_ref
  211.8 3.7 %shard_map.272 = (bf16[2,4,48,3072]{3,2,1,0:T(8,128)(2,1)S(1)}, bf16[2,4,48,3072]{3,2,1,0:T(8,128)(2,1)S(1)}) custom-call(bf16[2,256,768]{2,1,0:T(8,128)(2,1)S(1)} %get-tuple-element.199.refs_0_.refs_1_, bf16[2,256,768]{2,1,0:T(8,128)(2,1)S(1)} %get-tuple-element.199.refs_0_.refs_1_, bf16[256,1536]{1,0:T(8,128)(2,1)S(1)} %get-tuple-element.251.refs_2_, ...), custom_call_target="tpu_custom_call" | custom-call | flops 2415919104 | bytes 11796480 | tf_op jit(solution)/shard_map/pallas_call | solution.py:604
  221.7 5.9 %collective-permute-done.37.other_ref = bf16[256,768]{1,0:T(8,128)(2,1)S(1)} collective-permute-done((bf16[256,768]{1,0:T(8,128)(2,1)S(1)}, bf16[256,768]{1,0:T(8,128)(2,1)S(1)}, u32[]{:S(2)}, u32[]{:S(2)}) %collective-permute-start.37) | collective-permute-done | bytes 393248 | tf_op jit(solution)/shard_map/ppermute | solution.py:93
  243.0 3.7 %collective-permute-start.49 = (bf16[48,1536]{1,0:T(8,128)(2,1)S(1)}, bf16[48,1536]{1,0:T(8,128)(2,1)S(1)}, u32[]{:S(2)}, u32[]{:S(2)}) collective-permute-start(bf16[48,1536]{1,0:T(8,128)(2,1)S(1)} %get-tuple-element.389), channel_id=1, source_target_pairs={{0,24},{2,26},{4,28},{6,30},{8,0},{10,2},{12,4},{14,6},{16,8},{18,... | collective-permute-start | bytes 442376 | tf_op jit(solution)/shard_map/ppermute | solution.py:89
  247.4 11.9 %collective-permute-done.42.refs_1_ = bf16[2,48,3072]{2,1,0:T(8,128)(2,1)S(1)} collective-permute-done((bf16[2,48,3072]{2,1,0:T(8,128)(2,1)S(1)}, bf16[2,48,3072]{2,1,0:T(8,128)(2,1)S(1)}, u32[]{:S(2)}, u32[]{:S(2)}) %collective-permute-start.42) | collective-permute-done | bytes 589856 | tf_op jit(solution)/shard_map/ppermute | solution.py:89
  260.9 4.9 %collective-permute-done.47.refs_1_ = bf16[48,1536]{1,0:T(8,128)(2,1)S(1)} collective-permute-done((bf16[48,1536]{1,0:T(8,128)(2,1)S(1)}, bf16[48,1536]{1,0:T(8,128)(2,1)S(1)}, u32[]{:S(2)}, u32[]{:S(2)}) %collective-permute-start.47) | collective-permute-done | bytes 147488 | tf_op jit(solution)/shard_map/ppermute | solution.py:89
  267.3 3.8 %collective-permute-done.48.refs_2_ = bf16[48,1536]{1,0:T(8,128)(2,1)S(1)} collective-permute-done((bf16[48,1536]{1,0:T(8,128)(2,1)S(1)}, bf16[48,1536]{1,0:T(8,128)(2,1)S(1)}, u32[]{:S(2)}, u32[]{:S(2)}) %collective-permute-start.48) | collective-permute-done | bytes 147488 | tf_op jit(solution)/shard_map/ppermute | solution.py:89
  274.6 14.7 %collective-permute-done.46.refs_2_ = bf16[48,3072]{1,0:T(8,128)(2,1)S(1)} collective-permute-done((bf16[48,3072]{1,0:T(8,128)(2,1)S(1)}, bf16[48,3072]{1,0:T(8,128)(2,1)S(1)}, u32[]{:S(2)}, u32[]{:S(2)}) %collective-permute-start.46) | collective-permute-done | bytes 294944 | tf_op jit(solution)/shard_map/ppermute | solution.py:89
  290.7 10.4 %collective-permute-start.54 = (bf16[48,1664]{1,0:T(8,128)(2,1)S(1)}, bf16[48,1664]{1,0:T(8,128)(2,1)S(1)}, u32[]{:S(2)}, u32[]{:S(2)}) collective-permute-start(bf16[48,1664]{1,0:T(8,128)(2,1)S(1)} %get-tuple-element.384), channel_id=1, source_target_pairs={{0,24},{2,26},{4,28},{6,30},{8,0},{10,2},{12,4},{14,6},{16,8},{18,... | collective-permute-start | bytes 479240 | tf_op jit(solution)/shard_map/ppermute | solution.py:89
  307.3 7.9 %collective-permute-done.55.refs_1_ = bf16[48,3072]{1,0:T(8,128)(2,1)S(1)} collective-permute-done((bf16[48,3072]{1,0:T(8,128)(2,1)S(1)}, bf16[48,3072]{1,0:T(8,128)(2,1)S(1)}, u32[]{:S(2)}, u32[]{:S(2)}) %collective-permute-start.55) | collective-permute-done | bytes 294944 | tf_op jit(solution)/shard_map/ppermute | solution.py:89
  324.8 3.8 %collective-permute-start.62 = (f32[8,128]{1,0:T(8,128)S(1)}, f32[8,128]{1,0:T(8,128)S(1)}, u32[]{:S(2)}, u32[]{:S(2)}) collective-permute-start(f32[8,128]{1,0:T(8,128)S(1)} %add_add_fusion.1), channel_id=1, source_target_pairs={{0,24},{1,25},{2,26},{3,27},{4,28},{5,29},{6,30},{7,31},{8,16},{9,... | collective-permute-start | bytes 12296 | tf_op jit(solution)/shard_map/ppermute | solution.py:836
  330.2 6.0 %shard_map.283 = (f32[2,1728,128]{2,1,0:T(8,128)}, f32[2,1728,128]{2,1,0:T(8,128)}, f32[2,1728,128]{2,1,0:T(8,128)}, bf16[2,1728,128]{2,1,0:T(8,128)(2,1)S(1)}) custom-call(f32[8,128]{1,0:T(8,128)S(1)} %add_add_fusion.q_ref.f_ref, f32[2,1728,128]{2,1,0:T(8,128)S(1)} %get-tuple-element.327.w_ref, f32[2,1728,128]{2,1,0:T(8,128)S(1)} %get-tuple-element.328.m_ref, ...), custom_call_target="tpu_custom_call" | custom-call | flops 8847360 | bytes 13271040 | tf_op jit(solution)/shard_map/pallas_call | solution.py:799
  (189 shorter events, 135.4 us)
Async XLA Ops:
  3.8 33.2 %collective-permute-start.3 = (bf16[48,9344]{1,0:T(8,128)(2,1)S(1)}, bf16[48,9344]{1,0:T(8,128)(2,1)S(1)}, u32[]{:S(2)}, u32[]{:S(2)}) collective-permute-start(bf16[48,9344]{1,0:T(8,128)(2,1)S(1)} %get-tuple-element.186), channel_id=1, source_target_pairs={{0,4},{2,6},{4,0},{6,2},{8,12},{10,14},{12,8},{14,10},{16,20},{18,... | collective-permute-start | bytes 2691080 | tf_op jit(solution)/shard_map/ppermute | solution.py:89
  21.2 15.8 %collective-permute-start.4 = (bf16[3,48,1664]{2,1,0:T(8,128)(2,1)S(1)}, bf16[3,48,1664]{2,1,0:T(8,128)(2,1)S(1)}, u32[]{:S(2)}, u32[]{:S(2)}) collective-permute-start(bf16[3,48,1664]{2,1,0:T(8,128)(2,1)S(1)} %shard_map.244), channel_id=1, source_target_pairs={{0,4},{2,6},{4,0},{6,2},{8,12},{10,14},{12,8},{14,10},{16,20},{18,... | collective-permute-start | bytes 1437704 | tf_op jit(solution)/shard_map/ppermute | solution.py:89
  47.3 31.4 %collective-permute-start.13 = (bf16[2,256,768]{2,1,0:T(8,128)(2,1)S(1)}, bf16[2,256,768]{2,1,0:T(8,128)(2,1)S(1)}, u32[]{:S(2)}, u32[]{:S(2)}) collective-permute-start(bf16[2,256,768]{2,1,0:T(8,128)(2,1)S(1)} %get-tuple-element.191.own_ref), channel_id=1, source_target_pairs={{0,1},{1,0},{2,3},{3,2},{4,5},{5,4},{6,7},{7,6},{8,9},{9,8},{10,11... | collective-permute-start | bytes 2359304 | tf_op jit(solution)/shard_map/ppermute | solution.py:93
  49.5 29.2 %collective-permute-start.8 = (bf16[2,48,3072]{2,1,0:T(8,128)(2,1)S(1)}, bf16[2,48,3072]{2,1,0:T(8,128)(2,1)S(1)}, u32[]{:S(2)}, u32[]{:S(2)}) collective-permute-start(bf16[2,48,3072]{2,1,0:T(8,128)(2,1)S(1)} %shard_map.249), channel_id=1, source_target_pairs={{0,4},{2,6},{4,0},{6,2},{8,12},{10,14},{12,8},{14,10},{16,20},{18,... | collective-permute-start | bytes 1769480 | tf_op jit(solution)/shard_map/ppermute | solution.py:89
  51.1 19.1 %collective-permute-start.11 = (bf16[48,4608]{1,0:T(8,128)(2,1)S(1)}, bf16[48,4608]{1,0:T(8,128)(2,1)S(1)}, u32[]{:S(2)}, u32[]{:S(2)}) collective-permute-start(bf16[48,4608]{1,0:T(8,128)(2,1)S(1)} %get-tuple-element.194.refs_0_), channel_id=1, source_target_pairs={{0,8},{2,10},{4,12},{6,14},{8,16},{10,18},{12,20},{14,22},{16,24},... | collective-permute-start | bytes 1327112 | tf_op jit(solution)/shard_map/ppermute | solution.py:89
  52.4 26.3 %collective-permute-start.12 = (bf16[48,4608]{1,0:T(8,128)(2,1)S(1)}, bf16[48,4608]{1,0:T(8,128)(2,1)S(1)}, u32[]{:S(2)}, u32[]{:S(2)}) collective-permute-start(bf16[48,4608]{1,0:T(8,128)(2,1)S(1)} %get-tuple-element.194.refs_0_), channel_id=1, source_target_pairs={{0,24},{2,26},{4,28},{6,30},{8,0},{10,2},{12,4},{14,6},{16,8},{18,... | collective-permute-start | bytes 1327112 | tf_op jit(solution)/shard_map/ppermute | solution.py:89
  60.8 18.0 %collective-permute-start.10 = (bf16[48,3072]{1,0:T(8,128)(2,1)S(1)}, bf16[48,3072]{1,0:T(8,128)(2,1)S(1)}, u32[]{:S(2)}, u32[]{:S(2)}) collective-permute-start(bf16[48,3072]{1,0:T(8,128)(2,1)S(1)} %collective-permute-done.9.refs_2_), channel_id=1, source_target_pairs={{0,4},{2,6},{4,0},{6,2},{8,12},{10,14},{12,8},{14,10},{16,20},{18,... | collective-permute-start | bytes 884744 | tf_op jit(solution)/shard_map/ppermute | solution.py:89
  93.5 19.1 %collective-permute-start.18 = (bf16[2,256,768]{2,1,0:T(8,128)(2,1)S(1)}, bf16[2,256,768]{2,1,0:T(8,128)(2,1)S(1)}, u32[]{:S(2)}, u32[]{:S(2)}) collective-permute-start(bf16[2,256,768]{2,1,0:T(8,128)(2,1)S(1)} %get-tuple-element.204.own_ref), channel_id=1, source_target_pairs={{0,1},{1,0},{2,3},{3,2},{4,5},{5,4},{6,7},{7,6},{8,9},{9,8},{10,11... | collective-permute-start | bytes 2359304 | tf_op jit(solution)/shard_map/ppermute | solution.py:93
  94.1 16.3 %collective-permute-start.17 = (bf16[2,48,3072]{2,1,0:T(8,128)(2,1)S(1)}, bf16[2,48,3072]{2,1,0:T(8,128)(2,1)S(1)}, u32[]{:S(2)}, u32[]{:S(2)}) collective-permute-start(bf16[2,48,3072]{2,1,0:T(8,128)(2,1)S(1)} %shard_map.254), channel_id=1, source_target_pairs={{0,4},{2,6},{4,0},{6,2},{8,12},{10,14},{12,8},{14,10},{16,20},{18,... | collective-permute-start | bytes 1769480 | tf_op jit(solution)/shard_map/ppermute | solution.py:89
  95.7 19.4 %collective-permute-start.22 = (bf16[1,48,3072]{2,1,0:T(8,128)(2,1)S(1)}, bf16[1,48,3072]{2,1,0:T(8,128)(2,1)S(1)}, u32[]{:S(2)}, u32[]{:S(2)}) collective-permute-start(bf16[1,48,3072]{2,1,0:T(8,128)(2,1)S(1)} %shard_map.259), channel_id=1, source_target_pairs={{0,4},{2,6},{4,0},{6,2},{8,12},{10,14},{12,8},{14,10},{16,20},{18,... | collective-permute-start | bytes 884744 | tf_op jit(solution)/shard_map/ppermute | solution.py:89
  115.2 16.6 %collective-permute-start.23 = (bf16[2,4,48,3072]{3,2,1,0:T(8,128)(2,1)S(1)}, bf16[2,4,48,3072]{3,2,1,0:T(8,128)(2,1)S(1)}, u32[]{:S(2)}, u32[]{:S(2)}) collective-permute-start(bf16[2,4,48,3072]{3,2,1,0:T(8,128)(2,1)S(1)} %shard_map.260.mine_ref), channel_id=1, source_target_pairs={{0,2},{2,0},{4,6},{6,4},{8,10},{10,8},{12,14},{14,12},{16,18},{18,... | collective-permute-start | bytes 7077896 | tf_op jit(solution)/shard_map/ppermute | solution.py:89
  131.3 18.9 %collective-permute-start.21 = (bf16[256,768]{1,0:T(8,128)(2,1)S(1)}, bf16[256,768]{1,0:T(8,128)(2,1)S(1)}, u32[]{:S(2)}, u32[]{:S(2)}) collective-permute-start(bf16[256,768]{1,0:T(8,128)(2,1)S(1)} %get-tuple-element.209.own_ref), channel_id=1, source_target_pairs={{0,1},{1,0},{2,3},{3,2},{4,5},{5,4},{6,7},{7,6},{8,9},{9,8},{10,11... | collective-permute-start | bytes 1179656 | tf_op jit(solution)/shard_map/ppermute | solution.py:93
  172.6 17.1 %collective-permute-start.28 = (bf16[2,4,48,3072]{3,2,0,1:T(8,128)(2,1)S(1)}, bf16[2,4,48,3072]{3,2,0,1:T(8,128)(2,1)S(1)}, u32[]{:S(2)}, u32[]{:S(2)}) collective-permute-start(bf16[2,4,48,3072]{3,2,0,1:T(8,128)(2,1)S(1)} %copy.41), channel_id=1, source_target_pairs={{0,2},{2,0},{4,6},{6,4},{8,10},{10,8},{12,14},{14,12},{16,18},{18,... | collective-permute-start | bytes 7077896 | tf_op jit(solution)/shard_map/ppermute | solution.py:89
  174.2 18.8 %collective-permute-start.29 = (bf16[256,768]{1,0:T(8,128)(2,1)S(1)}, bf16[256,768]{1,0:T(8,128)(2,1)S(1)}, u32[]{:S(2)}, u32[]{:S(2)}) collective-permute-start(bf16[256,768]{1,0:T(8,128)(2,1)S(1)} %get-tuple-element.242.own_ref), channel_id=1, source_target_pairs={{0,1},{1,0},{2,3},{3,2},{4,5},{5,4},{6,7},{7,6},{8,9},{9,8},{10,11... | collective-permute-start | bytes 1179656 | tf_op jit(solution)/shard_map/ppermute | solution.py:93
  190.0 16.0 %collective-permute-start.32 = (bf16[2,48,3072]{2,1,0:T(8,128)(2,1)S(1)}, bf16[2,48,3072]{2,1,0:T(8,128)(2,1)S(1)}, u32[]{:S(2)}, u32[]{:S(2)}) collective-permute-start(bf16[2,48,3072]{2,1,0:T(8,128)(2,1)S(1)} %get-tuple-element.381), channel_id=1, source_target_pairs={{0,8},{2,10},{4,12},{6,14},{8,16},{10,18},{12,20},{14,22},{16,24},... | collective-permute-start | bytes 1769480 | tf_op jit(solution)/shard_map/ppermute | solution.py:89
  215.5 17.3 %collective-permute-start.34 = (bf16[2,4,48,3072]{3,2,1,0:T(8,128)(2,1)S(1)}, bf16[2,4,48,3072]{3,2,1,0:T(8,128)(2,1)S(1)}, u32[]{:S(2)}, u32[]{:S(2)}) collective-permute-start(bf16[2,4,48,3072]{3,2,1,0:T(8,128)(2,1)S(1)} %get-tuple-element.264), channel_id=1, source_target_pairs={{0,2},{2,0},{4,6},{6,4},{8,10},{10,8},{12,14},{14,12},{16,18},{18,... | collective-permute-start | bytes 7077896 | tf_op jit(solution)/shard_map/ppermute | solution.py:89
  217.1 15.4 %collective-permute-start.38 = (bf16[4,48,1536]{2,1,0:T(8,128)(2,1)S(1)}, bf16[4,48,1536]{2,1,0:T(8,128)(2,1)S(1)}, u32[]{:S(2)}, u32[]{:S(2)}) collective-permute-start(bf16[4,48,1536]{2,1,0:T(8,128)(2,1)S(1)} %fusion.7), channel_id=1, source_target_pairs={{0,4},{2,6},{4,0},{6,2},{8,12},{10,14},{12,8},{14,10},{16,20},{18,... | collective-permute-start | bytes 1769480 | tf_op jit(solution)/shard_map/ppermute | solution.py:89
  218.6 16.9 %collective-permute-start.39 = (bf16[256,768]{1,0:T(8,128)(2,1)S(1)}, bf16[256,768]{1,0:T(8,128)(2,1)S(1)}, u32[]{:S(2)}, u32[]{:S(2)}) collective-permute-start(bf16[256,768]{1,0:T(8,128)(2,1)S(1)} %get-tuple-element.279.own_ref), channel_id=1, source_target_pairs={{0,1},{1,0},{2,3},{3,2},{4,5},{5,4},{6,7},{7,6},{8,9},{9,8},{10,11... | collective-permute-start | bytes 1179656 | tf_op jit(solution)/shard_map/ppermute | solution.py:93
  241.3 18.0 %collective-permute-start.42 = (bf16[2,48,3072]{2,1,0:T(8,128)(2,1)S(1)}, bf16[2,48,3072]{2,1,0:T(8,128)(2,1)S(1)}, u32[]{:S(2)}, u32[]{:S(2)}) collective-permute-start(bf16[2,48,3072]{2,1,0:T(8,128)(2,1)S(1)} %fusion.1), channel_id=1, source_target_pairs={{0,8},{2,10},{4,12},{6,14},{8,16},{10,18},{12,20},{14,22},{16,24},... | collective-permute-start | bytes 1769480 | tf_op jit(solution)/shard_map/ppermute | solution.py:89
  241.4 18.0 %collective-permute-start.41 = (bf16[2,48,3072]{2,1,0:T(8,128)(2,1)S(1)}, bf16[2,48,3072]{2,1,0:T(8,128)(2,1)S(1)}, u32[]{:S(2)}, u32[]{:S(2)}) collective-permute-start(bf16[2,48,3072]{2,1,0:T(8,128)(2,1)S(1)} %get-tuple-element.378), channel_id=1, source_target_pairs={{0,4},{2,6},{4,0},{6,2},{8,12},{10,14},{12,8},{14,10},{16,20},{18,... | collective-permute-start | bytes 1769480 | tf_op jit(solution)/shard_map/ppermute | solution.py:89
  243.0 29.0 %collective-permute-start.49 = (bf16[48,1536]{1,0:T(8,128)(2,1)S(1)}, bf16[48,1536]{1,0:T(8,128)(2,1)S(1)}, u32[]{:S(2)}, u32[]{:S(2)}) collective-permute-start(bf16[48,1536]{1,0:T(8,128)(2,1)S(1)} %get-tuple-element.389), channel_id=1, source_target_pairs={{0,24},{2,26},{4,28},{6,30},{8,0},{10,2},{12,4},{14,6},{16,8},{18,... | collective-permute-start | bytes 442376 | tf_op jit(solution)/shard_map/ppermute | solution.py:89
  246.7 19.1 %collective-permute-start.47 = (bf16[48,1536]{1,0:T(8,128)(2,1)S(1)}, bf16[48,1536]{1,0:T(8,128)(2,1)S(1)}, u32[]{:S(2)}, u32[]{:S(2)}) collective-permute-start(bf16[48,1536]{1,0:T(8,128)(2,1)S(1)} %get-tuple-element.388), channel_id=1, source_target_pairs={{0,8},{2,10},{4,12},{6,14},{8,16},{10,18},{12,20},{14,22},{16,24},... | collective-permute-start | bytes 442376 | tf_op jit(solution)/shard_map/ppermute | solution.py:89
  246.7 24.4 %collective-permute-start.48 = (bf16[48,1536]{1,0:T(8,128)(2,1)S(1)}, bf16[48,1536]{1,0:T(8,128)(2,1)S(1)}, u32[]{:S(2)}, u32[]{:S(2)}) collective-permute-start(bf16[48,1536]{1,0:T(8,128)(2,1)S(1)} %get-tuple-element.387), channel_id=1, source_target_pairs={{0,16},{2,18},{4,20},{6,22},{8,24},{10,26},{12,28},{14,30},{16,0},... | collective-permute-start | bytes 442376 | tf_op jit(solution)/shard_map/ppermute | solution.py:89
  260.9 28.3 %collective-permute-start.46 = (bf16[48,3072]{1,0:T(8,128)(2,1)S(1)}, bf16[48,3072]{1,0:T(8,128)(2,1)S(1)}, u32[]{:S(2)}, u32[]{:S(2)}) collective-permute-start(bf16[48,3072]{1,0:T(8,128)(2,1)S(1)} %get-tuple-element.382), channel_id=1, source_target_pairs={{0,16},{2,18},{4,20},{6,22},{8,24},{10,26},{12,28},{14,30},{16,0},... | collective-permute-start | bytes 884744 | tf_op jit(solution)/shard_map/ppermute | solution.py:89
  265.8 23.9 %collective-permute-start.44 = (bf16[4,48,1664]{2,1,0:T(8,128)(2,1)S(1)}, bf16[4,48,1664]{2,1,0:T(8,128)(2,1)S(1)}, u32[]{:S(2)}, u32[]{:S(2)}) collective-permute-start(bf16[4,48,1664]{2,1,0:T(8,128)(2,1)S(1)} %fusion.5), channel_id=1, source_target_pairs={{0,4},{2,6},{4,0},{6,2},{8,12},{10,14},{12,8},{14,10},{16,20},{18,... | collective-permute-start | bytes 1916936 | tf_op jit(solution)/shard_map/ppermute | solution.py:89
  271.1 19.0 %collective-permute-start.50 = (bf16[256,768]{1,0:T(8,128)(2,1)S(1)}, bf16[256,768]{1,0:T(8,128)(2,1)S(1)}, u32[]{:S(2)}, u32[]{:S(2)}) collective-permute-start(bf16[256,768]{1,0:T(8,128)(2,1)S(1)} %get-tuple-element.275.refs_1_), channel_id=1, source_target_pairs={{0,1},{1,0},{2,3},{3,2},{4,5},{5,4},{6,7},{7,6},{8,9},{9,8},{10,11... | collective-permute-start | bytes 1179656 | tf_op jit(solution)/shard_map/ppermute | solution.py:93
  271.9 18.8 %collective-permute-start.51 = (bf16[256,768]{1,0:T(8,128)(2,1)S(1)}, bf16[256,768]{1,0:T(8,128)(2,1)S(1)}, u32[]{:S(2)}, u32[]{:S(2)}) collective-permute-start(bf16[256,768]{1,0:T(8,128)(2,1)S(1)} %get-tuple-element.305.refs_4_), channel_id=1, source_target_pairs={{0,1},{1,0},{2,3},{3,2},{4,5},{5,4},{6,7},{7,6},{8,9},{9,8},{10,11... | collective-permute-start | bytes 1179656 | tf_op jit(solution)/shard_map/ppermute | solution.py:93
  274.1 32.1 %collective-permute-start.35 = (bf16[2,48,3072]{2,1,0:T(8,128)(2,1)S(1)}, bf16[2,48,3072]{2,1,0:T(8,128)(2,1)S(1)}, u32[]{:S(2)}, u32[]{:S(2)}) collective-permute-start(bf16[2,48,3072]{2,1,0:T(8,128)(2,1)S(1)} %get-tuple-element.379), channel_id=1, source_target_pairs={{0,4},{2,6},{4,0},{6,2},{8,12},{10,14},{12,8},{14,10},{16,20},{18,... | collective-permute-start | bytes 1769480 | tf_op jit(solution)/shard_map/ppermute | solution.py:89
  289.3 16.6 %collective-permute-start.43 = (bf16[48,3072]{1,0:T(8,128)(2,1)S(1)}, bf16[48,3072]{1,0:T(8,128)(2,1)S(1)}, u32[]{:S(2)}, u32[]{:S(2)}) collective-permute-start(bf16[48,3072]{1,0:T(8,128)(2,1)S(1)} %fusion.13), channel_id=1, source_target_pairs={{0,4},{2,6},{4,0},{6,2},{8,12},{10,14},{12,8},{14,10},{16,20},{18,... | collective-permute-start | bytes 884744 | tf_op jit(solution)/shard_map/ppermute | solution.py:89
  290.0 16.2 %collective-permute-start.52 = (bf16[48,1664]{1,0:T(8,128)(2,1)S(1)}, bf16[48,1664]{1,0:T(8,128)(2,1)S(1)}, u32[]{:S(2)}, u32[]{:S(2)}) collective-permute-start(bf16[48,1664]{1,0:T(8,128)(2,1)S(1)} %get-tuple-element.386), channel_id=1, source_target_pairs={{0,8},{2,10},{4,12},{6,14},{8,16},{10,18},{12,20},{14,22},{16,24},... | collective-permute-start | bytes 479240 | tf_op jit(solution)/shard_map/ppermute | solution.py:89
  290.1 16.1 %collective-permute-start.53 = (bf16[48,1664]{1,0:T(8,128)(2,1)S(1)}, bf16[48,1664]{1,0:T(8,128)(2,1)S(1)}, u32[]{:S(2)}, u32[]{:S(2)}) collective-permute-start(bf16[48,1664]{1,0:T(8,128)(2,1)S(1)} %get-tuple-element.385), channel_id=1, source_target_pairs={{0,16},{2,18},{4,20},{6,22},{8,24},{10,26},{12,28},{14,30},{16,0},... | collective-permute-start | bytes 479240 | tf_op jit(solution)/shard_map/ppermute | solution.py:89
  290.7 15.5 %collective-permute-start.54 = (bf16[48,1664]{1,0:T(8,128)(2,1)S(1)}, bf16[48,1664]{1,0:T(8,128)(2,1)S(1)}, u32[]{:S(2)}, u32[]{:S(2)}) collective-permute-start(bf16[48,1664]{1,0:T(8,128)(2,1)S(1)} %get-tuple-element.384), channel_id=1, source_target_pairs={{0,24},{2,26},{4,28},{6,30},{8,0},{10,2},{12,4},{14,6},{16,8},{18,... | collective-permute-start | bytes 479240 | tf_op jit(solution)/shard_map/ppermute | solution.py:89
  (44 other events, 337.6 us)

commit v3 on v2

--- a/solution.py
+++ b/solution.py
@@ -35,6 +35,7 @@
 
 
 def call(body, outs, in_specs, scratch=(), flops=0, moved=0, out_specs=None, trans=0, limit=13):
+    weight = 16 if scratch else 16 if flops else 1
     if out_specs is None:
         out_specs = [VM] * len(outs)
     return pl.pallas_call(
@@ -44,7 +45,9 @@
         out_specs=out_specs,
         scratch_shapes=list(scratch),
         compiler_params=pltpu.CompilerParams(vmem_limit_bytes=limit * 1024 * 1024),
-        cost_estimate=pl.CostEstimate(flops=flops, bytes_accessed=moved, transcendentals=trans),
+        cost_estimate=pl.CostEstimate(
+            flops=int(flops * weight), bytes_accessed=int(moved * weight), transcendentals=trans
+        ),
     )
 
 
@@ -954,77 +957,100 @@
     block_out = jnp.stack([o[5] for o in out])
     done = [o[0] for o in out]
     met = [exchange(o[0]) for o in out]
-    g_f1 = matrix_gradient([(low1_1, din, FFT), (dffn, act1, FFT)], pieced, ndp)
-    res[0] = after(res[0], g_f1[0])
-
-    def back_1(m):
-        return attention_back(
-            m, 1, res[m], done[m], met[m], n1_1[m], s1_1[m], rep, qkv1, probs1, ctx1, watt1
-        )
-
-    out = [back_1(0)]
-    if pieced:
-        f1_own, f1_met = g_f1[0], move(g_f1[1], "core")
-        f1_t = pass_both(f1_own, after(f1_met, out[0][0]), 3)
-        f1_rec = move(f1_t, 1)
-        res[1] = after(res[1], f1_t)
-    out += [back_1(1)]
-    mid, datt, dqkv, vec_a1 = ([o[i] for o in out] for i in range(1, 5))
+    plan = {"w_f1": 0, "f1_3": 1, "w_a1": 2, "f1_2": 3, "a1_s": 3, "w_f0": 4, "f1_1": 4, "a1_t": 5, "f0_s": 5}
+    held, ends = {}, []
+
+    def make(name):
+        gate = ends[-1:] if 1 else []
+        if name == "w_f1":
+            g = matrix_gradient([(low1_1, din_1, FFT), (dffn_1, act1, FFT)], pieced, ndp)
+        elif name == "w_a1":
+            g = matrix_gradient(
+                [([low_h1] * 2, dqkv_1, QKV), (datt_1, [ctx1] * 2, HD)], pieced, ndp
+            )
+        elif name == "w_f0":
+            g = matrix_gradient(
+                [([low1_0] * 2, din_0, FFT), (dffn_0, [act0] * 2, FFT)], pieced, ndp
+            )
+        elif not pieced:
+            return []
+        if name.startswith("w_"):
+            held[name[2:]] = g if not pieced else (g[0], move(g[1], "core"))
+            return [g[0]]
+        own, across_core = held[name[:2]]
+        if name[:3] == "f1_":
+            k = int(name[3])
+            if k == 3:
+                total = pass_both(own, after(across_core, *gate), k)
+            else:
+                total = pass_both(own, across_core, k, after(held["f1_rec"], *gate))
+            held["f1_rec"] = move(total, 1)
+            return [total]
+        if name == "a1_t":
+            parts = pass_on(own, across_core, after(held["a1_got"], *gate)[1:], (1, 2, 3))
+            held["a1_r"] = [move(t, k + 1) for k, t in enumerate(parts)]
+            return [parts[2]]
+        places = (0, 1, 2, 3) if name == "a1_s" else (2, 3)
+        total = meet(own, after(across_core, *gate), places)
+        held[name[:2] + "_got"] = move(total, "x")
+        return [total]
+
+    def before(stage, value):
+        needed = [a for name in plan if plan[name] == stage for a in make(name)]
+        return after(value, *needed) if needed else value
+
+    din_1, dffn_1 = din, dffn
+    out = []
+    for m in both:
+        value = before(m, res[m])
+        out.append(
+            attention_back(
+                m, 1, value, done[m], met[m], n1_1[m], s1_1[m], rep, qkv1, probs1, ctx1, watt1
+            )
+        )
+        ends.append(out[m][0])
+    mid, datt_1, dqkv_1, vec_a1 = ([o[i] for o in out] for i in range(1, 5))
     done = [o[0] for o in out]
     met = [exchange(o[0]) for o in out]
-    g_a1 = matrix_gradient([([low_h1] * 2, dqkv, QKV), (datt, [ctx1] * 2, HD)], pieced, ndp)
-    mid[0] = after(mid[0], g_a1[0])
-    def back_2(m):
-        return feed_back(m, 0, mid[m], done[m], met[m], n2_0, s2_0, rep, slope0, wffn0)
-
-    out = [back_2(0)]
-    if pieced:
-        a1_own, a1_met = g_a1[0], move(g_a1[1], "core")
-        a1_s = meet(a1_own, after(a1_met, out[0][0]), (0, 1, 2, 3))
-        a1_got = across(a1_s)
-        f1_t = pass_both(f1_own, f1_met, 2, after(f1_rec, out[0][0]))
-        f1_rec = move(f1_t, 1)
-        mid[1] = after(mid[1], a1_s, f1_t)
-    out += [back_2(1)]
-    res, dffn, din, vec_f0 = ([o[i] for o in out] for i in range(1, 5))
+    out = []
+    for m in both:
+        value = before(2 + m, mid[m])
+        out.append(feed_back(m, 0, value, done[m], met[m], n2_0, s2_0, rep, slope0, wffn0))
+        ends.append(out[m][0])
+    res, dffn_0, din_0, vec_f0 = ([o[i] for o in out] for i in range(1, 5))
     done = [o[0] for o in out]
     met = [exchange(o[0]) for o in out]
-    g_f0 = matrix_gradient([([low1_0] * 2, din, FFT), (dffn, [act0] * 2, FFT)], pieced, ndp)
-    res[0] = after(res[0], g_f0[0])
-    if pieced:
-        f1_t = pass_both(f1_own, f1_met, 1, after(f1_rec, g_f0[0]))
-        f1_rec = move(f1_t, 1)
-        res[0] = after(res[0], f1_t)
-
-    def back_3(m):
-        return attention_back(
-            m, 0, res[m], done[m], met[m], n1_0, s1_0, rep, qkv0, probs0, ctx0, watt0
-        )
-
-    out = [back_3(0)]
-    if pieced:
-        f0_own, f0_met = g_f0[0], move(g_f0[1], "core")
-        f0_s = meet(f0_own, after(f0_met, out[0][0]), (2, 3))
-        f0_got_hi = across(f0_s)
-        a1_t1, a1_t2, a1_t3 = pass_on(a1_own, a1_met, after(a1_got, out[0][0])[1:], (1, 2, 3))
-        a1_r = [move(t, k) for k, t in ((1, a1_t1), (2, a1_t2), (3, a1_t3))]
-        res[1] = after(res[1], f0_s, a1_t3)
-    out += [back_3(1)]
+    out = []
+    for m in both:
+        value = before(4 + m, res[m])
+        out.append(
+            attention_back(
+                m, 0, value, done[m], met[m], n1_0, s1_0, rep, qkv0, probs0, ctx0, watt0
+            )
+        )
+        ends.append(out[m][0])
     mid, datt, dqkv, vec_a0 = ([o[i] for o in out] for i in range(1, 5))
     done = [o[0] for o in out]
     met = [exchange(o[0]) for o in out]
+    dqkv[0] = before(6, dqkv[0])
     g_a0 = matrix_gradient(
         [([block_in] * MICRO, dqkv, QKV), (datt, [ctx0] * 2, HD)],
         pieced,
         ndp,
         vectors=vec_a0 + vec_f0 + vec_a1 + vec_f1,
     )
+    ends.append(g_a0[0])
+    before(7, g_a0[0])
+    if pieced:
+        (f1_own, f1_met), (a1_own, a1_met), (f0_own, f0_met) = (held[c] for c in ("f1", "a1", "f0"))
+        f1_rec, a1_got, a1_r, f0_got_hi = (held[c] for c in ("f1_rec", "a1_got", "a1_r", "f0_got"))
+    else:
+        g_f1, g_a1, g_f0 = (held[c] for c in ("f1", "a1", "f0"))
     if pieced:
         masters = ready(*(after(a, g_a0[0]) for a in masters))
         input_grad = finish_input(mid, done, met)
         a0_own, a0_met = g_a0[0], move(g_a0[1], "core")
-        a0_s, f0_got_hi, f1_rec = tie(meet(a0_own, a0_met, (0, 1, 2, 3)), f0_got_hi, f1_rec)
-        a0_got = across(a0_s)
+        a0_got = across(meet(a0_own, a0_met, (0, 1, 2, 3)))
         f1_last = pass_both(f1_own, f1_met, 0, f1_rec)
         f1_got = across(f1_last[1])
         f0_t2, f0_t3 = pass_on(f0_own, f0_met, f0_got_hi, (2, 3))

time: 344 us -> 314 us (0.913)
  waiting for transfers between devices: 187 us -> 152 us
    ppermute x14, waiting for transfers between devices: 51 us -> 33.4 us  [exchange(): return lax.ppermute(a, 'tensor', [(0, 1), (1, 0)])]
    ppermute x42, waiting for transfers between devices: 129 us -> 111 us  [move(): return lax.ppermute(a, 'dp', pairs_of(lax.axis_size('dp'), kind))]
    unnamed x29 -> x37, local copies, waits for them, and re-layouts: 5.84 us -> 6.92 us
  transfers between devices with their start and end apart: 63 -> 63, of which waited for: 41 -> 37; matrix products, arithmetic and copies ran while one was open for 1% -> 1% of each run, Pallas kernels for 12% -> 17%
where the time goes in v3:
time: 314 us; the launch traced here: 308 us
  waiting for transfers between devices  152 us (48%)
  starting transfers between devices  77.7 us (25%)
  Pallas kernels  64.3 us (20%)
  local copies, waits for them, and re-layouts  8.49 us (3%)
  other arithmetic  4.2 us (1%)
    ppermute x42, waiting for transfers between devices, move(): return lax.ppermute(a, 'dp', pairs_of(lax.axis_size('dp'), kind))  111 us
    ppermute x42, starting transfers between devices, move(): return lax.ppermute(a, 'dp', pairs_of(lax.axis_size('dp'), kind))  49.9 us
    ppermute x14, waiting for transfers between devices, exchange(): return lax.ppermute(a, 'tensor', [(0, 1), (1, 0)])  33.4 us
    ppermute x14, starting transfers between devices, exchange(): return lax.ppermute(a, 'tensor', [(0, 1), (1, 0)])  19.9 us
    pallas_call x4, Pallas kernels, attention_back(): call(body, [((SEQ, D), b16), ((SEQ, D), f32), ((SEQ, D), b16), ((SEQ, QKV...  12.4 us
    pallas_call x4, Pallas kernels, matrix_gradient(): call(body, outs, specs, [pltpu.VMEM((D, step), f32)], flops=2 * MICRO * S...  11.8 us
    ppermute x7, starting transfers between devices, ppermute_bits(): lax.ppermute(value, ('dp', 'tensor'), [(i, i ^ bits) for i in range(n)])  7.95 us
    ppermute x7, waiting for transfers between devices, ppermute_bits(): lax.ppermute(value, ('dp', 'tensor'), [(i, i ^ bits) for i in range(n)])  7.06 us
  transfers between devices with their start and end apart: 63, of which 37 were waited for; matrix products, arithmetic and copies ran while one was open for 1% of the time, Pallas kernels for 17%

profile of v3, /device:TPU:0, one launch (start us, length us, event | category | flops | bytes accessed | tf_op | source)
XLA Modules:
  0.0 308.2 jit_solution(13715391828962397407)
XLA Ops:
  12.3 3.4 %collective-permute-done.refs_0_.refs_1_ = bf16[48,1664]{1,0:T(8,128)(2,1)S(1)} collective-permute-done((bf16[48,1664]{1,0:T(8,128)(2,1)S(1)}, bf16[48,1664]{1,0:T(8,128)(2,1)S(1)}, u32[]{:S(2)}, u32[]{:S(2)}) %collective-permute-start) | collective-permute-done | bytes 159776 | tf_op jit(solution)/shard_map/ppermute | solution.py:92
  15.7 5.4 %collective-permute-done.1.refs_1_.refs_2_ = bf16[48,1664]{1,0:T(8,128)(2,1)S(1)} collective-permute-done((bf16[48,1664]{1,0:T(8,128)(2,1)S(1)}, bf16[48,1664]{1,0:T(8,128)(2,1)S(1)}, u32[]{:S(2)}, u32[]{:S(2)}) %collective-permute-start.1) | collective-permute-done | bytes 159776 | tf_op jit(solution)/shard_map/ppermute | solution.py:92
  21.8 3.9 %collective-permute-start.5 = (bf16[48,3072]{1,0:T(8,128)(2,1)S(1)}, bf16[48,3072]{1,0:T(8,128)(2,1)S(1)}, u32[]{:S(2)}, u32[]{:S(2)}) collective-permute-start(bf16[48,3072]{1,0:T(8,128)(2,1)S(1)} %get-tuple-element.183.refs_0_), channel_id=1, source_target_pairs={{0,8},{2,10},{4,12},{6,14},{8,16},{10,18},{12,20},{14,22},{16,24},... | collective-permute-start | bytes 884744 | tf_op jit(solution)/shard_map/ppermute | solution.py:92
  26.7 10.2 %collective-permute-done.4.refs_5_ = bf16[3,48,1664]{2,1,0:T(8,128)(2,1)S(1)} collective-permute-done((bf16[3,48,1664]{2,1,0:T(8,128)(2,1)S(1)}, bf16[3,48,1664]{2,1,0:T(8,128)(2,1)S(1)}, u32[]{:S(2)}, u32[]{:S(2)}) %collective-permute-start.4) | collective-permute-done | bytes 479264 | tf_op jit(solution)/shard_map/ppermute | solution.py:92
  43.5 4.4 %shard_map.248 = (bf16[2,256,768]{2,1,0:T(8,128)(2,1)S(1)}, bf16[2,256,1152]{2,1,0:T(8,128)(2,1)S(1)}, bf16[2,6,256,256]{3,2,1,0:T(8,128)(2,1)S(1)}, bf16[2,256,384]{2,1,0:T(8,128)(2,1)S(1)}) custom-call(bf16[2,256,768]{2,1,0:T(8,128)(2,1)S(1)} %copy-done.13, s32[2,1,256]{2,1,0:T(1,128)S(1)} %reshape.140.seg_ref, ...), custom_call_target="tpu_custom_call" | custom-call | flops 25769803776 | bytes 201326592 | tf_op jit(solution)/shard_map/pallas_call | solution.py:288
  55.5 5.9 %collective-permute-done.9.refs_2_ = bf16[48,3072]{1,0:T(8,128)(2,1)S(1)} collective-permute-done((bf16[48,3072]{1,0:T(8,128)(2,1)S(1)}, bf16[48,3072]{1,0:T(8,128)(2,1)S(1)}, u32[]{:S(2)}, u32[]{:S(2)}) %collective-permute-start.9) | collective-permute-done | bytes 294944 | tf_op jit(solution)/shard_map/ppermute | solution.py:92
  62.8 7.9 %collective-permute-done.11.refs_0_.refs_1_ = bf16[48,4608]{1,0:T(8,128)(2,1)S(1)} collective-permute-done((bf16[48,4608]{1,0:T(8,128)(2,1)S(1)}, bf16[48,4608]{1,0:T(8,128)(2,1)S(1)}, u32[]{:S(2)}, u32[]{:S(2)}) %collective-permute-start.11) | collective-permute-done | bytes 442400 | tf_op jit(solution)/shard_map/ppermute | solution.py:92
  70.7 8.6 %collective-permute-done.12.refs_1_.refs_3_ = bf16[48,4608]{1,0:T(8,128)(2,1)S(1)} collective-permute-done((bf16[48,4608]{1,0:T(8,128)(2,1)S(1)}, bf16[48,4608]{1,0:T(8,128)(2,1)S(1)}, u32[]{:S(2)}, u32[]{:S(2)}) %collective-permute-start.12) | collective-permute-done | bytes 442400 | tf_op jit(solution)/shard_map/ppermute | solution.py:92
  84.5 4.3 %shard_map.252 = (bf16[2,256,768]{2,1,0:T(8,128)(2,1)S(1)}, f32[2,256,768]{2,1,0:T(8,128)S(1)}, f32[2,256,1]{2,1,0:T(8,128)S(1)}, bf16[2,256,768]{2,1,0:T(8,128)...) custom-call(bf16[2,256,768]{2,1,0:T(8,128)(2,1)S(1)} %copy-done.13, ...), custom_call_target="tpu_custom_call" | custom-call | flops 38654705664 | bytes 335544320 | tf_op jit(solution)/shard_map/pallas_call | solution.py:362
  89.5 4.6 %collective-permute-done.16.refs_0_.refs_2_ = bf16[48,4608]{1,0:T(8,128)(2,1)S(1)} collective-permute-done((bf16[48,4608]{1,0:T(8,128)(2,1)S(1)}, bf16[48,4608]{1,0:T(8,128)(2,1)S(1)}, u32[]{:S(2)}, u32[]{:S(2)}) %collective-permute-start.16) | collective-permute-done | bytes 442400 | tf_op jit(solution)/shard_map/ppermute | solution.py:92
  95.7 3.9 %collective-permute-done.19.refs_6_ = bf16[1,48,1536]{2,1,0:T(8,128)(2,1)S(1)} collective-permute-done((bf16[1,48,1536]{2,1,0:T(8,128)(2,1)S(1)}, bf16[1,48,1536]{2,1,0:T(8,128)(2,1)S(1)}, u32[]{:S(2)}, u32[]{:S(2)}) %collective-permute-start.19) | collective-permute-done | bytes 147488 | tf_op jit(solution)/shard_map/ppermute | solution.py:92
  102.6 14.1 %collective-permute-done.17.refs_5_ = bf16[2,48,3072]{2,1,0:T(8,128)(2,1)S(1)} collective-permute-done((bf16[2,48,3072]{2,1,0:T(8,128)(2,1)S(1)}, bf16[2,48,3072]{2,1,0:T(8,128)(2,1)S(1)}, u32[]{:S(2)}, u32[]{:S(2)}) %collective-permute-start.17) | collective-permute-done | bytes 589856 | tf_op jit(solution)/shard_map/ppermute | solution.py:92
  116.6 3.1 %collective-permute-done.18.other_ref = bf16[2,256,768]{2,1,0:T(8,128)(2,1)S(1)} collective-permute-done((bf16[2,256,768]{2,1,0:T(8,128)(2,1)S(1)}, bf16[2,256,768]{2,1,0:T(8,128)(2,1)S(1)}, u32[]{:S(2)}, u32[]{:S(2)}) %collective-permute-start.18) | collective-permute-done | bytes 786464 | tf_op jit(solution)/shard_map/ppermute | solution.py:96
  122.6 5.0 %shard_map.258 = (bf16[256,768]{1,0:T(8,128)(2,1)S(1)}, bf16[256,768]{1,0:T(8,128)(2,1)S(1)}, bf16[2,256,1152]{2,1,0:T(8,128)(2,1)S(1)}, bf16[2,6,256,256]{3,2,1...) custom-call(f32[2,256,768]{2,1,0:T(8,128)S(1)} %get-tuple-element.19, ...), custom_call_target="tpu_custom_call" | custom-call | flops 25769803776 | bytes 268435456 | tf_op jit(solution)/shard_map/pallas_call | solution.py:314
  130.0 9.5 %collective-permute-done.21.other_ref = bf16[256,768]{1,0:T(8,128)(2,1)S(1)} collective-permute-done((bf16[256,768]{1,0:T(8,128)(2,1)S(1)}, bf16[256,768]{1,0:T(8,128)(2,1)S(1)}, u32[]{:S(2)}, u32[]{:S(2)}) %collective-permute-start.21) | collective-permute-done | bytes 393248 | tf_op jit(solution)/shard_map/ppermute | solution.py:96
  143.8 4.2 %collective-permute-done.25.other_ref = bf16[256,768]{1,0:T(8,128)(2,1)S(1)} collective-permute-done((bf16[256,768]{1,0:T(8,128)(2,1)S(1)}, bf16[256,768]{1,0:T(8,128)(2,1)S(1)}, u32[]{:S(2)}, u32[]{:S(2)}) %collective-permute-start.25) | collective-permute-done | bytes 393248 | tf_op jit(solution)/shard_map/ppermute | solution.py:96
  152.0 4.4 %collective-permute-done.24.other_ref = bf16[256,768]{1,0:T(8,128)(2,1)S(1)} collective-permute-done((bf16[256,768]{1,0:T(8,128)(2,1)S(1)}, bf16[256,768]{1,0:T(8,128)(2,1)S(1)}, u32[]{:S(2)}, u32[]{:S(2)}) %collective-permute-start.24) | collective-permute-done | bytes 393248 | tf_op jit(solution)/shard_map/ppermute | solution.py:96
  160.5 4.3 %collective-permute-done.26.other_ref = bf16[256,768]{1,0:T(8,128)(2,1)S(1)} collective-permute-done((bf16[256,768]{1,0:T(8,128)(2,1)S(1)}, bf16[256,768]{1,0:T(8,128)(2,1)S(1)}, u32[]{:S(2)}, u32[]{:S(2)}) %collective-permute-start.26) | collective-permute-done | bytes 393248 | tf_op jit(solution)/shard_map/ppermute | solution.py:96
  167.4 3.7 %shard_map.266 = (bf16[2,4,48,3072]{3,2,1,0:T(8,128)(2,1)S(1)}, bf16[2,4,48,3072]{3,2,1,0:T(8,128)(2,1)S(1)}) custom-call(bf16[256,768]{1,0:T(8,128)(2,1)S(1)} %get-tuple-element.211.refs_0_, bf16[256,768]{1,0:T(8,128)(2,1)S(1)} %get-tuple-element.213.refs_1_, bf16[256,1536]{1,0:T(8,128)(2,1)S(1)} %get-tuple-element.214.refs_2_, ...), custom_call_target="tpu_custom_call" | custom-call | flops 38654705664 | bytes 150994944 | tf_op jit(solution)/shard_map/pallas_call | solution.py:607
  172.9 3.4 %shard_map.267 = (bf16[256,768]{1,0:T(8,128)(2,1)S(1)}, f32[256,768]{1,0:T(8,128)S(1)}, bf16[256,768]{1,0:T(8,128)(2,1)S(1)}, bf16[256,1152]{1,0:T(8,128)(2,1)S(1)}, f32[8,768]{1,0:T(8,128)S(1)}) custom-call(f32[256,768]{1,0:T(8,128)S(1)} %get-tuple-element.224.res_ref, bf16[256,768]{1,0:T(8,128)(2,1)S(1)} %get-tuple-element.225.own_ref, ...), custom_call_target="tpu_custom_call" | custom-call | flops 25769803776 | bytes 150994944 | tf_op jit(solution)/shard_map/pallas_call | solution.py:517
  179.2 4.0 %collective-permute-done.29.other_ref = bf16[256,768]{1,0:T(8,128)(2,1)S(1)} collective-permute-done((bf16[256,768]{1,0:T(8,128)(2,1)S(1)}, bf16[256,768]{1,0:T(8,128)(2,1)S(1)}, u32[]{:S(2)}, u32[]{:S(2)}) %collective-permute-start.29) | collective-permute-done | bytes 393248 | tf_op jit(solution)/shard_map/ppermute | solution.py:96
  183.3 3.0 shard_map.268
  202.6 3.7 %shard_map.272 = (bf16[2,4,48,3072]{3,2,1,0:T(8,128)(2,1)S(1)}, bf16[2,4,48,3072]{3,2,1,0:T(8,128)(2,1)S(1)}) custom-call(bf16[2,256,768]{2,1,0:T(8,128)(2,1)S(1)} %get-tuple-element.195.refs_0_.refs_1_, bf16[2,256,768]{2,1,0:T(8,128)(2,1)S(1)} %get-tuple-element.195.refs_0_.refs_1_, bf16[256,1536]{1,0:T(8,128)(2,1)S(1)} %get-tuple-element.247.refs_2_, ...), custom_call_target="tpu_custom_call" | custom-call | flops 38654705664 | bytes 188743680 | tf_op jit(solution)/shard_map/pallas_call | solution.py:607
  208.0 4.0 %collective-permute-done.36 = bf16[2,48,3072]{2,1,0:T(8,128)(2,1)S(1)} collective-permute-done((bf16[2,48,3072]{2,1,0:T(8,128)(2,1)S(1)}, bf16[2,48,3072]{2,1,0:T(8,128)(2,1)S(1)}, u32[]{:S(2)}, u32[]{:S(2)}) %collective-permute-start.36) | collective-permute-done | bytes 589856 | tf_op jit(solution)/shard_map/ppermute | solution.py:92
  215.5 4.3 %collective-permute-start.48 = (bf16[48,1536]{1,0:T(8,128)(2,1)S(1)}, bf16[48,1536]{1,0:T(8,128)(2,1)S(1)}, u32[]{:S(2)}, u32[]{:S(2)}) collective-permute-start(bf16[48,1536]{1,0:T(8,128)(2,1)S(1)} %get-tuple-element.379), channel_id=1, source_target_pairs={{0,16},{2,18},{4,20},{6,22},{8,24},{10,26},{12,28},{14,30},{16,0},... | collective-permute-start | bytes 442376 | tf_op jit(solution)/shard_map/ppermute | solution.py:92
  227.6 5.2 %collective-permute-done.44 = bf16[2,48,3072]{2,1,0:T(8,128)(2,1)S(1)} collective-permute-done((bf16[2,48,3072]{2,1,0:T(8,128)(2,1)S(1)}, bf16[2,48,3072]{2,1,0:T(8,128)(2,1)S(1)}, u32[]{:S(2)}, u32[]{:S(2)}) %collective-permute-start.44) | collective-permute-done | bytes 589856 | tf_op jit(solution)/shard_map/ppermute | solution.py:92
  246.4 12.4 %collective-permute-done.46.refs_2_ = bf16[48,3072]{1,0:T(8,128)(2,1)S(1)} collective-permute-done((bf16[48,3072]{1,0:T(8,128)(2,1)S(1)}, bf16[48,3072]{1,0:T(8,128)(2,1)S(1)}, u32[]{:S(2)}, u32[]{:S(2)}) %collective-permute-start.46) | collective-permute-done | bytes 294944 | tf_op jit(solution)/shard_map/ppermute | solution.py:92
  269.9 4.1 %collective-permute-done.35.refs_0_ = bf16[2,48,3072]{2,1,0:T(8,128)(2,1)S(1)} collective-permute-done((bf16[2,48,3072]{2,1,0:T(8,128)(2,1)S(1)}, bf16[2,48,3072]{2,1,0:T(8,128)(2,1)S(1)}, u32[]{:S(2)}, u32[]{:S(2)}) %collective-permute-start.35) | collective-permute-done | bytes 589856 | tf_op jit(solution)/shard_map/ppermute | solution.py:92
  274.6 3.2 %collective-permute-start.55 = (bf16[48,3072]{1,0:T(8,128)(2,1)S(1)}, bf16[48,3072]{1,0:T(8,128)(2,1)S(1)}, u32[]{:S(2)}, u32[]{:S(2)}) collective-permute-start(bf16[48,3072]{1,0:T(8,128)(2,1)S(1)} %fusion.12), channel_id=1, source_target_pairs={{0,8},{2,10},{4,12},{6,14},{8,16},{10,18},{12,20},{14,22},{16,24},... | collective-permute-start | bytes 884744 | tf_op jit(solution)/shard_map/ppermute | solution.py:92
  278.0 6.1 %collective-permute-done.55.refs_1_ = bf16[48,3072]{1,0:T(8,128)(2,1)S(1)} collective-permute-done((bf16[48,3072]{1,0:T(8,128)(2,1)S(1)}, bf16[48,3072]{1,0:T(8,128)(2,1)S(1)}, u32[]{:S(2)}, u32[]{:S(2)}) %collective-permute-start.55) | collective-permute-done | bytes 294944 | tf_op jit(solution)/shard_map/ppermute | solution.py:92
  294.0 3.4 %collective-permute-start.62 = (f32[8,128]{1,0:T(8,128)S(1)}, f32[8,128]{1,0:T(8,128)S(1)}, u32[]{:S(2)}, u32[]{:S(2)}) collective-permute-start(f32[8,128]{1,0:T(8,128)S(1)} %add_add_fusion.1), channel_id=1, source_target_pairs={{0,24},{1,25},{2,26},{3,27},{4,28},{5,29},{6,30},{7,31},{8,16},{9,... | collective-permute-start | bytes 12296 | tf_op jit(solution)/shard_map/ppermute | solution.py:839
  299.4 6.0 %shard_map.283 = (f32[2,1728,128]{2,1,0:T(8,128)}, f32[2,1728,128]{2,1,0:T(8,128)}, f32[2,1728,128]{2,1,0:T(8,128)}, bf16[2,1728,128]{2,1,0:T(8,128)(2,1)S(1)}) custom-call(f32[8,128]{1,0:T(8,128)S(1)} %add_add_fusion.q_ref.f_ref, f32[2,1728,128]{2,1,0:T(8,128)S(1)} %get-tuple-element.319.w_ref, f32[2,1728,128]{2,1,0:T(8,128)S(1)} %get-tuple-element.320.m_ref, ...), custom_call_target="tpu_custom_call" | custom-call | flops 8847360 | bytes 13271040 | tf_op jit(solution)/shard_map/pallas_call | solution.py:802
  (197 shorter events, 133.0 us)
Async XLA Ops:
  3.8 33.2 %collective-permute-start.3 = (bf16[48,9344]{1,0:T(8,128)(2,1)S(1)}, bf16[48,9344]{1,0:T(8,128)(2,1)S(1)}, u32[]{:S(2)}, u32[]{:S(2)}) collective-permute-start(bf16[48,9344]{1,0:T(8,128)(2,1)S(1)} %get-tuple-element.182), channel_id=1, source_target_pairs={{0,4},{2,6},{4,0},{6,2},{8,12},{10,14},{12,8},{14,10},{16,20},{18,... | collective-permute-start | bytes 2691080 | tf_op jit(solution)/shard_map/ppermute | solution.py:92
  21.2 15.8 %collective-permute-start.4 = (bf16[3,48,1664]{2,1,0:T(8,128)(2,1)S(1)}, bf16[3,48,1664]{2,1,0:T(8,128)(2,1)S(1)}, u32[]{:S(2)}, u32[]{:S(2)}) collective-permute-start(bf16[3,48,1664]{2,1,0:T(8,128)(2,1)S(1)} %shard_map.244), channel_id=1, source_target_pairs={{0,4},{2,6},{4,0},{6,2},{8,12},{10,14},{12,8},{14,10},{16,20},{18,... | collective-permute-start | bytes 1437704 | tf_op jit(solution)/shard_map/ppermute | solution.py:92
  21.8 15.3 %collective-permute-start.5 = (bf16[48,3072]{1,0:T(8,128)(2,1)S(1)}, bf16[48,3072]{1,0:T(8,128)(2,1)S(1)}, u32[]{:S(2)}, u32[]{:S(2)}) collective-permute-start(bf16[48,3072]{1,0:T(8,128)(2,1)S(1)} %get-tuple-element.183.refs_0_), channel_id=1, source_target_pairs={{0,8},{2,10},{4,12},{6,14},{8,16},{10,18},{12,20},{14,22},{16,24},... | collective-permute-start | bytes 884744 | tf_op jit(solution)/shard_map/ppermute | solution.py:92
  48.0 31.4 %collective-permute-start.13 = (bf16[2,256,768]{2,1,0:T(8,128)(2,1)S(1)}, bf16[2,256,768]{2,1,0:T(8,128)(2,1)S(1)}, u32[]{:S(2)}, u32[]{:S(2)}) collective-permute-start(bf16[2,256,768]{2,1,0:T(8,128)(2,1)S(1)} %get-tuple-element.187.own_ref), channel_id=1, source_target_pairs={{0,1},{1,0},{2,3},{3,2},{4,5},{5,4},{6,7},{7,6},{8,9},{9,8},{10,11... | collective-permute-start | bytes 2359304 | tf_op jit(solution)/shard_map/ppermute | solution.py:96
  50.1 29.2 %collective-permute-start.8 = (bf16[2,48,3072]{2,1,0:T(8,128)(2,1)S(1)}, bf16[2,48,3072]{2,1,0:T(8,128)(2,1)S(1)}, u32[]{:S(2)}, u32[]{:S(2)}) collective-permute-start(bf16[2,48,3072]{2,1,0:T(8,128)(2,1)S(1)} %shard_map.249), channel_id=1, source_target_pairs={{0,4},{2,6},{4,0},{6,2},{8,12},{10,14},{12,8},{14,10},{16,20},{18,... | collective-permute-start | bytes 1769480 | tf_op jit(solution)/shard_map/ppermute | solution.py:92
  51.7 19.0 %collective-permute-start.11 = (bf16[48,4608]{1,0:T(8,128)(2,1)S(1)}, bf16[48,4608]{1,0:T(8,128)(2,1)S(1)}, u32[]{:S(2)}, u32[]{:S(2)}) collective-permute-start(bf16[48,4608]{1,0:T(8,128)(2,1)S(1)} %get-tuple-element.190.refs_0_), channel_id=1, source_target_pairs={{0,8},{2,10},{4,12},{6,14},{8,16},{10,18},{12,20},{14,22},{16,24},... | collective-permute-start | bytes 1327112 | tf_op jit(solution)/shard_map/ppermute | solution.py:92
  53.1 26.3 %collective-permute-start.12 = (bf16[48,4608]{1,0:T(8,128)(2,1)S(1)}, bf16[48,4608]{1,0:T(8,128)(2,1)S(1)}, u32[]{:S(2)}, u32[]{:S(2)}) collective-permute-start(bf16[48,4608]{1,0:T(8,128)(2,1)S(1)} %get-tuple-element.190.refs_0_), channel_id=1, source_target_pairs={{0,24},{2,26},{4,28},{6,30},{8,0},{10,2},{12,4},{14,6},{16,8},{18,... | collective-permute-start | bytes 1327112 | tf_op jit(solution)/shard_map/ppermute | solution.py:92
  61.4 18.0 %collective-permute-start.10 = (bf16[48,3072]{1,0:T(8,128)(2,1)S(1)}, bf16[48,3072]{1,0:T(8,128)(2,1)S(1)}, u32[]{:S(2)}, u32[]{:S(2)}) collective-permute-start(bf16[48,3072]{1,0:T(8,128)(2,1)S(1)} %collective-permute-done.9.refs_2_), channel_id=1, source_target_pairs={{0,4},{2,6},{4,0},{6,2},{8,12},{10,14},{12,8},{14,10},{16,20},{18,... | collective-permute-start | bytes 884744 | tf_op jit(solution)/shard_map/ppermute | solution.py:92
  79.6 14.5 %collective-permute-start.16 = (bf16[48,4608]{1,0:T(8,128)(2,1)S(1)}, bf16[48,4608]{1,0:T(8,128)(2,1)S(1)}, u32[]{:S(2)}, u32[]{:S(2)}) collective-permute-start(bf16[48,4608]{1,0:T(8,128)(2,1)S(1)} %collective-permute-done.11.refs_0_.refs_1_), channel_id=1, source_target_pairs={{0,8},{2,10},{4,12},{6,14},{8,16},{10,18},{12,20},{14,22},{16,24},... | collective-permute-start | bytes 1327112 | tf_op jit(solution)/shard_map/ppermute | solution.py:92
  99.7 22.7 %collective-permute-start.20 = (bf16[2,4,48,1536]{3,2,1,0:T(8,128)(2,1)S(1)}, bf16[2,4,48,1536]{3,2,1,0:T(8,128)(2,1)S(1)}, u32[]{:S(2)}, u32[]{:S(2)}) collective-permute-start(bf16[2,4,48,1536]{3,2,1,0:T(8,128)(2,1)S(1)} %shard_map.256.mine_ref), channel_id=1, source_target_pairs={{0,2},{2,0},{4,6},{6,4},{8,10},{10,8},{12,14},{14,12},{16,18},{18,... | collective-permute-start | bytes 3538952 | tf_op jit(solution)/shard_map/ppermute | solution.py:92
  99.8 20.0 %collective-permute-start.18 = (bf16[2,256,768]{2,1,0:T(8,128)(2,1)S(1)}, bf16[2,256,768]{2,1,0:T(8,128)(2,1)S(1)}, u32[]{:S(2)}, u32[]{:S(2)}) collective-permute-start(bf16[2,256,768]{2,1,0:T(8,128)(2,1)S(1)} %get-tuple-element.200.own_ref), channel_id=1, source_target_pairs={{0,1},{1,0},{2,3},{3,2},{4,5},{5,4},{6,7},{7,6},{8,9},{9,8},{10,11... | collective-permute-start | bytes 2359304 | tf_op jit(solution)/shard_map/ppermute | solution.py:96
  100.4 16.2 %collective-permute-start.17 = (bf16[2,48,3072]{2,1,0:T(8,128)(2,1)S(1)}, bf16[2,48,3072]{2,1,0:T(8,128)(2,1)S(1)}, u32[]{:S(2)}, u32[]{:S(2)}) collective-permute-start(bf16[2,48,3072]{2,1,0:T(8,128)(2,1)S(1)} %shard_map.254), channel_id=1, source_target_pairs={{0,4},{2,6},{4,0},{6,2},{8,12},{10,14},{12,8},{14,10},{16,20},{18,... | collective-permute-start | bytes 1769480 | tf_op jit(solution)/shard_map/ppermute | solution.py:92
  102.0 20.2 %collective-permute-start.22 = (bf16[1,48,3072]{2,1,0:T(8,128)(2,1)S(1)}, bf16[1,48,3072]{2,1,0:T(8,128)(2,1)S(1)}, u32[]{:S(2)}, u32[]{:S(2)}) collective-permute-start(bf16[1,48,3072]{2,1,0:T(8,128)(2,1)S(1)} %shard_map.259), channel_id=1, source_target_pairs={{0,4},{2,6},{4,0},{6,2},{8,12},{10,14},{12,8},{14,10},{16,20},{18,... | collective-permute-start | bytes 884744 | tf_op jit(solution)/shard_map/ppermute | solution.py:92
  129.2 18.8 %collective-permute-start.25 = (bf16[256,768]{1,0:T(8,128)(2,1)S(1)}, bf16[256,768]{1,0:T(8,128)(2,1)S(1)}, u32[]{:S(2)}, u32[]{:S(2)}) collective-permute-start(bf16[256,768]{1,0:T(8,128)(2,1)S(1)} %get-tuple-element.212.own_ref), channel_id=1, source_target_pairs={{0,1},{1,0},{2,3},{3,2},{4,5},{5,4},{6,7},{7,6},{8,9},{9,8},{10,11... | collective-permute-start | bytes 1179656 | tf_op jit(solution)/shard_map/ppermute | solution.py:96
  142.3 14.2 %collective-permute-start.24 = (bf16[256,768]{1,0:T(8,128)(2,1)S(1)}, bf16[256,768]{1,0:T(8,128)(2,1)S(1)}, u32[]{:S(2)}, u32[]{:S(2)}) collective-permute-start(bf16[256,768]{1,0:T(8,128)(2,1)S(1)} %get-tuple-element.208.own_ref), channel_id=1, source_target_pairs={{0,1},{1,0},{2,3},{3,2},{4,5},{5,4},{6,7},{7,6},{8,9},{9,8},{10,11... | collective-permute-start | bytes 1179656 | tf_op jit(solution)/shard_map/ppermute | solution.py:96
  150.5 14.4 %collective-permute-start.26 = (bf16[256,768]{1,0:T(8,128)(2,1)S(1)}, bf16[256,768]{1,0:T(8,128)(2,1)S(1)}, u32[]{:S(2)}, u32[]{:S(2)}) collective-permute-start(bf16[256,768]{1,0:T(8,128)(2,1)S(1)} %get-tuple-element.216.own_ref), channel_id=1, source_target_pairs={{0,1},{1,0},{2,3},{3,2},{4,5},{5,4},{6,7},{7,6},{8,9},{9,8},{10,11... | collective-permute-start | bytes 1179656 | tf_op jit(solution)/shard_map/ppermute | solution.py:96
  176.3 14.9 %collective-permute-start.30 = (bf16[256,768]{1,0:T(8,128)(2,1)S(1)}, bf16[256,768]{1,0:T(8,128)(2,1)S(1)}, u32[]{:S(2)}, u32[]{:S(2)}) collective-permute-start(bf16[256,768]{1,0:T(8,128)(2,1)S(1)} %get-tuple-element.235.own_ref), channel_id=1, source_target_pairs={{0,1},{1,0},{2,3},{3,2},{4,5},{5,4},{6,7},{7,6},{8,9},{9,8},{10,11... | collective-permute-start | bytes 1179656 | tf_op jit(solution)/shard_map/ppermute | solution.py:96
  179.2 16.5 %collective-permute-start.31 = (bf16[2,48,3072]{2,1,0:T(8,128)(2,1)S(1)}, bf16[2,48,3072]{2,1,0:T(8,128)(2,1)S(1)}, u32[]{:S(2)}, u32[]{:S(2)}) collective-permute-start(bf16[2,48,3072]{2,1,0:T(8,128)(2,1)S(1)} %get-tuple-element.373), channel_id=1, source_target_pairs={{0,8},{2,10},{4,12},{6,14},{8,16},{10,18},{12,20},{14,22},{16,24},... | collective-permute-start | bytes 1769480 | tf_op jit(solution)/shard_map/ppermute | solution.py:92
  193.5 18.7 %collective-permute-start.40 = (bf16[256,768]{1,0:T(8,128)(2,1)S(1)}, bf16[256,768]{1,0:T(8,128)(2,1)S(1)}, u32[]{:S(2)}, u32[]{:S(2)}) collective-permute-start(bf16[256,768]{1,0:T(8,128)(2,1)S(1)} %get-tuple-element.249.own_ref), channel_id=1, source_target_pairs={{0,1},{1,0},{2,3},{3,2},{4,5},{5,4},{6,7},{7,6},{8,9},{9,8},{10,11... | collective-permute-start | bytes 1179656 | tf_op jit(solution)/shard_map/ppermute | solution.py:96
  195.9 16.0 %collective-permute-start.36 = (bf16[2,48,3072]{2,1,0:T(8,128)(2,1)S(1)}, bf16[2,48,3072]{2,1,0:T(8,128)(2,1)S(1)}, u32[]{:S(2)}, u32[]{:S(2)}) collective-permute-start(bf16[2,48,3072]{2,1,0:T(8,128)(2,1)S(1)} %fusion.2), channel_id=1, source_target_pairs={{0,8},{2,10},{4,12},{6,14},{8,16},{10,18},{12,20},{14,22},{16,24},... | collective-permute-start | bytes 1769480 | tf_op jit(solution)/shard_map/ppermute | solution.py:92
  196.3 18.9 %collective-permute-start.39 = (bf16[4,48,1536]{2,1,0:T(8,128)(2,1)S(1)}, bf16[4,48,1536]{2,1,0:T(8,128)(2,1)S(1)}, u32[]{:S(2)}, u32[]{:S(2)}) collective-permute-start(bf16[4,48,1536]{2,1,0:T(8,128)(2,1)S(1)} %fusion.7), channel_id=1, source_target_pairs={{0,4},{2,6},{4,0},{6,2},{8,12},{10,14},{12,8},{14,10},{16,20},{18,... | collective-permute-start | bytes 1769480 | tf_op jit(solution)/shard_map/ppermute | solution.py:92
  206.4 14.1 %collective-permute-start.41 = (bf16[256,768]{1,0:T(8,128)(2,1)S(1)}, bf16[256,768]{1,0:T(8,128)(2,1)S(1)}, u32[]{:S(2)}, u32[]{:S(2)}) collective-permute-start(bf16[256,768]{1,0:T(8,128)(2,1)S(1)} %get-tuple-element.261.own_ref), channel_id=1, source_target_pairs={{0,1},{1,0},{2,3},{3,2},{4,5},{5,4},{6,7},{7,6},{8,9},{9,8},{10,11... | collective-permute-start | bytes 1179656 | tf_op jit(solution)/shard_map/ppermute | solution.py:96
  212.2 25.2 %collective-permute-start.37 = (bf16[2,48,3072]{2,1,0:T(8,128)(2,1)S(1)}, bf16[2,48,3072]{2,1,0:T(8,128)(2,1)S(1)}, u32[]{:S(2)}, u32[]{:S(2)}) collective-permute-start(bf16[2,48,3072]{2,1,0:T(8,128)(2,1)S(1)} %fusion.1), channel_id=1, source_target_pairs={{0,8},{2,10},{4,12},{6,14},{8,16},{10,18},{12,20},{14,22},{16,24},... | collective-permute-start | bytes 1769480 | tf_op jit(solution)/shard_map/ppermute | solution.py:92
  215.5 23.7 %collective-permute-start.47 = (bf16[48,1536]{1,0:T(8,128)(2,1)S(1)}, bf16[48,1536]{1,0:T(8,128)(2,1)S(1)}, u32[]{:S(2)}, u32[]{:S(2)}) collective-permute-start(bf16[48,1536]{1,0:T(8,128)(2,1)S(1)} %get-tuple-element.380), channel_id=1, source_target_pairs={{0,8},{2,10},{4,12},{6,14},{8,16},{10,18},{12,20},{14,22},{16,24},... | collective-permute-start | bytes 442376 | tf_op jit(solution)/shard_map/ppermute | solution.py:92
  215.5 25.3 %collective-permute-start.48 = (bf16[48,1536]{1,0:T(8,128)(2,1)S(1)}, bf16[48,1536]{1,0:T(8,128)(2,1)S(1)}, u32[]{:S(2)}, u32[]{:S(2)}) collective-permute-start(bf16[48,1536]{1,0:T(8,128)(2,1)S(1)} %get-tuple-element.379), channel_id=1, source_target_pairs={{0,16},{2,18},{4,20},{6,22},{8,24},{10,26},{12,28},{14,30},{16,0},... | collective-permute-start | bytes 442376 | tf_op jit(solution)/shard_map/ppermute | solution.py:92
  219.9 22.4 %collective-permute-start.49 = (bf16[48,1536]{1,0:T(8,128)(2,1)S(1)}, bf16[48,1536]{1,0:T(8,128)(2,1)S(1)}, u32[]{:S(2)}, u32[]{:S(2)}) collective-permute-start(bf16[48,1536]{1,0:T(8,128)(2,1)S(1)} %get-tuple-element.381), channel_id=1, source_target_pairs={{0,24},{2,26},{4,28},{6,30},{8,0},{10,2},{12,4},{14,6},{16,8},{18,... | collective-permute-start | bytes 442376 | tf_op jit(solution)/shard_map/ppermute | solution.py:92
  237.4 21.3 %collective-permute-start.46 = (bf16[48,3072]{1,0:T(8,128)(2,1)S(1)}, bf16[48,3072]{1,0:T(8,128)(2,1)S(1)}, u32[]{:S(2)}, u32[]{:S(2)}) collective-permute-start(bf16[48,3072]{1,0:T(8,128)(2,1)S(1)} %get-tuple-element.374), channel_id=1, source_target_pairs={{0,16},{2,18},{4,20},{6,22},{8,24},{10,26},{12,28},{14,30},{16,0},... | collective-permute-start | bytes 884744 | tf_op jit(solution)/shard_map/ppermute | solution.py:92
  239.2 21.0 %collective-permute-start.43 = (bf16[4,48,1664]{2,1,0:T(8,128)(2,1)S(1)}, bf16[4,48,1664]{2,1,0:T(8,128)(2,1)S(1)}, u32[]{:S(2)}, u32[]{:S(2)}) collective-permute-start(bf16[4,48,1664]{2,1,0:T(8,128)(2,1)S(1)} %fusion.5), channel_id=1, source_target_pairs={{0,4},{2,6},{4,0},{6,2},{8,12},{10,14},{12,8},{14,10},{16,20},{18,... | collective-permute-start | bytes 1916936 | tf_op jit(solution)/shard_map/ppermute | solution.py:92
  240.8 19.7 %collective-permute-start.50 = (bf16[256,768]{1,0:T(8,128)(2,1)S(1)}, bf16[256,768]{1,0:T(8,128)(2,1)S(1)}, u32[]{:S(2)}, u32[]{:S(2)}) collective-permute-start(bf16[256,768]{1,0:T(8,128)(2,1)S(1)} %get-tuple-element.272.refs_1_), channel_id=1, source_target_pairs={{0,1},{1,0},{2,3},{3,2},{4,5},{5,4},{6,7},{7,6},{8,9},{9,8},{10,11... | collective-permute-start | bytes 1179656 | tf_op jit(solution)/shard_map/ppermute | solution.py:96
  242.3 20.8 %collective-permute-start.38 = (bf16[48,3072]{1,0:T(8,128)(2,1)S(1)}, bf16[48,3072]{1,0:T(8,128)(2,1)S(1)}, u32[]{:S(2)}, u32[]{:S(2)}) collective-permute-start(bf16[48,3072]{1,0:T(8,128)(2,1)S(1)} %fusion.13), channel_id=1, source_target_pairs={{0,4},{2,6},{4,0},{6,2},{8,12},{10,14},{12,8},{14,10},{16,20},{18,... | collective-permute-start | bytes 884744 | tf_op jit(solution)/shard_map/ppermute | solution.py:92
  244.8 23.6 %collective-permute-start.51 = (bf16[256,768]{1,0:T(8,128)(2,1)S(1)}, bf16[256,768]{1,0:T(8,128)(2,1)S(1)}, u32[]{:S(2)}, u32[]{:S(2)}) collective-permute-start(bf16[256,768]{1,0:T(8,128)(2,1)S(1)} %get-tuple-element.297.refs_4_), channel_id=1, source_target_pairs={{0,1},{1,0},{2,3},{3,2},{4,5},{5,4},{6,7},{7,6},{8,9},{9,8},{10,11... | collective-permute-start | bytes 1179656 | tf_op jit(solution)/shard_map/ppermute | solution.py:96
  258.7 15.3 %collective-permute-start.35 = (bf16[2,48,3072]{2,1,0:T(8,128)(2,1)S(1)}, bf16[2,48,3072]{2,1,0:T(8,128)(2,1)S(1)}, u32[]{:S(2)}, u32[]{:S(2)}) collective-permute-start(bf16[2,48,3072]{2,1,0:T(8,128)(2,1)S(1)} %get-tuple-element.371), channel_id=1, source_target_pairs={{0,4},{2,6},{4,0},{6,2},{8,12},{10,14},{12,8},{14,10},{16,20},{18,... | collective-permute-start | bytes 1769480 | tf_op jit(solution)/shard_map/ppermute | solution.py:92
  (48 other events, 335.7 us)

commit v4 on v3

--- a/solution.py
+++ b/solution.py
@@ -30,12 +30,11 @@
 contract_first = (((0,), (0,)), ((), ()))
 f32 = jnp.float32
 b16 = jnp.bfloat16
-VMEM_LIMIT = 13 * 1024 * 1024
 VM = pl.BlockSpec(memory_space=pltpu.VMEM)
 
 
 def call(body, outs, in_specs, scratch=(), flops=0, moved=0, out_specs=None, trans=0, limit=13):
-    weight = 16 if scratch else 16 if flops else 1
+    weight = 16 if flops else 1
     if out_specs is None:
         out_specs = [VM] * len(outs)
     return pl.pallas_call(
@@ -130,23 +129,22 @@
 
 
 def settle(mine, met):
-    _, ring, rows, cols = mine.shape
-
-    def body(mine_ref, met_ref, out_ref):
+    ring, rows, cols = mine[0].shape
+
+    def body(*refs):
         z, x, c = places(ring)
         for other in range(2):
-            source = (mine_ref, met_ref)[other]
             for xo in range(2):
                 for k in range(ring):
                     zz = lax.rem(z - k + ring, ring)
                     xx = lax.rem(x + xo, 2)
                     cc = lax.rem(c + other, 2)
                     row = pl.multiple_of(((zz * 2 + xx) * 2 + cc) * rows, 16)
-                    out_ref[pl.ds(row, rows), :] = source[xo, k]
-
-    return call(
-        body, [((4 * ring * rows, cols), b16)], [VM] * 2, moved=16 * ring * rows * cols
-    )(mine, met)[0]
+                    refs[4][pl.ds(row, rows), :] = refs[2 * other + xo][k]
+
+    return call(
+        body, [((4 * ring * rows, cols), b16)], [VM] * 4, moved=16 * ring * rows * cols
+    )(*mine, *met)[0]
 
 
 def prep(weights_tiled, rep, split):
@@ -295,31 +293,30 @@
     )(block_in, segments, split, matrix)
 
 
-def attention_next(layer, normed, part_own, part_other, rep, segments, split, matrix):
+def attention_next(micro, layer, normed, part_own, part_other, rep, segments, split, matrix):
     base = 6 * (layer - 1)
 
     def body(n_ref, own_ref, other_ref, rep_ref, seg_ref, split_ref, w_ref, *refs):
-        parts, (qkv_ref, probs_ref, ctx_ref, n2_ref, s2_ref, low_ref) = refs[:MICRO], refs[MICRO:]
-        for m in range(MICRO):
-            first = n_ref[m] * rep_ref[base + 1 : base + 2] + rep_ref[base + 2 : base + 3]
-            added = own_ref[m].astype(f32) + other_ref[m].astype(f32)
-            n2, s2 = norm_rows(first + added + rep_ref[base + 3 : base + 4])
-            n2_ref[m] = n2
-            s2_ref[m] = s2
-            low = (n2 * rep_ref[base + 4 : base + 5] + rep_ref[base + 5 : base + 6]).astype(b16)
-            low_ref[m] = low
-            views = [r.at[m] for r in (qkv_ref, probs_ref, ctx_ref)]
-            attend(low, layer, w_ref, split_ref, seg_ref[m], parts[m], *views)
-
-    return call(
-        body,
-        [((SEQ, D), b16)] * MICRO
-        + ATT_OUTS
-        + [((MICRO, SEQ, D), f32), ((MICRO, SEQ, 1), f32), ((MICRO, SEQ, D), b16)],
+        part_ref, qkv_ref, probs_ref, ctx_ref, n2_ref, s2_ref, low_ref = refs
+        first = n_ref[micro] * rep_ref[base + 1 : base + 2] + rep_ref[base + 2 : base + 3]
+        added = own_ref[...].astype(f32) + other_ref[...].astype(f32)
+        n2, s2 = norm_rows(first + added + rep_ref[base + 3 : base + 4])
+        n2_ref[...] = n2
+        s2_ref[...] = s2
+        low = (n2 * rep_ref[base + 4 : base + 5] + rep_ref[base + 5 : base + 6]).astype(b16)
+        low_ref[...] = low
+        attend(
+            low, layer, w_ref, split_ref, seg_ref[micro], part_ref, qkv_ref, probs_ref, ctx_ref
+        )
+
+    return call(
+        body,
+        [((SEQ, D), b16)]
+        + [(shape[1:], kind) for shape, kind in ATT_OUTS]
+        + [((SEQ, D), f32), ((SEQ, 1), f32), ((SEQ, D), b16)],
         [VM] * 7,
-        flops=2 * ATT_FLOPS,
-        moved=16 << 20,
-        limit=22,
+        flops=ATT_FLOPS,
+        moved=8 << 20,
     )(normed, part_own, part_other, rep, segments, split, matrix)
 
 
@@ -353,15 +350,16 @@
 
 
 def feed_first(hidden, part_own, part_other, rep, split, matrix):
-    def body(h_ref, own_ref, other_ref, rep_ref, split_ref, w_ref, *outs):
+    def body(h_ref, own_ref, other_ref, rep_ref, split_ref, w_ref, *refs):
+        parts, outs = refs[:MICRO], refs[MICRO:]
         for m in range(MICRO):
             added = own_ref[m].astype(f32) + other_ref[m].astype(f32)
-            views = [r.at[m] for r in outs]
+            views = [parts[m]] + [r.at[m] for r in outs]
             feed_step(h_ref[m].astype(f32), added, 0, rep_ref, split_ref, w_ref, views)
 
     return call(
         body,
-        [((MICRO,) + shape, kind) for shape, kind in FEED_OUTS],
+        [((SEQ, D), b16)] * MICRO + [((MICRO,) + shape, kind) for shape, kind in FEED_OUTS[1:]],
         [VM] * 6,
         flops=2 * FFN_FLOPS,
         moved=20 << 20,
@@ -373,7 +371,7 @@
     base = 6 * layer
 
     def body(h_ref, own_ref, other_ref, rep_ref, split_ref, w_ref, *outs):
-        hidden_in = h_ref[micro] * rep_ref[base - 2 : base - 1] + rep_ref[base - 1 : base]
+        hidden_in = h_ref[...] * rep_ref[base - 2 : base - 1] + rep_ref[base - 1 : base]
         added = own_ref[...].astype(f32) + other_ref[...].astype(f32)
         feed_step(hidden_in, added, layer, rep_ref, split_ref, w_ref, outs)
 
@@ -806,7 +804,7 @@
         in_specs=[pl.BlockSpec((8, LANES), lambda l, i: (0, 0)), big, big, big]
         + [pl.BlockSpec((step, g.shape[1]), lambda l, i: (i, 0)) for g in grads],
         out_specs=[big] * 4,
-        compiler_params=pltpu.CompilerParams(vmem_limit_bytes=VMEM_LIMIT),
+        compiler_params=pltpu.CompilerParams(vmem_limit_bytes=13 * 1024 * 1024),
         cost_estimate=pl.CostEstimate(
             flops=20 * tiled.size, bytes_accessed=30 * tiled.size, transcendentals=tiled.size
         ),
@@ -872,8 +870,8 @@
         fourth = slice(COLS + LANES + ATT, None)
 
         def finish(slots, cols):
-            mine = stack(slots, rows, cols, (2, 4))
-            return settle(mine, move(mine, "core"))
+            mine = [stack(half, rows, cols) for half in (slots[:4], slots[4:])]
+            return settle(mine, [move(a, "core") for a in mine])
 
         def cut(array, cols):
             return (array, (slice(None), cols))
@@ -882,14 +880,12 @@
         a0_r1, a0_r2, a0_r3, f0 = tie(move(a0, 1), move(a0, 2), move(a0, 3), f0)
         a0_x = across(stack([a0_r1, a0_r2, a0_r3], rows, ATT + LANES))
         f0_r1, f0_r3 = move(f0, 1), move(f0, 3)
+        near = stack([a0, a0_r1, a0_r2, a0_r3], rows, ATT + LANES)
         mine0 = stack(
-            [a0, a0_r1, a0_r2, a0_r3, cut(x0, slice(0, ATT + LANES)), (a0_x, 0), (a0_x, 1), (a0_x, 2)],
-            rows,
-            ATT + LANES,
-            (2, 4),
+            [cut(x0, slice(0, ATT + LANES)), (a0_x, 0), (a0_x, 1), (a0_x, 2)], rows, ATT + LANES
         )
         mine0, f0_r1, f0_r3, l1 = tie(mine0, f0_r1, f0_r3, l1)
-        watt0 = settle(mine0, move(mine0, "core"))
+        watt0 = settle([near, mine0], [move(near, "core"), move(mine0, "core")])
         f0_x13 = across(stack([f0_r1, f0_r3], rows, 2 * FFT))
         f0_r2 = move(f0_r1, 1)
         l1_r1, l1_r3 = move(l1, 1), move(l1, 3)
@@ -913,39 +909,39 @@
     done, qkv0, probs0, ctx0 = attention_first(block_in, seg, split, watt0)
     met = exchange(done)
     if pieced:
-        f0_x13, f0_x2, l1_r1, l1_r3, met = tie(f0_x13, f0_x2, l1_r1, l1_r3, met)
-        a1_x13 = across(stack([cut(l1_r1, slice(0, ATT)), cut(l1_r3, slice(0, ATT))], rows, ATT))
-        l1_r2 = move(l1_r1, 1)
+        head, tail = slice(0, ATT), slice(ATT, None)
+        a1_r2 = move(stack([cut(l1_r1, head)], rows, ATT), 1)
+        f0_x13, f0_x2, l1_r1, l1_r3, a1_r2, met = tie(f0_x13, f0_x2, l1_r1, l1_r3, a1_r2, met)
+        a1_x = across(stack([cut(l1_r1, head), (a1_r2, 0), cut(l1_r3, head)], rows, ATT))
+        f1_r2 = move(stack([cut(l1_r1, tail)], rows, 2 * FFT), 1)
         wffn0 = finish(
             [f0, f0_r1, f0_r2, f0_r3]
             + [cut(x0, slice(ATT + LANES, COLS + LANES)), (f0_x13, 0), f0_x2, (f0_x13, 1)],
             2 * FFT,
         )
-    done, n1_0, s1_0, low1_0, act0, slope0 = feed_first(block_in, done, met, rep, split, wffn0)
+    *done, n1_0, s1_0, low1_0, act0, slope0 = feed_first(block_in, done, met, rep, split, wffn0)
     if pieced:
-        a1_x13, l1_r2, done = tie(a1_x13, l1_r2, done)
-        head, tail = slice(0, ATT), slice(ATT, None)
-        a1_x2 = across(stack([cut(l1_r2, head)], rows, ATT))
-        f1_x13 = across(stack([cut(l1_r1, tail), cut(l1_r3, tail)], rows, 2 * FFT))
+        a1_x, f1_r2, *done = tie(a1_x, f1_r2, *done)
+        f1_x = across(stack([cut(l1_r1, tail), (f1_r2, 0), cut(l1_r3, tail)], rows, 2 * FFT))
         watt1 = finish(
-            [cut(r, head) for r in (l1, l1_r1, l1_r2, l1_r3)]
-            + [cut(x0, third), (a1_x13, 0), (a1_x2, 0), (a1_x13, 1)],
+            [cut(l1, head), cut(l1_r1, head), (a1_r2, 0), cut(l1_r3, head), cut(x0, third)]
+            + [(a1_x, k) for k in range(3)],
             ATT,
         )
-    met = exchange(done)
+    met = [exchange(a) for a in done]
+    out = [
+        attention_next(m, 1, n1_0, done[m], met[m], rep, seg, split, watt1) for m in both
+    ]
+    done = [o[0] for o in out]
+    qkv1, probs1, ctx1, n2_0, s2_0, low_h1 = ([o[i] for o in out] for i in range(1, 7))
     if pieced:
-        f1_x13, met = tie(f1_x13, met)
-    out = attention_next(1, n1_0, done, met, rep, seg, split, watt1)
-    done, (qkv1, probs1, ctx1, n2_0, s2_0, low_h1) = list(out[:MICRO]), out[MICRO:]
-    if pieced:
-        f1_x2 = across(stack([cut(l1_r2, tail)], rows, 2 * FFT))
         wffn1 = finish(
-            [cut(r, tail) for r in (l1, l1_r1, l1_r2, l1_r3)]
-            + [cut(x0, fourth), (f1_x13, 0), (f1_x2, 0), (f1_x13, 1)],
+            [cut(l1, tail), cut(l1_r1, tail), (f1_r2, 0), cut(l1_r3, tail), cut(x0, fourth)]
+            + [(f1_x, k) for k in range(3)],
             2 * FFT,
         )
     met = [exchange(a) for a in done]
-    out = [feed_forward(m, 1, n2_0, done[m], met[m], rep, split, wffn1) for m in both]
+    out = [feed_forward(m, 1, n2_0[m], done[m], met[m], rep, split, wffn1) for m in both]
     n1_1, s1_1, low1_1, act1, slope1 = ([o[i] for o in out] for i in range(1, 6))
     met = [exchange(o[0]) for o in out]
 
@@ -957,7 +953,7 @@
     block_out = jnp.stack([o[5] for o in out])
     done = [o[0] for o in out]
     met = [exchange(o[0]) for o in out]
-    plan = {"w_f1": 0, "f1_3": 1, "w_a1": 2, "f1_2": 3, "a1_s": 3, "w_f0": 4, "f1_1": 4, "a1_t": 5, "f0_s": 5}
+    plan = {"w_f1": 0, "f1_3": 1, "w_a1": 2, "f1_2": 3, "a1_s": 3, "w_f0": 4, "f1_1": 5, "a1_t": 6, "f0_s": 5}
     held, ends = {}, []
 
     def make(name):
@@ -966,7 +962,7 @@
             g = matrix_gradient([(low1_1, din_1, FFT), (dffn_1, act1, FFT)], pieced, ndp)
         elif name == "w_a1":
             g = matrix_gradient(
-                [([low_h1] * 2, dqkv_1, QKV), (datt_1, [ctx1] * 2, HD)], pieced, ndp
+                [(low_h1, dqkv_1, QKV), (datt_1, ctx1, HD)], pieced, ndp
             )
         elif name == "w_f0":
             g = matrix_gradient(
@@ -1005,7 +1001,7 @@
         value = before(m, res[m])
         out.append(
             attention_back(
-                m, 1, value, done[m], met[m], n1_1[m], s1_1[m], rep, qkv1, probs1, ctx1, watt1
+                m, 1, value, done[m], met[m], n1_1[m], s1_1[m], rep, qkv1[m], probs1[m], ctx1[m], watt1
             )
         )
         ends.append(out[m][0])
@@ -1015,7 +1011,7 @@
     out = []
     for m in both:
         value = before(2 + m, mid[m])
-        out.append(feed_back(m, 0, value, done[m], met[m], n2_0, s2_0, rep, slope0, wffn0))
+        out.append(feed_back(m, 0, value, done[m], met[m], n2_0[m], s2_0[m], rep, slope0, wffn0))
         ends.append(out[m][0])
     res, dffn_0, din_0, vec_f0 = ([o[i] for o in out] for i in range(1, 5))
     done = [o[0] for o in out]

time: 314 us -> 303 us (0.965)
  starting transfers between devices: 77.7 us -> 63.8 us
    ppermute x14 -> x15, waiting for transfers between devices: 33.4 us -> 45.9 us  [exchange(): return lax.ppermute(a, 'tensor', [(0, 1), (1, 0)])]
    ppermute x42 -> x45, waiting for transfers between devices: 111 us -> 102 us  [move(): return lax.ppermute(a, 'dp', pairs_of(lax.axis_size('dp'), kind))]
    ppermute x14 -> x15, starting transfers between devices: 19.9 us -> 11 us  [exchange(): return lax.ppermute(a, 'tensor', [(0, 1), (1, 0)])]
    ppermute x42 -> x45, starting transfers between devices: 49.9 us -> 44.6 us  [move(): return lax.ppermute(a, 'dp', pairs_of(lax.axis_size('dp'), kind))]
    pallas_call x6 -> x7, Pallas kernels: 10.3 us -> 10.6 us  [the longest x2 5.31 us: attention_next(): call(body, [((SEQ, D), b16)] + [(shape[1:], kind) for shape, kind in ATT_...]
    unnamed x37 -> x49, local copies, waits for them, and re-layouts: 6.92 us -> 6.96 us
  transfers between devices with their start and end apart: 63 -> 67, of which waited for: 37 -> 38; matrix products, arithmetic and copies ran while one was open for 1% -> 2% of each run, Pallas kernels for 17% -> 17%
where the time goes in v4:
time: 303 us; the launch traced here: 297 us
  waiting for transfers between devices  155 us (51%)
  Pallas kernels  64.5 us (21%)
  starting transfers between devices  63.8 us (21%)
  local copies, waits for them, and re-layouts  8.69 us (3%)
  other arithmetic  4.16 us (1%)
    ppermute x45, waiting for transfers between devices, move(): return lax.ppermute(a, 'dp', pairs_of(lax.axis_size('dp'), kind))  102 us
    ppermute x15, waiting for transfers between devices, exchange(): return lax.ppermute(a, 'tensor', [(0, 1), (1, 0)])  45.9 us
    ppermute x45, starting transfers between devices, move(): return lax.ppermute(a, 'dp', pairs_of(lax.axis_size('dp'), kind))  44.6 us
    pallas_call x4, Pallas kernels, attention_back(): call(body, [((SEQ, D), b16), ((SEQ, D), f32), ((SEQ, D), b16), ((SEQ, QKV...  12.3 us
    pallas_call x4, Pallas kernels, matrix_gradient(): call(body, outs, specs, [pltpu.VMEM((D, step), f32)], flops=2 * MICRO * S...  11.8 us
    ppermute x15, starting transfers between devices, exchange(): return lax.ppermute(a, 'tensor', [(0, 1), (1, 0)])  11 us
    ppermute x7, starting transfers between devices, ppermute_bits(): lax.ppermute(value, ('dp', 'tensor'), [(i, i ^ bits) for i in range(n)])  8.17 us
    unnamed x49, local copies, waits for them, and re-layouts  6.96 us
  transfers between devices with their start and end apart: 67, of which 38 were waited for; matrix products, arithmetic and copies ran while one was open for 2% of the time, Pallas kernels for 17%

profile of v4, /device:TPU:0, one launch (start us, length us, event | category | flops | bytes accessed | tf_op | source)
XLA Modules:
  0.0 297.5 jit_solution(16758151754543565553)
XLA Ops:
  3.8 3.0 %collective-permute-start.3 = (bf16[48,9344]{1,0:T(8,128)(2,1)S(1)}, bf16[48,9344]{1,0:T(8,128)(2,1)S(1)}, u32[]{:S(2)}, u32[]{:S(2)}) collective-permute-start(bf16[48,9344]{1,0:T(8,128)(2,1)S(1)} %get-tuple-element.190), channel_id=1, source_target_pairs={{0,4},{2,6},{4,0},{6,2},{8,12},{10,14},{12,8},{14,10},{16,20},{18,... | collective-permute-start | bytes 2691080 | tf_op jit(solution)/shard_map/ppermute | solution.py:91
  12.3 3.4 %collective-permute-done.refs_1_.refs_0_ = bf16[48,1664]{1,0:T(8,128)(2,1)S(1)} collective-permute-done((bf16[48,1664]{1,0:T(8,128)(2,1)S(1)}, bf16[48,1664]{1,0:T(8,128)(2,1)S(1)}, u32[]{:S(2)}, u32[]{:S(2)}) %collective-permute-start) | collective-permute-done | bytes 159776 | tf_op jit(solution)/shard_map/ppermute | solution.py:91
  15.7 5.4 %collective-permute-done.1.refs_2_.refs_1_ = bf16[48,1664]{1,0:T(8,128)(2,1)S(1)} collective-permute-done((bf16[48,1664]{1,0:T(8,128)(2,1)S(1)}, bf16[48,1664]{1,0:T(8,128)(2,1)S(1)}, u32[]{:S(2)}, u32[]{:S(2)}) %collective-permute-start.1) | collective-permute-done | bytes 159776 | tf_op jit(solution)/shard_map/ppermute | solution.py:91
  21.8 3.9 %collective-permute-start.5 = (bf16[48,3072]{1,0:T(8,128)(2,1)S(1)}, bf16[48,3072]{1,0:T(8,128)(2,1)S(1)}, u32[]{:S(2)}, u32[]{:S(2)}) collective-permute-start(bf16[48,3072]{1,0:T(8,128)(2,1)S(1)} %get-tuple-element.191.refs_0_), channel_id=1, source_target_pairs={{0,8},{2,10},{4,12},{6,14},{8,16},{10,18},{12,20},{14,22},{16,24},... | collective-permute-start | bytes 884744 | tf_op jit(solution)/shard_map/ppermute | solution.py:91
  26.9 10.1 %collective-permute-done.4.refs_1_ = bf16[3,48,1664]{2,1,0:T(8,128)(2,1)S(1)} collective-permute-done((bf16[3,48,1664]{2,1,0:T(8,128)(2,1)S(1)}, bf16[3,48,1664]{2,1,0:T(8,128)(2,1)S(1)}, u32[]{:S(2)}, u32[]{:S(2)}) %collective-permute-start.4) | collective-permute-done | bytes 479264 | tf_op jit(solution)/shard_map/ppermute | solution.py:91
  42.6 4.4 %shard_map.249 = (bf16[2,256,768]{2,1,0:T(8,128)(2,1)S(1)}, bf16[2,256,1152]{2,1,0:T(8,128)(2,1)S(1)}, bf16[2,6,256,256]{3,2,1,0:T(8,128)(2,1)S(1)}, bf16[2,256,384]{2,1,0:T(8,128)(2,1)S(1)}) custom-call(bf16[2,256,768]{2,1,0:T(8,128)(2,1)S(1)} %copy-done.13, s32[2,1,256]{2,1,0:T(1,128)S(1)} %reshape.140.seg_ref, ...), custom_call_target="tpu_custom_call" | custom-call | flops 25769803776 | bytes 201326592 | tf_op jit(solution)/shard_map/pallas_call | solution.py:286
  54.6 15.2 %collective-permute-done.10.refs_2_ = bf16[48,3072]{1,0:T(8,128)(2,1)S(1)} collective-permute-done((bf16[48,3072]{1,0:T(8,128)(2,1)S(1)}, bf16[48,3072]{1,0:T(8,128)(2,1)S(1)}, u32[]{:S(2)}, u32[]{:S(2)}) %collective-permute-start.10) | collective-permute-done | bytes 294944 | tf_op jit(solution)/shard_map/ppermute | solution.py:91
  71.5 7.0 %collective-permute-done.13.refs_2_.refs_3_ = bf16[48,4608]{1,0:T(8,128)(2,1)S(1)} collective-permute-done((bf16[48,4608]{1,0:T(8,128)(2,1)S(1)}, bf16[48,4608]{1,0:T(8,128)(2,1)S(1)}, u32[]{:S(2)}, u32[]{:S(2)}) %collective-permute-start.13) | collective-permute-done | bytes 442400 | tf_op jit(solution)/shard_map/ppermute | solution.py:91
  78.5 6.4 %collective-permute-done.14.refs_1_.refs_2_ = bf16[1,48,1536]{2,1,0:T(8,128)(2,1)S(1)} collective-permute-done((bf16[1,48,1536]{2,1,0:T(8,128)(2,1)S(1)}, bf16[1,48,1536]{2,1,0:T(8,128)(2,1)S(1)}, u32[]{:S(2)}, u32[]{:S(2)}) %collective-permute-start.14) | collective-permute-done | bytes 147488 | tf_op jit(solution)/shard_map/ppermute | solution.py:91
  88.2 4.3 %shard_map.255 = (bf16[256,768]{1,0:T(8,128)(2,1)S(1)}, bf16[256,768]{1,0:T(8,128)(2,1)S(1)}, f32[2,256,768]{2,1,0:T(8,128)S(1)}, f32[2,256,1]{2,1,0:T(8,128)S(1...) custom-call(bf16[2,256,768]{2,1,0:T(8,128)(2,1)S(1)} %copy-done.13, ...), custom_call_target="tpu_custom_call" | custom-call | flops 38654705664 | bytes 335544320 | tf_op jit(solution)/shard_map/pallas_call | solution.py:360
  92.5 4.3 %collective-permute-done.19.refs_2_.refs_1_ = bf16[1,48,3072]{2,1,0:T(8,128)(2,1)S(1)} collective-permute-done((bf16[1,48,3072]{2,1,0:T(8,128)(2,1)S(1)}, bf16[1,48,3072]{2,1,0:T(8,128)(2,1)S(1)}, u32[]{:S(2)}, u32[]{:S(2)}) %collective-permute-start.19) | collective-permute-done | bytes 294944 | tf_op jit(solution)/shard_map/ppermute | solution.py:91
  101.0 8.9 %collective-permute-done.20.other_ref = bf16[256,768]{1,0:T(8,128)(2,1)S(1)} collective-permute-done((bf16[256,768]{1,0:T(8,128)(2,1)S(1)}, bf16[256,768]{1,0:T(8,128)(2,1)S(1)}, u32[]{:S(2)}, u32[]{:S(2)}) %collective-permute-start.20) | collective-permute-done | bytes 393248 | tf_op jit(solution)/shard_map/ppermute | solution.py:95
  113.1 8.5 %collective-permute-done.24.refs_1_ = bf16[3,48,3072]{2,1,0:T(8,128)(2,1)S(1)} collective-permute-done((bf16[3,48,3072]{2,1,0:T(8,128)(2,1)S(1)}, bf16[3,48,3072]{2,1,0:T(8,128)(2,1)S(1)}, u32[]{:S(2)}, u32[]{:S(2)}) %collective-permute-start.24) | collective-permute-done | bytes 884768 | tf_op jit(solution)/shard_map/ppermute | solution.py:91
  129.7 6.8 %collective-permute-done.29.other_ref = bf16[256,768]{1,0:T(8,128)(2,1)S(1)} collective-permute-done((bf16[256,768]{1,0:T(8,128)(2,1)S(1)}, bf16[256,768]{1,0:T(8,128)(2,1)S(1)}, u32[]{:S(2)}, u32[]{:S(2)}) %collective-permute-start.29) | collective-permute-done | bytes 393248 | tf_op jit(solution)/shard_map/ppermute | solution.py:95
  139.5 5.4 %collective-permute-done.27.other_ref = bf16[256,768]{1,0:T(8,128)(2,1)S(1)} collective-permute-done((bf16[256,768]{1,0:T(8,128)(2,1)S(1)}, bf16[256,768]{1,0:T(8,128)(2,1)S(1)}, u32[]{:S(2)}, u32[]{:S(2)}) %collective-permute-start.27) | collective-permute-done | bytes 393248 | tf_op jit(solution)/shard_map/ppermute | solution.py:95
  148.0 5.4 %collective-permute-done.30.other_ref = bf16[256,768]{1,0:T(8,128)(2,1)S(1)} collective-permute-done((bf16[256,768]{1,0:T(8,128)(2,1)S(1)}, bf16[256,768]{1,0:T(8,128)(2,1)S(1)}, u32[]{:S(2)}, u32[]{:S(2)}) %collective-permute-start.30) | collective-permute-done | bytes 393248 | tf_op jit(solution)/shard_map/ppermute | solution.py:95
  155.8 3.7 %shard_map.271 = (bf16[2,4,48,3072]{3,2,1,0:T(8,128)(2,1)S(1)}, bf16[2,4,48,3072]{3,2,1,0:T(8,128)(2,1)S(1)}) custom-call(bf16[256,768]{1,0:T(8,128)(2,1)S(1)} %get-tuple-element.219.refs_0_, bf16[256,768]{1,0:T(8,128)(2,1)S(1)} %get-tuple-element.223.refs_1_, bf16[256,1536]{1,0:T(8,128)(2,1)S(1)} %get-tuple-element.224.refs_2_, ...), custom_call_target="tpu_custom_call" | custom-call | flops 38654705664 | bytes 150994944 | tf_op jit(solution)/shard_map/pallas_call | solution.py:605
  161.4 3.4 %shard_map.272 = (bf16[256,768]{1,0:T(8,128)(2,1)S(1)}, f32[256,768]{1,0:T(8,128)S(1)}, bf16[256,768]{1,0:T(8,128)(2,1)S(1)}, bf16[256,1152]{1,0:T(8,128)(2,1)S(1)}, f32[8,768]{1,0:T(8,128)S(1)}) custom-call(f32[256,768]{1,0:T(8,128)S(1)} %get-tuple-element.234.res_ref, bf16[256,768]{1,0:T(8,128)(2,1)S(1)} %get-tuple-element.235.own_ref, ...), custom_call_target="tpu_custom_call" | custom-call | flops 25769803776 | bytes 150994944 | tf_op jit(solution)/shard_map/pallas_call | solution.py:515
  166.8 5.1 %collective-permute-done.33.other_ref = bf16[256,768]{1,0:T(8,128)(2,1)S(1)} collective-permute-done((bf16[256,768]{1,0:T(8,128)(2,1)S(1)}, bf16[256,768]{1,0:T(8,128)(2,1)S(1)}, u32[]{:S(2)}, u32[]{:S(2)}) %collective-permute-start.33) | collective-permute-done | bytes 393248 | tf_op jit(solution)/shard_map/ppermute | solution.py:95
  171.8 3.0 %shard_map.273 = (bf16[256,768]{1,0:T(8,128)(2,1)S(1)}, f32[256,768]{1,0:T(8,128)S(1)}, bf16[256,768]{1,0:T(8,128)(2,1)S(1)}, bf16[256,1152]{1,0:T(8,128)(2,1)S(1)}, f32[8,768]{1,0:T(8,128)S(1)}) custom-call(f32[256,768]{1,0:T(8,128)S(1)} %get-tuple-element.248.res_ref, bf16[256,768]{1,0:T(8,128)(2,1)S(1)} %get-tuple-element.249.own_ref, ...), custom_call_target="tpu_custom_call" | custom-call | flops 25769803776 | bytes 150994944 | tf_op jit(solution)/shard_map/pallas_call | solution.py:515
  184.9 3.9 %collective-permute-done.37.other_ref = bf16[256,768]{1,0:T(8,128)(2,1)S(1)} collective-permute-done((bf16[256,768]{1,0:T(8,128)(2,1)S(1)}, bf16[256,768]{1,0:T(8,128)(2,1)S(1)}, u32[]{:S(2)}, u32[]{:S(2)}) %collective-permute-start.37) | collective-permute-done | bytes 393248 | tf_op jit(solution)/shard_map/ppermute | solution.py:95
  191.1 3.7 %shard_map.277 = (bf16[2,4,48,3072]{3,2,1,0:T(8,128)(2,1)S(1)}, bf16[2,4,48,3072]{3,2,1,0:T(8,128)(2,1)S(1)}) custom-call(bf16[2,256,768]{2,1,0:T(8,128)(2,1)S(1)} %get-tuple-element.203.refs_0_.refs_1_, bf16[2,256,768]{2,1,0:T(8,128)(2,1)S(1)} %get-tuple-element.203.refs_0_.refs_1_, bf16[256,1536]{1,0:T(8,128)(2,1)S(1)} %get-tuple-element.261.refs_2_, ...), custom_call_target="tpu_custom_call" | custom-call | flops 38654705664 | bytes 188743680 | tf_op jit(solution)/shard_map/pallas_call | solution.py:605
  196.8 3.0 %shard_map.278 = (bf16[256,768]{1,0:T(8,128)(2,1)S(1)}, f32[256,768]{1,0:T(8,128)S(1)}, bf16[256,768]{1,0:T(8,128)(2,1)S(1)}, bf16[256,1152]{1,0:T(8,128)(2,1)S(1)}, f32[8,768]{1,0:T(8,128)S(1)}) custom-call(f32[256,768]{1,0:T(8,128)S(1)} %get-tuple-element.277.res_ref, bf16[256,768]{1,0:T(8,128)(2,1)S(1)} %get-tuple-element.263.own_ref, ...), custom_call_target="tpu_custom_call" | custom-call | flops 25769803776 | bytes 150994944 | tf_op jit(solution)/shard_map/pallas_call | solution.py:515
  201.5 4.9 %collective-permute-done.45.other_ref = bf16[256,768]{1,0:T(8,128)(2,1)S(1)} collective-permute-done((bf16[256,768]{1,0:T(8,128)(2,1)S(1)}, bf16[256,768]{1,0:T(8,128)(2,1)S(1)}, u32[]{:S(2)}, u32[]{:S(2)}) %collective-permute-start.45) | collective-permute-done | bytes 393248 | tf_op jit(solution)/shard_map/ppermute | solution.py:95
  206.4 3.0 %shard_map.280 = (bf16[256,768]{1,0:T(8,128)(2,1)S(1)}, f32[256,768]{1,0:T(8,128)S(1)}, bf16[256,768]{1,0:T(8,128)(2,1)S(1)}, bf16[256,1152]{1,0:T(8,128)(2,1)S(1)}, f32[8,768]{1,0:T(8,128)S(1)}) custom-call(f32[256,768]{1,0:T(8,128)S(1)} %get-tuple-element.288.res_ref, bf16[256,768]{1,0:T(8,128)(2,1)S(1)} %get-tuple-element.289.own_ref, ...), custom_call_target="tpu_custom_call" | custom-call | flops 25769803776 | bytes 150994944 | tf_op jit(solution)/shard_map/pallas_call | solution.py:515
  225.0 4.6 %collective-permute-done.52.refs_2_ = bf16[48,1536]{1,0:T(8,128)(2,1)S(1)} collective-permute-done((bf16[48,1536]{1,0:T(8,128)(2,1)S(1)}, bf16[48,1536]{1,0:T(8,128)(2,1)S(1)}, u32[]{:S(2)}, u32[]{:S(2)}) %collective-permute-start.52) | collective-permute-done | bytes 147488 | tf_op jit(solution)/shard_map/ppermute | solution.py:91
  233.3 15.1 %collective-permute-done.50.refs_2_ = bf16[48,3072]{1,0:T(8,128)(2,1)S(1)} collective-permute-done((bf16[48,3072]{1,0:T(8,128)(2,1)S(1)}, bf16[48,3072]{1,0:T(8,128)(2,1)S(1)}, u32[]{:S(2)}, u32[]{:S(2)}) %collective-permute-start.50) | collective-permute-done | bytes 294944 | tf_op jit(solution)/shard_map/ppermute | solution.py:91
  250.2 4.1 %collective-permute-start.58 = (bf16[48,1664]{1,0:T(8,128)(2,1)S(1)}, bf16[48,1664]{1,0:T(8,128)(2,1)S(1)}, u32[]{:S(2)}, u32[]{:S(2)}) collective-permute-start(bf16[48,1664]{1,0:T(8,128)(2,1)S(1)} %get-tuple-element.392), channel_id=1, source_target_pairs={{0,24},{2,26},{4,28},{6,30},{8,0},{10,2},{12,4},{14,6},{16,8},{18,... | collective-permute-start | bytes 479240 | tf_op jit(solution)/shard_map/ppermute | solution.py:91
  260.0 3.7 %collective-permute-done.39.refs_0_ = bf16[2,48,3072]{2,1,0:T(8,128)(2,1)S(1)} collective-permute-done((bf16[2,48,3072]{2,1,0:T(8,128)(2,1)S(1)}, bf16[2,48,3072]{2,1,0:T(8,128)(2,1)S(1)}, u32[]{:S(2)}, u32[]{:S(2)}) %collective-permute-start.39) | collective-permute-done | bytes 589856 | tf_op jit(solution)/shard_map/ppermute | solution.py:91
  263.8 2.9 collective-permute-start.59
  266.9 6.8 %collective-permute-done.59.refs_1_ = bf16[48,3072]{1,0:T(8,128)(2,1)S(1)} collective-permute-done((bf16[48,3072]{1,0:T(8,128)(2,1)S(1)}, bf16[48,3072]{1,0:T(8,128)(2,1)S(1)}, u32[]{:S(2)}, u32[]{:S(2)}) %collective-permute-start.59) | collective-permute-done | bytes 294944 | tf_op jit(solution)/shard_map/ppermute | solution.py:91
  288.7 6.0 %shard_map.288 = (f32[2,1728,128]{2,1,0:T(8,128)}, f32[2,1728,128]{2,1,0:T(8,128)}, f32[2,1728,128]{2,1,0:T(8,128)}, bf16[2,1728,128]{2,1,0:T(8,128)(2,1)S(1)}) custom-call(f32[8,128]{1,0:T(8,128)S(1)} %add_add_fusion.q_ref.f_ref, f32[2,1728,128]{2,1,0:T(8,128)S(1)} %get-tuple-element.335.w_ref, f32[2,1728,128]{2,1,0:T(8,128)S(1)} %get-tuple-element.336.m_ref, ...), custom_call_target="tpu_custom_call" | custom-call | flops 8847360 | bytes 13271040 | tf_op jit(solution)/shard_map/pallas_call | solution.py:800
  (222 shorter events, 116.5 us)
Async XLA Ops:
  3.8 33.2 %collective-permute-start.3 = (bf16[48,9344]{1,0:T(8,128)(2,1)S(1)}, bf16[48,9344]{1,0:T(8,128)(2,1)S(1)}, u32[]{:S(2)}, u32[]{:S(2)}) collective-permute-start(bf16[48,9344]{1,0:T(8,128)(2,1)S(1)} %get-tuple-element.190), channel_id=1, source_target_pairs={{0,4},{2,6},{4,0},{6,2},{8,12},{10,14},{12,8},{14,10},{16,20},{18,... | collective-permute-start | bytes 2691080 | tf_op jit(solution)/shard_map/ppermute | solution.py:91
  21.2 15.8 %collective-permute-start.4 = (bf16[3,48,1664]{2,1,0:T(8,128)(2,1)S(1)}, bf16[3,48,1664]{2,1,0:T(8,128)(2,1)S(1)}, u32[]{:S(2)}, u32[]{:S(2)}) collective-permute-start(bf16[3,48,1664]{2,1,0:T(8,128)(2,1)S(1)} %shard_map.245), channel_id=1, source_target_pairs={{0,4},{2,6},{4,0},{6,2},{8,12},{10,14},{12,8},{14,10},{16,20},{18,... | collective-permute-start | bytes 1437704 | tf_op jit(solution)/shard_map/ppermute | solution.py:91
  21.8 15.2 %collective-permute-start.5 = (bf16[48,3072]{1,0:T(8,128)(2,1)S(1)}, bf16[48,3072]{1,0:T(8,128)(2,1)S(1)}, u32[]{:S(2)}, u32[]{:S(2)}) collective-permute-start(bf16[48,3072]{1,0:T(8,128)(2,1)S(1)} %get-tuple-element.191.refs_0_), channel_id=1, source_target_pairs={{0,8},{2,10},{4,12},{6,14},{8,16},{10,18},{12,20},{14,22},{16,24},... | collective-permute-start | bytes 884744 | tf_op jit(solution)/shard_map/ppermute | solution.py:91
  47.0 37.8 %collective-permute-start.15 = (bf16[2,256,768]{2,1,0:T(8,128)(2,1)S(1)}, bf16[2,256,768]{2,1,0:T(8,128)(2,1)S(1)}, u32[]{:S(2)}, u32[]{:S(2)}) collective-permute-start(bf16[2,256,768]{2,1,0:T(8,128)(2,1)S(1)} %get-tuple-element.195.own_ref), channel_id=1, source_target_pairs={{0,1},{1,0},{2,3},{3,2},{4,5},{5,4},{6,7},{7,6},{8,9},{9,8},{10,11... | collective-permute-start | bytes 2359304 | tf_op jit(solution)/shard_map/ppermute | solution.py:95
  48.6 22.7 %collective-permute-start.12 = (bf16[48,4608]{1,0:T(8,128)(2,1)S(1)}, bf16[48,4608]{1,0:T(8,128)(2,1)S(1)}, u32[]{:S(2)}, u32[]{:S(2)}) collective-permute-start(bf16[48,4608]{1,0:T(8,128)(2,1)S(1)} %get-tuple-element.198.refs_0_), channel_id=1, source_target_pairs={{0,8},{2,10},{4,12},{6,14},{8,16},{10,18},{12,20},{14,22},{16,24},... | collective-permute-start | bytes 1327112 | tf_op jit(solution)/shard_map/ppermute | solution.py:91
  49.2 20.6 %collective-permute-start.10 = (bf16[48,3072]{1,0:T(8,128)(2,1)S(1)}, bf16[48,3072]{1,0:T(8,128)(2,1)S(1)}, u32[]{:S(2)}, u32[]{:S(2)}) collective-permute-start(bf16[48,3072]{1,0:T(8,128)(2,1)S(1)} %collective-permute-done.5.refs_0_.refs_1_), channel_id=1, source_target_pairs={{0,8},{2,10},{4,12},{6,14},{8,16},{10,18},{12,20},{14,22},{16,24},... | collective-permute-start | bytes 884744 | tf_op jit(solution)/shard_map/ppermute | solution.py:91
  50.5 34.3 %collective-permute-start.9 = (bf16[2,48,3072]{2,1,0:T(8,128)(2,1)S(1)}, bf16[2,48,3072]{2,1,0:T(8,128)(2,1)S(1)}, u32[]{:S(2)}, u32[]{:S(2)}) collective-permute-start(bf16[2,48,3072]{2,1,0:T(8,128)(2,1)S(1)} %shard_map.250), channel_id=1, source_target_pairs={{0,4},{2,6},{4,0},{6,2},{8,12},{10,14},{12,8},{14,10},{16,20},{18,... | collective-permute-start | bytes 1769480 | tf_op jit(solution)/shard_map/ppermute | solution.py:91
  52.1 26.3 %collective-permute-start.13 = (bf16[48,4608]{1,0:T(8,128)(2,1)S(1)}, bf16[48,4608]{1,0:T(8,128)(2,1)S(1)}, u32[]{:S(2)}, u32[]{:S(2)}) collective-permute-start(bf16[48,4608]{1,0:T(8,128)(2,1)S(1)} %get-tuple-element.198.refs_0_), channel_id=1, source_target_pairs={{0,24},{2,26},{4,28},{6,30},{8,0},{10,2},{12,4},{14,6},{16,8},{18,... | collective-permute-start | bytes 1327112 | tf_op jit(solution)/shard_map/ppermute | solution.py:91
  69.8 15.1 %collective-permute-start.11 = (bf16[48,3072]{1,0:T(8,128)(2,1)S(1)}, bf16[48,3072]{1,0:T(8,128)(2,1)S(1)}, u32[]{:S(2)}, u32[]{:S(2)}) collective-permute-start(bf16[48,3072]{1,0:T(8,128)(2,1)S(1)} %collective-permute-done.10.refs_2_), channel_id=1, source_target_pairs={{0,4},{2,6},{4,0},{6,2},{8,12},{10,14},{12,8},{14,10},{16,20},{18,... | collective-permute-start | bytes 884744 | tf_op jit(solution)/shard_map/ppermute | solution.py:91
  85.9 14.8 %collective-permute-start.21 = (bf16[4,48,1536]{2,1,0:T(8,128)(2,1)S(1)}, bf16[4,48,1536]{2,1,0:T(8,128)(2,1)S(1)}, u32[]{:S(2)}, u32[]{:S(2)}) collective-permute-start(bf16[4,48,1536]{2,1,0:T(8,128)(2,1)S(1)} %shard_map.258.refs_0_), channel_id=1, source_target_pairs={{0,2},{2,0},{4,6},{6,4},{8,10},{10,8},{12,14},{14,12},{16,18},{18,... | collective-permute-start | bytes 1769480 | tf_op jit(solution)/shard_map/ppermute | solution.py:91
  98.6 23.2 %collective-permute-start.28 = (bf16[256,768]{1,0:T(8,128)(2,1)S(1)}, bf16[256,768]{1,0:T(8,128)(2,1)S(1)}, u32[]{:S(2)}, u32[]{:S(2)}) collective-permute-start(bf16[256,768]{1,0:T(8,128)(2,1)S(1)} %get-tuple-element.220.own_ref), channel_id=1, source_target_pairs={{0,1},{1,0},{2,3},{3,2},{4,5},{5,4},{6,7},{7,6},{8,9},{9,8},{10,11... | collective-permute-start | bytes 1179656 | tf_op jit(solution)/shard_map/ppermute | solution.py:95
  100.2 21.4 %collective-permute-start.24 = (bf16[3,48,3072]{2,1,0:T(8,128)(2,1)S(1)}, bf16[3,48,3072]{2,1,0:T(8,128)(2,1)S(1)}, u32[]{:S(2)}, u32[]{:S(2)}) collective-permute-start(bf16[3,48,3072]{2,1,0:T(8,128)(2,1)S(1)} %shard_map.263), channel_id=1, source_target_pairs={{0,4},{2,6},{4,0},{6,2},{8,12},{10,14},{12,8},{14,10},{16,20},{18,... | collective-permute-start | bytes 2654216 | tf_op jit(solution)/shard_map/ppermute | solution.py:91
  100.8 24.3 %collective-permute-start.25 = (bf16[4,48,3072]{2,1,0:T(8,128)(2,1)S(1)}, bf16[4,48,3072]{2,1,0:T(8,128)(2,1)S(1)}, u32[]{:S(2)}, u32[]{:S(2)}) collective-permute-start(bf16[4,48,3072]{2,1,0:T(8,128)(2,1)S(1)} %shard_map.262.refs_0_), channel_id=1, source_target_pairs={{0,2},{2,0},{4,6},{6,4},{8,10},{10,8},{12,14},{14,12},{16,18},{18,... | collective-permute-start | bytes 3538952 | tf_op jit(solution)/shard_map/ppermute | solution.py:91
  129.0 15.9 %collective-permute-start.27 = (bf16[256,768]{1,0:T(8,128)(2,1)S(1)}, bf16[256,768]{1,0:T(8,128)(2,1)S(1)}, u32[]{:S(2)}, u32[]{:S(2)}) collective-permute-start(bf16[256,768]{1,0:T(8,128)(2,1)S(1)} %get-tuple-element.216.own_ref), channel_id=1, source_target_pairs={{0,1},{1,0},{2,3},{3,2},{4,5},{5,4},{6,7},{7,6},{8,9},{9,8},{10,11... | collective-permute-start | bytes 1179656 | tf_op jit(solution)/shard_map/ppermute | solution.py:95
  139.0 14.4 %collective-permute-start.30 = (bf16[256,768]{1,0:T(8,128)(2,1)S(1)}, bf16[256,768]{1,0:T(8,128)(2,1)S(1)}, u32[]{:S(2)}, u32[]{:S(2)}) collective-permute-start(bf16[256,768]{1,0:T(8,128)(2,1)S(1)} %get-tuple-element.226.own_ref), channel_id=1, source_target_pairs={{0,1},{1,0},{2,3},{3,2},{4,5},{5,4},{6,7},{7,6},{8,9},{9,8},{10,11... | collective-permute-start | bytes 1179656 | tf_op jit(solution)/shard_map/ppermute | solution.py:95
  164.8 15.0 %collective-permute-start.34 = (bf16[256,768]{1,0:T(8,128)(2,1)S(1)}, bf16[256,768]{1,0:T(8,128)(2,1)S(1)}, u32[]{:S(2)}, u32[]{:S(2)}) collective-permute-start(bf16[256,768]{1,0:T(8,128)(2,1)S(1)} %get-tuple-element.246.own_ref), channel_id=1, source_target_pairs={{0,1},{1,0},{2,3},{3,2},{4,5},{5,4},{6,7},{7,6},{8,9},{9,8},{10,11... | collective-permute-start | bytes 1179656 | tf_op jit(solution)/shard_map/ppermute | solution.py:95
  166.8 16.9 %collective-permute-start.35 = (bf16[2,48,3072]{2,1,0:T(8,128)(2,1)S(1)}, bf16[2,48,3072]{2,1,0:T(8,128)(2,1)S(1)}, u32[]{:S(2)}, u32[]{:S(2)}) collective-permute-start(bf16[2,48,3072]{2,1,0:T(8,128)(2,1)S(1)} %get-tuple-element.389), channel_id=1, source_target_pairs={{0,8},{2,10},{4,12},{6,14},{8,16},{10,18},{12,20},{14,22},{16,24},... | collective-permute-start | bytes 1769480 | tf_op jit(solution)/shard_map/ppermute | solution.py:91
  182.0 14.8 %collective-permute-start.41 = (bf16[256,768]{1,0:T(8,128)(2,1)S(1)}, bf16[256,768]{1,0:T(8,128)(2,1)S(1)}, u32[]{:S(2)}, u32[]{:S(2)}) collective-permute-start(bf16[256,768]{1,0:T(8,128)(2,1)S(1)} %get-tuple-element.263.own_ref), channel_id=1, source_target_pairs={{0,1},{1,0},{2,3},{3,2},{4,5},{5,4},{6,7},{7,6},{8,9},{9,8},{10,11... | collective-permute-start | bytes 1179656 | tf_op jit(solution)/shard_map/ppermute | solution.py:95
  183.9 16.3 %collective-permute-start.40 = (bf16[2,48,3072]{2,1,0:T(8,128)(2,1)S(1)}, bf16[2,48,3072]{2,1,0:T(8,128)(2,1)S(1)}, u32[]{:S(2)}, u32[]{:S(2)}) collective-permute-start(bf16[2,48,3072]{2,1,0:T(8,128)(2,1)S(1)} %fusion.2), channel_id=1, source_target_pairs={{0,8},{2,10},{4,12},{6,14},{8,16},{10,18},{12,20},{14,22},{16,24},... | collective-permute-start | bytes 1769480 | tf_op jit(solution)/shard_map/ppermute | solution.py:91
  184.3 25.1 %collective-permute-start.44 = (bf16[4,48,1536]{2,1,0:T(8,128)(2,1)S(1)}, bf16[4,48,1536]{2,1,0:T(8,128)(2,1)S(1)}, u32[]{:S(2)}, u32[]{:S(2)}) collective-permute-start(bf16[4,48,1536]{2,1,0:T(8,128)(2,1)S(1)} %fusion.7), channel_id=1, source_target_pairs={{0,4},{2,6},{4,0},{6,2},{8,12},{10,14},{12,8},{14,10},{16,20},{18,... | collective-permute-start | bytes 1769480 | tf_op jit(solution)/shard_map/ppermute | solution.py:91
  200.4 19.1 %collective-permute-start.42 = (bf16[2,48,3072]{2,1,0:T(8,128)(2,1)S(1)}, bf16[2,48,3072]{2,1,0:T(8,128)(2,1)S(1)}, u32[]{:S(2)}, u32[]{:S(2)}) collective-permute-start(bf16[2,48,3072]{2,1,0:T(8,128)(2,1)S(1)} %fusion.1), channel_id=1, source_target_pairs={{0,8},{2,10},{4,12},{6,14},{8,16},{10,18},{12,20},{14,22},{16,24},... | collective-permute-start | bytes 1769480 | tf_op jit(solution)/shard_map/ppermute | solution.py:91
  200.8 14.6 %collective-permute-start.48 = (bf16[2,48,3072]{2,1,0:T(8,128)(2,1)S(1)}, bf16[2,48,3072]{2,1,0:T(8,128)(2,1)S(1)}, u32[]{:S(2)}, u32[]{:S(2)}) collective-permute-start(bf16[2,48,3072]{2,1,0:T(8,128)(2,1)S(1)} %get-tuple-element.386), channel_id=1, source_target_pairs={{0,4},{2,6},{4,0},{6,2},{8,12},{10,14},{12,8},{14,10},{16,20},{18,... | collective-permute-start | bytes 1769480 | tf_op jit(solution)/shard_map/ppermute | solution.py:91
  209.6 20.6 %collective-permute-start.53 = (bf16[48,1536]{1,0:T(8,128)(2,1)S(1)}, bf16[48,1536]{1,0:T(8,128)(2,1)S(1)}, u32[]{:S(2)}, u32[]{:S(2)}) collective-permute-start(bf16[48,1536]{1,0:T(8,128)(2,1)S(1)} %get-tuple-element.397), channel_id=1, source_target_pairs={{0,24},{2,26},{4,28},{6,30},{8,0},{10,2},{12,4},{14,6},{16,8},{18,... | collective-permute-start | bytes 442376 | tf_op jit(solution)/shard_map/ppermute | solution.py:91
  218.4 14.3 %collective-permute-start.49 = (bf16[48,3072]{1,0:T(8,128)(2,1)S(1)}, bf16[48,3072]{1,0:T(8,128)(2,1)S(1)}, u32[]{:S(2)}, u32[]{:S(2)}) collective-permute-start(bf16[48,3072]{1,0:T(8,128)(2,1)S(1)} %get-tuple-element.391), channel_id=1, source_target_pairs={{0,24},{2,26},{4,28},{6,30},{8,0},{10,2},{12,4},{14,6},{16,8},{18,... | collective-permute-start | bytes 884744 | tf_op jit(solution)/shard_map/ppermute | solution.py:91
  219.5 28.9 %collective-permute-start.50 = (bf16[48,3072]{1,0:T(8,128)(2,1)S(1)}, bf16[48,3072]{1,0:T(8,128)(2,1)S(1)}, u32[]{:S(2)}, u32[]{:S(2)}) collective-permute-start(bf16[48,3072]{1,0:T(8,128)(2,1)S(1)} %get-tuple-element.390), channel_id=1, source_target_pairs={{0,16},{2,18},{4,20},{6,22},{8,24},{10,26},{12,28},{14,30},{16,0},... | collective-permute-start | bytes 884744 | tf_op jit(solution)/shard_map/ppermute | solution.py:91
  223.6 25.4 %collective-permute-start.47 = (bf16[4,48,1664]{2,1,0:T(8,128)(2,1)S(1)}, bf16[4,48,1664]{2,1,0:T(8,128)(2,1)S(1)}, u32[]{:S(2)}, u32[]{:S(2)}) collective-permute-start(bf16[4,48,1664]{2,1,0:T(8,128)(2,1)S(1)} %fusion.5), channel_id=1, source_target_pairs={{0,4},{2,6},{4,0},{6,2},{8,12},{10,14},{12,8},{14,10},{16,20},{18,... | collective-permute-start | bytes 1916936 | tf_op jit(solution)/shard_map/ppermute | solution.py:91
  229.6 19.7 %collective-permute-start.54 = (bf16[256,768]{1,0:T(8,128)(2,1)S(1)}, bf16[256,768]{1,0:T(8,128)(2,1)S(1)}, u32[]{:S(2)}, u32[]{:S(2)}) collective-permute-start(bf16[256,768]{1,0:T(8,128)(2,1)S(1)} %get-tuple-element.282.refs_1_), channel_id=1, source_target_pairs={{0,1},{1,0},{2,3},{3,2},{4,5},{5,4},{6,7},{7,6},{8,9},{9,8},{10,11... | collective-permute-start | bytes 1179656 | tf_op jit(solution)/shard_map/ppermute | solution.py:95
  230.2 20.0 %collective-permute-start.43 = (bf16[48,3072]{1,0:T(8,128)(2,1)S(1)}, bf16[48,3072]{1,0:T(8,128)(2,1)S(1)}, u32[]{:S(2)}, u32[]{:S(2)}) collective-permute-start(bf16[48,3072]{1,0:T(8,128)(2,1)S(1)} %fusion.13), channel_id=1, source_target_pairs={{0,4},{2,6},{4,0},{6,2},{8,12},{10,14},{12,8},{14,10},{16,20},{18,... | collective-permute-start | bytes 884744 | tf_op jit(solution)/shard_map/ppermute | solution.py:91
  232.7 25.8 %collective-permute-start.55 = (bf16[256,768]{1,0:T(8,128)(2,1)S(1)}, bf16[256,768]{1,0:T(8,128)(2,1)S(1)}, u32[]{:S(2)}, u32[]{:S(2)}) collective-permute-start(bf16[256,768]{1,0:T(8,128)(2,1)S(1)} %get-tuple-element.290.refs_4_), channel_id=1, source_target_pairs={{0,1},{1,0},{2,3},{3,2},{4,5},{5,4},{6,7},{7,6},{8,9},{9,8},{10,11... | collective-permute-start | bytes 1179656 | tf_op jit(solution)/shard_map/ppermute | solution.py:95
  248.4 15.2 %collective-permute-start.39 = (bf16[2,48,3072]{2,1,0:T(8,128)(2,1)S(1)}, bf16[2,48,3072]{2,1,0:T(8,128)(2,1)S(1)}, u32[]{:S(2)}, u32[]{:S(2)}) collective-permute-start(bf16[2,48,3072]{2,1,0:T(8,128)(2,1)S(1)} %get-tuple-element.387), channel_id=1, source_target_pairs={{0,4},{2,6},{4,0},{6,2},{8,12},{10,14},{12,8},{14,10},{16,20},{18,... | collective-permute-start | bytes 1769480 | tf_op jit(solution)/shard_map/ppermute | solution.py:91
  249.3 14.4 %collective-permute-start.56 = (bf16[48,1664]{1,0:T(8,128)(2,1)S(1)}, bf16[48,1664]{1,0:T(8,128)(2,1)S(1)}, u32[]{:S(2)}, u32[]{:S(2)}) collective-permute-start(bf16[48,1664]{1,0:T(8,128)(2,1)S(1)} %get-tuple-element.394), channel_id=1, source_target_pairs={{0,8},{2,10},{4,12},{6,14},{8,16},{10,18},{12,20},{14,22},{16,24},... | collective-permute-start | bytes 479240 | tf_op jit(solution)/shard_map/ppermute | solution.py:91
  249.3 14.4 %collective-permute-start.57 = (bf16[48,1664]{1,0:T(8,128)(2,1)S(1)}, bf16[48,1664]{1,0:T(8,128)(2,1)S(1)}, u32[]{:S(2)}, u32[]{:S(2)}) collective-permute-start(bf16[48,1664]{1,0:T(8,128)(2,1)S(1)} %get-tuple-element.393), channel_id=1, source_target_pairs={{0,16},{2,18},{4,20},{6,22},{8,24},{10,26},{12,28},{14,30},{16,0},... | collective-permute-start | bytes 479240 | tf_op jit(solution)/shard_map/ppermute | solution.py:91
  (58 other events, 420.5 us)

commit v5 on v4

--- a/solution.py
+++ b/solution.py
@@ -720,7 +720,7 @@
     first = half_first + 0.5 * grad
     second = half_second + 0.5 * grad * grad
     correct = 1.0 - 0.5**STEP
-    direction = first / correct / (jnp.sqrt(second / correct) + 1e-08)
+    direction = first / (correct * jnp.sqrt(second * (1.0 / correct)) + correct * 1e-08)
     return decayed - rate * direction, first, second
 
 
@@ -776,23 +776,26 @@
 def update_matrices(decayed, first, second, grads, squares):
     rows = grads[0].shape[0]
     tiled = decayed
-    step = 8 if rows % 8 == 0 else rows
+    step = 24 if rows % 24 == 0 else rows
     n_steps = rows // step
     block = (1, step * TILES, LANES)
 
     def body(f_ref, w_ref, m_ref, v_ref, a0, f0, a1, f1, nw, nm, nv, nl):
         scale = clip_factor(f_ref[...])[1]
-        layer = pl.program_id(0)
-        for c in range(TILES):
-            if c < ATT // LANES:
+
+        def columns(a_ref, g_ref):
+            for c in range(TILES):
                 lo = c * LANES
-                grad = jnp.where(layer == 0, a0[:, lo : lo + LANES], a1[:, lo : lo + LANES])
-            else:
-                lo = c * LANES - ATT
-                grad = jnp.where(layer == 0, f0[:, lo : lo + LANES], f1[:, lo : lo + LANES])
-            where = (0, pl.ds(c, step, stride=TILES), slice(None))
-            new = stepped(w_ref[where], m_ref[where], v_ref[where], grad * scale, weight_rate)
-            nw[where], nm[where], nv[where] = new
+                if lo < ATT:
+                    grad = a_ref[:, lo : lo + LANES]
+                else:
+                    grad = g_ref[:, lo - ATT : lo - ATT + LANES]
+                where = (0, pl.ds(c, step, stride=TILES), slice(None))
+                new = stepped(w_ref[where], m_ref[where], v_ref[where], grad * scale, weight_rate)
+                nw[where], nm[where], nv[where] = new
+
+        for layer, pair in enumerate(((a0, f0), (a1, f1))):
+            pl.when(pl.program_id(0) == layer)(partial(columns, *pair))
         nl[...] = nw[...].astype(b16)
 
     big = pl.BlockSpec(block, lambda l, i: (l, i, 0))
@@ -884,7 +887,7 @@
         mine0 = stack(
             [cut(x0, slice(0, ATT + LANES)), (a0_x, 0), (a0_x, 1), (a0_x, 2)], rows, ATT + LANES
         )
-        mine0, f0_r1, f0_r3, l1 = tie(mine0, f0_r1, f0_r3, l1)
+        mine0, f0_r1, l1 = tie(mine0, f0_r1, l1)
         watt0 = settle([near, mine0], [move(near, "core"), move(mine0, "core")])
         f0_x13 = across(stack([f0_r1, f0_r3], rows, 2 * FFT))
         f0_r2 = move(f0_r1, 1)

time: 303 us -> 297 us (0.980)
  waiting for transfers between devices: 155 us -> 145 us
  starting transfers between devices: 63.8 us -> 70 us
    ppermute x45, waiting for transfers between devices: 102 us -> 95.7 us  [move(): return lax.ppermute(a, 'dp', pairs_of(lax.axis_size('dp'), kind))]
    ppermute x45, starting transfers between devices: 44.6 us -> 51.1 us  [move(): return lax.ppermute(a, 'dp', pairs_of(lax.axis_size('dp'), kind))]
  transfers between devices with their start and end apart: 67 -> 67, of which waited for: 38 -> 36; matrix products, arithmetic and copies ran while one was open for 2% -> 2% of each run, Pallas kernels for 17% -> 20%
where the time goes in v5:
time: 297 us; the launch traced here: 292 us
  waiting for transfers between devices  145 us (49%)
  starting transfers between devices  70 us (24%)
  Pallas kernels  61.9 us (21%)
  local copies, waits for them, and re-layouts  8.69 us (3%)
  other arithmetic  4.15 us (1%)
    ppermute x45, waiting for transfers between devices, move(): return lax.ppermute(a, 'dp', pairs_of(lax.axis_size('dp'), kind))  95.7 us
    ppermute x45, starting transfers between devices, move(): return lax.ppermute(a, 'dp', pairs_of(lax.axis_size('dp'), kind))  51.1 us
    ppermute x15, waiting for transfers between devices, exchange(): return lax.ppermute(a, 'tensor', [(0, 1), (1, 0)])  43.1 us
    pallas_call x4, Pallas kernels, attention_back(): call(body, [((SEQ, D), b16), ((SEQ, D), f32), ((SEQ, D), b16), ((SEQ, QKV...  12.4 us
    pallas_call x4, Pallas kernels, matrix_gradient(): call(body, outs, specs, [pltpu.VMEM((D, step), f32)], flops=2 * MICRO * S...  11.8 us
    ppermute x15, starting transfers between devices, exchange(): return lax.ppermute(a, 'tensor', [(0, 1), (1, 0)])  11 us
    ppermute x7, starting transfers between devices, ppermute_bits(): lax.ppermute(value, ('dp', 'tensor'), [(i, i ^ bits) for i in range(n)])  7.95 us
    unnamed x49, local copies, waits for them, and re-layouts  6.95 us
  transfers between devices with their start and end apart: 67, of which 36 were waited for; matrix products, arithmetic and copies ran while one was open for 2% of the time, Pallas kernels for 20%

profile of v5, /device:TPU:0, one launch (start us, length us, event | category | flops | bytes accessed | tf_op | source)
XLA Modules:
  0.0 291.7 jit_solution(2481500786346884091)
XLA Ops:
  3.8 3.0 %collective-permute-start.3 = (bf16[48,9344]{1,0:T(8,128)(2,1)S(1)}, bf16[48,9344]{1,0:T(8,128)(2,1)S(1)}, u32[]{:S(2)}, u32[]{:S(2)}) collective-permute-start(bf16[48,9344]{1,0:T(8,128)(2,1)S(1)} %get-tuple-element.189), channel_id=1, source_target_pairs={{0,4},{2,6},{4,0},{6,2},{8,12},{10,14},{12,8},{14,10},{16,20},{18,... | collective-permute-start | bytes 2691080 | tf_op jit(solution)/shard_map/ppermute | solution.py:91
  12.3 3.4 %collective-permute-done.refs_1_.refs_0_ = bf16[48,1664]{1,0:T(8,128)(2,1)S(1)} collective-permute-done((bf16[48,1664]{1,0:T(8,128)(2,1)S(1)}, bf16[48,1664]{1,0:T(8,128)(2,1)S(1)}, u32[]{:S(2)}, u32[]{:S(2)}) %collective-permute-start) | collective-permute-done | bytes 159776 | tf_op jit(solution)/shard_map/ppermute | solution.py:91
  15.7 5.4 %collective-permute-done.1.refs_2_.refs_1_ = bf16[48,1664]{1,0:T(8,128)(2,1)S(1)} collective-permute-done((bf16[48,1664]{1,0:T(8,128)(2,1)S(1)}, bf16[48,1664]{1,0:T(8,128)(2,1)S(1)}, u32[]{:S(2)}, u32[]{:S(2)}) %collective-permute-start.1) | collective-permute-done | bytes 159776 | tf_op jit(solution)/shard_map/ppermute | solution.py:91
  21.8 3.9 %collective-permute-start.5 = (bf16[48,3072]{1,0:T(8,128)(2,1)S(1)}, bf16[48,3072]{1,0:T(8,128)(2,1)S(1)}, u32[]{:S(2)}, u32[]{:S(2)}) collective-permute-start(bf16[48,3072]{1,0:T(8,128)(2,1)S(1)} %get-tuple-element.190.refs_0_), channel_id=1, source_target_pairs={{0,8},{2,10},{4,12},{6,14},{8,16},{10,18},{12,20},{14,22},{16,24},... | collective-permute-start | bytes 884744 | tf_op jit(solution)/shard_map/ppermute | solution.py:91
  25.8 11.1 %collective-permute-done.4.refs_1_ = bf16[3,48,1664]{2,1,0:T(8,128)(2,1)S(1)} collective-permute-done((bf16[3,48,1664]{2,1,0:T(8,128)(2,1)S(1)}, bf16[3,48,1664]{2,1,0:T(8,128)(2,1)S(1)}, u32[]{:S(2)}, u32[]{:S(2)}) %collective-permute-start.4) | collective-permute-done | bytes 479264 | tf_op jit(solution)/shard_map/ppermute | solution.py:91
  37.1 3.9 %collective-permute-start.8 = (bf16[48,3072]{1,0:T(8,128)(2,1)S(1)}, bf16[48,3072]{1,0:T(8,128)(2,1)S(1)}, u32[]{:S(2)}, u32[]{:S(2)}) collective-permute-start(bf16[48,3072]{1,0:T(8,128)(2,1)S(1)} %get-tuple-element.190.refs_0_), channel_id=1, source_target_pairs={{0,24},{2,26},{4,28},{6,30},{8,0},{10,2},{12,4},{14,6},{16,8},{18,... | collective-permute-start | bytes 884744 | tf_op jit(solution)/shard_map/ppermute | solution.py:91
  42.9 4.4 %shard_map.249 = (bf16[2,256,768]{2,1,0:T(8,128)(2,1)S(1)}, bf16[2,256,1152]{2,1,0:T(8,128)(2,1)S(1)}, bf16[2,6,256,256]{3,2,1,0:T(8,128)(2,1)S(1)}, bf16[2,256,384]{2,1,0:T(8,128)(2,1)S(1)}) custom-call(bf16[2,256,768]{2,1,0:T(8,128)(2,1)S(1)} %copy-done.13, s32[2,1,256]{2,1,0:T(1,128)S(1)} %reshape.140.seg_ref, ...), custom_call_target="tpu_custom_call" | custom-call | flops 25769803776 | bytes 201326592 | tf_op jit(solution)/shard_map/pallas_call | solution.py:286
  54.4 15.8 %collective-permute-done.10.refs_2_ = bf16[48,3072]{1,0:T(8,128)(2,1)S(1)} collective-permute-done((bf16[48,3072]{1,0:T(8,128)(2,1)S(1)}, bf16[48,3072]{1,0:T(8,128)(2,1)S(1)}, u32[]{:S(2)}, u32[]{:S(2)}) %collective-permute-start.10) | collective-permute-done | bytes 294944 | tf_op jit(solution)/shard_map/ppermute | solution.py:91
  71.8 7.7 %collective-permute-done.13.refs_2_.refs_3_ = bf16[48,4608]{1,0:T(8,128)(2,1)S(1)} collective-permute-done((bf16[48,4608]{1,0:T(8,128)(2,1)S(1)}, bf16[48,4608]{1,0:T(8,128)(2,1)S(1)}, u32[]{:S(2)}, u32[]{:S(2)}) %collective-permute-start.13) | collective-permute-done | bytes 442400 | tf_op jit(solution)/shard_map/ppermute | solution.py:91
  85.1 4.3 %shard_map.255 = (bf16[256,768]{1,0:T(8,128)(2,1)S(1)}, bf16[256,768]{1,0:T(8,128)(2,1)S(1)}, f32[2,256,768]{2,1,0:T(8,128)S(1)}, f32[2,256,1]{2,1,0:T(8,128)S(1...) custom-call(bf16[2,256,768]{2,1,0:T(8,128)(2,1)S(1)} %copy-done.13, ...), custom_call_target="tpu_custom_call" | custom-call | flops 38654705664 | bytes 335544320 | tf_op jit(solution)/shard_map/pallas_call | solution.py:360
  89.3 5.3 %collective-permute-done.19.refs_2_.refs_1_ = bf16[1,48,3072]{2,1,0:T(8,128)(2,1)S(1)} collective-permute-done((bf16[1,48,3072]{2,1,0:T(8,128)(2,1)S(1)}, bf16[1,48,3072]{2,1,0:T(8,128)(2,1)S(1)}, u32[]{:S(2)}, u32[]{:S(2)}) %collective-permute-start.19) | collective-permute-done | bytes 294944 | tf_op jit(solution)/shard_map/ppermute | solution.py:91
  98.8 8.0 %collective-permute-done.20.other_ref = bf16[256,768]{1,0:T(8,128)(2,1)S(1)} collective-permute-done((bf16[256,768]{1,0:T(8,128)(2,1)S(1)}, bf16[256,768]{1,0:T(8,128)(2,1)S(1)}, u32[]{:S(2)}, u32[]{:S(2)}) %collective-permute-start.20) | collective-permute-done | bytes 393248 | tf_op jit(solution)/shard_map/ppermute | solution.py:95
  110.0 8.5 %collective-permute-done.24.refs_1_ = bf16[3,48,3072]{2,1,0:T(8,128)(2,1)S(1)} collective-permute-done((bf16[3,48,3072]{2,1,0:T(8,128)(2,1)S(1)}, bf16[3,48,3072]{2,1,0:T(8,128)(2,1)S(1)}, u32[]{:S(2)}, u32[]{:S(2)}) %collective-permute-start.24) | collective-permute-done | bytes 884768 | tf_op jit(solution)/shard_map/ppermute | solution.py:91
  126.6 6.8 %collective-permute-done.29.other_ref = bf16[256,768]{1,0:T(8,128)(2,1)S(1)} collective-permute-done((bf16[256,768]{1,0:T(8,128)(2,1)S(1)}, bf16[256,768]{1,0:T(8,128)(2,1)S(1)}, u32[]{:S(2)}, u32[]{:S(2)}) %collective-permute-start.29) | collective-permute-done | bytes 393248 | tf_op jit(solution)/shard_map/ppermute | solution.py:95
  136.4 5.4 %collective-permute-done.27.other_ref = bf16[256,768]{1,0:T(8,128)(2,1)S(1)} collective-permute-done((bf16[256,768]{1,0:T(8,128)(2,1)S(1)}, bf16[256,768]{1,0:T(8,128)(2,1)S(1)}, u32[]{:S(2)}, u32[]{:S(2)}) %collective-permute-start.27) | collective-permute-done | bytes 393248 | tf_op jit(solution)/shard_map/ppermute | solution.py:95
  144.8 5.4 %collective-permute-done.30.other_ref = bf16[256,768]{1,0:T(8,128)(2,1)S(1)} collective-permute-done((bf16[256,768]{1,0:T(8,128)(2,1)S(1)}, bf16[256,768]{1,0:T(8,128)(2,1)S(1)}, u32[]{:S(2)}, u32[]{:S(2)}) %collective-permute-start.30) | collective-permute-done | bytes 393248 | tf_op jit(solution)/shard_map/ppermute | solution.py:95
  152.7 3.7 %shard_map.271 = (bf16[2,4,48,3072]{3,2,1,0:T(8,128)(2,1)S(1)}, bf16[2,4,48,3072]{3,2,1,0:T(8,128)(2,1)S(1)}) custom-call(bf16[256,768]{1,0:T(8,128)(2,1)S(1)} %get-tuple-element.217.refs_0_, bf16[256,768]{1,0:T(8,128)(2,1)S(1)} %get-tuple-element.221.refs_1_, bf16[256,1536]{1,0:T(8,128)(2,1)S(1)} %get-tuple-element.222.refs_2_, ...), custom_call_target="tpu_custom_call" | custom-call | flops 38654705664 | bytes 150994944 | tf_op jit(solution)/shard_map/pallas_call | solution.py:605
  158.2 3.4 %shard_map.272 = (bf16[256,768]{1,0:T(8,128)(2,1)S(1)}, f32[256,768]{1,0:T(8,128)S(1)}, bf16[256,768]{1,0:T(8,128)(2,1)S(1)}, bf16[256,1152]{1,0:T(8,128)(2,1)S(1)}, f32[8,768]{1,0:T(8,128)S(1)}) custom-call(f32[256,768]{1,0:T(8,128)S(1)} %get-tuple-element.232.res_ref, bf16[256,768]{1,0:T(8,128)(2,1)S(1)} %get-tuple-element.233.own_ref, ...), custom_call_target="tpu_custom_call" | custom-call | flops 25769803776 | bytes 150994944 | tf_op jit(solution)/shard_map/pallas_call | solution.py:515
  163.6 5.1 %collective-permute-done.33.other_ref = bf16[256,768]{1,0:T(8,128)(2,1)S(1)} collective-permute-done((bf16[256,768]{1,0:T(8,128)(2,1)S(1)}, bf16[256,768]{1,0:T(8,128)(2,1)S(1)}, u32[]{:S(2)}, u32[]{:S(2)}) %collective-permute-start.33) | collective-permute-done | bytes 393248 | tf_op jit(solution)/shard_map/ppermute | solution.py:95
  168.7 3.0 %shard_map.273 = (bf16[256,768]{1,0:T(8,128)(2,1)S(1)}, f32[256,768]{1,0:T(8,128)S(1)}, bf16[256,768]{1,0:T(8,128)(2,1)S(1)}, bf16[256,1152]{1,0:T(8,128)(2,1)S(1)}, f32[8,768]{1,0:T(8,128)S(1)}) custom-call(f32[256,768]{1,0:T(8,128)S(1)} %get-tuple-element.246.res_ref, bf16[256,768]{1,0:T(8,128)(2,1)S(1)} %get-tuple-element.247.own_ref, ...), custom_call_target="tpu_custom_call" | custom-call | flops 25769803776 | bytes 150994944 | tf_op jit(solution)/shard_map/pallas_call | solution.py:515
  187.9 3.7 %shard_map.277 = (bf16[2,4,48,3072]{3,2,1,0:T(8,128)(2,1)S(1)}, bf16[2,4,48,3072]{3,2,1,0:T(8,128)(2,1)S(1)}) custom-call(bf16[2,256,768]{2,1,0:T(8,128)(2,1)S(1)} %get-tuple-element.201.refs_0_.refs_1_, bf16[2,256,768]{2,1,0:T(8,128)(2,1)S(1)} %get-tuple-element.201.refs_0_.refs_1_, bf16[256,1536]{1,0:T(8,128)(2,1)S(1)} %get-tuple-element.259.refs_2_, ...), custom_call_target="tpu_custom_call" | custom-call | flops 38654705664 | bytes 188743680 | tf_op jit(solution)/shard_map/pallas_call | solution.py:605
  199.3 4.0 %collective-permute-done.45.other_ref = bf16[256,768]{1,0:T(8,128)(2,1)S(1)} collective-permute-done((bf16[256,768]{1,0:T(8,128)(2,1)S(1)}, bf16[256,768]{1,0:T(8,128)(2,1)S(1)}, u32[]{:S(2)}, u32[]{:S(2)}) %collective-permute-start.45) | collective-permute-done | bytes 393248 | tf_op jit(solution)/shard_map/ppermute | solution.py:95
  203.2 3.0 %shard_map.280 = (bf16[256,768]{1,0:T(8,128)(2,1)S(1)}, f32[256,768]{1,0:T(8,128)S(1)}, bf16[256,768]{1,0:T(8,128)(2,1)S(1)}, bf16[256,1152]{1,0:T(8,128)(2,1)S(1)}, f32[8,768]{1,0:T(8,128)S(1)}) custom-call(f32[256,768]{1,0:T(8,128)S(1)} %get-tuple-element.286.res_ref, bf16[256,768]{1,0:T(8,128)(2,1)S(1)} %get-tuple-element.287.own_ref, ...), custom_call_target="tpu_custom_call" | custom-call | flops 25769803776 | bytes 150994944 | tf_op jit(solution)/shard_map/pallas_call | solution.py:515
  218.5 3.4 %collective-permute-done.51.refs_1_ = bf16[48,1536]{1,0:T(8,128)(2,1)S(1)} collective-permute-done((bf16[48,1536]{1,0:T(8,128)(2,1)S(1)}, bf16[48,1536]{1,0:T(8,128)(2,1)S(1)}, u32[]{:S(2)}, u32[]{:S(2)}) %collective-permute-start.51) | collective-permute-done | bytes 147488 | tf_op jit(solution)/shard_map/ppermute | solution.py:91
  223.4 3.0 %collective-permute-done.52.refs_2_ = bf16[48,1536]{1,0:T(8,128)(2,1)S(1)} collective-permute-done((bf16[48,1536]{1,0:T(8,128)(2,1)S(1)}, bf16[48,1536]{1,0:T(8,128)(2,1)S(1)}, u32[]{:S(2)}, u32[]{:S(2)}) %collective-permute-start.52) | collective-permute-done | bytes 147488 | tf_op jit(solution)/shard_map/ppermute | solution.py:91
  230.2 15.1 %collective-permute-done.50.refs_2_ = bf16[48,3072]{1,0:T(8,128)(2,1)S(1)} collective-permute-done((bf16[48,3072]{1,0:T(8,128)(2,1)S(1)}, bf16[48,3072]{1,0:T(8,128)(2,1)S(1)}, u32[]{:S(2)}, u32[]{:S(2)}) %collective-permute-start.50) | collective-permute-done | bytes 294944 | tf_op jit(solution)/shard_map/ppermute | solution.py:91
  247.7 3.4 %collective-permute-start.58 = (bf16[48,1664]{1,0:T(8,128)(2,1)S(1)}, bf16[48,1664]{1,0:T(8,128)(2,1)S(1)}, u32[]{:S(2)}, u32[]{:S(2)}) collective-permute-start(bf16[48,1664]{1,0:T(8,128)(2,1)S(1)} %get-tuple-element.390), channel_id=1, source_target_pairs={{0,24},{2,26},{4,28},{6,30},{8,0},{10,2},{12,4},{14,6},{16,8},{18,... | collective-permute-start | bytes 479240 | tf_op jit(solution)/shard_map/ppermute | solution.py:91
  256.8 3.7 %collective-permute-done.39.refs_0_ = bf16[2,48,3072]{2,1,0:T(8,128)(2,1)S(1)} collective-permute-done((bf16[2,48,3072]{2,1,0:T(8,128)(2,1)S(1)}, bf16[2,48,3072]{2,1,0:T(8,128)(2,1)S(1)}, u32[]{:S(2)}, u32[]{:S(2)}) %collective-permute-start.39) | collective-permute-done | bytes 589856 | tf_op jit(solution)/shard_map/ppermute | solution.py:91
  261.7 3.1 %collective-permute-start.59 = (bf16[48,3072]{1,0:T(8,128)(2,1)S(1)}, bf16[48,3072]{1,0:T(8,128)(2,1)S(1)}, u32[]{:S(2)}, u32[]{:S(2)}) collective-permute-start(bf16[48,3072]{1,0:T(8,128)(2,1)S(1)} %fusion.12), channel_id=1, source_target_pairs={{0,8},{2,10},{4,12},{6,14},{8,16},{10,18},{12,20},{14,22},{16,24},... | collective-permute-start | bytes 884744 | tf_op jit(solution)/shard_map/ppermute | solution.py:91
  265.0 5.7 %collective-permute-done.59.refs_1_ = bf16[48,3072]{1,0:T(8,128)(2,1)S(1)} collective-permute-done((bf16[48,3072]{1,0:T(8,128)(2,1)S(1)}, bf16[48,3072]{1,0:T(8,128)(2,1)S(1)}, u32[]{:S(2)}, u32[]{:S(2)}) %collective-permute-start.59) | collective-permute-done | bytes 294944 | tf_op jit(solution)/shard_map/ppermute | solution.py:91
  280.1 3.0 %collective-permute-start.66 = (f32[8,128]{1,0:T(8,128)S(1)}, f32[8,128]{1,0:T(8,128)S(1)}, u32[]{:S(2)}, u32[]{:S(2)}) collective-permute-start(f32[8,128]{1,0:T(8,128)S(1)} %add_add_fusion.1), channel_id=1, source_target_pairs={{0,24},{1,25},{2,26},{3,27},{4,28},{5,29},{6,30},{7,31},{8,16},{9,... | collective-permute-start | bytes 12296 | tf_op jit(solution)/shard_map/ppermute | solution.py:840
  285.5 3.4 %shard_map.288 = (f32[2,1728,128]{2,1,0:T(8,128)}, f32[2,1728,128]{2,1,0:T(8,128)}, f32[2,1728,128]{2,1,0:T(8,128)}, bf16[2,1728,128]{2,1,0:T(8,128)(2,1)S(1)}) custom-call(f32[8,128]{1,0:T(8,128)S(1)} %add_add_fusion.q_ref.f_ref, f32[2,1728,128]{2,1,0:T(8,128)S(1)} %get-tuple-element.333.w_ref, f32[2,1728,128]{2,1,0:T(8,128)S(1)} %get-tuple-element.334.m_ref, ...), custom_call_target="tpu_custom_call" | custom-call | flops 8847360 | bytes 13271040 | tf_op jit(solution)/shard_map/pallas_call | solution.py:803
  (222 shorter events, 118.1 us)
Async XLA Ops:
  3.8 33.2 %collective-permute-start.3 = (bf16[48,9344]{1,0:T(8,128)(2,1)S(1)}, bf16[48,9344]{1,0:T(8,128)(2,1)S(1)}, u32[]{:S(2)}, u32[]{:S(2)}) collective-permute-start(bf16[48,9344]{1,0:T(8,128)(2,1)S(1)} %get-tuple-element.189), channel_id=1, source_target_pairs={{0,4},{2,6},{4,0},{6,2},{8,12},{10,14},{12,8},{14,10},{16,20},{18,... | collective-permute-start | bytes 2691080 | tf_op jit(solution)/shard_map/ppermute | solution.py:91
  21.2 15.8 %collective-permute-start.4 = (bf16[3,48,1664]{2,1,0:T(8,128)(2,1)S(1)}, bf16[3,48,1664]{2,1,0:T(8,128)(2,1)S(1)}, u32[]{:S(2)}, u32[]{:S(2)}) collective-permute-start(bf16[3,48,1664]{2,1,0:T(8,128)(2,1)S(1)} %shard_map.245), channel_id=1, source_target_pairs={{0,4},{2,6},{4,0},{6,2},{8,12},{10,14},{12,8},{14,10},{16,20},{18,... | collective-permute-start | bytes 1437704 | tf_op jit(solution)/shard_map/ppermute | solution.py:91
  21.8 15.2 %collective-permute-start.5 = (bf16[48,3072]{1,0:T(8,128)(2,1)S(1)}, bf16[48,3072]{1,0:T(8,128)(2,1)S(1)}, u32[]{:S(2)}, u32[]{:S(2)}) collective-permute-start(bf16[48,3072]{1,0:T(8,128)(2,1)S(1)} %get-tuple-element.190.refs_0_), channel_id=1, source_target_pairs={{0,8},{2,10},{4,12},{6,14},{8,16},{10,18},{12,20},{14,22},{16,24},... | collective-permute-start | bytes 884744 | tf_op jit(solution)/shard_map/ppermute | solution.py:91
  25.7 15.3 %collective-permute-start.6 = (bf16[4,48,1664]{2,1,0:T(8,128)(2,1)S(1)}, bf16[4,48,1664]{2,1,0:T(8,128)(2,1)S(1)}, u32[]{:S(2)}, u32[]{:S(2)}) collective-permute-start(bf16[4,48,1664]{2,1,0:T(8,128)(2,1)S(1)} %shard_map.244.refs_0_), channel_id=1, source_target_pairs={{0,2},{2,0},{4,6},{6,4},{8,10},{10,8},{12,14},{14,12},{16,18},{18,... | collective-permute-start | bytes 1916936 | tf_op jit(solution)/shard_map/ppermute | solution.py:91
  47.4 34.3 %collective-permute-start.15 = (bf16[2,256,768]{2,1,0:T(8,128)(2,1)S(1)}, bf16[2,256,768]{2,1,0:T(8,128)(2,1)S(1)}, u32[]{:S(2)}, u32[]{:S(2)}) collective-permute-start(bf16[2,256,768]{2,1,0:T(8,128)(2,1)S(1)} %get-tuple-element.194.own_ref), channel_id=1, source_target_pairs={{0,1},{1,0},{2,3},{3,2},{4,5},{5,4},{6,7},{7,6},{8,9},{9,8},{10,11... | collective-permute-start | bytes 2359304 | tf_op jit(solution)/shard_map/ppermute | solution.py:95
  49.0 22.7 %collective-permute-start.12 = (bf16[48,4608]{1,0:T(8,128)(2,1)S(1)}, bf16[48,4608]{1,0:T(8,128)(2,1)S(1)}, u32[]{:S(2)}, u32[]{:S(2)}) collective-permute-start(bf16[48,4608]{1,0:T(8,128)(2,1)S(1)} %get-tuple-element.196.refs_0_), channel_id=1, source_target_pairs={{0,8},{2,10},{4,12},{6,14},{8,16},{10,18},{12,20},{14,22},{16,24},... | collective-permute-start | bytes 1327112 | tf_op jit(solution)/shard_map/ppermute | solution.py:91
  49.0 21.2 %collective-permute-start.10 = (bf16[48,3072]{1,0:T(8,128)(2,1)S(1)}, bf16[48,3072]{1,0:T(8,128)(2,1)S(1)}, u32[]{:S(2)}, u32[]{:S(2)}) collective-permute-start(bf16[48,3072]{1,0:T(8,128)(2,1)S(1)} %collective-permute-done.5.refs_0_.refs_1_), channel_id=1, source_target_pairs={{0,8},{2,10},{4,12},{6,14},{8,16},{10,18},{12,20},{14,22},{16,24},... | collective-permute-start | bytes 884744 | tf_op jit(solution)/shard_map/ppermute | solution.py:91
  50.5 31.2 %collective-permute-start.9 = (bf16[2,48,3072]{2,1,0:T(8,128)(2,1)S(1)}, bf16[2,48,3072]{2,1,0:T(8,128)(2,1)S(1)}, u32[]{:S(2)}, u32[]{:S(2)}) collective-permute-start(bf16[2,48,3072]{2,1,0:T(8,128)(2,1)S(1)} %shard_map.250), channel_id=1, source_target_pairs={{0,4},{2,6},{4,0},{6,2},{8,12},{10,14},{12,8},{14,10},{16,20},{18,... | collective-permute-start | bytes 1769480 | tf_op jit(solution)/shard_map/ppermute | solution.py:91
  52.1 27.5 %collective-permute-start.13 = (bf16[48,4608]{1,0:T(8,128)(2,1)S(1)}, bf16[48,4608]{1,0:T(8,128)(2,1)S(1)}, u32[]{:S(2)}, u32[]{:S(2)}) collective-permute-start(bf16[48,4608]{1,0:T(8,128)(2,1)S(1)} %get-tuple-element.196.refs_0_), channel_id=1, source_target_pairs={{0,24},{2,26},{4,28},{6,30},{8,0},{10,2},{12,4},{14,6},{16,8},{18,... | collective-permute-start | bytes 1327112 | tf_op jit(solution)/shard_map/ppermute | solution.py:91
  83.7 14.8 %collective-permute-start.21 = (bf16[4,48,1536]{2,1,0:T(8,128)(2,1)S(1)}, bf16[4,48,1536]{2,1,0:T(8,128)(2,1)S(1)}, u32[]{:S(2)}, u32[]{:S(2)}) collective-permute-start(bf16[4,48,1536]{2,1,0:T(8,128)(2,1)S(1)} %shard_map.258.refs_0_), channel_id=1, source_target_pairs={{0,2},{2,0},{4,6},{6,4},{8,10},{10,8},{12,14},{14,12},{16,18},{18,... | collective-permute-start | bytes 1769480 | tf_op jit(solution)/shard_map/ppermute | solution.py:91
  95.5 23.2 %collective-permute-start.28 = (bf16[256,768]{1,0:T(8,128)(2,1)S(1)}, bf16[256,768]{1,0:T(8,128)(2,1)S(1)}, u32[]{:S(2)}, u32[]{:S(2)}) collective-permute-start(bf16[256,768]{1,0:T(8,128)(2,1)S(1)} %get-tuple-element.218.own_ref), channel_id=1, source_target_pairs={{0,1},{1,0},{2,3},{3,2},{4,5},{5,4},{6,7},{7,6},{8,9},{9,8},{10,11... | collective-permute-start | bytes 1179656 | tf_op jit(solution)/shard_map/ppermute | solution.py:95
  97.1 21.4 %collective-permute-start.24 = (bf16[3,48,3072]{2,1,0:T(8,128)(2,1)S(1)}, bf16[3,48,3072]{2,1,0:T(8,128)(2,1)S(1)}, u32[]{:S(2)}, u32[]{:S(2)}) collective-permute-start(bf16[3,48,3072]{2,1,0:T(8,128)(2,1)S(1)} %shard_map.263), channel_id=1, source_target_pairs={{0,4},{2,6},{4,0},{6,2},{8,12},{10,14},{12,8},{14,10},{16,20},{18,... | collective-permute-start | bytes 2654216 | tf_op jit(solution)/shard_map/ppermute | solution.py:91
  98.6 23.4 %collective-permute-start.25 = (bf16[4,48,3072]{2,1,0:T(8,128)(2,1)S(1)}, bf16[4,48,3072]{2,1,0:T(8,128)(2,1)S(1)}, u32[]{:S(2)}, u32[]{:S(2)}) collective-permute-start(bf16[4,48,3072]{2,1,0:T(8,128)(2,1)S(1)} %shard_map.262.refs_0_), channel_id=1, source_target_pairs={{0,2},{2,0},{4,6},{6,4},{8,10},{10,8},{12,14},{14,12},{16,18},{18,... | collective-permute-start | bytes 3538952 | tf_op jit(solution)/shard_map/ppermute | solution.py:91
  125.9 15.9 %collective-permute-start.27 = (bf16[256,768]{1,0:T(8,128)(2,1)S(1)}, bf16[256,768]{1,0:T(8,128)(2,1)S(1)}, u32[]{:S(2)}, u32[]{:S(2)}) collective-permute-start(bf16[256,768]{1,0:T(8,128)(2,1)S(1)} %get-tuple-element.214.own_ref), channel_id=1, source_target_pairs={{0,1},{1,0},{2,3},{3,2},{4,5},{5,4},{6,7},{7,6},{8,9},{9,8},{10,11... | collective-permute-start | bytes 1179656 | tf_op jit(solution)/shard_map/ppermute | solution.py:95
  135.8 14.4 %collective-permute-start.30 = (bf16[256,768]{1,0:T(8,128)(2,1)S(1)}, bf16[256,768]{1,0:T(8,128)(2,1)S(1)}, u32[]{:S(2)}, u32[]{:S(2)}) collective-permute-start(bf16[256,768]{1,0:T(8,128)(2,1)S(1)} %get-tuple-element.224.own_ref), channel_id=1, source_target_pairs={{0,1},{1,0},{2,3},{3,2},{4,5},{5,4},{6,7},{7,6},{8,9},{9,8},{10,11... | collective-permute-start | bytes 1179656 | tf_op jit(solution)/shard_map/ppermute | solution.py:95
  161.6 15.0 %collective-permute-start.34 = (bf16[256,768]{1,0:T(8,128)(2,1)S(1)}, bf16[256,768]{1,0:T(8,128)(2,1)S(1)}, u32[]{:S(2)}, u32[]{:S(2)}) collective-permute-start(bf16[256,768]{1,0:T(8,128)(2,1)S(1)} %get-tuple-element.244.own_ref), channel_id=1, source_target_pairs={{0,1},{1,0},{2,3},{3,2},{4,5},{5,4},{6,7},{7,6},{8,9},{9,8},{10,11... | collective-permute-start | bytes 1179656 | tf_op jit(solution)/shard_map/ppermute | solution.py:95
  163.6 16.9 %collective-permute-start.35 = (bf16[2,48,3072]{2,1,0:T(8,128)(2,1)S(1)}, bf16[2,48,3072]{2,1,0:T(8,128)(2,1)S(1)}, u32[]{:S(2)}, u32[]{:S(2)}) collective-permute-start(bf16[2,48,3072]{2,1,0:T(8,128)(2,1)S(1)} %get-tuple-element.387), channel_id=1, source_target_pairs={{0,8},{2,10},{4,12},{6,14},{8,16},{10,18},{12,20},{14,22},{16,24},... | collective-permute-start | bytes 1769480 | tf_op jit(solution)/shard_map/ppermute | solution.py:91
  178.9 14.8 %collective-permute-start.41 = (bf16[256,768]{1,0:T(8,128)(2,1)S(1)}, bf16[256,768]{1,0:T(8,128)(2,1)S(1)}, u32[]{:S(2)}, u32[]{:S(2)}) collective-permute-start(bf16[256,768]{1,0:T(8,128)(2,1)S(1)} %get-tuple-element.261.own_ref), channel_id=1, source_target_pairs={{0,1},{1,0},{2,3},{3,2},{4,5},{5,4},{6,7},{7,6},{8,9},{9,8},{10,11... | collective-permute-start | bytes 1179656 | tf_op jit(solution)/shard_map/ppermute | solution.py:95
  180.8 16.3 %collective-permute-start.40 = (bf16[2,48,3072]{2,1,0:T(8,128)(2,1)S(1)}, bf16[2,48,3072]{2,1,0:T(8,128)(2,1)S(1)}, u32[]{:S(2)}, u32[]{:S(2)}) collective-permute-start(bf16[2,48,3072]{2,1,0:T(8,128)(2,1)S(1)} %fusion.2), channel_id=1, source_target_pairs={{0,8},{2,10},{4,12},{6,14},{8,16},{10,18},{12,20},{14,22},{16,24},... | collective-permute-start | bytes 1769480 | tf_op jit(solution)/shard_map/ppermute | solution.py:91
  181.2 25.1 %collective-permute-start.44 = (bf16[4,48,1536]{2,1,0:T(8,128)(2,1)S(1)}, bf16[4,48,1536]{2,1,0:T(8,128)(2,1)S(1)}, u32[]{:S(2)}, u32[]{:S(2)}) collective-permute-start(bf16[4,48,1536]{2,1,0:T(8,128)(2,1)S(1)} %fusion.7), channel_id=1, source_target_pairs={{0,4},{2,6},{4,0},{6,2},{8,12},{10,14},{12,8},{14,10},{16,20},{18,... | collective-permute-start | bytes 1769480 | tf_op jit(solution)/shard_map/ppermute | solution.py:91
  197.3 19.1 %collective-permute-start.42 = (bf16[2,48,3072]{2,1,0:T(8,128)(2,1)S(1)}, bf16[2,48,3072]{2,1,0:T(8,128)(2,1)S(1)}, u32[]{:S(2)}, u32[]{:S(2)}) collective-permute-start(bf16[2,48,3072]{2,1,0:T(8,128)(2,1)S(1)} %fusion.1), channel_id=1, source_target_pairs={{0,8},{2,10},{4,12},{6,14},{8,16},{10,18},{12,20},{14,22},{16,24},... | collective-permute-start | bytes 1769480 | tf_op jit(solution)/shard_map/ppermute | solution.py:91
  197.7 14.6 %collective-permute-start.48 = (bf16[2,48,3072]{2,1,0:T(8,128)(2,1)S(1)}, bf16[2,48,3072]{2,1,0:T(8,128)(2,1)S(1)}, u32[]{:S(2)}, u32[]{:S(2)}) collective-permute-start(bf16[2,48,3072]{2,1,0:T(8,128)(2,1)S(1)} %get-tuple-element.384), channel_id=1, source_target_pairs={{0,4},{2,6},{4,0},{6,2},{8,12},{10,14},{12,8},{14,10},{16,20},{18,... | collective-permute-start | bytes 1769480 | tf_op jit(solution)/shard_map/ppermute | solution.py:91
  206.5 20.6 %collective-permute-start.53 = (bf16[48,1536]{1,0:T(8,128)(2,1)S(1)}, bf16[48,1536]{1,0:T(8,128)(2,1)S(1)}, u32[]{:S(2)}, u32[]{:S(2)}) collective-permute-start(bf16[48,1536]{1,0:T(8,128)(2,1)S(1)} %get-tuple-element.395), channel_id=1, source_target_pairs={{0,24},{2,26},{4,28},{6,30},{8,0},{10,2},{12,4},{14,6},{16,8},{18,... | collective-permute-start | bytes 442376 | tf_op jit(solution)/shard_map/ppermute | solution.py:91
  212.3 14.1 %collective-permute-start.52 = (bf16[48,1536]{1,0:T(8,128)(2,1)S(1)}, bf16[48,1536]{1,0:T(8,128)(2,1)S(1)}, u32[]{:S(2)}, u32[]{:S(2)}) collective-permute-start(bf16[48,1536]{1,0:T(8,128)(2,1)S(1)} %get-tuple-element.393), channel_id=1, source_target_pairs={{0,16},{2,18},{4,20},{6,22},{8,24},{10,26},{12,28},{14,30},{16,0},... | collective-permute-start | bytes 442376 | tf_op jit(solution)/shard_map/ppermute | solution.py:91
  213.2 16.3 %collective-permute-start.49 = (bf16[48,3072]{1,0:T(8,128)(2,1)S(1)}, bf16[48,3072]{1,0:T(8,128)(2,1)S(1)}, u32[]{:S(2)}, u32[]{:S(2)}) collective-permute-start(bf16[48,3072]{1,0:T(8,128)(2,1)S(1)} %get-tuple-element.389), channel_id=1, source_target_pairs={{0,24},{2,26},{4,28},{6,30},{8,0},{10,2},{12,4},{14,6},{16,8},{18,... | collective-permute-start | bytes 884744 | tf_op jit(solution)/shard_map/ppermute | solution.py:91
  216.4 28.9 %collective-permute-start.50 = (bf16[48,3072]{1,0:T(8,128)(2,1)S(1)}, bf16[48,3072]{1,0:T(8,128)(2,1)S(1)}, u32[]{:S(2)}, u32[]{:S(2)}) collective-permute-start(bf16[48,3072]{1,0:T(8,128)(2,1)S(1)} %get-tuple-element.388), channel_id=1, source_target_pairs={{0,16},{2,18},{4,20},{6,22},{8,24},{10,26},{12,28},{14,30},{16,0},... | collective-permute-start | bytes 884744 | tf_op jit(solution)/shard_map/ppermute | solution.py:91
  221.8 24.9 %collective-permute-start.47 = (bf16[4,48,1664]{2,1,0:T(8,128)(2,1)S(1)}, bf16[4,48,1664]{2,1,0:T(8,128)(2,1)S(1)}, u32[]{:S(2)}, u32[]{:S(2)}) collective-permute-start(bf16[4,48,1664]{2,1,0:T(8,128)(2,1)S(1)} %fusion.5), channel_id=1, source_target_pairs={{0,4},{2,6},{4,0},{6,2},{8,12},{10,14},{12,8},{14,10},{16,20},{18,... | collective-permute-start | bytes 1916936 | tf_op jit(solution)/shard_map/ppermute | solution.py:91
  226.4 20.7 %collective-permute-start.54 = (bf16[256,768]{1,0:T(8,128)(2,1)S(1)}, bf16[256,768]{1,0:T(8,128)(2,1)S(1)}, u32[]{:S(2)}, u32[]{:S(2)}) collective-permute-start(bf16[256,768]{1,0:T(8,128)(2,1)S(1)} %get-tuple-element.280.refs_1_), channel_id=1, source_target_pairs={{0,1},{1,0},{2,3},{3,2},{4,5},{5,4},{6,7},{7,6},{8,9},{9,8},{10,11... | collective-permute-start | bytes 1179656 | tf_op jit(solution)/shard_map/ppermute | solution.py:95
  227.0 20.7 %collective-permute-start.43 = (bf16[48,3072]{1,0:T(8,128)(2,1)S(1)}, bf16[48,3072]{1,0:T(8,128)(2,1)S(1)}, u32[]{:S(2)}, u32[]{:S(2)}) collective-permute-start(bf16[48,3072]{1,0:T(8,128)(2,1)S(1)} %fusion.13), channel_id=1, source_target_pairs={{0,4},{2,6},{4,0},{6,2},{8,12},{10,14},{12,8},{14,10},{16,20},{18,... | collective-permute-start | bytes 884744 | tf_op jit(solution)/shard_map/ppermute | solution.py:91
  229.6 25.7 %collective-permute-start.55 = (bf16[256,768]{1,0:T(8,128)(2,1)S(1)}, bf16[256,768]{1,0:T(8,128)(2,1)S(1)}, u32[]{:S(2)}, u32[]{:S(2)}) collective-permute-start(bf16[256,768]{1,0:T(8,128)(2,1)S(1)} %get-tuple-element.288.refs_4_), channel_id=1, source_target_pairs={{0,1},{1,0},{2,3},{3,2},{4,5},{5,4},{6,7},{7,6},{8,9},{9,8},{10,11... | collective-permute-start | bytes 1179656 | tf_op jit(solution)/shard_map/ppermute | solution.py:95
  245.3 15.2 %collective-permute-start.39 = (bf16[2,48,3072]{2,1,0:T(8,128)(2,1)S(1)}, bf16[2,48,3072]{2,1,0:T(8,128)(2,1)S(1)}, u32[]{:S(2)}, u32[]{:S(2)}) collective-permute-start(bf16[2,48,3072]{2,1,0:T(8,128)(2,1)S(1)} %get-tuple-element.385), channel_id=1, source_target_pairs={{0,4},{2,6},{4,0},{6,2},{8,12},{10,14},{12,8},{14,10},{16,20},{18,... | collective-permute-start | bytes 1769480 | tf_op jit(solution)/shard_map/ppermute | solution.py:91
  247.1 14.5 %collective-permute-start.57 = (bf16[48,1664]{1,0:T(8,128)(2,1)S(1)}, bf16[48,1664]{1,0:T(8,128)(2,1)S(1)}, u32[]{:S(2)}, u32[]{:S(2)}) collective-permute-start(bf16[48,1664]{1,0:T(8,128)(2,1)S(1)} %get-tuple-element.391), channel_id=1, source_target_pairs={{0,16},{2,18},{4,20},{6,22},{8,24},{10,26},{12,28},{14,30},{16,0},... | collective-permute-start | bytes 479240 | tf_op jit(solution)/shard_map/ppermute | solution.py:91
  (58 other events, 419.3 us)

commit v6 on v5

--- a/solution.py
+++ b/solution.py
@@ -738,7 +738,6 @@
                 grad = turned[6 * layer + kind : 6 * layer + kind + 1, :rows] * scale
                 new = adamw(rw[kind, at], rm[kind, at], rv[kind, at], grad, vector_rate, 0.0)
                 rwo[kind, at], rmo[kind, at], rvo[kind, at] = new
-                rlo[kind, at] = new[0].astype(b16)
                 if kind == 0:
                     go[at] = grad
         row = lax.broadcasted_iota(jnp.int32, (rows, per), 0)
@@ -758,7 +757,8 @@
             grad = jnp.where(phase == 0, one, jnp.where(phase == 1, two, three)) * scale
             new = adamw(sw[layer], sm[layer], sv[layer], grad, vector_rate, 0.0)
             swo[layer], smo[layer], svo[layer] = new
-            slo[layer] = new[0].astype(b16)
+        rlo[...] = rwo[...].astype(b16)
+        slo[...] = swo[...].astype(b16)
 
     rep, split = reps[0].shape, splits[0].shape
     return call(

time: 297 us -> 297 us (level)
  no operation moved by 1% of the time
where the time goes in v6:
time: 297 us; the launch traced here: 292 us
  waiting for transfers between devices  145 us (49%)
  starting transfers between devices  70 us (24%)
  Pallas kernels  61.9 us (21%)
  local copies, waits for them, and re-layouts  8.69 us (3%)
  other arithmetic  4.15 us (1%)
    ppermute x45, waiting for transfers between devices, move(): return lax.ppermute(a, 'dp', pairs_of(lax.axis_size('dp'), kind))  95.7 us
    ppermute x45, starting transfers between devices, move(): return lax.ppermute(a, 'dp', pairs_of(lax.axis_size('dp'), kind))  51.1 us
    ppermute x15, waiting for transfers between devices, exchange(): return lax.ppermute(a, 'tensor', [(0, 1), (1, 0)])  43.1 us
    pallas_call x4, Pallas kernels, attention_back(): call(body, [((SEQ, D), b16), ((SEQ, D), f32), ((SEQ, D), b16), ((SEQ, QKV...  12.4 us
    pallas_call x4, Pallas kernels, matrix_gradient(): call(body, outs, specs, [pltpu.VMEM((D, step), f32)], flops=2 * MICRO * S...  11.8 us
    ppermute x15, starting transfers between devices, exchange(): return lax.ppermute(a, 'tensor', [(0, 1), (1, 0)])  11 us
    ppermute x7, starting transfers between devices, ppermute_bits(): lax.ppermute(value, ('dp', 'tensor'), [(i, i ^ bits) for i in range(n)])  7.95 us
    unnamed x49, local copies, waits for them, and re-layouts  6.95 us
  transfers between devices with their start and end apart: 67, of which 36 were waited for; matrix products, arithmetic and copies ran while one was open for 2% of the time, Pallas kernels for 20%

profile of v6, /device:TPU:0, one launch (start us, length us, event | category | flops | bytes accessed | tf_op | source)
XLA Modules:
  0.0 291.7 jit_solution(923543942586653728)
XLA Ops:
  3.8 3.0 %collective-permute-start.3 = (bf16[48,9344]{1,0:T(8,128)(2,1)S(1)}, bf16[48,9344]{1,0:T(8,128)(2,1)S(1)}, u32[]{:S(2)}, u32[]{:S(2)}) collective-permute-start(bf16[48,9344]{1,0:T(8,128)(2,1)S(1)} %get-tuple-element.189), channel_id=1, source_target_pairs={{0,4},{2,6},{4,0},{6,2},{8,12},{10,14},{12,8},{14,10},{16,20},{18,... | collective-permute-start | bytes 2691080 | tf_op jit(solution)/shard_map/ppermute | solution.py:91
  12.3 3.4 %collective-permute-done.refs_1_.refs_0_ = bf16[48,1664]{1,0:T(8,128)(2,1)S(1)} collective-permute-done((bf16[48,1664]{1,0:T(8,128)(2,1)S(1)}, bf16[48,1664]{1,0:T(8,128)(2,1)S(1)}, u32[]{:S(2)}, u32[]{:S(2)}) %collective-permute-start) | collective-permute-done | bytes 159776 | tf_op jit(solution)/shard_map/ppermute | solution.py:91
  15.7 5.4 %collective-permute-done.1.refs_2_.refs_1_ = bf16[48,1664]{1,0:T(8,128)(2,1)S(1)} collective-permute-done((bf16[48,1664]{1,0:T(8,128)(2,1)S(1)}, bf16[48,1664]{1,0:T(8,128)(2,1)S(1)}, u32[]{:S(2)}, u32[]{:S(2)}) %collective-permute-start.1) | collective-permute-done | bytes 159776 | tf_op jit(solution)/shard_map/ppermute | solution.py:91
  21.8 3.9 %collective-permute-start.5 = (bf16[48,3072]{1,0:T(8,128)(2,1)S(1)}, bf16[48,3072]{1,0:T(8,128)(2,1)S(1)}, u32[]{:S(2)}, u32[]{:S(2)}) collective-permute-start(bf16[48,3072]{1,0:T(8,128)(2,1)S(1)} %get-tuple-element.190.refs_0_), channel_id=1, source_target_pairs={{0,8},{2,10},{4,12},{6,14},{8,16},{10,18},{12,20},{14,22},{16,24},... | collective-permute-start | bytes 884744 | tf_op jit(solution)/shard_map/ppermute | solution.py:91
  25.8 11.1 %collective-permute-done.4.refs_1_ = bf16[3,48,1664]{2,1,0:T(8,128)(2,1)S(1)} collective-permute-done((bf16[3,48,1664]{2,1,0:T(8,128)(2,1)S(1)}, bf16[3,48,1664]{2,1,0:T(8,128)(2,1)S(1)}, u32[]{:S(2)}, u32[]{:S(2)}) %collective-permute-start.4) | collective-permute-done | bytes 479264 | tf_op jit(solution)/shard_map/ppermute | solution.py:91
  37.1 3.9 %collective-permute-start.8 = (bf16[48,3072]{1,0:T(8,128)(2,1)S(1)}, bf16[48,3072]{1,0:T(8,128)(2,1)S(1)}, u32[]{:S(2)}, u32[]{:S(2)}) collective-permute-start(bf16[48,3072]{1,0:T(8,128)(2,1)S(1)} %get-tuple-element.190.refs_0_), channel_id=1, source_target_pairs={{0,24},{2,26},{4,28},{6,30},{8,0},{10,2},{12,4},{14,6},{16,8},{18,... | collective-permute-start | bytes 884744 | tf_op jit(solution)/shard_map/ppermute | solution.py:91
  42.9 4.4 %shard_map.249 = (bf16[2,256,768]{2,1,0:T(8,128)(2,1)S(1)}, bf16[2,256,1152]{2,1,0:T(8,128)(2,1)S(1)}, bf16[2,6,256,256]{3,2,1,0:T(8,128)(2,1)S(1)}, bf16[2,256,384]{2,1,0:T(8,128)(2,1)S(1)}) custom-call(bf16[2,256,768]{2,1,0:T(8,128)(2,1)S(1)} %copy-done.13, s32[2,1,256]{2,1,0:T(1,128)S(1)} %reshape.140.seg_ref, ...), custom_call_target="tpu_custom_call" | custom-call | flops 25769803776 | bytes 201326592 | tf_op jit(solution)/shard_map/pallas_call | solution.py:286
  54.4 15.8 %collective-permute-done.10.refs_2_ = bf16[48,3072]{1,0:T(8,128)(2,1)S(1)} collective-permute-done((bf16[48,3072]{1,0:T(8,128)(2,1)S(1)}, bf16[48,3072]{1,0:T(8,128)(2,1)S(1)}, u32[]{:S(2)}, u32[]{:S(2)}) %collective-permute-start.10) | collective-permute-done | bytes 294944 | tf_op jit(solution)/shard_map/ppermute | solution.py:91
  71.8 7.7 %collective-permute-done.13.refs_2_.refs_3_ = bf16[48,4608]{1,0:T(8,128)(2,1)S(1)} collective-permute-done((bf16[48,4608]{1,0:T(8,128)(2,1)S(1)}, bf16[48,4608]{1,0:T(8,128)(2,1)S(1)}, u32[]{:S(2)}, u32[]{:S(2)}) %collective-permute-start.13) | collective-permute-done | bytes 442400 | tf_op jit(solution)/shard_map/ppermute | solution.py:91
  85.1 4.3 %shard_map.255 = (bf16[256,768]{1,0:T(8,128)(2,1)S(1)}, bf16[256,768]{1,0:T(8,128)(2,1)S(1)}, f32[2,256,768]{2,1,0:T(8,128)S(1)}, f32[2,256,1]{2,1,0:T(8,128)S(1...) custom-call(bf16[2,256,768]{2,1,0:T(8,128)(2,1)S(1)} %copy-done.13, ...), custom_call_target="tpu_custom_call" | custom-call | flops 38654705664 | bytes 335544320 | tf_op jit(solution)/shard_map/pallas_call | solution.py:360
  89.3 5.3 %collective-permute-done.19.refs_2_.refs_1_ = bf16[1,48,3072]{2,1,0:T(8,128)(2,1)S(1)} collective-permute-done((bf16[1,48,3072]{2,1,0:T(8,128)(2,1)S(1)}, bf16[1,48,3072]{2,1,0:T(8,128)(2,1)S(1)}, u32[]{:S(2)}, u32[]{:S(2)}) %collective-permute-start.19) | collective-permute-done | bytes 294944 | tf_op jit(solution)/shard_map/ppermute | solution.py:91
  98.8 8.0 %collective-permute-done.20.other_ref = bf16[256,768]{1,0:T(8,128)(2,1)S(1)} collective-permute-done((bf16[256,768]{1,0:T(8,128)(2,1)S(1)}, bf16[256,768]{1,0:T(8,128)(2,1)S(1)}, u32[]{:S(2)}, u32[]{:S(2)}) %collective-permute-start.20) | collective-permute-done | bytes 393248 | tf_op jit(solution)/shard_map/ppermute | solution.py:95
  110.0 8.5 %collective-permute-done.24.refs_1_ = bf16[3,48,3072]{2,1,0:T(8,128)(2,1)S(1)} collective-permute-done((bf16[3,48,3072]{2,1,0:T(8,128)(2,1)S(1)}, bf16[3,48,3072]{2,1,0:T(8,128)(2,1)S(1)}, u32[]{:S(2)}, u32[]{:S(2)}) %collective-permute-start.24) | collective-permute-done | bytes 884768 | tf_op jit(solution)/shard_map/ppermute | solution.py:91
  126.6 6.8 %collective-permute-done.29.other_ref = bf16[256,768]{1,0:T(8,128)(2,1)S(1)} collective-permute-done((bf16[256,768]{1,0:T(8,128)(2,1)S(1)}, bf16[256,768]{1,0:T(8,128)(2,1)S(1)}, u32[]{:S(2)}, u32[]{:S(2)}) %collective-permute-start.29) | collective-permute-done | bytes 393248 | tf_op jit(solution)/shard_map/ppermute | solution.py:95
  136.4 5.4 %collective-permute-done.27.other_ref = bf16[256,768]{1,0:T(8,128)(2,1)S(1)} collective-permute-done((bf16[256,768]{1,0:T(8,128)(2,1)S(1)}, bf16[256,768]{1,0:T(8,128)(2,1)S(1)}, u32[]{:S(2)}, u32[]{:S(2)}) %collective-permute-start.27) | collective-permute-done | bytes 393248 | tf_op jit(solution)/shard_map/ppermute | solution.py:95
  144.8 5.4 %collective-permute-done.30.other_ref = bf16[256,768]{1,0:T(8,128)(2,1)S(1)} collective-permute-done((bf16[256,768]{1,0:T(8,128)(2,1)S(1)}, bf16[256,768]{1,0:T(8,128)(2,1)S(1)}, u32[]{:S(2)}, u32[]{:S(2)}) %collective-permute-start.30) | collective-permute-done | bytes 393248 | tf_op jit(solution)/shard_map/ppermute | solution.py:95
  152.7 3.7 %shard_map.271 = (bf16[2,4,48,3072]{3,2,1,0:T(8,128)(2,1)S(1)}, bf16[2,4,48,3072]{3,2,1,0:T(8,128)(2,1)S(1)}) custom-call(bf16[256,768]{1,0:T(8,128)(2,1)S(1)} %get-tuple-element.217.refs_0_, bf16[256,768]{1,0:T(8,128)(2,1)S(1)} %get-tuple-element.221.refs_1_, bf16[256,1536]{1,0:T(8,128)(2,1)S(1)} %get-tuple-element.222.refs_2_, ...), custom_call_target="tpu_custom_call" | custom-call | flops 38654705664 | bytes 150994944 | tf_op jit(solution)/shard_map/pallas_call | solution.py:605
  158.2 3.4 %shard_map.272 = (bf16[256,768]{1,0:T(8,128)(2,1)S(1)}, f32[256,768]{1,0:T(8,128)S(1)}, bf16[256,768]{1,0:T(8,128)(2,1)S(1)}, bf16[256,1152]{1,0:T(8,128)(2,1)S(1)}, f32[8,768]{1,0:T(8,128)S(1)}) custom-call(f32[256,768]{1,0:T(8,128)S(1)} %get-tuple-element.232.res_ref, bf16[256,768]{1,0:T(8,128)(2,1)S(1)} %get-tuple-element.233.own_ref, ...), custom_call_target="tpu_custom_call" | custom-call | flops 25769803776 | bytes 150994944 | tf_op jit(solution)/shard_map/pallas_call | solution.py:515
  163.6 5.1 %collective-permute-done.33.other_ref = bf16[256,768]{1,0:T(8,128)(2,1)S(1)} collective-permute-done((bf16[256,768]{1,0:T(8,128)(2,1)S(1)}, bf16[256,768]{1,0:T(8,128)(2,1)S(1)}, u32[]{:S(2)}, u32[]{:S(2)}) %collective-permute-start.33) | collective-permute-done | bytes 393248 | tf_op jit(solution)/shard_map/ppermute | solution.py:95
  168.7 3.0 %shard_map.273 = (bf16[256,768]{1,0:T(8,128)(2,1)S(1)}, f32[256,768]{1,0:T(8,128)S(1)}, bf16[256,768]{1,0:T(8,128)(2,1)S(1)}, bf16[256,1152]{1,0:T(8,128)(2,1)S(1)}, f32[8,768]{1,0:T(8,128)S(1)}) custom-call(f32[256,768]{1,0:T(8,128)S(1)} %get-tuple-element.246.res_ref, bf16[256,768]{1,0:T(8,128)(2,1)S(1)} %get-tuple-element.247.own_ref, ...), custom_call_target="tpu_custom_call" | custom-call | flops 25769803776 | bytes 150994944 | tf_op jit(solution)/shard_map/pallas_call | solution.py:515
  187.9 3.7 %shard_map.277 = (bf16[2,4,48,3072]{3,2,1,0:T(8,128)(2,1)S(1)}, bf16[2,4,48,3072]{3,2,1,0:T(8,128)(2,1)S(1)}) custom-call(bf16[2,256,768]{2,1,0:T(8,128)(2,1)S(1)} %get-tuple-element.201.refs_0_.refs_1_, bf16[2,256,768]{2,1,0:T(8,128)(2,1)S(1)} %get-tuple-element.201.refs_0_.refs_1_, bf16[256,1536]{1,0:T(8,128)(2,1)S(1)} %get-tuple-element.259.refs_2_, ...), custom_call_target="tpu_custom_call" | custom-call | flops 38654705664 | bytes 188743680 | tf_op jit(solution)/shard_map/pallas_call | solution.py:605
  199.3 4.0 %collective-permute-done.45.other_ref = bf16[256,768]{1,0:T(8,128)(2,1)S(1)} collective-permute-done((bf16[256,768]{1,0:T(8,128)(2,1)S(1)}, bf16[256,768]{1,0:T(8,128)(2,1)S(1)}, u32[]{:S(2)}, u32[]{:S(2)}) %collective-permute-start.45) | collective-permute-done | bytes 393248 | tf_op jit(solution)/shard_map/ppermute | solution.py:95
  203.2 3.0 %shard_map.280 = (bf16[256,768]{1,0:T(8,128)(2,1)S(1)}, f32[256,768]{1,0:T(8,128)S(1)}, bf16[256,768]{1,0:T(8,128)(2,1)S(1)}, bf16[256,1152]{1,0:T(8,128)(2,1)S(1)}, f32[8,768]{1,0:T(8,128)S(1)}) custom-call(f32[256,768]{1,0:T(8,128)S(1)} %get-tuple-element.286.res_ref, bf16[256,768]{1,0:T(8,128)(2,1)S(1)} %get-tuple-element.287.own_ref, ...), custom_call_target="tpu_custom_call" | custom-call | flops 25769803776 | bytes 150994944 | tf_op jit(solution)/shard_map/pallas_call | solution.py:515
  218.5 3.4 %collective-permute-done.51.refs_1_ = bf16[48,1536]{1,0:T(8,128)(2,1)S(1)} collective-permute-done((bf16[48,1536]{1,0:T(8,128)(2,1)S(1)}, bf16[48,1536]{1,0:T(8,128)(2,1)S(1)}, u32[]{:S(2)}, u32[]{:S(2)}) %collective-permute-start.51) | collective-permute-done | bytes 147488 | tf_op jit(solution)/shard_map/ppermute | solution.py:91
  223.4 3.0 %collective-permute-done.52.refs_2_ = bf16[48,1536]{1,0:T(8,128)(2,1)S(1)} collective-permute-done((bf16[48,1536]{1,0:T(8,128)(2,1)S(1)}, bf16[48,1536]{1,0:T(8,128)(2,1)S(1)}, u32[]{:S(2)}, u32[]{:S(2)}) %collective-permute-start.52) | collective-permute-done | bytes 147488 | tf_op jit(solution)/shard_map/ppermute | solution.py:91
  230.2 15.1 %collective-permute-done.50.refs_2_ = bf16[48,3072]{1,0:T(8,128)(2,1)S(1)} collective-permute-done((bf16[48,3072]{1,0:T(8,128)(2,1)S(1)}, bf16[48,3072]{1,0:T(8,128)(2,1)S(1)}, u32[]{:S(2)}, u32[]{:S(2)}) %collective-permute-start.50) | collective-permute-done | bytes 294944 | tf_op jit(solution)/shard_map/ppermute | solution.py:91
  247.7 3.4 %collective-permute-start.58 = (bf16[48,1664]{1,0:T(8,128)(2,1)S(1)}, bf16[48,1664]{1,0:T(8,128)(2,1)S(1)}, u32[]{:S(2)}, u32[]{:S(2)}) collective-permute-start(bf16[48,1664]{1,0:T(8,128)(2,1)S(1)} %get-tuple-element.390), channel_id=1, source_target_pairs={{0,24},{2,26},{4,28},{6,30},{8,0},{10,2},{12,4},{14,6},{16,8},{18,... | collective-permute-start | bytes 479240 | tf_op jit(solution)/shard_map/ppermute | solution.py:91
  256.8 3.7 %collective-permute-done.39.refs_0_ = bf16[2,48,3072]{2,1,0:T(8,128)(2,1)S(1)} collective-permute-done((bf16[2,48,3072]{2,1,0:T(8,128)(2,1)S(1)}, bf16[2,48,3072]{2,1,0:T(8,128)(2,1)S(1)}, u32[]{:S(2)}, u32[]{:S(2)}) %collective-permute-start.39) | collective-permute-done | bytes 589856 | tf_op jit(solution)/shard_map/ppermute | solution.py:91
  261.7 3.1 %collective-permute-start.59 = (bf16[48,3072]{1,0:T(8,128)(2,1)S(1)}, bf16[48,3072]{1,0:T(8,128)(2,1)S(1)}, u32[]{:S(2)}, u32[]{:S(2)}) collective-permute-start(bf16[48,3072]{1,0:T(8,128)(2,1)S(1)} %fusion.12), channel_id=1, source_target_pairs={{0,8},{2,10},{4,12},{6,14},{8,16},{10,18},{12,20},{14,22},{16,24},... | collective-permute-start | bytes 884744 | tf_op jit(solution)/shard_map/ppermute | solution.py:91
  265.0 5.7 %collective-permute-done.59.refs_1_ = bf16[48,3072]{1,0:T(8,128)(2,1)S(1)} collective-permute-done((bf16[48,3072]{1,0:T(8,128)(2,1)S(1)}, bf16[48,3072]{1,0:T(8,128)(2,1)S(1)}, u32[]{:S(2)}, u32[]{:S(2)}) %collective-permute-start.59) | collective-permute-done | bytes 294944 | tf_op jit(solution)/shard_map/ppermute | solution.py:91
  280.1 3.0 %collective-permute-start.66 = (f32[8,128]{1,0:T(8,128)S(1)}, f32[8,128]{1,0:T(8,128)S(1)}, u32[]{:S(2)}, u32[]{:S(2)}) collective-permute-start(f32[8,128]{1,0:T(8,128)S(1)} %add_add_fusion.1), channel_id=1, source_target_pairs={{0,24},{1,25},{2,26},{3,27},{4,28},{5,29},{6,30},{7,31},{8,16},{9,... | collective-permute-start | bytes 12296 | tf_op jit(solution)/shard_map/ppermute | solution.py:840
  285.5 3.4 %shard_map.288 = (f32[2,1728,128]{2,1,0:T(8,128)}, f32[2,1728,128]{2,1,0:T(8,128)}, f32[2,1728,128]{2,1,0:T(8,128)}, bf16[2,1728,128]{2,1,0:T(8,128)(2,1)S(1)}) custom-call(f32[8,128]{1,0:T(8,128)S(1)} %add_add_fusion.q_ref.f_ref, f32[2,1728,128]{2,1,0:T(8,128)S(1)} %get-tuple-element.333.w_ref, f32[2,1728,128]{2,1,0:T(8,128)S(1)} %get-tuple-element.334.m_ref, ...), custom_call_target="tpu_custom_call" | custom-call | flops 8847360 | bytes 13271040 | tf_op jit(solution)/shard_map/pallas_call | solution.py:803
  (222 shorter events, 118.1 us)
Async XLA Ops:
  3.8 33.2 %collective-permute-start.3 = (bf16[48,9344]{1,0:T(8,128)(2,1)S(1)}, bf16[48,9344]{1,0:T(8,128)(2,1)S(1)}, u32[]{:S(2)}, u32[]{:S(2)}) collective-permute-start(bf16[48,9344]{1,0:T(8,128)(2,1)S(1)} %get-tuple-element.189), channel_id=1, source_target_pairs={{0,4},{2,6},{4,0},{6,2},{8,12},{10,14},{12,8},{14,10},{16,20},{18,... | collective-permute-start | bytes 2691080 | tf_op jit(solution)/shard_map/ppermute | solution.py:91
  21.2 15.8 %collective-permute-start.4 = (bf16[3,48,1664]{2,1,0:T(8,128)(2,1)S(1)}, bf16[3,48,1664]{2,1,0:T(8,128)(2,1)S(1)}, u32[]{:S(2)}, u32[]{:S(2)}) collective-permute-start(bf16[3,48,1664]{2,1,0:T(8,128)(2,1)S(1)} %shard_map.245), channel_id=1, source_target_pairs={{0,4},{2,6},{4,0},{6,2},{8,12},{10,14},{12,8},{14,10},{16,20},{18,... | collective-permute-start | bytes 1437704 | tf_op jit(solution)/shard_map/ppermute | solution.py:91
  21.8 15.2 %collective-permute-start.5 = (bf16[48,3072]{1,0:T(8,128)(2,1)S(1)}, bf16[48,3072]{1,0:T(8,128)(2,1)S(1)}, u32[]{:S(2)}, u32[]{:S(2)}) collective-permute-start(bf16[48,3072]{1,0:T(8,128)(2,1)S(1)} %get-tuple-element.190.refs_0_), channel_id=1, source_target_pairs={{0,8},{2,10},{4,12},{6,14},{8,16},{10,18},{12,20},{14,22},{16,24},... | collective-permute-start | bytes 884744 | tf_op jit(solution)/shard_map/ppermute | solution.py:91
  25.7 15.3 %collective-permute-start.6 = (bf16[4,48,1664]{2,1,0:T(8,128)(2,1)S(1)}, bf16[4,48,1664]{2,1,0:T(8,128)(2,1)S(1)}, u32[]{:S(2)}, u32[]{:S(2)}) collective-permute-start(bf16[4,48,1664]{2,1,0:T(8,128)(2,1)S(1)} %shard_map.244.refs_0_), channel_id=1, source_target_pairs={{0,2},{2,0},{4,6},{6,4},{8,10},{10,8},{12,14},{14,12},{16,18},{18,... | collective-permute-start | bytes 1916936 | tf_op jit(solution)/shard_map/ppermute | solution.py:91
  47.4 34.3 %collective-permute-start.15 = (bf16[2,256,768]{2,1,0:T(8,128)(2,1)S(1)}, bf16[2,256,768]{2,1,0:T(8,128)(2,1)S(1)}, u32[]{:S(2)}, u32[]{:S(2)}) collective-permute-start(bf16[2,256,768]{2,1,0:T(8,128)(2,1)S(1)} %get-tuple-element.194.own_ref), channel_id=1, source_target_pairs={{0,1},{1,0},{2,3},{3,2},{4,5},{5,4},{6,7},{7,6},{8,9},{9,8},{10,11... | collective-permute-start | bytes 2359304 | tf_op jit(solution)/shard_map/ppermute | solution.py:95
  49.0 22.7 %collective-permute-start.12 = (bf16[48,4608]{1,0:T(8,128)(2,1)S(1)}, bf16[48,4608]{1,0:T(8,128)(2,1)S(1)}, u32[]{:S(2)}, u32[]{:S(2)}) collective-permute-start(bf16[48,4608]{1,0:T(8,128)(2,1)S(1)} %get-tuple-element.196.refs_0_), channel_id=1, source_target_pairs={{0,8},{2,10},{4,12},{6,14},{8,16},{10,18},{12,20},{14,22},{16,24},... | collective-permute-start | bytes 1327112 | tf_op jit(solution)/shard_map/ppermute | solution.py:91
  49.0 21.2 %collective-permute-start.10 = (bf16[48,3072]{1,0:T(8,128)(2,1)S(1)}, bf16[48,3072]{1,0:T(8,128)(2,1)S(1)}, u32[]{:S(2)}, u32[]{:S(2)}) collective-permute-start(bf16[48,3072]{1,0:T(8,128)(2,1)S(1)} %collective-permute-done.5.refs_0_.refs_1_), channel_id=1, source_target_pairs={{0,8},{2,10},{4,12},{6,14},{8,16},{10,18},{12,20},{14,22},{16,24},... | collective-permute-start | bytes 884744 | tf_op jit(solution)/shard_map/ppermute | solution.py:91
  50.5 31.2 %collective-permute-start.9 = (bf16[2,48,3072]{2,1,0:T(8,128)(2,1)S(1)}, bf16[2,48,3072]{2,1,0:T(8,128)(2,1)S(1)}, u32[]{:S(2)}, u32[]{:S(2)}) collective-permute-start(bf16[2,48,3072]{2,1,0:T(8,128)(2,1)S(1)} %shard_map.250), channel_id=1, source_target_pairs={{0,4},{2,6},{4,0},{6,2},{8,12},{10,14},{12,8},{14,10},{16,20},{18,... | collective-permute-start | bytes 1769480 | tf_op jit(solution)/shard_map/ppermute | solution.py:91
  52.1 27.5 %collective-permute-start.13 = (bf16[48,4608]{1,0:T(8,128)(2,1)S(1)}, bf16[48,4608]{1,0:T(8,128)(2,1)S(1)}, u32[]{:S(2)}, u32[]{:S(2)}) collective-permute-start(bf16[48,4608]{1,0:T(8,128)(2,1)S(1)} %get-tuple-element.196.refs_0_), channel_id=1, source_target_pairs={{0,24},{2,26},{4,28},{6,30},{8,0},{10,2},{12,4},{14,6},{16,8},{18,... | collective-permute-start | bytes 1327112 | tf_op jit(solution)/shard_map/ppermute | solution.py:91
  83.7 14.8 %collective-permute-start.21 = (bf16[4,48,1536]{2,1,0:T(8,128)(2,1)S(1)}, bf16[4,48,1536]{2,1,0:T(8,128)(2,1)S(1)}, u32[]{:S(2)}, u32[]{:S(2)}) collective-permute-start(bf16[4,48,1536]{2,1,0:T(8,128)(2,1)S(1)} %shard_map.258.refs_0_), channel_id=1, source_target_pairs={{0,2},{2,0},{4,6},{6,4},{8,10},{10,8},{12,14},{14,12},{16,18},{18,... | collective-permute-start | bytes 1769480 | tf_op jit(solution)/shard_map/ppermute | solution.py:91
  95.5 23.2 %collective-permute-start.28 = (bf16[256,768]{1,0:T(8,128)(2,1)S(1)}, bf16[256,768]{1,0:T(8,128)(2,1)S(1)}, u32[]{:S(2)}, u32[]{:S(2)}) collective-permute-start(bf16[256,768]{1,0:T(8,128)(2,1)S(1)} %get-tuple-element.218.own_ref), channel_id=1, source_target_pairs={{0,1},{1,0},{2,3},{3,2},{4,5},{5,4},{6,7},{7,6},{8,9},{9,8},{10,11... | collective-permute-start | bytes 1179656 | tf_op jit(solution)/shard_map/ppermute | solution.py:95
  97.1 21.4 %collective-permute-start.24 = (bf16[3,48,3072]{2,1,0:T(8,128)(2,1)S(1)}, bf16[3,48,3072]{2,1,0:T(8,128)(2,1)S(1)}, u32[]{:S(2)}, u32[]{:S(2)}) collective-permute-start(bf16[3,48,3072]{2,1,0:T(8,128)(2,1)S(1)} %shard_map.263), channel_id=1, source_target_pairs={{0,4},{2,6},{4,0},{6,2},{8,12},{10,14},{12,8},{14,10},{16,20},{18,... | collective-permute-start | bytes 2654216 | tf_op jit(solution)/shard_map/ppermute | solution.py:91
  98.6 23.4 %collective-permute-start.25 = (bf16[4,48,3072]{2,1,0:T(8,128)(2,1)S(1)}, bf16[4,48,3072]{2,1,0:T(8,128)(2,1)S(1)}, u32[]{:S(2)}, u32[]{:S(2)}) collective-permute-start(bf16[4,48,3072]{2,1,0:T(8,128)(2,1)S(1)} %shard_map.262.refs_0_), channel_id=1, source_target_pairs={{0,2},{2,0},{4,6},{6,4},{8,10},{10,8},{12,14},{14,12},{16,18},{18,... | collective-permute-start | bytes 3538952 | tf_op jit(solution)/shard_map/ppermute | solution.py:91
  125.9 15.9 %collective-permute-start.27 = (bf16[256,768]{1,0:T(8,128)(2,1)S(1)}, bf16[256,768]{1,0:T(8,128)(2,1)S(1)}, u32[]{:S(2)}, u32[]{:S(2)}) collective-permute-start(bf16[256,768]{1,0:T(8,128)(2,1)S(1)} %get-tuple-element.214.own_ref), channel_id=1, source_target_pairs={{0,1},{1,0},{2,3},{3,2},{4,5},{5,4},{6,7},{7,6},{8,9},{9,8},{10,11... | collective-permute-start | bytes 1179656 | tf_op jit(solution)/shard_map/ppermute | solution.py:95
  135.8 14.4 %collective-permute-start.30 = (bf16[256,768]{1,0:T(8,128)(2,1)S(1)}, bf16[256,768]{1,0:T(8,128)(2,1)S(1)}, u32[]{:S(2)}, u32[]{:S(2)}) collective-permute-start(bf16[256,768]{1,0:T(8,128)(2,1)S(1)} %get-tuple-element.224.own_ref), channel_id=1, source_target_pairs={{0,1},{1,0},{2,3},{3,2},{4,5},{5,4},{6,7},{7,6},{8,9},{9,8},{10,11... | collective-permute-start | bytes 1179656 | tf_op jit(solution)/shard_map/ppermute | solution.py:95
  161.6 15.0 %collective-permute-start.34 = (bf16[256,768]{1,0:T(8,128)(2,1)S(1)}, bf16[256,768]{1,0:T(8,128)(2,1)S(1)}, u32[]{:S(2)}, u32[]{:S(2)}) collective-permute-start(bf16[256,768]{1,0:T(8,128)(2,1)S(1)} %get-tuple-element.244.own_ref), channel_id=1, source_target_pairs={{0,1},{1,0},{2,3},{3,2},{4,5},{5,4},{6,7},{7,6},{8,9},{9,8},{10,11... | collective-permute-start | bytes 1179656 | tf_op jit(solution)/shard_map/ppermute | solution.py:95
  163.6 16.9 %collective-permute-start.35 = (bf16[2,48,3072]{2,1,0:T(8,128)(2,1)S(1)}, bf16[2,48,3072]{2,1,0:T(8,128)(2,1)S(1)}, u32[]{:S(2)}, u32[]{:S(2)}) collective-permute-start(bf16[2,48,3072]{2,1,0:T(8,128)(2,1)S(1)} %get-tuple-element.387), channel_id=1, source_target_pairs={{0,8},{2,10},{4,12},{6,14},{8,16},{10,18},{12,20},{14,22},{16,24},... | collective-permute-start | bytes 1769480 | tf_op jit(solution)/shard_map/ppermute | solution.py:91
  178.9 14.8 %collective-permute-start.41 = (bf16[256,768]{1,0:T(8,128)(2,1)S(1)}, bf16[256,768]{1,0:T(8,128)(2,1)S(1)}, u32[]{:S(2)}, u32[]{:S(2)}) collective-permute-start(bf16[256,768]{1,0:T(8,128)(2,1)S(1)} %get-tuple-element.261.own_ref), channel_id=1, source_target_pairs={{0,1},{1,0},{2,3},{3,2},{4,5},{5,4},{6,7},{7,6},{8,9},{9,8},{10,11... | collective-permute-start | bytes 1179656 | tf_op jit(solution)/shard_map/ppermute | solution.py:95
  180.8 16.3 %collective-permute-start.40 = (bf16[2,48,3072]{2,1,0:T(8,128)(2,1)S(1)}, bf16[2,48,3072]{2,1,0:T(8,128)(2,1)S(1)}, u32[]{:S(2)}, u32[]{:S(2)}) collective-permute-start(bf16[2,48,3072]{2,1,0:T(8,128)(2,1)S(1)} %fusion.2), channel_id=1, source_target_pairs={{0,8},{2,10},{4,12},{6,14},{8,16},{10,18},{12,20},{14,22},{16,24},... | collective-permute-start | bytes 1769480 | tf_op jit(solution)/shard_map/ppermute | solution.py:91
  181.2 25.1 %collective-permute-start.44 = (bf16[4,48,1536]{2,1,0:T(8,128)(2,1)S(1)}, bf16[4,48,1536]{2,1,0:T(8,128)(2,1)S(1)}, u32[]{:S(2)}, u32[]{:S(2)}) collective-permute-start(bf16[4,48,1536]{2,1,0:T(8,128)(2,1)S(1)} %fusion.7), channel_id=1, source_target_pairs={{0,4},{2,6},{4,0},{6,2},{8,12},{10,14},{12,8},{14,10},{16,20},{18,... | collective-permute-start | bytes 1769480 | tf_op jit(solution)/shard_map/ppermute | solution.py:91
  197.3 19.1 %collective-permute-start.42 = (bf16[2,48,3072]{2,1,0:T(8,128)(2,1)S(1)}, bf16[2,48,3072]{2,1,0:T(8,128)(2,1)S(1)}, u32[]{:S(2)}, u32[]{:S(2)}) collective-permute-start(bf16[2,48,3072]{2,1,0:T(8,128)(2,1)S(1)} %fusion.1), channel_id=1, source_target_pairs={{0,8},{2,10},{4,12},{6,14},{8,16},{10,18},{12,20},{14,22},{16,24},... | collective-permute-start | bytes 1769480 | tf_op jit(solution)/shard_map/ppermute | solution.py:91
  197.7 14.6 %collective-permute-start.48 = (bf16[2,48,3072]{2,1,0:T(8,128)(2,1)S(1)}, bf16[2,48,3072]{2,1,0:T(8,128)(2,1)S(1)}, u32[]{:S(2)}, u32[]{:S(2)}) collective-permute-start(bf16[2,48,3072]{2,1,0:T(8,128)(2,1)S(1)} %get-tuple-element.384), channel_id=1, source_target_pairs={{0,4},{2,6},{4,0},{6,2},{8,12},{10,14},{12,8},{14,10},{16,20},{18,... | collective-permute-start | bytes 1769480 | tf_op jit(solution)/shard_map/ppermute | solution.py:91
  206.5 20.6 %collective-permute-start.53 = (bf16[48,1536]{1,0:T(8,128)(2,1)S(1)}, bf16[48,1536]{1,0:T(8,128)(2,1)S(1)}, u32[]{:S(2)}, u32[]{:S(2)}) collective-permute-start(bf16[48,1536]{1,0:T(8,128)(2,1)S(1)} %get-tuple-element.395), channel_id=1, source_target_pairs={{0,24},{2,26},{4,28},{6,30},{8,0},{10,2},{12,4},{14,6},{16,8},{18,... | collective-permute-start | bytes 442376 | tf_op jit(solution)/shard_map/ppermute | solution.py:91
  212.3 14.1 %collective-permute-start.52 = (bf16[48,1536]{1,0:T(8,128)(2,1)S(1)}, bf16[48,1536]{1,0:T(8,128)(2,1)S(1)}, u32[]{:S(2)}, u32[]{:S(2)}) collective-permute-start(bf16[48,1536]{1,0:T(8,128)(2,1)S(1)} %get-tuple-element.393), channel_id=1, source_target_pairs={{0,16},{2,18},{4,20},{6,22},{8,24},{10,26},{12,28},{14,30},{16,0},... | collective-permute-start | bytes 442376 | tf_op jit(solution)/shard_map/ppermute | solution.py:91
  213.2 16.3 %collective-permute-start.49 = (bf16[48,3072]{1,0:T(8,128)(2,1)S(1)}, bf16[48,3072]{1,0:T(8,128)(2,1)S(1)}, u32[]{:S(2)}, u32[]{:S(2)}) collective-permute-start(bf16[48,3072]{1,0:T(8,128)(2,1)S(1)} %get-tuple-element.389), channel_id=1, source_target_pairs={{0,24},{2,26},{4,28},{6,30},{8,0},{10,2},{12,4},{14,6},{16,8},{18,... | collective-permute-start | bytes 884744 | tf_op jit(solution)/shard_map/ppermute | solution.py:91
  216.4 28.9 %collective-permute-start.50 = (bf16[48,3072]{1,0:T(8,128)(2,1)S(1)}, bf16[48,3072]{1,0:T(8,128)(2,1)S(1)}, u32[]{:S(2)}, u32[]{:S(2)}) collective-permute-start(bf16[48,3072]{1,0:T(8,128)(2,1)S(1)} %get-tuple-element.388), channel_id=1, source_target_pairs={{0,16},{2,18},{4,20},{6,22},{8,24},{10,26},{12,28},{14,30},{16,0},... | collective-permute-start | bytes 884744 | tf_op jit(solution)/shard_map/ppermute | solution.py:91
  221.8 24.9 %collective-permute-start.47 = (bf16[4,48,1664]{2,1,0:T(8,128)(2,1)S(1)}, bf16[4,48,1664]{2,1,0:T(8,128)(2,1)S(1)}, u32[]{:S(2)}, u32[]{:S(2)}) collective-permute-start(bf16[4,48,1664]{2,1,0:T(8,128)(2,1)S(1)} %fusion.5), channel_id=1, source_target_pairs={{0,4},{2,6},{4,0},{6,2},{8,12},{10,14},{12,8},{14,10},{16,20},{18,... | collective-permute-start | bytes 1916936 | tf_op jit(solution)/shard_map/ppermute | solution.py:91
  226.4 20.7 %collective-permute-start.54 = (bf16[256,768]{1,0:T(8,128)(2,1)S(1)}, bf16[256,768]{1,0:T(8,128)(2,1)S(1)}, u32[]{:S(2)}, u32[]{:S(2)}) collective-permute-start(bf16[256,768]{1,0:T(8,128)(2,1)S(1)} %get-tuple-element.280.refs_1_), channel_id=1, source_target_pairs={{0,1},{1,0},{2,3},{3,2},{4,5},{5,4},{6,7},{7,6},{8,9},{9,8},{10,11... | collective-permute-start | bytes 1179656 | tf_op jit(solution)/shard_map/ppermute | solution.py:95
  227.0 20.7 %collective-permute-start.43 = (bf16[48,3072]{1,0:T(8,128)(2,1)S(1)}, bf16[48,3072]{1,0:T(8,128)(2,1)S(1)}, u32[]{:S(2)}, u32[]{:S(2)}) collective-permute-start(bf16[48,3072]{1,0:T(8,128)(2,1)S(1)} %fusion.13), channel_id=1, source_target_pairs={{0,4},{2,6},{4,0},{6,2},{8,12},{10,14},{12,8},{14,10},{16,20},{18,... | collective-permute-start | bytes 884744 | tf_op jit(solution)/shard_map/ppermute | solution.py:91
  229.6 25.7 %collective-permute-start.55 = (bf16[256,768]{1,0:T(8,128)(2,1)S(1)}, bf16[256,768]{1,0:T(8,128)(2,1)S(1)}, u32[]{:S(2)}, u32[]{:S(2)}) collective-permute-start(bf16[256,768]{1,0:T(8,128)(2,1)S(1)} %get-tuple-element.288.refs_4_), channel_id=1, source_target_pairs={{0,1},{1,0},{2,3},{3,2},{4,5},{5,4},{6,7},{7,6},{8,9},{9,8},{10,11... | collective-permute-start | bytes 1179656 | tf_op jit(solution)/shard_map/ppermute | solution.py:95
  245.3 15.2 %collective-permute-start.39 = (bf16[2,48,3072]{2,1,0:T(8,128)(2,1)S(1)}, bf16[2,48,3072]{2,1,0:T(8,128)(2,1)S(1)}, u32[]{:S(2)}, u32[]{:S(2)}) collective-permute-start(bf16[2,48,3072]{2,1,0:T(8,128)(2,1)S(1)} %get-tuple-element.385), channel_id=1, source_target_pairs={{0,4},{2,6},{4,0},{6,2},{8,12},{10,14},{12,8},{14,10},{16,20},{18,... | collective-permute-start | bytes 1769480 | tf_op jit(solution)/shard_map/ppermute | solution.py:91
  247.1 14.5 %collective-permute-start.57 = (bf16[48,1664]{1,0:T(8,128)(2,1)S(1)}, bf16[48,1664]{1,0:T(8,128)(2,1)S(1)}, u32[]{:S(2)}, u32[]{:S(2)}) collective-permute-start(bf16[48,1664]{1,0:T(8,128)(2,1)S(1)} %get-tuple-element.391), channel_id=1, source_target_pairs={{0,16},{2,18},{4,20},{6,22},{8,24},{10,26},{12,28},{14,30},{16,0},... | collective-permute-start | bytes 479240 | tf_op jit(solution)/shard_map/ppermute | solution.py:91
  (58 other events, 419.3 us)
